TPU v7x, 512 devices: a whole 4x4x16 slice. The times are simulated.
512 devices in a mesh: pipe: 4 (over x), sp: 32 (over z, core), dp: 4 (over y).
Axes of the slice: x: 4, y: 4, z: 16, core: 2. Of those that a mesh axis runs over, the one named last changes fastest.
Arguments:
- fresh_input: bfloat16 [4, 4, 128, 240, 128], P('pipe', 'dp', 'sp'), may hold values from -6 to 6
- saved_input: bfloat16 [4, 4, 128, 240, 128], P('pipe', 'dp', 'sp'), may hold values from -6 to 6
- output_grad: bfloat16 [4, 4, 128, 240, 128], P('pipe', 'dp', 'sp'), may hold values from -6 to 6
- expand_weight: bfloat16 [4, 128, 768], P('pipe'), may hold values from -0.5 to 0.5
- reduce_weight: bfloat16 [4, 768, 128], P('pipe'), may hold values from -0.21875 to 0.21875
- filter_weight: float32 [4, 2, 120, 128], P('pipe'), may hold values from -6 to 6
- cycle_table: int32 [128], replicated, may hold values from 0 to 127, each once
Outputs:
- next_input: bfloat16 [4, 4, 128, 240, 128], P('pipe', 'dp', 'sp')
- input_grad: bfloat16 [4, 4, 128, 240, 128], P('pipe', 'dp', 'sp')
- expand_grad: float32 [4, 128, 768], P('pipe', None, 'dp')
- reduce_grad: float32 [4, 768, 128], P('pipe', 'dp')
- filter_grad: float32 [4, 2, 120, 128], P('pipe')
Inputs may be any that keep to these rules, and one draw needn't show every extreme that they name: `cycle_table`: each of 0 .. 127 appears once; values 120 or more mark empty cycle slots.
All inputs are finite; a program needn't handle non-finite values.
Results may differ from a plain program's by a relative error of at most 0.025.
Values may be sent and summed in bfloat16 or wider, within the bound.
No kernel may reach another device: no remote copies, remote signals or barrier semaphores. Data moves between devices by JAX's collectives and lax.ppermute only.
A program may use at most 64 MiB of HBM per device.

v0:
```python
import math

import jax
import jax.numpy as jnp
from jax import lax
from jax.sharding import Mesh
from jax.sharding import PartitionSpec as P

NLAT = 120
NLON = 240
SP = ("sp_0", "sp_1")
SP_DP = ("sp_0", "sp_1", "dp")


ROOT_HALF = 0.7071067811865476
INV_ROOT_TAU = 0.3989422804014327


def from_behind(block, axis, distance):
    devices = range(lax.axis_size(axis))
    route = [(i - distance, i) for i in devices if i - distance in devices]
    return lax.ppermute(block, axis, route)


def one_axis_at_a_time(shard, axes):
    for axis in axes:
        shard = lax.psum(shard, axis)
    return shard


def in_blocks(shard, dim, peers):
    lengths = shard.shape
    blocks = shard.reshape(*lengths[:dim], peers, lengths[dim] // peers, *lengths[dim + 1 :])
    return jnp.moveaxis(blocks, dim, 0)


def summed_on_arrival(shard, axis, dim):
    blocks = in_blocks(shard, dim, lax.axis_size(axis))
    arrived = lax.all_to_all(blocks, axis, split_axis=0, concat_axis=0, tiled=True)
    return arrived.astype(jnp.float32).sum(axis=0)


def total_of_pieces(shard, axis):
    return lax.all_gather(shard, axis).astype(jnp.float32).sum(0)


def gelu_value(pre_act):
    return 0.5 * pre_act * (1.0 + lax.erf(pre_act * ROOT_HALF))


def gelu_slope(pre_act):
    return (
        0.5 * (1.0 + lax.erf(pre_act * ROOT_HALF))
        + pre_act * jnp.exp(-0.5 * pre_act * pre_act) * INV_ROOT_TAU
    )


def legendre(lat_index, order_index, cycles):
    lat_ok = (lat_index < cycles).astype(jnp.float32)
    order_ok = (order_index < cycles).astype(jnp.float32)
    colatitude = math.pi * (jnp.minimum(lat_index, cycles - 1).astype(jnp.float32) + 0.5) / cycles
    cosine = jnp.cos(colatitude)[None, :]
    sine_value = jnp.sin(colatitude)[None, :]
    order_value = jnp.minimum(order_index, cycles - 1).astype(jnp.float32)[:, None]
    log_start = 0.5 * (
        jnp.log((2.0 * order_value + 1.0) / (4.0 * math.pi))
        + lax.lgamma(2.0 * order_value + 1.0)
        - 2.0 * lax.lgamma(order_value + 1.0)
        - order_value * math.log(4.0)
    ) + order_value * jnp.log(sine_value)
    starting = jnp.exp(log_start)
    zero_rows = jnp.zeros_like(starting)

    def advance(state_pair, degree):
        previous, earlier = state_pair
        degree_value = degree.astype(jnp.float32)
        upper_term = jnp.maximum(4.0 * degree_value * degree_value - 1.0, 0.0)
        ratio_main = jnp.sqrt(
            upper_term / jnp.maximum(degree_value * degree_value - order_value * order_value, 1.0)
        )
        ratio_back = jnp.sqrt(
            jnp.maximum((degree_value - 1.0) ** 2 - order_value * order_value, 0.0)
            / jnp.maximum(4.0 * (degree_value - 1.0) ** 2 - 1.0, 1.0)
        )
        rising = ratio_main * (cosine * previous - ratio_back * earlier)
        current = jnp.where(
            degree_value == order_value,
            starting,
            jnp.where(degree_value > order_value, rising, 0.0),
        )
        return ((current, previous), current)

    _, stacked = lax.scan(advance, (zero_rows, zero_rows), jnp.arange(cycles, dtype=jnp.int32))
    valid_mask = order_ok[:, None] * lat_ok[None, :]
    return jnp.transpose(stacked, (1, 0, 2)) * valid_mask[:, None, :]


def cycle_weights(lat_index, cycles):
    valid_cycle = (lat_index < cycles).astype(jnp.float32)
    colatitude = math.pi * (jnp.minimum(lat_index, cycles - 1).astype(jnp.float32) + 0.5) / cycles
    return math.pi / cycles * jnp.sin(colatitude) * valid_cycle


def fourier_tables(order_index, cycles, points):
    valid_order = (order_index < cycles).astype(jnp.float32)[None, :]
    order_value = jnp.minimum(order_index, cycles - 1)
    longitude = jnp.arange(points, dtype=jnp.int32)
    phase_angle = (
        2.0
        * math.pi
        / points
        * (longitude[:, None] * order_value[None, :] % points).astype(jnp.float32)
    )
    scaled = valid_order * (2.0 * math.pi / points)
    forward = jnp.concatenate(
        [jnp.cos(phase_angle) * scaled, -jnp.sin(phase_angle) * scaled], axis=1
    )
    order_scale = jnp.where(order_value == 0, 1.0, 2.0)[None, :] * valid_order / (2.0 * math.pi)
    inverse = jnp.concatenate(
        [jnp.cos(phase_angle) * order_scale, -jnp.sin(phase_angle) * order_scale], axis=1
    ).T
    return (forward.astype(jnp.bfloat16), inverse.astype(jnp.bfloat16))


def joint_orders(coeffs):
    return lax.all_to_all(coeffs, SP, split_axis=3, concat_axis=1, tiled=True)


def joint_cycles(values):
    return lax.all_to_all(values, SP, split_axis=1, concat_axis=3, tiled=True)


def spectral_pass(tokens, filt, forward, analysis, synthesis, inverse, to_orders, to_cycles):
    batch_count, row_count, points, chan_count = tokens.shape
    order_count = forward.shape[1] // 2
    coeffs = jnp.einsum(
        "sjnc,nk->sjkc", tokens, forward, preferred_element_type=jnp.float32
    ).astype(jnp.bfloat16)
    coeffs = coeffs.reshape(batch_count, row_count, 2, order_count, chan_count)
    arrived = to_orders(coeffs)
    spectra = jnp.einsum("tlj,sjrtc->strlc", analysis, arrived, preferred_element_type=jnp.float32)
    real_part = filt[0] * spectra[:, :, 0] - filt[1] * spectra[:, :, 1]
    imag_part = filt[0] * spectra[:, :, 1] + filt[1] * spectra[:, :, 0]
    filtered = jnp.stack([real_part, imag_part], axis=2).astype(jnp.bfloat16)
    values = jnp.einsum(
        "tlj,strlc->sjrtc", synthesis, filtered, preferred_element_type=jnp.float32
    ).astype(jnp.bfloat16)
    returned = to_cycles(values).reshape(batch_count, row_count, 2 * order_count, chan_count)
    spatial = jnp.einsum("sjkc,kn->sjnc", returned, inverse, preferred_element_type=jnp.float32)
    return (spatial, spectra)


def mlp_pass(tokens, spatial, expand, contract, cycle_mask):
    grid_shape = tokens.shape
    flat_rows = (tokens.astype(jnp.float32) + spatial).reshape(-1, grid_shape[-1])
    mixed_b = flat_rows.astype(jnp.bfloat16)
    hidden_pre = jnp.dot(mixed_b, expand, preferred_element_type=jnp.float32)
    hidden = gelu_value(hidden_pre).astype(jnp.bfloat16)
    result = flat_rows + jnp.dot(hidden, contract, preferred_element_type=jnp.float32)
    result = (result.reshape(grid_shape) * cycle_mask[:, None, None]).astype(jnp.bfloat16)
    return (result, mixed_b, hidden_pre, hidden)


def backward_rows(cotangent, cycle_mask, mixed_b, hidden_pre, hidden, expand, contract):
    chan_count = cotangent.shape[-1]
    masked = (cotangent * cycle_mask.astype(jnp.bfloat16)[:, None, None]).reshape(-1, chan_count)
    grad_reduce = jnp.dot(hidden.T, masked, preferred_element_type=jnp.float32)
    grad_hidden = jnp.dot(masked, contract.T, preferred_element_type=jnp.float32)
    grad_pre = (grad_hidden * gelu_slope(hidden_pre)).astype(jnp.bfloat16)
    grad_expand = jnp.dot(mixed_b.T, grad_pre, preferred_element_type=jnp.float32)
    grad_mixed = masked.astype(jnp.float32) + jnp.dot(
        grad_pre, expand.T, preferred_element_type=jnp.float32
    )
    return (grad_mixed, grad_expand, grad_reduce)


def on_device(
    fresh_input, saved_input, output_grad, expand_weight, reduce_weight, filter_weight, cycle_table
):
    slot_count = fresh_input.shape[2]
    position = lax.axis_index(SP)
    order_table = jnp.arange(slot_count * lax.axis_size(SP), dtype=jnp.int32)
    own_cycles = lax.dynamic_slice_in_dim(cycle_table, position * slot_count, slot_count)
    own_orders = lax.dynamic_slice_in_dim(order_table, position * slot_count, slot_count)
    cycle_mask = (own_cycles < NLAT).astype(jnp.float32)
    table = legendre(cycle_table, own_orders, NLAT)
    analysis = (table * cycle_weights(cycle_table, NLAT)[None, None, :]).astype(jnp.bfloat16)
    synthesis = table.astype(jnp.bfloat16)
    forward, inverse = fourier_tables(order_table, NLAT, NLON)
    filt = filter_weight[0]
    expand = expand_weight[0]
    contract = reduce_weight[0]
    fresh = fresh_input[0, 0]
    saved = saved_input[0, 0]
    spatial, spectra = spectral_pass(
        jnp.stack([fresh, saved]),
        filt,
        forward,
        analysis,
        synthesis,
        inverse,
        joint_orders,
        joint_cycles,
    )
    fresh_spatial = spatial[0]
    saved_spatial = spatial[1]
    saved_spectra = spectra[1]
    block = mlp_pass(fresh, fresh_spatial, expand, contract, cycle_mask)[0]
    next_input = from_behind(block[None, None], "pipe", 1)
    _, mixed_b, hidden_pre, hidden = mlp_pass(saved, saved_spatial, expand, contract, cycle_mask)
    grad_mixed, grad_expand, grad_reduce = backward_rows(
        output_grad[0, 0], cycle_mask, mixed_b, hidden_pre, hidden, expand, contract
    )
    grid_shape = saved.shape
    row_count, points, chan_count = grid_shape
    order_count = forward.shape[1] // 2
    grad_rows = grad_mixed.reshape(grid_shape).astype(jnp.bfloat16)
    grad_values = jnp.einsum(
        "jnc,kn->jkc", grad_rows, inverse, preferred_element_type=jnp.float32
    ).astype(jnp.bfloat16)
    grad_values = grad_values.reshape(row_count, 2, order_count, chan_count)
    arrived = lax.all_to_all(grad_values, SP, split_axis=2, concat_axis=0, tiled=True)
    grad_filtered = jnp.einsum(
        "tlj,jrtc->trlc", synthesis, arrived, preferred_element_type=jnp.float32
    )
    filter_real = jnp.sum(
        grad_filtered[:, 0] * saved_spectra[:, 0] + grad_filtered[:, 1] * saved_spectra[:, 1],
        axis=0,
    )
    filter_imag = jnp.sum(
        grad_filtered[:, 1] * saved_spectra[:, 0] - grad_filtered[:, 0] * saved_spectra[:, 1],
        axis=0,
    )
    grad_spectra = jnp.stack(
        [
            filt[0] * grad_filtered[:, 0] + filt[1] * grad_filtered[:, 1],
            filt[0] * grad_filtered[:, 1] - filt[1] * grad_filtered[:, 0],
        ],
        axis=1,
    ).astype(jnp.bfloat16)
    grad_coeffs = jnp.einsum(
        "tlj,trlc->jrtc", analysis, grad_spectra, preferred_element_type=jnp.float32
    ).astype(jnp.bfloat16)
    returned = lax.all_to_all(grad_coeffs, SP, split_axis=0, concat_axis=2, tiled=True)
    grad_tokens = jnp.einsum(
        "jkc,nk->jnc",
        returned.reshape(row_count, 2 * order_count, chan_count),
        forward,
        preferred_element_type=jnp.float32,
    )
    input_grad = (
        (grad_mixed.reshape(grid_shape) + grad_tokens) * cycle_mask[:, None, None]
    ).astype(jnp.bfloat16)
    sent_back = from_behind(input_grad[None, None], "pipe", -1)
    filter_grad = one_axis_at_a_time(jnp.stack([filter_real, filter_imag]), SP_DP)
    shares = (
        summed_on_arrival(grad_expand.astype(jnp.bfloat16), "dp", 1),
        summed_on_arrival(grad_reduce.astype(jnp.bfloat16), "dp", 0),
    )
    expand_grad, reduce_grad = (
        total_of_pieces(shares[0].astype(jnp.bfloat16), SP).astype(jnp.float32),
        total_of_pieces(shares[1].astype(jnp.bfloat16), SP).astype(jnp.float32),
    )
    return (next_input, sent_back, expand_grad[None], reduce_grad[None], filter_grad[None])


def solution(mesh):
    finer = Mesh(
        mesh.devices.reshape(mesh.shape["pipe"], 16, 2, mesh.shape["dp"]),
        ("pipe", "sp_0", "sp_1", "dp"),
    )
    in_specs = (
        P("pipe", "dp", SP, None, None),
        P("pipe", "dp", SP, None, None),
        P("pipe", "dp", SP, None, None),
        P("pipe", None, None),
        P("pipe", None, None),
        P("pipe", None, None, None),
        P(),
    )
    out_specs = (
        P("pipe", "dp", SP, None, None),
        P("pipe", "dp", SP, None, None),
        P("pipe", None, "dp"),
        P("pipe", "dp", None),
        P("pipe", None, None, None),
    )
    return jax.shard_map(
        on_device, mesh=finer, in_specs=in_specs, out_specs=out_specs, check_vma=False
    )
```

profile of v0, /device:TPU:1, one launch (start us, length us, event | category | flops | bytes accessed | tf_op | source)
XLA Modules:
  0.0 563.0 jit_solution(15364229615342538682)
XLA Ops:
  9.2 1.4 convolution_convert_fusion.1
  10.6 1.3 copy.46
  12.0 16.7 %all-to-all-start = ((bf16[2,4,2,128,128]{4,2,1,0,3:T(2,128)(2,1)}), bf16[2,4,2,128,128]{4,2,1,0,3:T(2,128)(2,1)S(1)}, u32[]{:S(2)}, u32[]{:S(2)}) async-start(bf16[2,4,2,128,128]{4,2,1,0,3:T(2,128)(2,1)} %copy.46), calls=%async_computation | async-start | bytes 1048576 | tf_op jit(solution)/shard_map/all_to_all | solution.py:126
  29.0 164.7 %while.18 = (s32[]{:T(128)}, f32[4,128]{1,0:T(4,128)S(1)}, f32[4,128]{1,0:T(4,128)S(1)}, f32[120,4,128]{2,1,0:T(4,128)S(1)}, s32[120]{0:T(128)S(1)}, /*index=5*/...) while((s32[]{:T(128)}, f32[4,128]{1,0:T(4,128)S(1)}, ...), condition=%wide.region_1.2_spmd.clone, body=%wide.region_0.1_spmd.clone.sunk | while | flops 4654 | bytes 14747 | solution.py:93
  195.7 1.1 copy.50
  196.8 12.3 %all-to-all-start.1 = ((bf16[2,128,2,4,128]{4,2,0,3,1:T(2,128)(2,1)}), bf16[2,128,2,4,128]{4,2,0,3,1:T(2,128)(2,1)S(1)}, u32[]{:S(2)}, u32[]{:S(2)}) async-start(bf16[2,128,2,4,128]{4,2,0,3,1:T(2,128)(2,1)} %copy.50), calls=%async_computation.1 | async-start | bytes 1048576 | tf_op jit(solution)/shard_map/all_to_all | solution.py:130
  210.3 32.4 %all-to-all-done.1 = bf16[2,128,2,4,128]{4,2,0,3,1:T(2,128)(2,1)S(1)} async-done(((bf16[2,128,2,4,128]{4,2,0,3,1:T(2,128)(2,1)}), bf16[2,128,2,4,128]{4,2,0,3,1:T(2,128)(2,1)S(1)}, u32[]{:S(2)}, u32[]{:S(2)}) %all-to-all-start.1) | async-done | bytes 524320 | tf_op jit(solution)/shard_map/all_to_all | solution.py:130
  243.6 1.1 fusion.76
  245.2 1.4 fusion.7
  247.6 1.0 copy.53
  248.6 4.0 all-to-all-start.2
  253.5 1.8 fusion.25
  255.3 19.3 %all-to-all-done.2 = bf16[4,2,128,128]{3,1,0,2:T(2,128)(2,1)S(1)} async-done(((bf16[4,2,128,128]{3,1,0,2:T(2,128)(2,1)}), bf16[4,2,128,128]{3,1,0,2:T(2,128)(2,1)S(1)}, u32[]{:S(2)}, u32[]{:S(2)}) %all-to-all-start.2) | async-done | bytes 262176 | tf_op jit(solution)/shard_map/all_to_all | solution.py:222
  274.7 1.2 convolution_bitcast_fusion.3
  275.8 1.2 add_reduce_fusion
  277.7 1.3 convolution_convert_fusion.4
  279.9 4.3 all-to-all-start.4
  284.2 110.5 %all-reduce.4.cloned.1.call-done = f32[2,120,128]{2,1,0:T(8,128)} async-done(((f32[2,120,128]{2,1,0:T(8,128)}), f32[2,120,128]{2,1,0:T(8,128)}) %all-reduce.4.cloned.1.call-update) | async-done | bytes 122896 | tf_op jit(solution)/shard_map/psum | solution.py:27
  395.7 2.7 fusion.16
  398.4 9.0 %all_to_all.76 = bf16[4,192,128]{2,1,0:T(8,128)(2,1)S(1)} all-to-all(bf16[4,192,128]{2,1,0:T(8,128)(2,1)S(1)} %bitcast.190), channel_id=1, replica_groups=mesh['pipe'=4,'sp_0'=16,'sp_1'=2,'dp'=4] {'dp'}, dimensions={0} | all-to-all | bytes 393216 | tf_op jit(solution)/shard_map/all_to_all | solution.py:39
  409.2 18.6 %all-to-all-start.3 = ((bf16[128,2,4,128]{3,1,2,0:T(2,128)(2,1)}), bf16[128,2,4,128]{3,1,2,0:T(2,128)(2,1)S(1)}, u32[]{:S(2)}, u32[]{:S(2)}) async-start(bf16[128,2,4,128]{3,1,2,0:T(2,128)(2,1)} %copy.57), calls=%async_computation.3 | async-start | bytes 524288 | tf_op jit(solution)/shard_map/all_to_all | solution.py:244
  428.2 1.0 fusion.14
  429.3 3.1 collective-permute-start
  432.4 19.4 %all-to-all-done.3 = bf16[128,2,4,128]{3,1,2,0:T(2,128)(2,1)S(1)} async-done(((bf16[128,2,4,128]{3,1,2,0:T(2,128)(2,1)}), bf16[128,2,4,128]{3,1,2,0:T(2,128)(2,1)S(1)}, u32[]{:S(2)}, u32[]{:S(2)}) %all-to-all-start.3) | async-done | bytes 262176 | tf_op jit(solution)/shard_map/all_to_all | solution.py:244
  452.3 1.3 collective-permute-start.1
  453.7 7.5 %collective-permute-done.1 = bf16[1,1,4,240,128]{4,3,2,1,0:T(8,128)(2,1)S(1)} collective-permute-done((bf16[1,1,4,240,128]{4,3,2,1,0:T(8,128)(2,1)S(1)}, bf16[1,1,4,240,128]{4,3,2,1,0:T(8,128)(2,1)S(1)}, u32[]{:S(2)}, u32[]{:S(2)}) %collective-permute-start.1) | collective-permute-done | bytes 245792 | tf_op jit(solution)/shard_map/ppermute | solution.py:22
  461.2 21.4 %all-gather.5.cloned.1.call-done = bf16[4096,192]{0,1:T(8,128)(2,1)} async-done(((bf16[128,192]{0,1:T(8,128)(2,1)}), bf16[4096,192]{0,1:T(8,128)(2,1)}) %all-gather.5.cloned.1.call-update) | async-done | bytes 1572880 | tf_op jit(solution)/shard_map/all_gather | solution.py:44
  482.6 1.7 convert_bitcast_fusion
  484.9 1.1 bitcast_reduce_fusion
  486.0 64.7 %all-gather.7.cloned.1.call-done = bf16[6144,128]{1,0:T(8,128)(2,1)} async-done(((bf16[192,128]{1,0:T(8,128)(2,1)}), bf16[6144,128]{1,0:T(8,128)(2,1)}) %all-gather.7.cloned.1.call-update) | async-done | bytes 1572880 | tf_op jit(solution)/shard_map/all_gather | solution.py:44
  550.7 2.3 convert_reduce_fusion
  554.4 1.6 copy.104
  (588 shorter events, 98.4 us)
Async XLA Ops:
  8.0 236.7 %copy-start = (bf16[1,128,768]{2,1,0:T(8,128)(2,1)S(1)}, bf16[1,128,768]{2,1,0:T(8,128)(2,1)}, u32[]{:S(2)}) copy-start(bf16[1,128,768]{2,1,0:T(8,128)(2,1)} %param.12) | copy-start | bytes 589828
  8.0 20.9 %copy-start.21 = (s32[128]{0:T(128)S(1)}, s32[128]{0:T(128)}, u32[]{:S(2)}) copy-start(s32[128]{0:T(128)} %param.15) | copy-start | bytes 1540
  8.0 185.8 %copy-start.20 = (f32[1,2,120,128]{3,2,1,0:T(8,128)S(1)}, f32[1,2,120,128]{3,2,1,0:T(8,128)}, u32[]{:S(2)}) copy-start(f32[1,2,120,128]{3,2,1,0:T(8,128)} %param.14) | copy-start | bytes 368644
  8.6 2.0 copy-start.18
  8.6 234.6 %copy-start.6 = (bf16[240,128]{1,0:T(8,128)(2,1)}, bf16[240,128]{1,0:T(8,128)(2,1)S(1)}, u32[]{:S(2)}) copy-start(bf16[240,128]{1,0:T(8,128)(2,1)S(1)} %get-tuple-element.233) | copy-start | bytes 184324
  8.6 234.6 %copy-start.8 = (bf16[240,128]{1,0:T(8,128)(2,1)}, bf16[240,128]{1,0:T(8,128)(2,1)S(1)}, u32[]{:S(2)}) copy-start(bf16[240,128]{1,0:T(8,128)(2,1)S(1)} %get-tuple-element.234) | copy-start | bytes 184324
  12.0 182.7 %all-to-all-start = ((bf16[2,4,2,128,128]{4,2,1,0,3:T(2,128)(2,1)}), bf16[2,4,2,128,128]{4,2,1,0,3:T(2,128)(2,1)S(1)}, u32[]{:S(2)}, u32[]{:S(2)}) async-start(bf16[2,4,2,128,128]{4,2,1,0,3:T(2,128)(2,1)} %copy.46), calls=%async_computation | async-start | bytes 1048576 | tf_op jit(solution)/shard_map/all_to_all | solution.py:126
  194.9 14.4 %copy-start.2 = (bf16[1,1,4,240,128]{4,3,2,1,0:T(8,128)(2,1)S(1)}, bf16[1,1,4,240,128]{4,3,2,1,0:T(8,128)(2,1)}, u32[]{:S(2)}) copy-start(bf16[1,1,4,240,128]{4,3,2,1,0:T(8,128)(2,1)} %param.11) | copy-start | bytes 737284
  196.8 46.7 %copy-start.5 = (bf16[1,1,4,240,128]{4,3,2,1,0:T(8,128)(2,1)S(1)}, bf16[1,1,4,240,128]{4,3,2,1,0:T(8,128)(2,1)}, u32[]{:S(2)}) copy-start(bf16[1,1,4,240,128]{4,3,2,1,0:T(8,128)(2,1)} %param.10) | copy-start | bytes 737284
  196.8 46.7 %copy-start.13 = (bf16[1,1,4,240,128]{4,3,2,1,0:T(8,128)(2,1)S(1)}, bf16[1,1,4,240,128]{4,3,2,1,0:T(8,128)(2,1)}, u32[]{:S(2)}) copy-start(bf16[1,1,4,240,128]{4,3,2,1,0:T(8,128)(2,1)} %param.9) | copy-start | bytes 737284
  196.8 45.8 %all-to-all-start.1 = ((bf16[2,128,2,4,128]{4,2,0,3,1:T(2,128)(2,1)}), bf16[2,128,2,4,128]{4,2,0,3,1:T(2,128)(2,1)S(1)}, u32[]{:S(2)}, u32[]{:S(2)}) async-start(bf16[2,128,2,4,128]{4,2,0,3,1:T(2,128)(2,1)} %copy.50), calls=%async_computation.1 | async-start | bytes 1048576 | tf_op jit(solution)/shard_map/all_to_all | solution.py:130
  210.3 36.4 %copy-start.3 = (bf16[960,128]{1,0:T(8,128)(2,1)}, bf16[960,128]{1,0:T(8,128)(2,1)S(1)}, u32[]{:S(2)}) copy-start(bf16[960,128]{1,0:T(8,128)(2,1)S(1)} %bitcast_multiply_fusion) | copy-start | bytes 737284
  245.2 2.1 copy-start.7
  245.2 2.1 copy-start.9
  248.6 26.0 %all-to-all-start.2 = ((bf16[4,2,128,128]{3,1,0,2:T(2,128)(2,1)}), bf16[4,2,128,128]{3,1,0,2:T(2,128)(2,1)S(1)}, u32[]{:S(2)}, u32[]{:S(2)}) async-start(bf16[4,2,128,128]{3,1,0,2:T(2,128)(2,1)} %copy.53), calls=%async_computation.2 | async-start | bytes 524288 | tf_op jit(solution)/shard_map/all_to_all | solution.py:222
  252.6 142.2 %all-reduce.4.cloned.1.call-start = ((), (), s32[]{:S(2)}) async-start(), calls=%async_computation.6 | async-start | bytes 245760 | tf_op jit(solution)/shard_map/psum | solution.py:27
  274.7 121.0 %copy-start.4 = (bf16[960,128]{1,0:T(8,128)(2,1)S(1)}, bf16[960,128]{1,0:T(8,128)(2,1)}, u32[]{:S(2)}) copy-start(bf16[960,128]{1,0:T(8,128)(2,1)} %copy-done.3) | copy-start | bytes 737284
  279.9 128.1 %copy-start.10 = (bf16[4,120,128,1]{2,0,1,3:T(4,128)(2,1)S(1)}, bf16[4,120,128,1]{2,0,1,3:T(4,128)(2,1)}, u32[]{:S(2)}) copy-start(bf16[4,120,128,1]{2,0,1,3:T(4,128)(2,1)} %get-tuple-element.227) | copy-start | bytes 368644
  279.9 114.9 %all-to-all-start.4 = ((bf16[4,128,192]{1,2,0:T(8,128)(2,1)}), bf16[4,128,192]{1,2,0:T(8,128)(2,1)S(1)}, u32[]{:S(2)}, u32[]{:S(2)}) async-start(bf16[4,128,192]{1,2,0:T(8,128)(2,1)} %bitcast.55), calls=%async_computation.4 | async-start | bytes 393216 | tf_op jit(solution)/shard_map/all_to_all | solution.py:39
  284.2 169.4 %all-reduce.6.cloned.1.call-start = ((), (), s32[]{:S(2)}) async-start(), calls=%async_computation.7 | async-start | bytes 245760 | tf_op jit(solution)/shard_map/psum | solution.py:27
  394.8 87.8 %all-gather.5.cloned.1.call-start = ((), (), s32[]{:S(2)}) async-start(), calls=%async_computation.9 | async-start | bytes 1622016 | tf_op jit(solution)/shard_map/all_gather | solution.py:44
  395.6 32.6 %copy-start.11 = (f32[1,4,240,128]{3,2,1,0:T(8,128)S(1)}, f32[1,4,240,128]{3,2,1,0:T(8,128)}, u32[]{:S(2)}) copy-start(f32[1,4,240,128]{3,2,1,0:T(8,128)} %get-tuple-element.222) | copy-start | bytes 1474564
  395.6 32.6 %copy-start.14 = (bf16[1,1,4,240,128]{4,3,2,1,0:T(8,128)(2,1)S(1)}, bf16[1,1,4,240,128]{4,3,2,1,0:T(8,128)(2,1)}, u32[]{:S(2)}) copy-start(bf16[1,1,4,240,128]{4,3,2,1,0:T(8,128)(2,1)} %param.9) | copy-start | bytes 737284
  395.6 32.6 %copy-start.15 = (bf16[1,4,240,128]{3,2,1,0:T(8,128)(2,1)S(1)}, bf16[1,4,240,128]{3,2,1,0:T(8,128)(2,1)}, u32[]{:S(2)}) copy-start(bf16[1,4,240,128]{3,2,1,0:T(8,128)(2,1)} %get-tuple-element.220) | copy-start | bytes 737284
  395.6 32.6 %copy-start.23 = (bf16[1,768,128]{2,1,0:T(8,128)(2,1)S(1)}, bf16[1,768,128]{2,1,0:T(8,128)(2,1)}, u32[]{:S(2)}) copy-start(bf16[1,768,128]{2,1,0:T(8,128)(2,1)} %param.13) | copy-start | bytes 589828
  395.6 155.1 %all-gather.7.cloned.1.call-start = ((), (), s32[]{:S(2)}) async-start(), calls=%async_computation.10 | async-start | bytes 1622016 | tf_op jit(solution)/shard_map/all_gather | solution.py:44
  409.2 42.5 %all-to-all-start.3 = ((bf16[128,2,4,128]{3,1,2,0:T(2,128)(2,1)}), bf16[128,2,4,128]{3,1,2,0:T(2,128)(2,1)S(1)}, u32[]{:S(2)}, u32[]{:S(2)}) async-start(bf16[128,2,4,128]{3,1,2,0:T(2,128)(2,1)} %copy.57), calls=%async_computation.3 | async-start | bytes 524288 | tf_op jit(solution)/shard_map/all_to_all | solution.py:244
  427.9 125.1 %all-reduce.8.cloned.1.call-start = ((), (), s32[]{:S(2)}) async-start(), calls=%async_computation.8 | async-start | bytes 245760 | tf_op jit(solution)/shard_map/psum | solution.py:27
  428.2 23.9 %copy-start.17 = (bf16[240,128]{1,0:T(8,128)(2,1)S(1)}, bf16[240,128]{1,0:T(8,128)(2,1)}, u32[]{:S(2)}) copy-start(bf16[240,128]{1,0:T(8,128)(2,1)} %copy-done.16) | copy-start | bytes 184324
  428.2 23.9 %copy-start.19 = (bf16[240,128]{1,0:T(8,128)(2,1)S(1)}, bf16[240,128]{1,0:T(8,128)(2,1)}, u32[]{:S(2)}) copy-start(bf16[240,128]{1,0:T(8,128)(2,1)} %copy-done.18) | copy-start | bytes 184324
  429.3 24.3 %collective-permute-start = (bf16[1,1,4,240,128]{4,3,2,1,0:T(8,128)(2,1)S(1)}, bf16[1,1,4,240,128]{4,3,2,1,0:T(8,128)(2,1)S(1)}, u32[]{:S(2)}, u32[]{:S(2)}) collective-permute-start(bf16[1,1,4,240,128]{4,3,2,1,0:T(8,128)(2,1)S(1)} %multiply_convert_fusion.5), channel_id=1, source_target_pairs={{0,128},{128,256},{256,384},{1,129},{129,257},{257,385},{2,130},{1... | collective-permute-start | bytes 737288 | tf_op jit(solution)/shard_map/ppermute | solution.py:22
  452.3 8.9 %collective-permute-start.1 = (bf16[1,1,4,240,128]{4,3,2,1,0:T(8,128)(2,1)S(1)}, bf16[1,1,4,240,128]{4,3,2,1,0:T(8,128)(2,1)S(1)}, u32[]{:S(2)}, u32[]{:S(2)}) collective-permute-start(bf16[1,1,4,240,128]{4,3,2,1,0:T(8,128)(2,1)S(1)} %fusion.18), channel_id=1, source_target_pairs={{128,0},{256,128},{384,256},{129,1},{257,129},{385,257},{130,2},{2... | collective-permute-start | bytes 737288 | tf_op jit(solution)/shard_map/ppermute | solution.py:22
  (4 other events, 5.5 us)
Sparse Core Ops, SparseCore 0:
  277.9 116.8 all-reduce.3
  397.9 45.9 all-reduce.5
  453.8 46.9 all-reduce.7
Sparse Core Ops, SparseCore 1:
  397.9 84.6 all-gather.4
  485.2 65.5 all-gather.6
where the time goes:
time: 565 us; the launch traced here: 563 us
  waiting for transfers between devices  275 us (49%)
  local copies, waits for them, and re-layouts  81.9 us (14%)
  loops' own time  80.9 us (14%)
  starting transfers between devices  60.8 us (11%)
  other arithmetic  27.5 us (5%)
  between operations  15.8 us (3%)
  matrix products  11.8 us (2%)
  blocking collectives  8.99 us (2%)
    psum x3, waiting for transfers between devices, one_axis_at_a_time(): shard = lax.psum(shard, axis)  111 us
    all_gather x2, waiting for transfers between devices, total_of_pieces(): return lax.all_gather(shard, axis).astype(jnp.float32).sum(0)  86.1 us
    another operation x1, loops' own time, legendre(): lax.scan(advance, (zero_rows, zero_rows), jnp.arange(cycles, dtype=jnp.in...  80.9 us
    dynamic_slice x120, local copies, waits for them, and re-layouts, legendre(): lax.scan(advance, (zero_rows, zero_rows), jnp.arange(cycles, dtype=jnp.in...  70.4 us
    all_to_all x1, waiting for transfers between devices, joint_cycles(): return lax.all_to_all(values, SP, split_axis=1, concat_axis=3, tiled=True)  32.4 us
    all_to_all x1, waiting for transfers between devices, on_device(): lax.all_to_all(grad_coeffs, SP, split_axis=0, concat_axis=2, tiled=True)  19.4 us
    all_to_all x1, waiting for transfers between devices, on_device(): lax.all_to_all(grad_values, SP, split_axis=2, concat_axis=0, tiled=True)  19.3 us
    all_to_all x1, starting transfers between devices, on_device(): lax.all_to_all(grad_coeffs, SP, split_axis=0, concat_axis=2, tiled=True)  18.6 us
  transfers between devices with their start and end apart: 12, of which 7 were waited for; matrix products, arithmetic and copies ran while one was open for 18% of the time, Pallas kernels for 0%

commit v1 on v0

v1 whole, which is shorter than its diff:
```python
import functools
import math

import jax
import jax.numpy as jnp
import numpy as np
from jax import lax
from jax.experimental import pallas as pl
from jax.experimental.pallas import tpu as pltpu
from jax.sharding import Mesh
from jax.sharding import PartitionSpec as P

NLAT = 120
NLON = 240
CH = 128
HID = 768
ROWS = 4
PEERS = 32
LANES = 128
SP = ("sp_0", "sp_1")

ROOT_HALF = 0.7071067811865476
INV_ROOT_TAU = 0.3989422804014327
F32 = jnp.float32
BF16 = jnp.bfloat16


def fourier_constants():
    order = np.arange(128)
    live = (order < NLAT).astype(np.float64)
    value = np.minimum(order, NLAT - 1)
    phase = 2.0 * math.pi / NLON * ((np.arange(NLON)[:, None] * value[None, :]) % NLON)
    scaled = live * (2.0 * math.pi / NLON)
    forward = np.stack([np.cos(phase) * scaled, -np.sin(phase) * scaled], axis=1)
    factor = np.where(value == 0, 1.0, 2.0) * live / (2.0 * math.pi)
    inverse = np.stack([np.cos(phase) * factor, -np.sin(phase) * factor], axis=1)

    def arranged(table):
        table = table.reshape(NLON, 2, PEERS, ROWS).transpose(0, 2, 1, 3)
        return table.reshape(NLON, 256).astype(np.float32).astype(jnp.bfloat16)

    return arranged(forward), arranged(inverse)


def order_constants():
    table = np.zeros((PEERS, 3, 8, LANES), np.float32)
    for position in range(PEERS):
        for row in range(8):
            slot = position * ROWS + row % ROWS
            m = min(slot, NLAT - 1)
            log_start = 0.5 * (
                math.log((2.0 * m + 1.0) / (4.0 * math.pi))
                + math.lgamma(2.0 * m + 1.0)
                - 2.0 * math.lgamma(m + 1.0)
                - m * math.log(4.0)
            )
            table[position, 0, row] = m
            table[position, 1, row] = log_start
            table[position, 2, row] = float(slot < NLAT)
    return table


def tables_kernel(geo_ref, order_ref, ana_ref, syn_ref, work_ref):
    shape = (8, LANES)
    cosine = jnp.broadcast_to(geo_ref[0:1, :], shape)
    log_sine = jnp.broadcast_to(geo_ref[1:2, :], shape)
    weight = geo_ref[2:3, :]
    m = order_ref[0]
    keep = order_ref[2] * jnp.broadcast_to(geo_ref[3:4, :], shape)
    starting = jnp.exp(order_ref[1] + m * log_sine)
    squares = m * m
    previous = jnp.zeros(shape, F32)
    earlier = previous
    for degree in range(NLAT):
        upper = max(4.0 * degree * degree - 1.0, 0.0)
        lower = max(4.0 * (degree - 1.0) ** 2 - 1.0, 1.0)
        ratio_main = jnp.sqrt(upper / jnp.maximum(float(degree * degree) - squares, 1.0))
        ratio_back = jnp.sqrt(jnp.maximum((degree - 1.0) ** 2 - squares, 0.0) / lower)
        rising = ratio_main * (cosine * previous - ratio_back * earlier)
        current = jnp.where(m == float(degree), starting, jnp.where(m < float(degree), rising, 0.0))
        work_ref[degree * 8 : degree * 8 + 8, :] = current * keep
        previous, earlier = current, previous
    work_ref[NLAT * 8 :, :] = jnp.zeros((LANES * 8 - NLAT * 8, LANES), F32)
    for t in range(ROWS):
        table = work_ref[pl.ds(t, LANES, stride=8), :]
        syn_ref[t] = table.astype(BF16)
        ana_ref[t] = (table * weight).astype(BF16)


def to_blocks(out_ref, half, pair):
    blocks = [part.reshape(PEERS, 8, CH) for part in pair]
    out_ref[:, 16 * half : 16 * half + 16, :] = jnp.concatenate(blocks, axis=1).astype(BF16)


def from_blocks(block_ref, half):
    pair = block_ref[:, 16 * half : 16 * half + 16, :].astype(F32)
    return [pair[:, 8 * h : 8 * h + 8].reshape(256, CH).astype(BF16) for h in range(2)]


def matmul(left, right, dims=((1,), (0,))):
    return lax.dot_general(left, right, (dims, ((), ())), preferred_element_type=F32)


def coeffs_kernel(x_ref, forward_ref, out_ref):
    for half in range(2):
        to_blocks(out_ref, half, [matmul(forward_ref[...], x_ref[2 * half + h]) for h in range(2)])


def padded_filter(filt_ref):
    rest = jnp.zeros((LANES - NLAT, CH), F32)
    return [jnp.concatenate([filt_ref[part], rest], axis=0) for part in range(2)]


def spectral_kernel(arrived_ref, ana_ref, syn_ref, filt_ref, out_ref, *rest):
    spectra_ref = rest[0] if len(rest) == 3 else None
    came_ref, goes_ref = rest[-2:]
    came_ref[...] = arrived_ref[...].reshape(LANES * 8, CH).astype(F32)
    real, imag = padded_filter(filt_ref)
    for t in range(ROWS):
        parts = [came_ref[pl.ds(r * ROWS + t, LANES, stride=8), :] for r in range(2)]
        spectra = matmul(ana_ref[t], jnp.concatenate(parts, axis=1).astype(BF16))
        if spectra_ref is not None:
            spectra_ref[t] = spectra
        first, second = spectra[:, :CH], spectra[:, CH:]
        filtered = jnp.concatenate(
            [real * first - imag * second, real * second + imag * first], axis=1
        ).astype(BF16)
        values = matmul(syn_ref[t], filtered, ((0,), (0,)))
        for r in range(2):
            goes_ref[pl.ds(r * ROWS + t, LANES, stride=8), :] = values[:, r * CH : (r + 1) * CH]
    out_ref[...] = goes_ref[...].reshape(PEERS, 32, CH).astype(BF16)


def spectral_back_kernel(
    arrived_ref, spectra_ref, ana_ref, syn_ref, filt_ref, out_ref, grad_ref, came_ref, goes_ref
):
    came_ref[...] = arrived_ref[...].reshape(LANES * 8, CH).astype(F32)
    real, imag = padded_filter(filt_ref)
    total_real = jnp.zeros((LANES, CH), F32)
    total_imag = jnp.zeros((LANES, CH), F32)
    for t in range(ROWS):
        parts = [came_ref[pl.ds(r * ROWS + t, LANES, stride=8), :] for r in range(2)]
        grads = matmul(syn_ref[t], jnp.concatenate(parts, axis=1).astype(BF16))
        first, second = grads[:, :CH], grads[:, CH:]
        spectra = spectra_ref[t]
        s_first, s_second = spectra[:, :CH], spectra[:, CH:]
        total_real = total_real + (first * s_first + second * s_second)
        total_imag = total_imag + (second * s_first - first * s_second)
        grad_spectra = jnp.concatenate(
            [real * first + imag * second, real * second - imag * first], axis=1
        ).astype(BF16)
        coeffs = matmul(ana_ref[t], grad_spectra, ((0,), (0,)))
        for r in range(2):
            goes_ref[pl.ds(r * ROWS + t, LANES, stride=8), :] = coeffs[:, r * CH : (r + 1) * CH]
    out_ref[...] = goes_ref[...].reshape(PEERS, 32, CH).astype(BF16)
    grad_ref[0:LANES, :] = total_real.astype(BF16)
    grad_ref[LANES:, :] = total_imag.astype(BF16)


def live(cycle_ref, j):
    return jnp.where(cycle_ref[j] < NLAT, 1.0, 0.0).astype(F32)


def mlp_kernel(x_ref, values_ref, inverse_ref, expand_ref, reduce_ref, cycle_ref, out_ref):
    for half in range(2):
        values = from_blocks(values_ref, half)
        for h in range(2):
            j = 2 * half + h
            mixed = x_ref[j].astype(F32) + matmul(inverse_ref[...], values[h])
            pre = matmul(mixed.astype(BF16), expand_ref[...])
            hidden = (0.5 * pre * (1.0 + lax.erf(pre * ROOT_HALF))).astype(BF16)
            result = mixed + matmul(hidden, reduce_ref[...])
            out_ref[j] = (result * live(cycle_ref, j)).astype(BF16)


def mlp_back_kernel(
    x_ref,
    values_ref,
    cotangent_ref,
    inverse_ref,
    inverse_t_ref,
    expand_ref,
    reduce_ref,
    cycle_ref,
    out_ref,
    grad_mixed_ref,
    shares_ref,
    mixed_ref,
    masked_ref,
    hidden_ref,
    grad_pre_ref,
):
    for half in range(2):
        values = from_blocks(values_ref, half)
        grad_values = []
        for h in range(2):
            j = 2 * half + h
            rows = slice(j * NLON, (j + 1) * NLON)
            mixed = x_ref[j].astype(F32) + matmul(inverse_ref[...], values[h])
            mixed_b = mixed.astype(BF16)
            masked_f = cotangent_ref[j].astype(F32) * live(cycle_ref, j)
            masked = masked_f.astype(BF16)
            mixed_ref[rows, :] = mixed_b
            masked_ref[rows, :] = masked
            pre = matmul(mixed_b, expand_ref[...])
            normal = 0.5 * (1.0 + lax.erf(pre * ROOT_HALF))
            hidden_ref[rows, :] = (pre * normal).astype(BF16)
            slope = normal + pre * jnp.exp(-0.5 * pre * pre) * INV_ROOT_TAU
            grad_hidden = matmul(masked, reduce_ref[...], ((1,), (1,)))
            grad_pre = (grad_hidden * slope).astype(BF16)
            grad_pre_ref[rows, :] = grad_pre
            grad_mixed = masked_f + matmul(grad_pre, expand_ref[...], ((1,), (1,)))
            grad_mixed_ref[j] = grad_mixed
            grad_values.append(matmul(inverse_t_ref[...], grad_mixed.astype(BF16)))
        to_blocks(out_ref, half, grad_values)
    expand_grad = matmul(grad_pre_ref[...], mixed_ref[...], ((0,), (0,))).astype(BF16)
    reduce_grad = matmul(hidden_ref[...], masked_ref[...], ((0,), (0,))).astype(BF16)
    part = HID // 4
    for d in range(4):
        shares_ref[d, :part, :] = expand_grad[d * part : (d + 1) * part]
        shares_ref[d, part:, :] = reduce_grad[d * part : (d + 1) * part]


def input_grad_kernel(coeffs_ref, grad_mixed_ref, forward_ref, cycle_ref, out_ref):
    for half in range(2):
        values = from_blocks(coeffs_ref, half)
        for h in range(2):
            j = 2 * half + h
            total = grad_mixed_ref[j] + matmul(forward_ref[...], values[h])
            out_ref[j] = (total * live(cycle_ref, j)).astype(BF16)


def call(kernel, outs, args, scratch=(), flops=0, transcendentals=0, smem=()):
    specs = [
        pl.BlockSpec(memory_space=pltpu.SMEM if n in smem else pltpu.VMEM) for n in range(len(args))
    ]
    moved = sum(a.size * a.dtype.itemsize for a in (*args, *outs))
    return pl.pallas_call(
        kernel,
        out_shape=outs,
        in_specs=specs,
        out_specs=[pl.BlockSpec(memory_space=pltpu.VMEM)] * len(outs),
        scratch_shapes=list(scratch),
        compiler_params=pltpu.CompilerParams(vmem_limit_bytes=24 * 1024 * 1024),
        cost_estimate=pl.CostEstimate(
            flops=flops, bytes_accessed=moved, transcendentals=transcendentals
        ),
    )(*args)


BLOCKS = jax.ShapeDtypeStruct((PEERS, 32, CH), BF16)
TOKENS = jax.ShapeDtypeStruct((ROWS, NLON, CH), BF16)
SPECTRAL_SCRATCH = (pltpu.VMEM((LANES * 8, CH), F32), pltpu.VMEM((LANES * 8, CH), F32))


def exchange(blocks, axes):
    return lax.all_to_all(blocks, axes, split_axis=0, concat_axis=0, tiled=True)


def spread(block, axes, peers):
    return exchange(jnp.broadcast_to(block[None], (peers, *block.shape)), axes)


def total(blocks):
    return blocks.astype(F32).sum(axis=0)


def from_behind(block, axis, distance):
    devices = range(lax.axis_size(axis))
    route = [(i - distance, i) for i in devices if i - distance in devices]
    return lax.ppermute(block, axis, route)


def filter_total(part):
    halves = total(exchange(part.reshape(2, 128, CH), "sp_1"))
    quarters = total(exchange(halves.astype(BF16).reshape(4, 32, CH), "dp"))
    own = total(spread(quarters.astype(BF16), "sp_0", 16))
    return spread(own, ("sp_1", "dp"), 8).reshape(2, 128, CH)[:, :NLAT]


def share_total(shares):
    rows = 2 * HID // 4
    own = total(exchange(shares, "dp")).astype(BF16)
    piece = total(exchange(own.reshape(PEERS, rows // PEERS, CH), SP)).astype(BF16)
    both = spread(piece, SP, PEERS).astype(F32).reshape(2, HID // 4, CH)
    return both[0].T, both[1]


def on_device(
    forward_np,
    inverse_np,
    orders_np,
    fresh_input,
    saved_input,
    output_grad,
    expand_weight,
    reduce_weight,
    filter_weight,
    cycle_table,
):
    position = lax.axis_index(SP)
    fresh, saved, cotangent = fresh_input[0, 0], saved_input[0, 0], output_grad[0, 0]
    expand, contract, filt = expand_weight[0], reduce_weight[0], filter_weight[0]
    forward = jnp.asarray(forward_np)
    forward_t = jnp.asarray(np.ascontiguousarray(forward_np.T))
    inverse = jnp.asarray(inverse_np)
    inverse_t = jnp.asarray(np.ascontiguousarray(inverse_np.T))
    own_cycles = lax.dynamic_slice_in_dim(cycle_table, position * ROWS, ROWS)
    dft = 2 * ROWS * 256 * NLON * CH
    leg = 2 * 16 * 128 * 128 * CH
    mlp = 2 * ROWS * NLON * CH * HID

    saved_blocks = call(coeffs_kernel, [BLOCKS], [saved, forward_t], flops=dft)[0]
    saved_at_orders = exchange(saved_blocks, SP)
    fresh_blocks = call(coeffs_kernel, [BLOCKS], [fresh, forward_t], flops=dft)[0]
    fresh_at_orders = exchange(fresh_blocks, SP)

    lat_live = (cycle_table < NLAT).astype(F32)
    colatitude = math.pi * (jnp.minimum(cycle_table, NLAT - 1).astype(F32) + 0.5) / NLAT
    sine = jnp.sin(colatitude)
    geo = jnp.stack(
        [jnp.cos(colatitude), jnp.log(sine), math.pi / NLAT * sine * lat_live, lat_live]
    )
    order_rows = lax.dynamic_index_in_dim(jnp.asarray(orders_np), position, 0, keepdims=False)
    tables = jax.ShapeDtypeStruct((ROWS, LANES, LANES), BF16)
    ana, syn = call(
        tables_kernel,
        [tables, tables],
        [geo, order_rows],
        [pltpu.VMEM((LANES * 8, LANES), F32)],
        flops=4_000_000,
    )

    spectra_shape = jax.ShapeDtypeStruct((ROWS, LANES, 2 * CH), F32)
    saved_values, spectra = call(
        spectral_kernel,
        [BLOCKS, spectra_shape],
        [saved_at_orders, ana, syn, filt],
        SPECTRAL_SCRATCH,
        flops=leg,
    )
    saved_at_cycles = exchange(saved_values, SP)
    fresh_values = call(
        spectral_kernel, [BLOCKS], [fresh_at_orders, ana, syn, filt], SPECTRAL_SCRATCH, flops=leg
    )[0]
    fresh_at_cycles = exchange(fresh_values, SP)

    grad_values, grad_mixed, shares = call(
        mlp_back_kernel,
        [
            BLOCKS,
            jax.ShapeDtypeStruct((ROWS, NLON, CH), F32),
            jax.ShapeDtypeStruct((4, 2 * HID // 4, CH), BF16),
        ],
        [saved, saved_at_cycles, cotangent, inverse, inverse_t, expand, contract, own_cycles],
        [
            pltpu.VMEM((ROWS * NLON, CH), BF16),
            pltpu.VMEM((ROWS * NLON, CH), BF16),
            pltpu.VMEM((ROWS * NLON, HID), BF16),
            pltpu.VMEM((ROWS * NLON, HID), BF16),
        ],
        flops=5 * mlp + 2 * dft,
        transcendentals=2 * ROWS * NLON * HID,
        smem=(7,),
    )
    grads_at_orders = exchange(grad_values, SP)
    block = call(
        mlp_kernel,
        [TOKENS],
        [fresh, fresh_at_cycles, inverse, expand, contract, own_cycles],
        flops=2 * mlp + dft,
        transcendentals=ROWS * NLON * HID,
        smem=(5,),
    )[0]
    next_input = from_behind(block[None, None], "pipe", 1)
    expand_grad, reduce_grad = share_total(shares)

    grad_coeffs, filter_part = call(
        spectral_back_kernel,
        [BLOCKS, jax.ShapeDtypeStruct((256, CH), BF16)],
        [grads_at_orders, spectra, ana, syn, filt],
        SPECTRAL_SCRATCH,
        flops=leg,
    )
    coeffs_at_cycles = exchange(grad_coeffs, SP)
    filter_grad = filter_total(filter_part)
    input_grad = call(
        input_grad_kernel,
        [TOKENS],
        [coeffs_at_cycles, grad_mixed, forward, own_cycles],
        flops=dft,
        smem=(3,),
    )[0]
    sent_back = from_behind(input_grad[None, None], "pipe", -1)
    return (next_input, sent_back, expand_grad[None], reduce_grad[None], filter_grad[None])


def solution(mesh):
    finer = Mesh(
        mesh.devices.reshape(mesh.shape["pipe"], 16, 2, mesh.shape["dp"]),
        ("pipe", "sp_0", "sp_1", "dp"),
    )
    in_specs = (
        P("pipe", "dp", SP, None, None),
        P("pipe", "dp", SP, None, None),
        P("pipe", "dp", SP, None, None),
        P("pipe", None, None),
        P("pipe", None, None),
        P("pipe", None, None, None),
        P(),
    )
    out_specs = (
        P("pipe", "dp", SP, None, None),
        P("pipe", "dp", SP, None, None),
        P("pipe", None, "dp"),
        P("pipe", "dp", None),
        P("pipe", None, None, None),
    )
    forward, inverse = fourier_constants()
    program = functools.partial(on_device, forward, inverse, order_constants())
    return jax.shard_map(
        program, mesh=finer, in_specs=in_specs, out_specs=out_specs, check_vma=False
    )
```

time: 565 us -> 276 us (0.49)
  waiting for transfers between devices: 275 us -> 160 us
  loops' own time: 80.9 us -> 0 us
  local copies, waits for them, and re-layouts: 81.9 us -> 8.73 us
  other arithmetic: 27.5 us -> 0.83 us
  between operations: 15.8 us -> 0.89 us
  Pallas kernels: 0 us -> 14.2 us
  matrix products: 11.8 us -> 0 us
  blocking collectives: 8.99 us -> 19.1 us
  starting transfers between devices: 60.8 us -> 70.7 us
    psum x3 -> x0, waiting for transfers between devices: 111 us -> none  [one_axis_at_a_time(): shard = lax.psum(shard, axis)]
    all_gather x2 -> x0, waiting for transfers between devices: 86.1 us -> none  [total_of_pieces(): return lax.all_gather(shard, axis).astype(jnp.float32).sum(0)]
    all_to_all x5 -> x11, waiting for transfers between devices: 71.1 us -> 155 us  [exchange(): return lax.all_to_all(blocks, axes, split_axis=0, concat_axis=0, tiled=True)]
    another operation x1 -> x0, loops' own time: 80.9 us -> none  [legendre(): lax.scan(advance, (zero_rows, zero_rows), jnp.arange(cycles, dtype=jnp.in...]
    dynamic_slice x120 -> x1, local copies, waits for them, and re-layouts: 70.4 us -> 0.08 us  [on_device(): own_cycles = lax.dynamic_slice_in_dim(cycle_table, position * ROWS, ROWS)]
    pallas_call x0 -> x9, Pallas kernels: none -> 14.2 us  [call(): pl.pallas_call(kernel, out_shape=outs, in_specs=specs, out_specs=[pl.Bloc...]
    dot_general x14 -> x0, matrix products: 11.8 us -> none  [the longest x1 2.73 us: backward_rows(): grad_reduce = jnp.dot(hidden.T, masked, preferred_element_type=jnp.float32)]
    dynamic_update_slice x120 -> x0, other arithmetic: 10.8 us -> none  [legendre(): lax.scan(advance, (zero_rows, zero_rows), jnp.arange(cycles, dtype=jnp.in...]
  transfers between devices with their start and end apart: 12 -> 13, of which waited for: 7 -> 12; matrix products, arithmetic and copies ran while one was open for 18% -> 2% of each run, Pallas kernels for 0% -> 4%
where the time goes in v1:
time: 276 us; the launch traced here: 274 us
  waiting for transfers between devices  160 us (58%)
  starting transfers between devices  70.7 us (26%)
  blocking collectives  19.1 us (7%)
  Pallas kernels  14.2 us (5%)
  local copies, waits for them, and re-layouts  8.73 us (3%)
    all_to_all x11, waiting for transfers between devices, exchange(): return lax.all_to_all(blocks, axes, split_axis=0, concat_axis=0, tiled=True)  155 us
    all_to_all x11, starting transfers between devices, exchange(): return lax.all_to_all(blocks, axes, split_axis=0, concat_axis=0, tiled=True)  66.1 us
    all_to_all x2, blocking collectives, exchange(): return lax.all_to_all(blocks, axes, split_axis=0, concat_axis=0, tiled=True)  19.1 us
    pallas_call x9, Pallas kernels, call(): pl.pallas_call(kernel, out_shape=outs, in_specs=specs, out_specs=[pl.Bloc...  14.2 us
  transfers between devices with their start and end apart: 13, of which 12 were waited for; matrix products, arithmetic and copies ran while one was open for 2% of the time, Pallas kernels for 4%

profile of v1, /device:TPU:1, one launch (start us, length us, event | category | flops | bytes accessed | tf_op | source)
XLA Modules:
  0.0 274.5 jit_solution(4467965615019690558)
XLA Ops:
  3.5 16.9 %all-to-all-start.2 = ((bf16[32,32,128]{2,1,0:T(8,128)(2,1)}), bf16[32,32,128]{2,1,0:T(8,128)(2,1)S(1)}, u32[]{:S(2)}, u32[]{:S(2)}) async-start(bf16[32,32,128]{2,1,0:T(8,128)(2,1)} %shard_map.159), calls=%async_computation.2 | async-start | bytes 524288 | tf_op jit(solution)/shard_map/all_to_all | solution.py:257
  22.4 20.0 %all-to-all-done.2.arrived_ref = bf16[32,32,128]{2,1,0:T(8,128)(2,1)S(1)} async-done(((bf16[32,32,128]{2,1,0:T(8,128)(2,1)}), bf16[32,32,128]{2,1,0:T(8,128)(2,1)S(1)}, u32[]{:S(2)}, u32[]{:S(2)}) %all-to-all-start.2) | async-done | bytes 262176 | tf_op jit(solution)/shard_map/all_to_all | solution.py:257
  42.4 1.2 shard_map.160
  43.6 4.6 %all-to-all-start.3 = ((bf16[32,32,128]{2,1,0:T(8,128)(2,1)}), bf16[32,32,128]{2,1,0:T(8,128)(2,1)S(1)}, u32[]{:S(2)}, u32[]{:S(2)}) async-start(bf16[32,32,128]{2,1,0:T(8,128)(2,1)} %get-tuple-element.16), calls=%async_computation.3 | async-start | bytes 524288 | tf_op jit(solution)/shard_map/all_to_all | solution.py:257
  49.3 20.9 %all-to-all-done.3.values_ref = bf16[32,32,128]{2,1,0:T(8,128)(2,1)S(1)} async-done(((bf16[32,32,128]{2,1,0:T(8,128)(2,1)}), bf16[32,32,128]{2,1,0:T(8,128)(2,1)S(1)}, u32[]{:S(2)}, u32[]{:S(2)}) %all-to-all-start.3) | async-done | bytes 262176 | tf_op jit(solution)/shard_map/all_to_all | solution.py:257
  70.2 4.7 %all-to-all-start = ((bf16[32,32,128]{2,1,0:T(8,128)(2,1)}), bf16[32,32,128]{2,1,0:T(8,128)(2,1)S(1)}, u32[]{:S(2)}, u32[]{:S(2)}) async-start(bf16[32,32,128]{2,1,0:T(8,128)(2,1)} %shard_map.155), calls=%async_computation | async-start | bytes 524288 | tf_op jit(solution)/shard_map/all_to_all | solution.py:257
  75.0 5.0 %shard_map.161 = (bf16[32,32,128]{2,1,0:T(8,128)(2,1)}, f32[4,240,128]{2,1,0:T(8,128)S(1)}, bf16[4,384,128]{2,1,0:T(8,128)(2,1)}) custom-call(bf16[4,240,128]{2,1,0:T(8,128)(2,1)S(1)} %bitcast.30, bf16[32,32,128]{2,1,0:T(8,128)(2,1)S(1)} %all-to-all-done.3.values_ref, bf16[4,240,128]{2,1,0:T(8,128)(2,1)S(1)} %bitcast.35, bf16[240,256]{1,0:T(8,128)(2,1)S(1)} %copy-done.11, ...), custom_call_target="tpu_custom_call" | custom-call | flops 1069547520 | bytes 2539536 | tf_op jit(solution)/shard_map/pallas_call | solution.py:238
  80.1 16.8 %all-to-all-done.arrived_ref = bf16[32,32,128]{2,1,0:T(8,128)(2,1)S(1)} async-done(((bf16[32,32,128]{2,1,0:T(8,128)(2,1)}), bf16[32,32,128]{2,1,0:T(8,128)(2,1)S(1)}, u32[]{:S(2)}, u32[]{:S(2)}) %all-to-all-start) | async-done | bytes 262176 | tf_op jit(solution)/shard_map/all_to_all | solution.py:257
  96.9 4.7 %all-to-all-start.4 = ((bf16[32,32,128]{2,1,0:T(8,128)(2,1)}), bf16[32,32,128]{2,1,0:T(8,128)(2,1)S(1)}, u32[]{:S(2)}, u32[]{:S(2)}) async-start(bf16[32,32,128]{2,1,0:T(8,128)(2,1)} %get-tuple-element.17), calls=%async_computation.4 | async-start | bytes 524288 | tf_op jit(solution)/shard_map/all_to_all | solution.py:257
  101.6 1.2 shard_map.157
  102.8 20.8 %all-to-all-done.4.arrived_ref = bf16[32,32,128]{2,1,0:T(8,128)(2,1)S(1)} async-done(((bf16[32,32,128]{2,1,0:T(8,128)(2,1)}), bf16[32,32,128]{2,1,0:T(8,128)(2,1)S(1)}, u32[]{:S(2)}, u32[]{:S(2)}) %all-to-all-start.4) | async-done | bytes 262176 | tf_op jit(solution)/shard_map/all_to_all | solution.py:257
  123.6 4.7 %all-to-all-start.1 = ((bf16[32,32,128]{2,1,0:T(8,128)(2,1)}), bf16[32,32,128]{2,1,0:T(8,128)(2,1)S(1)}, u32[]{:S(2)}, u32[]{:S(2)}) async-start(bf16[32,32,128]{2,1,0:T(8,128)(2,1)} %shard_map.157), calls=%async_computation.1 | async-start | bytes 524288 | tf_op jit(solution)/shard_map/all_to_all | solution.py:257
  128.3 1.2 shard_map.162
  129.5 20.8 %all-to-all-done.1.values_ref = bf16[32,32,128]{2,1,0:T(8,128)(2,1)S(1)} async-done(((bf16[32,32,128]{2,1,0:T(8,128)(2,1)}), bf16[32,32,128]{2,1,0:T(8,128)(2,1)S(1)}, u32[]{:S(2)}, u32[]{:S(2)}) %all-to-all-start.1) | async-done | bytes 262176 | tf_op jit(solution)/shard_map/all_to_all | solution.py:257
  150.3 4.6 %all_to_all.65 = bf16[2,128,128]{2,1,0:T(8,128)(2,1)S(1)} all-to-all(bf16[2,128,128]{2,1,0:T(8,128)(2,1)S(1)} %bitcast.34), channel_id=1, replica_groups=mesh['pipe'=4,'sp_0'=16,'sp_1'=2,'dp'=4] {'sp_1'}, dimensions={0} | all-to-all | bytes 131072 | tf_op jit(solution)/shard_map/all_to_all | solution.py:257
  154.9 4.2 %all-to-all-start.6 = ((bf16[4,384,128]{2,1,0:T(8,128)(2,1)}), bf16[4,384,128]{2,1,0:T(8,128)(2,1)S(1)}, u32[]{:S(2)}, u32[]{:S(2)}) async-start(bf16[4,384,128]{2,1,0:T(8,128)(2,1)} %get-tuple-element.21), calls=%async_computation.6 | async-start | bytes 786432 | tf_op jit(solution)/shard_map/all_to_all | solution.py:257
  159.7 6.6 %all-to-all-done.6 = bf16[4,384,128]{2,1,0:T(8,128)(2,1)S(1)} async-done(((bf16[4,384,128]{2,1,0:T(8,128)(2,1)}), bf16[4,384,128]{2,1,0:T(8,128)(2,1)S(1)}, u32[]{:S(2)}, u32[]{:S(2)}) %all-to-all-start.6) | async-done | bytes 393248 | tf_op jit(solution)/shard_map/all_to_all | solution.py:257
  166.3 3.3 %all-to-all-start.10 = ((bf16[4,32,128]{2,1,0:T(8,128)(2,1)}), bf16[4,32,128]{2,1,0:T(8,128)(2,1)S(1)}, u32[]{:S(2)}, u32[]{:S(2)}) async-start(bf16[4,32,128]{2,1,0:T(8,128)(2,1)} %bitcast.16), calls=%async_computation.10 | async-start | bytes 65536 | tf_op jit(solution)/shard_map/all_to_all | solution.py:257
  170.3 3.5 %all-to-all-done.10 = bf16[4,32,128]{2,1,0:T(8,128)(2,1)S(1)} async-done(((bf16[4,32,128]{2,1,0:T(8,128)(2,1)}), bf16[4,32,128]{2,1,0:T(8,128)(2,1)S(1)}, u32[]{:S(2)}, u32[]{:S(2)}) %all-to-all-start.10) | async-done | bytes 32800 | tf_op jit(solution)/shard_map/all_to_all | solution.py:257
  173.8 6.5 %all-to-all-start.7 = ((bf16[32,12,128]{2,1,0:T(8,128)(2,1)}), bf16[32,12,128]{2,1,0:T(8,128)(2,1)S(1)}, u32[]{:S(2)}, u32[]{:S(2)}) async-start(bf16[32,12,128]{2,1,0:T(8,128)(2,1)} %reshape.29), calls=%async_computation.7 | async-start | bytes 262144 | tf_op jit(solution)/shard_map/all_to_all | solution.py:257
  180.3 16.2 %all-to-all-done.7 = bf16[32,12,128]{2,1,0:T(8,128)(2,1)S(1)} async-done(((bf16[32,12,128]{2,1,0:T(8,128)(2,1)}), bf16[32,12,128]{2,1,0:T(8,128)(2,1)S(1)}, u32[]{:S(2)}, u32[]{:S(2)}) %all-to-all-start.7) | async-done | bytes 98336 | tf_op jit(solution)/shard_map/all_to_all | solution.py:257
  196.5 14.5 %all_to_all.66 = bf16[16,32,128]{2,1,0:T(8,128)(2,1)S(1)} all-to-all(bf16[16,32,128]{2,1,0:T(8,128)(2,1)S(1)} %broadcast_in_dim.34), channel_id=1, replica_groups=mesh['pipe'=4,'sp_0'=16,'sp_1'=2,'dp'=4] {'sp_0'}, dimensions={0} | all-to-all | bytes 262144 | tf_op jit(solution)/shard_map/all_to_all | solution.py:257
  211.0 7.6 %all-to-all-start.5 = ((bf16[32,32,128]{2,1,0:T(8,128)(2,1)}), bf16[32,32,128]{2,1,0:T(8,128)(2,1)S(1)}, u32[]{:S(2)}, u32[]{:S(2)}) async-start(bf16[32,32,128]{2,1,0:T(8,128)(2,1)} %get-tuple-element.19), calls=%async_computation.5 | async-start | bytes 524288 | tf_op jit(solution)/shard_map/all_to_all | solution.py:257
  218.7 22.0 %all-to-all-done.5.coeffs_ref = bf16[32,32,128]{2,1,0:T(8,128)(2,1)S(1)} async-done(((bf16[32,32,128]{2,1,0:T(8,128)(2,1)}), bf16[32,32,128]{2,1,0:T(8,128)(2,1)S(1)}, u32[]{:S(2)}, u32[]{:S(2)}) %all-to-all-start.5) | async-done | bytes 262176 | tf_op jit(solution)/shard_map/all_to_all | solution.py:257
  241.3 4.5 %all-to-all-start.8 = ((bf16[32,12,128]{2,1,0:T(8,128)(2,1)}), bf16[32,12,128]{2,1,0:T(8,128)(2,1)S(1)}, u32[]{:S(2)}, u32[]{:S(2)}) async-start(bf16[32,12,128]{2,1,0:T(8,128)(2,1)} %broadcast_in_dim.32), calls=%async_computation.8 | async-start | bytes 262144 | tf_op jit(solution)/shard_map/all_to_all | solution.py:257
  245.8 2.2 shard_map.158
  248.0 3.3 %collective-permute-start = (bf16[1,1,4,240,128]{4,3,2,1,0:T(8,128)(2,1)S(1)}, bf16[1,1,4,240,128]{4,3,2,1,0:T(8,128)(2,1)S(1)}, u32[]{:S(2)}, u32[]{:S(2)}) collective-permute-start(bf16[1,1,4,240,128]{4,3,2,1,0:T(8,128)(2,1)S(1)} %bitcast.36), channel_id=1, source_target_pairs={{0,128},{128,256},{256,384},{1,129},{129,257},{257,385},{2,130},{1... | collective-permute-start | bytes 737288 | tf_op jit(solution)/shard_map/ppermute | solution.py:271
  251.3 5.0 %collective-permute-done = bf16[1,1,4,240,128]{4,3,2,1,0:T(8,128)(2,1)S(1)} collective-permute-done((bf16[1,1,4,240,128]{4,3,2,1,0:T(8,128)(2,1)S(1)}, bf16[1,1,4,240,128]{4,3,2,1,0:T(8,128)(2,1)S(1)}, u32[]{:S(2)}, u32[]{:S(2)}) %collective-permute-start) | collective-permute-done | bytes 245792 | tf_op jit(solution)/shard_map/ppermute | solution.py:271
  257.1 1.3 collective-permute-start.1
  258.4 3.6 %all-to-all-done.8 = bf16[32,12,128]{2,1,0:T(8,128)(2,1)S(1)} async-done(((bf16[32,12,128]{2,1,0:T(8,128)(2,1)}), bf16[32,12,128]{2,1,0:T(8,128)(2,1)S(1)}, u32[]{:S(2)}, u32[]{:S(2)}) %all-to-all-start.8) | async-done | bytes 98336 | tf_op jit(solution)/shard_map/all_to_all | solution.py:257
  262.7 4.6 %all-to-all-start.12 = ((f32[8,32,128]{2,1,0:T(8,128)}), f32[8,32,128]{2,1,0:T(8,128)S(1)}, u32[]{:S(2)}, u32[]{:S(2)}) async-start(f32[8,32,128]{2,1,0:T(8,128)} %broadcast_in_dim.35), calls=%async_computation.12 | async-start | bytes 262144 | tf_op jit(solution)/shard_map/all_to_all | solution.py:257
  268.6 3.8 %all-to-all-done.12 = f32[8,32,128]{2,1,0:T(8,128)S(1)} async-done(((f32[8,32,128]{2,1,0:T(8,128)}), f32[8,32,128]{2,1,0:T(8,128)S(1)}, u32[]{:S(2)}, u32[]{:S(2)}) %all-to-all-start.12) | async-done | bytes 131104 | tf_op jit(solution)/shard_map/all_to_all | solution.py:257
  (51 shorter events, 13.0 us)
Async XLA Ops:
  0.6 0.9 copy-start.1
  1.5 0.9 copy-start.3
  3.5 38.9 %copy-start = (f32[1,2,120,128]{3,2,1,0:T(8,128)S(1)}, f32[1,2,120,128]{3,2,1,0:T(8,128)}, u32[]{:S(2)}) copy-start(f32[1,2,120,128]{3,2,1,0:T(8,128)} %param.17) | copy-start | bytes 368644
  3.5 38.9 %all-to-all-start.2 = ((bf16[32,32,128]{2,1,0:T(8,128)(2,1)}), bf16[32,32,128]{2,1,0:T(8,128)(2,1)S(1)}, u32[]{:S(2)}, u32[]{:S(2)}) async-start(bf16[32,32,128]{2,1,0:T(8,128)(2,1)} %shard_map.159), calls=%async_computation.2 | async-start | bytes 524288 | tf_op jit(solution)/shard_map/all_to_all | solution.py:257
  20.4 0.7 copy-start.12
  43.6 4.7 %copy-start.2 = (bf16[256,240]{1,0:T(8,128)(2,1)S(1)}, bf16[256,240]{1,0:T(8,128)(2,1)}, u32[]{:S(2)}) copy-start(bf16[256,240]{1,0:T(8,128)(2,1)} %constant.57.clone.forward_ref) | copy-start | bytes 368644
  43.6 4.7 %copy-start.5 = (bf16[1,1,4,240,128]{4,3,2,1,0:T(8,128)(2,1)S(1)}, bf16[1,1,4,240,128]{4,3,2,1,0:T(8,128)(2,1)}, u32[]{:S(2)}) copy-start(bf16[1,1,4,240,128]{4,3,2,1,0:T(8,128)(2,1)} %param.12) | copy-start | bytes 737284
  43.6 26.7 %all-to-all-start.3 = ((bf16[32,32,128]{2,1,0:T(8,128)(2,1)}), bf16[32,32,128]{2,1,0:T(8,128)(2,1)S(1)}, u32[]{:S(2)}, u32[]{:S(2)}) async-start(bf16[32,32,128]{2,1,0:T(8,128)(2,1)} %get-tuple-element.16), calls=%async_computation.3 | async-start | bytes 524288 | tf_op jit(solution)/shard_map/all_to_all | solution.py:257
  48.3 26.8 %copy-start.8 = (bf16[1,128,768]{2,1,0:T(8,128)(2,1)S(1)}, bf16[1,128,768]{2,1,0:T(8,128)(2,1)}, u32[]{:S(2)}) copy-start(bf16[1,128,768]{2,1,0:T(8,128)(2,1)} %param.15) | copy-start | bytes 589828
  48.3 26.7 %copy-start.9 = (bf16[1,768,128]{2,1,0:T(8,128)(2,1)S(1)}, bf16[1,768,128]{2,1,0:T(8,128)(2,1)}, u32[]{:S(2)}) copy-start(bf16[1,768,128]{2,1,0:T(8,128)(2,1)} %param.16) | copy-start | bytes 589828
  48.3 26.7 %copy-start.10 = (bf16[256,240]{1,0:T(8,128)(2,1)S(1)}, bf16[256,240]{1,0:T(8,128)(2,1)}, u32[]{:S(2)}) copy-start(bf16[256,240]{1,0:T(8,128)(2,1)} %constant.59.clone.inverse_t_ref) | copy-start | bytes 368644
  48.3 26.7 %copy-start.11 = (bf16[240,256]{1,0:T(8,128)(2,1)S(1)}, bf16[240,256]{1,0:T(8,128)(2,1)}, u32[]{:S(2)}) copy-start(bf16[240,256]{1,0:T(8,128)(2,1)} %constant.58.clone.inverse_ref) | copy-start | bytes 368644
  49.3 25.7 %copy-start.4 = (bf16[1,1,4,240,128]{4,3,2,1,0:T(8,128)(2,1)S(1)}, bf16[1,1,4,240,128]{4,3,2,1,0:T(8,128)(2,1)}, u32[]{:S(2)}) copy-start(bf16[1,1,4,240,128]{4,3,2,1,0:T(8,128)(2,1)} %param.13) | copy-start | bytes 737284
  49.3 25.7 %copy-start.7 = (bf16[1,1,4,240,128]{4,3,2,1,0:T(8,128)(2,1)S(1)}, bf16[1,1,4,240,128]{4,3,2,1,0:T(8,128)(2,1)}, u32[]{:S(2)}) copy-start(bf16[1,1,4,240,128]{4,3,2,1,0:T(8,128)(2,1)} %param.14) | copy-start | bytes 737284
  70.2 26.7 %all-to-all-start = ((bf16[32,32,128]{2,1,0:T(8,128)(2,1)}), bf16[32,32,128]{2,1,0:T(8,128)(2,1)S(1)}, u32[]{:S(2)}, u32[]{:S(2)}) async-start(bf16[32,32,128]{2,1,0:T(8,128)(2,1)} %shard_map.155), calls=%async_computation | async-start | bytes 524288 | tf_op jit(solution)/shard_map/all_to_all | solution.py:257
  96.9 26.7 %all-to-all-start.4 = ((bf16[32,32,128]{2,1,0:T(8,128)(2,1)}), bf16[32,32,128]{2,1,0:T(8,128)(2,1)S(1)}, u32[]{:S(2)}, u32[]{:S(2)}) async-start(bf16[32,32,128]{2,1,0:T(8,128)(2,1)} %get-tuple-element.17), calls=%async_computation.4 | async-start | bytes 524288 | tf_op jit(solution)/shard_map/all_to_all | solution.py:257
  123.6 26.7 %all-to-all-start.1 = ((bf16[32,32,128]{2,1,0:T(8,128)(2,1)}), bf16[32,32,128]{2,1,0:T(8,128)(2,1)S(1)}, u32[]{:S(2)}, u32[]{:S(2)}) async-start(bf16[32,32,128]{2,1,0:T(8,128)(2,1)} %shard_map.157), calls=%async_computation.1 | async-start | bytes 524288 | tf_op jit(solution)/shard_map/all_to_all | solution.py:257
  154.9 11.4 %all-to-all-start.6 = ((bf16[4,384,128]{2,1,0:T(8,128)(2,1)}), bf16[4,384,128]{2,1,0:T(8,128)(2,1)S(1)}, u32[]{:S(2)}, u32[]{:S(2)}) async-start(bf16[4,384,128]{2,1,0:T(8,128)(2,1)} %get-tuple-element.21), calls=%async_computation.6 | async-start | bytes 786432 | tf_op jit(solution)/shard_map/all_to_all | solution.py:257
  166.3 7.5 %all-to-all-start.10 = ((bf16[4,32,128]{2,1,0:T(8,128)(2,1)}), bf16[4,32,128]{2,1,0:T(8,128)(2,1)S(1)}, u32[]{:S(2)}, u32[]{:S(2)}) async-start(bf16[4,32,128]{2,1,0:T(8,128)(2,1)} %bitcast.16), calls=%async_computation.10 | async-start | bytes 65536 | tf_op jit(solution)/shard_map/all_to_all | solution.py:257
  173.8 22.6 %all-to-all-start.7 = ((bf16[32,12,128]{2,1,0:T(8,128)(2,1)}), bf16[32,12,128]{2,1,0:T(8,128)(2,1)S(1)}, u32[]{:S(2)}, u32[]{:S(2)}) async-start(bf16[32,12,128]{2,1,0:T(8,128)(2,1)} %reshape.29), calls=%async_computation.7 | async-start | bytes 262144 | tf_op jit(solution)/shard_map/all_to_all | solution.py:257
  211.0 29.6 %all-to-all-start.5 = ((bf16[32,32,128]{2,1,0:T(8,128)(2,1)}), bf16[32,32,128]{2,1,0:T(8,128)(2,1)S(1)}, u32[]{:S(2)}, u32[]{:S(2)}) async-start(bf16[32,32,128]{2,1,0:T(8,128)(2,1)} %get-tuple-element.19), calls=%async_computation.5 | async-start | bytes 524288 | tf_op jit(solution)/shard_map/all_to_all | solution.py:257
  241.3 20.7 %all-to-all-start.8 = ((bf16[32,12,128]{2,1,0:T(8,128)(2,1)}), bf16[32,12,128]{2,1,0:T(8,128)(2,1)S(1)}, u32[]{:S(2)}, u32[]{:S(2)}) async-start(bf16[32,12,128]{2,1,0:T(8,128)(2,1)} %broadcast_in_dim.32), calls=%async_computation.8 | async-start | bytes 262144 | tf_op jit(solution)/shard_map/all_to_all | solution.py:257
  248.0 8.3 %copy-start.6 = (bf16[240,256]{1,0:T(8,128)(2,1)S(1)}, bf16[240,256]{1,0:T(8,128)(2,1)}, u32[]{:S(2)}) copy-start(bf16[240,256]{1,0:T(8,128)(2,1)} %constant.56.clone.forward_ref) | copy-start | bytes 368644
  248.0 8.2 %collective-permute-start = (bf16[1,1,4,240,128]{4,3,2,1,0:T(8,128)(2,1)S(1)}, bf16[1,1,4,240,128]{4,3,2,1,0:T(8,128)(2,1)S(1)}, u32[]{:S(2)}, u32[]{:S(2)}) collective-permute-start(bf16[1,1,4,240,128]{4,3,2,1,0:T(8,128)(2,1)S(1)} %bitcast.36), channel_id=1, source_target_pairs={{0,128},{128,256},{256,384},{1,129},{129,257},{257,385},{2,130},{1... | collective-permute-start | bytes 737288 | tf_op jit(solution)/shard_map/ppermute | solution.py:271
  257.1 16.0 %collective-permute-start.1 = (bf16[1,1,4,240,128]{4,3,2,1,0:T(8,128)(2,1)S(1)}, bf16[1,1,4,240,128]{4,3,2,1,0:T(8,128)(2,1)S(1)}, u32[]{:S(2)}, u32[]{:S(2)}) collective-permute-start(bf16[1,1,4,240,128]{4,3,2,1,0:T(8,128)(2,1)S(1)} %bitcast.33), channel_id=1, source_target_pairs={{128,0},{256,128},{384,256},{129,1},{257,129},{385,257},{130,2},{2... | collective-permute-start | bytes 737288 | tf_op jit(solution)/shard_map/ppermute | solution.py:271
  262.7 9.8 %all-to-all-start.12 = ((f32[8,32,128]{2,1,0:T(8,128)}), f32[8,32,128]{2,1,0:T(8,128)S(1)}, u32[]{:S(2)}, u32[]{:S(2)}) async-start(f32[8,32,128]{2,1,0:T(8,128)} %broadcast_in_dim.35), calls=%async_computation.12 | async-start | bytes 262144 | tf_op jit(solution)/shard_map/all_to_all | solution.py:257

commit v2 on v1

--- a/solution.py
+++ b/solution.py
@@ -111,10 +111,7 @@
     return [jnp.concatenate([filt_ref[part], rest], axis=0) for part in range(2)]
 
 
-def spectral_kernel(arrived_ref, ana_ref, syn_ref, filt_ref, out_ref, *rest):
-    spectra_ref = rest[0] if len(rest) == 3 else None
-    came_ref, goes_ref = rest[-2:]
-    came_ref[...] = arrived_ref[...].reshape(LANES * 8, CH).astype(F32)
+def spectral(came_ref, goes_ref, ana_ref, syn_ref, filt_ref, spectra_ref=None):
     real, imag = padded_filter(filt_ref)
     for t in range(ROWS):
         parts = [came_ref[pl.ds(r * ROWS + t, LANES, stride=8), :] for r in range(2)]
@@ -128,12 +125,36 @@
         values = matmul(syn_ref[t], filtered, ((0,), (0,)))
         for r in range(2):
             goes_ref[pl.ds(r * ROWS + t, LANES, stride=8), :] = values[:, r * CH : (r + 1) * CH]
+
+
+def saved_spectral_kernel(
+    arrived_ref, ana_ref, syn_ref, filt_ref, beside_ref, out_ref, spectra_ref, came_ref, goes_ref
+):
+    out_ref[:, 32:, :] = beside_ref[...]
+    came_ref[...] = arrived_ref[...].reshape(LANES * 8, CH).astype(F32)
+    spectral(came_ref, goes_ref, ana_ref, syn_ref, filt_ref, spectra_ref)
+    out_ref[:, :32, :] = goes_ref[...].reshape(PEERS, 32, CH).astype(BF16)
+
+
+def fresh_spectral_kernel(arrived_ref, ana_ref, syn_ref, filt_ref, out_ref, came_ref, goes_ref):
+    came_ref[...] = arrived_ref[:, 32:, :].reshape(LANES * 8, CH).astype(F32)
+    spectral(came_ref, goes_ref, ana_ref, syn_ref, filt_ref)
     out_ref[...] = goes_ref[...].reshape(PEERS, 32, CH).astype(BF16)
 
 
 def spectral_back_kernel(
-    arrived_ref, spectra_ref, ana_ref, syn_ref, filt_ref, out_ref, grad_ref, came_ref, goes_ref
+    arrived_ref,
+    spectra_ref,
+    ana_ref,
+    syn_ref,
+    filt_ref,
+    beside_ref,
+    out_ref,
+    grad_ref,
+    came_ref,
+    goes_ref,
 ):
+    out_ref[:, 32:, :] = beside_ref[...]
     came_ref[...] = arrived_ref[...].reshape(LANES * 8, CH).astype(F32)
     real, imag = padded_filter(filt_ref)
     total_real = jnp.zeros((LANES, CH), F32)
@@ -152,9 +173,9 @@
         coeffs = matmul(ana_ref[t], grad_spectra, ((0,), (0,)))
         for r in range(2):
             goes_ref[pl.ds(r * ROWS + t, LANES, stride=8), :] = coeffs[:, r * CH : (r + 1) * CH]
-    out_ref[...] = goes_ref[...].reshape(PEERS, 32, CH).astype(BF16)
-    grad_ref[0:LANES, :] = total_real.astype(BF16)
-    grad_ref[LANES:, :] = total_imag.astype(BF16)
+    out_ref[:, :32, :] = goes_ref[...].reshape(PEERS, 32, CH).astype(BF16)
+    grad_ref[:NLAT, :] = total_real[:NLAT]
+    grad_ref[NLAT:, :] = total_imag[:NLAT]
 
 
 def live(cycle_ref, j):
@@ -163,7 +184,7 @@
 
 def mlp_kernel(x_ref, values_ref, inverse_ref, expand_ref, reduce_ref, cycle_ref, out_ref):
     for half in range(2):
-        values = from_blocks(values_ref, half)
+        values = from_blocks(values_ref, 2 + half)
         for h in range(2):
             j = 2 * half + h
             mixed = x_ref[j].astype(F32) + matmul(inverse_ref[...], values[h])
@@ -248,6 +269,7 @@
     )(*args)
 
 
+PAIRED = jax.ShapeDtypeStruct((PEERS, 64, CH), BF16)
 BLOCKS = jax.ShapeDtypeStruct((PEERS, 32, CH), BF16)
 TOKENS = jax.ShapeDtypeStruct((ROWS, NLON, CH), BF16)
 SPECTRAL_SCRATCH = (pltpu.VMEM((LANES * 8, CH), F32), pltpu.VMEM((LANES * 8, CH), F32))
@@ -271,19 +293,37 @@
     return lax.ppermute(block, axis, route)
 
 
-def filter_total(part):
-    halves = total(exchange(part.reshape(2, 128, CH), "sp_1"))
-    quarters = total(exchange(halves.astype(BF16).reshape(4, 32, CH), "dp"))
-    own = total(spread(quarters.astype(BF16), "sp_0", 16))
-    return spread(own, ("sp_1", "dp"), 8).reshape(2, 128, CH)[:, :NLAT]
-
-
-def share_total(shares):
-    rows = 2 * HID // 4
-    own = total(exchange(shares, "dp")).astype(BF16)
-    piece = total(exchange(own.reshape(PEERS, rows // PEERS, CH), SP)).astype(BF16)
-    both = spread(piece, SP, PEERS).astype(F32).reshape(2, HID // 4, CH)
-    return both[0].T, both[1]
+def around(block, axis, distance):
+    count = lax.axis_size(axis)
+    return lax.ppermute(block, axis, [(i, (i + distance) % count) for i in range(count)])
+
+
+def scattered_total(blocks, axis):
+    count = lax.axis_size(axis)
+    me = lax.axis_index(axis)
+
+    def block_of(distance):
+        return lax.dynamic_index_in_dim(blocks, (me + distance) % count, 0, keepdims=False)
+
+    came = [around(block_of(k), axis, k) for k in range(1, count)]
+    return sum((block.astype(F32) for block in came), block_of(0).astype(F32))
+
+
+def shares_half(shares):
+    own = scattered_total(shares, "dp").astype(BF16)
+    return scattered_total(own.reshape(2, HID // 4, CH), "sp_1").astype(BF16)
+
+
+def gradient_totals(half, filter_part):
+    rows = HID // 4
+    quarter = scattered_total(filter_part.reshape(4, NLAT // 2, CH), "dp").astype(BF16)
+    mine = total(lax.all_gather(jnp.concatenate([half, quarter]), "sp_0"))
+    other = around(mine, "sp_1", 1)
+    first = lax.axis_index("sp_1") == 0
+    filter_own = mine[rows:] + other[rows:]
+    filter_grad = spread(filter_own, "dp", 4).reshape(2, NLAT, CH)
+    expand_grad = jnp.where(first, mine[:rows], other[:rows]).T
+    return expand_grad, jnp.where(first, other[:rows], mine[:rows]), filter_grad
 
 
 def on_device(
@@ -313,7 +353,6 @@
     saved_blocks = call(coeffs_kernel, [BLOCKS], [saved, forward_t], flops=dft)[0]
     saved_at_orders = exchange(saved_blocks, SP)
     fresh_blocks = call(coeffs_kernel, [BLOCKS], [fresh, forward_t], flops=dft)[0]
-    fresh_at_orders = exchange(fresh_blocks, SP)
 
     lat_live = (cycle_table < NLAT).astype(F32)
     colatitude = math.pi * (jnp.minimum(cycle_table, NLAT - 1).astype(F32) + 0.5) / NLAT
@@ -332,18 +371,14 @@
     )
 
     spectra_shape = jax.ShapeDtypeStruct((ROWS, LANES, 2 * CH), F32)
-    saved_values, spectra = call(
-        spectral_kernel,
-        [BLOCKS, spectra_shape],
-        [saved_at_orders, ana, syn, filt],
+    values_fresh, spectra = call(
+        saved_spectral_kernel,
+        [PAIRED, spectra_shape],
+        [saved_at_orders, ana, syn, filt, fresh_blocks],
         SPECTRAL_SCRATCH,
         flops=leg,
     )
-    saved_at_cycles = exchange(saved_values, SP)
-    fresh_values = call(
-        spectral_kernel, [BLOCKS], [fresh_at_orders, ana, syn, filt], SPECTRAL_SCRATCH, flops=leg
-    )[0]
-    fresh_at_cycles = exchange(fresh_values, SP)
+    values_fresh = exchange(values_fresh, SP)
 
     grad_values, grad_mixed, shares = call(
         mlp_back_kernel,
@@ -352,7 +387,7 @@
             jax.ShapeDtypeStruct((ROWS, NLON, CH), F32),
             jax.ShapeDtypeStruct((4, 2 * HID // 4, CH), BF16),
         ],
-        [saved, saved_at_cycles, cotangent, inverse, inverse_t, expand, contract, own_cycles],
+        [saved, values_fresh, cotangent, inverse, inverse_t, expand, contract, own_cycles],
         [
             pltpu.VMEM((ROWS * NLON, CH), BF16),
             pltpu.VMEM((ROWS * NLON, CH), BF16),
@@ -364,34 +399,37 @@
         smem=(7,),
     )
     grads_at_orders = exchange(grad_values, SP)
+    fresh_values = call(
+        fresh_spectral_kernel, [BLOCKS], [values_fresh, ana, syn, filt], SPECTRAL_SCRATCH, flops=leg
+    )[0]
+    half = shares_half(shares)
+
+    coeffs_fresh, filter_part = call(
+        spectral_back_kernel,
+        [PAIRED, jax.ShapeDtypeStruct((2 * NLAT, CH), F32)],
+        [grads_at_orders, spectra, ana, syn, filt, fresh_values],
+        SPECTRAL_SCRATCH,
+        flops=leg,
+    )
+    coeffs_fresh = exchange(coeffs_fresh, SP)
+    expand_grad, reduce_grad, filter_grad = gradient_totals(half, filter_part)
+    input_grad = call(
+        input_grad_kernel,
+        [TOKENS],
+        [coeffs_fresh, grad_mixed, forward, own_cycles],
+        flops=dft,
+        smem=(3,),
+    )[0]
+    sent_back = from_behind(input_grad[None, None], "pipe", -1)
     block = call(
         mlp_kernel,
         [TOKENS],
-        [fresh, fresh_at_cycles, inverse, expand, contract, own_cycles],
+        [fresh, coeffs_fresh, inverse, expand, contract, own_cycles],
         flops=2 * mlp + dft,
         transcendentals=ROWS * NLON * HID,
         smem=(5,),
     )[0]
     next_input = from_behind(block[None, None], "pipe", 1)
-    expand_grad, reduce_grad = share_total(shares)
-
-    grad_coeffs, filter_part = call(
-        spectral_back_kernel,
-        [BLOCKS, jax.ShapeDtypeStruct((256, CH), BF16)],
-        [grads_at_orders, spectra, ana, syn, filt],
-        SPECTRAL_SCRATCH,
-        flops=leg,
-    )
-    coeffs_at_cycles = exchange(grad_coeffs, SP)
-    filter_grad = filter_total(filter_part)
-    input_grad = call(
-        input_grad_kernel,
-        [TOKENS],
-        [coeffs_at_cycles, grad_mixed, forward, own_cycles],
-        flops=dft,
-        smem=(3,),
-    )[0]
-    sent_back = from_behind(input_grad[None, None], "pipe", -1)
     return (next_input, sent_back, expand_grad[None], reduce_grad[None], filter_grad[None])
 
 

time: 276 us -> 209 us (0.76)
  waiting for transfers between devices: 160 us -> 86.8 us
  blocking collectives: 19.1 us -> 29.8 us
    all_to_all x11 -> x5, waiting for transfers between devices: 155 us -> 79.4 us  [exchange(): return lax.all_to_all(blocks, axes, split_axis=0, concat_axis=0, tiled=True)]
    all_to_all x11 -> x5, starting transfers between devices: 66.1 us -> 33.6 us  [exchange(): return lax.all_to_all(blocks, axes, split_axis=0, concat_axis=0, tiled=True)]
    ppermute x0 -> x8, starting transfers between devices: none -> 31.3 us  [around(): lax.ppermute(block, axis, [(i, (i + distance) % count) for i in range(cou...]
    all_gather x0 -> x1, blocking collectives: none -> 29.8 us  [gradient_totals(): mine = total(lax.all_gather(jnp.concatenate([half, quarter]), 'sp_0'))]
    all_to_all x2 -> x0, blocking collectives: 19.1 us -> none  [exchange(): return lax.all_to_all(blocks, axes, split_axis=0, concat_axis=0, tiled=True)]
    ppermute x0 -> x8, waiting for transfers between devices: none -> 7.47 us  [around(): lax.ppermute(block, axis, [(i, (i + distance) % count) for i in range(cou...]
    ppermute x2, waiting for transfers between devices: 4.96 us -> 0.01 us  [from_behind(): return lax.ppermute(block, axis, route)]
  transfers between devices with their start and end apart: 13 -> 15, of which waited for: 12 -> 8; matrix products, arithmetic and copies ran while one was open for 2% -> 2% of each run, Pallas kernels for 4% -> 2%
where the time goes in v2:
time: 209 us; the launch traced here: 207 us
  waiting for transfers between devices  86.8 us (42%)
  starting transfers between devices  69.4 us (33%)
  blocking collectives  29.8 us (14%)
  Pallas kernels  12.3 us (6%)
  local copies, waits for them, and re-layouts  6.44 us (3%)
    all_to_all x5, waiting for transfers between devices, exchange(): return lax.all_to_all(blocks, axes, split_axis=0, concat_axis=0, tiled=True)  79.4 us
    all_to_all x5, starting transfers between devices, exchange(): return lax.all_to_all(blocks, axes, split_axis=0, concat_axis=0, tiled=True)  33.6 us
    ppermute x8, starting transfers between devices, around(): lax.ppermute(block, axis, [(i, (i + distance) % count) for i in range(cou...  31.3 us
    all_gather x1, blocking collectives, gradient_totals(): mine = total(lax.all_gather(jnp.concatenate([half, quarter]), 'sp_0'))  29.8 us
    pallas_call x9, Pallas kernels, call(): pl.pallas_call(kernel, out_shape=outs, in_specs=specs, out_specs=[pl.Bloc...  12.3 us
    ppermute x8, waiting for transfers between devices, around(): lax.ppermute(block, axis, [(i, (i + distance) % count) for i in range(cou...  7.47 us
    ppermute x2, starting transfers between devices, from_behind(): return lax.ppermute(block, axis, route)  4.42 us
    unnamed x32, local copies, waits for them, and re-layouts  4.25 us
  transfers between devices with their start and end apart: 15, of which 8 were waited for; matrix products, arithmetic and copies ran while one was open for 2% of the time, Pallas kernels for 2%

profile of v2, /device:TPU:1, one launch (start us, length us, event | category | flops | bytes accessed | tf_op | source)
XLA Modules:
  0.0 206.9 jit_solution(10519453990034214484)
XLA Ops:
  0.7 0.9 copy-done.1
  1.6 0.9 copy-done.3
  2.5 1.0 shard_map.155
  3.5 16.7 %all-to-all-start = ((bf16[32,32,128]{2,1,0:T(8,128)(2,1)}), bf16[32,32,128]{2,1,0:T(8,128)(2,1)S(1)}, u32[]{:S(2)}, u32[]{:S(2)}) async-start(bf16[32,32,128]{2,1,0:T(8,128)(2,1)} %shard_map.155), calls=%async_computation | async-start | bytes 524288 | tf_op jit(solution)/shard_map/all_to_all | solution.py:279
  22.0 20.2 %all-to-all-done.arrived_ref = bf16[32,32,128]{2,1,0:T(8,128)(2,1)S(1)} async-done(((bf16[32,32,128]{2,1,0:T(8,128)(2,1)}), bf16[32,32,128]{2,1,0:T(8,128)(2,1)S(1)}, u32[]{:S(2)}, u32[]{:S(2)}) %all-to-all-start) | async-done | bytes 262176 | tf_op jit(solution)/shard_map/all_to_all | solution.py:279
  42.3 1.3 shard_map.158
  43.6 4.5 %all-to-all-start.1 = ((bf16[32,64,128]{2,1,0:T(8,128)(2,1)}), bf16[32,64,128]{2,1,0:T(8,128)(2,1)S(1)}, u32[]{:S(2)}, u32[]{:S(2)}) async-start(bf16[32,64,128]{2,1,0:T(8,128)(2,1)} %get-tuple-element.16), calls=%async_computation.1 | async-start | bytes 1048576 | tf_op jit(solution)/shard_map/all_to_all | solution.py:279
  48.2 33.5 %all-to-all-done.1.values_ref.arrived_ref = bf16[32,64,128]{2,1,0:T(8,128)(2,1)S(1)} async-done(((bf16[32,64,128]{2,1,0:T(8,128)(2,1)}), bf16[32,64,128]{2,1,0:T(8,128)(2,1)S(1)}, u32[]{:S(2)}, u32[]{:S(2)}) %all-to-all-start.1) | async-done | bytes 524320 | tf_op jit(solution)/shard_map/all_to_all | solution.py:279
  81.7 0.9 copy-done.9
  82.6 4.3 %shard_map.159 = (bf16[32,32,128]{2,1,0:T(8,128)(2,1)}, f32[4,240,128]{2,1,0:T(8,128)S(1)}, bf16[4,384,128]{2,1,0:T(8,128)(2,1)S(1)}) custom-call(bf16[4,240,128]{2,1,0:T(8,128)(2,1)S(1)} %bitcast.60, bf16[32,64,128]{2,1,0:T(8,128)(2,1)S(1)} %all-to-all-done.1.values_ref.arrived_ref, bf16[4,240,128]{2,1,0:T(8,128)(2,1)S(1)} %bitcast.63, ...), custom_call_target="tpu_custom_call" | custom-call | flops 1069547520 | bytes 2801680 | tf_op jit(solution)/shard_map/pallas_call | solution.py:259
  87.0 4.3 %all-to-all-start.2 = ((bf16[32,32,128]{2,1,0:T(8,128)(2,1)}), bf16[32,32,128]{2,1,0:T(8,128)(2,1)S(1)}, u32[]{:S(2)}, u32[]{:S(2)}) async-start(bf16[32,32,128]{2,1,0:T(8,128)(2,1)} %get-tuple-element.17), calls=%async_computation.2 | async-start | bytes 524288 | tf_op jit(solution)/shard_map/all_to_all | solution.py:279
  91.8 21.5 %all-to-all-done.2.arrived_ref = bf16[32,32,128]{2,1,0:T(8,128)(2,1)S(1)} async-done(((bf16[32,32,128]{2,1,0:T(8,128)(2,1)}), bf16[32,32,128]{2,1,0:T(8,128)(2,1)S(1)}, u32[]{:S(2)}, u32[]{:S(2)}) %all-to-all-start.2) | async-done | bytes 262176 | tf_op jit(solution)/shard_map/all_to_all | solution.py:279
  113.3 1.3 shard_map.161
  114.6 4.7 %all-to-all-start.3 = ((bf16[32,64,128]{2,1,0:T(8,128)(2,1)}), bf16[32,64,128]{2,1,0:T(8,128)(2,1)S(1)}, u32[]{:S(2)}, u32[]{:S(2)}) async-start(bf16[32,64,128]{2,1,0:T(8,128)(2,1)} %get-tuple-element.19), calls=%async_computation.3 | async-start | bytes 1048576 | tf_op jit(solution)/shard_map/all_to_all | solution.py:279
  119.4 4.6 %collective-permute-start.4 = (bf16[384,128]{1,0:T(8,128)(2,1)S(1)}, bf16[384,128]{1,0:T(8,128)(2,1)S(1)}, u32[]{:S(2)}, u32[]{:S(2)}) collective-permute-start(bf16[384,128]{1,0:T(8,128)(2,1)S(1)} %get-tuple-element.24), channel_id=1, source_target_pairs={{0,3},{1,0},{2,1},{3,2},{4,7},{5,4},{6,5},{7,6},{8,11},{9,8},{10,9... | collective-permute-start | bytes 294920 | tf_op jit(solution)/shard_map/ppermute | solution.py:298
  124.0 2.3 %collective-permute-start.3 = (bf16[384,128]{1,0:T(8,128)(2,1)S(1)}, bf16[384,128]{1,0:T(8,128)(2,1)S(1)}, u32[]{:S(2)}, u32[]{:S(2)}) collective-permute-start(bf16[384,128]{1,0:T(8,128)(2,1)S(1)} %get-tuple-element.25), channel_id=1, source_target_pairs={{0,2},{1,3},{2,0},{3,1},{4,6},{5,7},{6,4},{7,5},{8,10},{9,11},{10,... | collective-permute-start | bytes 294920 | tf_op jit(solution)/shard_map/ppermute | solution.py:298
  126.3 2.6 %collective-permute-start.2 = (bf16[384,128]{1,0:T(8,128)(2,1)S(1)}, bf16[384,128]{1,0:T(8,128)(2,1)S(1)}, u32[]{:S(2)}, u32[]{:S(2)}) collective-permute-start(bf16[384,128]{1,0:T(8,128)(2,1)S(1)} %get-tuple-element.23), channel_id=1, source_target_pairs={{0,1},{1,2},{2,3},{3,0},{4,5},{5,6},{6,7},{7,4},{8,9},{9,10},{10,1... | collective-permute-start | bytes 294920 | tf_op jit(solution)/shard_map/ppermute | solution.py:298
  129.0 2.2 %collective-permute-done.3 = bf16[384,128]{1,0:T(8,128)(2,1)S(1)} collective-permute-done((bf16[384,128]{1,0:T(8,128)(2,1)S(1)}, bf16[384,128]{1,0:T(8,128)(2,1)S(1)}, u32[]{:S(2)}, u32[]{:S(2)}) %collective-permute-start.3) | collective-permute-done | bytes 98336 | tf_op jit(solution)/shard_map/ppermute | solution.py:298
  131.2 2.2 %collective-permute-done.2 = bf16[384,128]{1,0:T(8,128)(2,1)S(1)} collective-permute-done((bf16[384,128]{1,0:T(8,128)(2,1)S(1)}, bf16[384,128]{1,0:T(8,128)(2,1)S(1)}, u32[]{:S(2)}, u32[]{:S(2)}) %collective-permute-start.2) | collective-permute-done | bytes 98336 | tf_op jit(solution)/shard_map/ppermute | solution.py:298
  133.5 3.5 %collective-permute-start.5 = (bf16[192,128]{1,0:T(8,128)(2,1)S(1)}, bf16[192,128]{1,0:T(8,128)(2,1)S(1)}, u32[]{:S(2)}, u32[]{:S(2)}) collective-permute-start(bf16[192,128]{1,0:T(8,128)(2,1)S(1)} %dynamic-slice_bitcast_fusion.3), channel_id=1, source_target_pairs={{0,4},{4,0},{1,5},{5,1},{2,6},{6,2},{3,7},{7,3},{8,12},{12,8},{9,1... | collective-permute-start | bytes 147464 | tf_op jit(solution)/shard_map/ppermute | solution.py:298
  137.0 2.0 collective-permute-start.8
  139.0 3.2 %collective-permute-start.7 = (f32[60,128]{1,0:T(8,128)S(1)}, f32[60,128]{1,0:T(8,128)S(1)}, u32[]{:S(2)}, u32[]{:S(2)}) collective-permute-start(f32[60,128]{1,0:T(8,128)S(1)} %get-tuple-element.30), channel_id=1, source_target_pairs={{0,2},{1,3},{2,0},{3,1},{4,6},{5,7},{6,4},{7,5},{8,10},{9,11},{10,... | collective-permute-start | bytes 92168 | tf_op jit(solution)/shard_map/ppermute | solution.py:298
  142.2 2.8 %collective-permute-start.6 = (f32[60,128]{1,0:T(8,128)S(1)}, f32[60,128]{1,0:T(8,128)S(1)}, u32[]{:S(2)}, u32[]{:S(2)}) collective-permute-start(f32[60,128]{1,0:T(8,128)S(1)} %get-tuple-element.28), channel_id=1, source_target_pairs={{0,1},{1,2},{2,3},{3,0},{4,5},{5,6},{6,7},{7,4},{8,9},{9,10},{10,1... | collective-permute-start | bytes 92168 | tf_op jit(solution)/shard_map/ppermute | solution.py:298
  145.2 2.9 %collective-permute-done.6 = f32[60,128]{1,0:T(8,128)S(1)} collective-permute-done((f32[60,128]{1,0:T(8,128)S(1)}, f32[60,128]{1,0:T(8,128)S(1)}, u32[]{:S(2)}, u32[]{:S(2)}) %collective-permute-start.6) | collective-permute-done | bytes 30752 | tf_op jit(solution)/shard_map/ppermute | solution.py:298
  148.2 29.8 %all-gather.1 = bf16[16,252,128]{2,1,0:T(8,128)(2,1)S(1)} all-gather(bf16[1,252,128]{2,1,0:T(8,128)(2,1)S(1)} %maximum_bitcast_fusion), channel_id=2, replica_groups=mesh['pipe'=4,'sp_0'=16,'sp_1'=2,'dp'=4] {'sp_0'}, dimensions={0}, use_global_device_ids=true | all-gather | bytes 1096704 | tf_op jit(solution)/shard_map/all_gather | solution.py:320
  178.1 10.4 %collective-permute-start.9 = (f32[252,128]{1,0:T(8,128)S(1)}, f32[252,128]{1,0:T(8,128)S(1)}, u32[]{:S(2)}, u32[]{:S(2)}) collective-permute-start(f32[252,128]{1,0:T(8,128)S(1)} %convert_reduce_fusion), channel_id=1, source_target_pairs={{0,4},{4,0},{1,5},{5,1},{2,6},{6,2},{3,7},{7,3},{8,12},{12,8},{9,1... | collective-permute-start | bytes 387080 | tf_op jit(solution)/shard_map/ppermute | solution.py:298
  188.5 2.2 %shard_map.162 = bf16[4,240,128]{2,1,0:T(8,128)(2,1)S(1)} custom-call(bf16[4,240,128]{2,1,0:T(8,128)(2,1)S(1)} %bitcast.62, bf16[32,64,128]{2,1,0:T(8,128)(2,1)S(1)} %all-to-all-done.3.values_ref.coeffs_ref, bf16[240,256]{1,0:T(8,128)(2,1)S(1)} %copy-done.13, bf16[128,768]{1,0:T(8,128)(2,1)S(1)} %bitcast.66, bf16[768,128]{1,0:T(8,128)(2,1)S(1)} %bitcast.68, ...), custom_call_target="tpu_custom_call" | custom-call | flops 440401920 | bytes 1531920 | tf_op jit(solution)/shard_map/pallas_call | solution.py:259
  190.7 3.1 %collective-permute-start = (bf16[1,1,4,240,128]{4,3,2,1,0:T(8,128)(2,1)S(1)}, bf16[1,1,4,240,128]{4,3,2,1,0:T(8,128)(2,1)S(1)}, u32[]{:S(2)}, u32[]{:S(2)}) collective-permute-start(bf16[1,1,4,240,128]{4,3,2,1,0:T(8,128)(2,1)S(1)} %bitcast.64), channel_id=1, source_target_pairs={{0,128},{128,256},{256,384},{1,129},{129,257},{257,385},{2,130},{1... | collective-permute-start | bytes 737288 | tf_op jit(solution)/shard_map/ppermute | solution.py:293
  193.9 0.8 shard_map.163
  194.7 1.3 collective-permute-start.1
  196.7 3.3 %all-to-all-start.4 = ((f32[4,60,128]{2,1,0:T(8,128)}), f32[4,60,128]{2,1,0:T(8,128)S(1)}, u32[]{:S(2)}, u32[]{:S(2)}) async-start(f32[4,60,128]{2,1,0:T(8,128)} %broadcast_in_dim.22), calls=%async_computation.4 | async-start | bytes 262144 | tf_op jit(solution)/shard_map/all_to_all | solution.py:279
  200.7 4.1 %all-to-all-done.4 = f32[4,60,128]{2,1,0:T(8,128)S(1)} async-done(((f32[4,60,128]{2,1,0:T(8,128)}), f32[4,60,128]{2,1,0:T(8,128)S(1)}, u32[]{:S(2)}, u32[]{:S(2)}) %all-to-all-start.4) | async-done | bytes 122912 | tf_op jit(solution)/shard_map/all_to_all | solution.py:279
  (58 shorter events, 6.2 us)
Async XLA Ops:
  0.6 41.7 %copy-start = (f32[1,2,120,128]{3,2,1,0:T(8,128)S(1)}, f32[1,2,120,128]{3,2,1,0:T(8,128)}, u32[]{:S(2)}) copy-start(f32[1,2,120,128]{3,2,1,0:T(8,128)} %param.17) | copy-start | bytes 368644
  0.6 0.9 copy-start.1
  1.6 0.9 copy-start.3
  2.5 17.8 %copy-start.14 = (s32[128]{0:T(128)S(1)}, s32[128]{0:T(128)}, u32[]{:S(2)}) copy-start(s32[128]{0:T(128)} %param.18) | copy-start | bytes 1540
  2.5 19.1 %copy-start.2 = (bf16[256,240]{1,0:T(8,128)(2,1)S(1)}, bf16[256,240]{1,0:T(8,128)(2,1)}, u32[]{:S(2)}) copy-start(bf16[256,240]{1,0:T(8,128)(2,1)} %constant.124.clone.forward_ref) | copy-start | bytes 368644
  2.5 19.1 %copy-start.5 = (bf16[1,1,4,240,128]{4,3,2,1,0:T(8,128)(2,1)S(1)}, bf16[1,1,4,240,128]{4,3,2,1,0:T(8,128)(2,1)}, u32[]{:S(2)}) copy-start(bf16[1,1,4,240,128]{4,3,2,1,0:T(8,128)(2,1)} %param.12) | copy-start | bytes 737284
  3.5 38.7 %all-to-all-start = ((bf16[32,32,128]{2,1,0:T(8,128)(2,1)}), bf16[32,32,128]{2,1,0:T(8,128)(2,1)S(1)}, u32[]{:S(2)}, u32[]{:S(2)}) async-start(bf16[32,32,128]{2,1,0:T(8,128)(2,1)} %shard_map.155), calls=%async_computation | async-start | bytes 524288 | tf_op jit(solution)/shard_map/all_to_all | solution.py:279
  22.0 59.7 %copy-start.4 = (bf16[1,1,4,240,128]{4,3,2,1,0:T(8,128)(2,1)S(1)}, bf16[1,1,4,240,128]{4,3,2,1,0:T(8,128)(2,1)}, u32[]{:S(2)}) copy-start(bf16[1,1,4,240,128]{4,3,2,1,0:T(8,128)(2,1)} %param.13) | copy-start | bytes 737284
  22.0 59.7 %copy-start.7 = (bf16[1,1,4,240,128]{4,3,2,1,0:T(8,128)(2,1)S(1)}, bf16[1,1,4,240,128]{4,3,2,1,0:T(8,128)(2,1)}, u32[]{:S(2)}) copy-start(bf16[1,1,4,240,128]{4,3,2,1,0:T(8,128)(2,1)} %param.14) | copy-start | bytes 737284
  22.0 59.7 %copy-start.8 = (bf16[1,128,768]{2,1,0:T(8,128)(2,1)S(1)}, bf16[1,128,768]{2,1,0:T(8,128)(2,1)}, u32[]{:S(2)}) copy-start(bf16[1,128,768]{2,1,0:T(8,128)(2,1)} %param.15) | copy-start | bytes 589828
  22.0 59.7 %copy-start.11 = (bf16[256,240]{1,0:T(8,128)(2,1)S(1)}, bf16[256,240]{1,0:T(8,128)(2,1)}, u32[]{:S(2)}) copy-start(bf16[256,240]{1,0:T(8,128)(2,1)} %constant.126.clone.inverse_t_ref) | copy-start | bytes 368644
  22.0 59.7 %copy-start.12 = (bf16[240,256]{1,0:T(8,128)(2,1)S(1)}, bf16[240,256]{1,0:T(8,128)(2,1)}, u32[]{:S(2)}) copy-start(bf16[240,256]{1,0:T(8,128)(2,1)} %constant.125.clone.inverse_ref) | copy-start | bytes 368644
  43.6 38.1 %all-to-all-start.1 = ((bf16[32,64,128]{2,1,0:T(8,128)(2,1)}), bf16[32,64,128]{2,1,0:T(8,128)(2,1)S(1)}, u32[]{:S(2)}, u32[]{:S(2)}) async-start(bf16[32,64,128]{2,1,0:T(8,128)(2,1)} %get-tuple-element.16), calls=%async_computation.1 | async-start | bytes 1048576 | tf_op jit(solution)/shard_map/all_to_all | solution.py:279
  81.7 0.9 copy-start.9
  87.0 26.4 %all-to-all-start.2 = ((bf16[32,32,128]{2,1,0:T(8,128)(2,1)}), bf16[32,32,128]{2,1,0:T(8,128)(2,1)S(1)}, u32[]{:S(2)}, u32[]{:S(2)}) async-start(bf16[32,32,128]{2,1,0:T(8,128)(2,1)} %get-tuple-element.17), calls=%async_computation.2 | async-start | bytes 524288 | tf_op jit(solution)/shard_map/all_to_all | solution.py:279
  114.6 73.9 %all-to-all-start.3 = ((bf16[32,64,128]{2,1,0:T(8,128)(2,1)}), bf16[32,64,128]{2,1,0:T(8,128)(2,1)S(1)}, u32[]{:S(2)}, u32[]{:S(2)}) async-start(bf16[32,64,128]{2,1,0:T(8,128)(2,1)} %get-tuple-element.19), calls=%async_computation.3 | async-start | bytes 1048576 | tf_op jit(solution)/shard_map/all_to_all | solution.py:279
  119.4 9.6 %collective-permute-start.4 = (bf16[384,128]{1,0:T(8,128)(2,1)S(1)}, bf16[384,128]{1,0:T(8,128)(2,1)S(1)}, u32[]{:S(2)}, u32[]{:S(2)}) collective-permute-start(bf16[384,128]{1,0:T(8,128)(2,1)S(1)} %get-tuple-element.24), channel_id=1, source_target_pairs={{0,3},{1,0},{2,1},{3,2},{4,7},{5,4},{6,5},{7,6},{8,11},{9,8},{10,9... | collective-permute-start | bytes 294920 | tf_op jit(solution)/shard_map/ppermute | solution.py:298
  124.0 7.2 %collective-permute-start.3 = (bf16[384,128]{1,0:T(8,128)(2,1)S(1)}, bf16[384,128]{1,0:T(8,128)(2,1)S(1)}, u32[]{:S(2)}, u32[]{:S(2)}) collective-permute-start(bf16[384,128]{1,0:T(8,128)(2,1)S(1)} %get-tuple-element.25), channel_id=1, source_target_pairs={{0,2},{1,3},{2,0},{3,1},{4,6},{5,7},{6,4},{7,5},{8,10},{9,11},{10,... | collective-permute-start | bytes 294920 | tf_op jit(solution)/shard_map/ppermute | solution.py:298
  126.3 7.1 %collective-permute-start.2 = (bf16[384,128]{1,0:T(8,128)(2,1)S(1)}, bf16[384,128]{1,0:T(8,128)(2,1)S(1)}, u32[]{:S(2)}, u32[]{:S(2)}) collective-permute-start(bf16[384,128]{1,0:T(8,128)(2,1)S(1)} %get-tuple-element.23), channel_id=1, source_target_pairs={{0,1},{1,2},{2,3},{3,0},{4,5},{5,6},{6,7},{7,4},{8,9},{9,10},{10,1... | collective-permute-start | bytes 294920 | tf_op jit(solution)/shard_map/ppermute | solution.py:298
  133.5 11.5 %collective-permute-start.5 = (bf16[192,128]{1,0:T(8,128)(2,1)S(1)}, bf16[192,128]{1,0:T(8,128)(2,1)S(1)}, u32[]{:S(2)}, u32[]{:S(2)}) collective-permute-start(bf16[192,128]{1,0:T(8,128)(2,1)S(1)} %dynamic-slice_bitcast_fusion.3), channel_id=1, source_target_pairs={{0,4},{4,0},{1,5},{5,1},{2,6},{6,2},{3,7},{7,3},{8,12},{12,8},{9,1... | collective-permute-start | bytes 147464 | tf_op jit(solution)/shard_map/ppermute | solution.py:298
  137.0 8.1 %collective-permute-start.8 = (f32[60,128]{1,0:T(8,128)S(1)}, f32[60,128]{1,0:T(8,128)S(1)}, u32[]{:S(2)}, u32[]{:S(2)}) collective-permute-start(f32[60,128]{1,0:T(8,128)S(1)} %get-tuple-element.29), channel_id=1, source_target_pairs={{0,3},{1,0},{2,1},{3,2},{4,7},{5,4},{6,5},{7,6},{8,11},{9,8},{10,9... | collective-permute-start | bytes 92168 | tf_op jit(solution)/shard_map/ppermute | solution.py:298
  139.0 6.2 %collective-permute-start.7 = (f32[60,128]{1,0:T(8,128)S(1)}, f32[60,128]{1,0:T(8,128)S(1)}, u32[]{:S(2)}, u32[]{:S(2)}) collective-permute-start(f32[60,128]{1,0:T(8,128)S(1)} %get-tuple-element.30), channel_id=1, source_target_pairs={{0,2},{1,3},{2,0},{3,1},{4,6},{5,7},{6,4},{7,5},{8,10},{9,11},{10,... | collective-permute-start | bytes 92168 | tf_op jit(solution)/shard_map/ppermute | solution.py:298
  142.2 5.9 %collective-permute-start.6 = (f32[60,128]{1,0:T(8,128)S(1)}, f32[60,128]{1,0:T(8,128)S(1)}, u32[]{:S(2)}, u32[]{:S(2)}) collective-permute-start(f32[60,128]{1,0:T(8,128)S(1)} %get-tuple-element.28), channel_id=1, source_target_pairs={{0,1},{1,2},{2,3},{3,0},{4,5},{5,6},{6,7},{7,4},{8,9},{9,10},{10,1... | collective-permute-start | bytes 92168 | tf_op jit(solution)/shard_map/ppermute | solution.py:298
  148.1 40.4 %copy-start.10 = (bf16[1,768,128]{2,1,0:T(8,128)(2,1)S(1)}, bf16[1,768,128]{2,1,0:T(8,128)(2,1)}, u32[]{:S(2)}) copy-start(bf16[1,768,128]{2,1,0:T(8,128)(2,1)} %param.16) | copy-start | bytes 589828
  148.1 40.4 %copy-start.13 = (bf16[240,256]{1,0:T(8,128)(2,1)S(1)}, bf16[240,256]{1,0:T(8,128)(2,1)}, u32[]{:S(2)}) copy-start(bf16[240,256]{1,0:T(8,128)(2,1)} %constant.125.clone.inverse_ref) | copy-start | bytes 368644
  178.1 15.8 %copy-start.6 = (bf16[240,256]{1,0:T(8,128)(2,1)S(1)}, bf16[240,256]{1,0:T(8,128)(2,1)}, u32[]{:S(2)}) copy-start(bf16[240,256]{1,0:T(8,128)(2,1)} %constant.123.clone.forward_ref) | copy-start | bytes 368644
  178.1 17.9 %collective-permute-start.9 = (f32[252,128]{1,0:T(8,128)S(1)}, f32[252,128]{1,0:T(8,128)S(1)}, u32[]{:S(2)}, u32[]{:S(2)}) collective-permute-start(f32[252,128]{1,0:T(8,128)S(1)} %convert_reduce_fusion), channel_id=1, source_target_pairs={{0,4},{4,0},{1,5},{5,1},{2,6},{6,2},{3,7},{7,3},{8,12},{12,8},{9,1... | collective-permute-start | bytes 387080 | tf_op jit(solution)/shard_map/ppermute | solution.py:298
  190.7 14.8 %collective-permute-start = (bf16[1,1,4,240,128]{4,3,2,1,0:T(8,128)(2,1)S(1)}, bf16[1,1,4,240,128]{4,3,2,1,0:T(8,128)(2,1)S(1)}, u32[]{:S(2)}, u32[]{:S(2)}) collective-permute-start(bf16[1,1,4,240,128]{4,3,2,1,0:T(8,128)(2,1)S(1)} %bitcast.64), channel_id=1, source_target_pairs={{0,128},{128,256},{256,384},{1,129},{129,257},{257,385},{2,130},{1... | collective-permute-start | bytes 737288 | tf_op jit(solution)/shard_map/ppermute | solution.py:293
  194.7 10.8 %collective-permute-start.1 = (bf16[1,1,4,240,128]{4,3,2,1,0:T(8,128)(2,1)S(1)}, bf16[1,1,4,240,128]{4,3,2,1,0:T(8,128)(2,1)S(1)}, u32[]{:S(2)}, u32[]{:S(2)}) collective-permute-start(bf16[1,1,4,240,128]{4,3,2,1,0:T(8,128)(2,1)S(1)} %bitcast.58), channel_id=1, source_target_pairs={{128,0},{256,128},{384,256},{129,1},{257,129},{385,257},{130,2},{2... | collective-permute-start | bytes 737288 | tf_op jit(solution)/shard_map/ppermute | solution.py:293
  196.7 8.1 %all-to-all-start.4 = ((f32[4,60,128]{2,1,0:T(8,128)}), f32[4,60,128]{2,1,0:T(8,128)S(1)}, u32[]{:S(2)}, u32[]{:S(2)}) async-start(f32[4,60,128]{2,1,0:T(8,128)} %broadcast_in_dim.22), calls=%async_computation.4 | async-start | bytes 262144 | tf_op jit(solution)/shard_map/all_to_all | solution.py:279

commit v3 on v2

--- a/solution.py
+++ b/solution.py
@@ -149,12 +149,14 @@
     syn_ref,
     filt_ref,
     beside_ref,
+    shares_ref,
     out_ref,
     grad_ref,
     came_ref,
     goes_ref,
 ):
-    out_ref[:, 32:, :] = beside_ref[...]
+    out_ref[:, 32:64, :] = beside_ref[...]
+    out_ref[:, 64:, :] = shares_ref[...]
     came_ref[...] = arrived_ref[...].reshape(LANES * 8, CH).astype(F32)
     real, imag = padded_filter(filt_ref)
     total_real = jnp.zeros((LANES, CH), F32)
@@ -174,8 +176,7 @@
         for r in range(2):
             goes_ref[pl.ds(r * ROWS + t, LANES, stride=8), :] = coeffs[:, r * CH : (r + 1) * CH]
     out_ref[:, :32, :] = goes_ref[...].reshape(PEERS, 32, CH).astype(BF16)
-    grad_ref[:NLAT, :] = total_real[:NLAT]
-    grad_ref[NLAT:, :] = total_imag[:NLAT]
+    grad_ref[...] = jnp.concatenate([total_real[:NLAT], total_imag[:NLAT]], axis=0).astype(BF16)
 
 
 def live(cycle_ref, j):
@@ -251,6 +252,18 @@
             out_ref[j] = (total * live(cycle_ref, j)).astype(BF16)
 
 
+def share_piece_kernel(arrived_ref, out_ref):
+    piece = arrived_ref[:, 64:, :].astype(F32).sum(axis=0).astype(BF16)
+    out_ref[...] = jnp.broadcast_to(piece[None], out_ref.shape)
+
+
+def share_result_kernel(pieces_ref, expand_ref, reduce_ref):
+    half = PEERS // 2
+    for p in range(PEERS):
+        target = expand_ref if p < half else reduce_ref
+        target[(p % half) * 12 : (p % half) * 12 + 12, :] = pieces_ref[p].astype(F32)[:12]
+
+
 def call(kernel, outs, args, scratch=(), flops=0, transcendentals=0, smem=()):
     specs = [
         pl.BlockSpec(memory_space=pltpu.SMEM if n in smem else pltpu.VMEM) for n in range(len(args))
@@ -270,6 +283,8 @@
 
 
 PAIRED = jax.ShapeDtypeStruct((PEERS, 64, CH), BF16)
+TRIPLE = jax.ShapeDtypeStruct((PEERS, 80, CH), BF16)
+SHARES = jax.ShapeDtypeStruct((PEERS, 16, CH), BF16)
 BLOCKS = jax.ShapeDtypeStruct((PEERS, 32, CH), BF16)
 TOKENS = jax.ShapeDtypeStruct((ROWS, NLON, CH), BF16)
 SPECTRAL_SCRATCH = (pltpu.VMEM((LANES * 8, CH), F32), pltpu.VMEM((LANES * 8, CH), F32))
@@ -277,10 +292,6 @@
 
 def exchange(blocks, axes):
     return lax.all_to_all(blocks, axes, split_axis=0, concat_axis=0, tiled=True)
-
-
-def spread(block, axes, peers):
-    return exchange(jnp.broadcast_to(block[None], (peers, *block.shape)), axes)
 
 
 def total(blocks):
@@ -309,21 +320,18 @@
     return sum((block.astype(F32) for block in came), block_of(0).astype(F32))
 
 
-def shares_half(shares):
-    own = scattered_total(shares, "dp").astype(BF16)
-    return scattered_total(own.reshape(2, HID // 4, CH), "sp_1").astype(BF16)
-
-
-def gradient_totals(half, filter_part):
-    rows = HID // 4
-    quarter = scattered_total(filter_part.reshape(4, NLAT // 2, CH), "dp").astype(BF16)
-    mine = total(lax.all_gather(jnp.concatenate([half, quarter]), "sp_0"))
+def share_blocks_of(shares):
+    own = scattered_total(shares, "dp").astype(BF16).reshape(PEERS, 12, CH)
+    return jnp.pad(own, ((0, 0), (0, 4), (0, 0)))
+
+
+def filter_total(part):
+    over_dp = total(lax.all_gather(part, "dp")).astype(BF16)
+    half = scattered_total(over_dp.reshape(2, NLAT, CH), "sp_1").astype(BF16)
+    mine = total(lax.all_gather(half, "sp_0"))
     other = around(mine, "sp_1", 1)
     first = lax.axis_index("sp_1") == 0
-    filter_own = mine[rows:] + other[rows:]
-    filter_grad = spread(filter_own, "dp", 4).reshape(2, NLAT, CH)
-    expand_grad = jnp.where(first, mine[:rows], other[:rows]).T
-    return expand_grad, jnp.where(first, other[:rows], mine[:rows]), filter_grad
+    return jnp.stack([jnp.where(first, mine, other), jnp.where(first, other, mine)])
 
 
 def on_device(
@@ -402,17 +410,19 @@
     fresh_values = call(
         fresh_spectral_kernel, [BLOCKS], [values_fresh, ana, syn, filt], SPECTRAL_SCRATCH, flops=leg
     )[0]
-    half = shares_half(shares)
+    share_blocks = share_blocks_of(shares)
 
     coeffs_fresh, filter_part = call(
         spectral_back_kernel,
-        [PAIRED, jax.ShapeDtypeStruct((2 * NLAT, CH), F32)],
-        [grads_at_orders, spectra, ana, syn, filt, fresh_values],
+        [TRIPLE, jax.ShapeDtypeStruct((2 * NLAT, CH), BF16)],
+        [grads_at_orders, spectra, ana, syn, filt, fresh_values, share_blocks],
         SPECTRAL_SCRATCH,
         flops=leg,
     )
     coeffs_fresh = exchange(coeffs_fresh, SP)
-    expand_grad, reduce_grad, filter_grad = gradient_totals(half, filter_part)
+    filter_grad = filter_total(filter_part)
+    pieces = call(share_piece_kernel, [SHARES], [coeffs_fresh])[0]
+    pieces = exchange(pieces, SP)
     input_grad = call(
         input_grad_kernel,
         [TOKENS],
@@ -430,7 +440,9 @@
         smem=(5,),
     )[0]
     next_input = from_behind(block[None, None], "pipe", 1)
-    return (next_input, sent_back, expand_grad[None], reduce_grad[None], filter_grad[None])
+    part = jax.ShapeDtypeStruct((HID // 4, CH), F32)
+    expand_grad, reduce_grad = call(share_result_kernel, [part, part], [pieces])
+    return (next_input, sent_back, expand_grad.T[None], reduce_grad[None], filter_grad[None])
 
 
 def solution(mesh):

time: 209 us -> 212 us (1.014)
  blocking collectives: 29.8 us -> 46.7 us
  waiting for transfers between devices: 86.8 us -> 70.3 us
    all_to_all x5, waiting for transfers between devices: 79.4 us -> 59.3 us  [exchange(): return lax.all_to_all(blocks, axes, split_axis=0, concat_axis=0, tiled=True)]
    all_gather x1 -> x2, blocking collectives: 29.8 us -> 46.7 us  [the longest x1 36.4 us: filter_total(): mine = total(lax.all_gather(half, 'sp_0'))]
    all_to_all x5, starting transfers between devices: 33.6 us -> 50 us  [exchange(): return lax.all_to_all(blocks, axes, split_axis=0, concat_axis=0, tiled=True)]
    ppermute x8 -> x5, starting transfers between devices: 31.3 us -> 16.4 us  [around(): lax.ppermute(block, axis, [(i, (i + distance) % count) for i in range(cou...]
    ppermute x2, waiting for transfers between devices: 0.01 us -> 6.86 us  [from_behind(): return lax.ppermute(block, axis, route)]
    ppermute x8 -> x5, waiting for transfers between devices: 7.47 us -> 4.12 us  [around(): lax.ppermute(block, axis, [(i, (i + distance) % count) for i in range(cou...]
    pallas_call x9 -> x11, Pallas kernels: 12.3 us -> 13.6 us  [call(): pl.pallas_call(kernel, out_shape=outs, in_specs=specs, out_specs=[pl.Bloc...]
    unnamed x32 -> x30, local copies, waits for them, and re-layouts: 4.25 us -> 4.87 us
  transfers between devices with their start and end apart: 15 -> 12, of which waited for: 8 -> 7; matrix products, arithmetic and copies ran while one was open for 2% -> 2% of each run, Pallas kernels for 2% -> 2%
where the time goes in v3:
time: 212 us; the launch traced here: 211 us
  starting transfers between devices  70.8 us (33%)
  waiting for transfers between devices  70.3 us (33%)
  blocking collectives  46.7 us (22%)
  Pallas kernels  13.6 us (6%)
  local copies, waits for them, and re-layouts  6.45 us (3%)
    all_to_all x5, waiting for transfers between devices, exchange(): return lax.all_to_all(blocks, axes, split_axis=0, concat_axis=0, tiled=True)  59.3 us
    all_to_all x5, starting transfers between devices, exchange(): return lax.all_to_all(blocks, axes, split_axis=0, concat_axis=0, tiled=True)  50 us
    all_gather x1, blocking collectives, filter_total(): mine = total(lax.all_gather(half, 'sp_0'))  36.4 us
    ppermute x5, starting transfers between devices, around(): lax.ppermute(block, axis, [(i, (i + distance) % count) for i in range(cou...  16.4 us
    pallas_call x11, Pallas kernels, call(): pl.pallas_call(kernel, out_shape=outs, in_specs=specs, out_specs=[pl.Bloc...  13.6 us
    all_gather x1, blocking collectives, filter_total(): over_dp = total(lax.all_gather(part, 'dp')).astype(BF16)  10.2 us
    ppermute x2, waiting for transfers between devices, from_behind(): return lax.ppermute(block, axis, route)  6.86 us
    unnamed x30, local copies, waits for them, and re-layouts  4.87 us
  transfers between devices with their start and end apart: 12, of which 7 were waited for; matrix products, arithmetic and copies ran while one was open for 2% of the time, Pallas kernels for 2%

profile of v3, /device:TPU:1, one launch (start us, length us, event | category | flops | bytes accessed | tf_op | source)
XLA Modules:
  0.0 210.8 jit_solution(15122422551495778424)
XLA Ops:
  0.6 0.9 copy-done.2
  1.5 0.9 copy-done.4
  2.5 1.0 shard_map.155
  3.5 16.9 %all-to-all-start = ((bf16[32,32,128]{2,1,0:T(8,128)(2,1)}), bf16[32,32,128]{2,1,0:T(8,128)(2,1)S(1)}, u32[]{:S(2)}, u32[]{:S(2)}) async-start(bf16[32,32,128]{2,1,0:T(8,128)(2,1)} %shard_map.155), calls=%async_computation | async-start | bytes 524288 | tf_op jit(solution)/shard_map/all_to_all | solution.py:294
  22.7 19.7 %all-to-all-done.arrived_ref = bf16[32,32,128]{2,1,0:T(8,128)(2,1)S(1)} async-done(((bf16[32,32,128]{2,1,0:T(8,128)(2,1)}), bf16[32,32,128]{2,1,0:T(8,128)(2,1)S(1)}, u32[]{:S(2)}, u32[]{:S(2)}) %all-to-all-start) | async-done | bytes 262176 | tf_op jit(solution)/shard_map/all_to_all | solution.py:294
  42.4 1.3 shard_map.158
  43.7 4.7 %all-to-all-start.1 = ((bf16[32,64,128]{2,1,0:T(8,128)(2,1)}), bf16[32,64,128]{2,1,0:T(8,128)(2,1)S(1)}, u32[]{:S(2)}, u32[]{:S(2)}) async-start(bf16[32,64,128]{2,1,0:T(8,128)(2,1)} %get-tuple-element.18), calls=%async_computation.1 | async-start | bytes 1048576 | tf_op jit(solution)/shard_map/all_to_all | solution.py:294
  48.4 33.5 %all-to-all-done.1.values_ref.arrived_ref = bf16[32,64,128]{2,1,0:T(8,128)(2,1)S(1)} async-done(((bf16[32,64,128]{2,1,0:T(8,128)(2,1)}), bf16[32,64,128]{2,1,0:T(8,128)(2,1)S(1)}, u32[]{:S(2)}, u32[]{:S(2)}) %all-to-all-start.1) | async-done | bytes 524320 | tf_op jit(solution)/shard_map/all_to_all | solution.py:294
  81.9 0.9 copy-done.11
  82.9 4.3 %shard_map.159 = (bf16[32,32,128]{2,1,0:T(8,128)(2,1)}, f32[4,240,128]{2,1,0:T(8,128)S(1)}, bf16[4,384,128]{2,1,0:T(8,128)(2,1)S(1)}) custom-call(bf16[4,240,128]{2,1,0:T(8,128)(2,1)S(1)} %bitcast.52, bf16[32,64,128]{2,1,0:T(8,128)(2,1)S(1)} %all-to-all-done.1.values_ref.arrived_ref, bf16[4,240,128]{2,1,0:T(8,128)(2,1)S(1)} %bitcast.59, ...), custom_call_target="tpu_custom_call" | custom-call | flops 1069547520 | bytes 2801680 | tf_op jit(solution)/shard_map/pallas_call | solution.py:272
  87.2 4.3 %all-to-all-start.2 = ((bf16[32,32,128]{2,1,0:T(8,128)(2,1)}), bf16[32,32,128]{2,1,0:T(8,128)(2,1)S(1)}, u32[]{:S(2)}, u32[]{:S(2)}) async-start(bf16[32,32,128]{2,1,0:T(8,128)(2,1)} %get-tuple-element.19), calls=%async_computation.2 | async-start | bytes 524288 | tf_op jit(solution)/shard_map/all_to_all | solution.py:294
  91.6 0.7 dynamic-slice_bitcast_fusion.2
  92.3 3.2 %collective-permute-start = (bf16[384,128]{1,0:T(8,128)(2,1)}, bf16[384,128]{1,0:T(8,128)(2,1)}, u32[]{:S(2)}, u32[]{:S(2)}) collective-permute-start(bf16[384,128]{1,0:T(8,128)(2,1)} %get-tuple-element.27), channel_id=1, source_target_pairs={{0,1},{1,2},{2,3},{3,0},{4,5},{5,6},{6,7},{7,4},{8,9},{9,10},{10,1... | collective-permute-start | bytes 294920 | tf_op jit(solution)/shard_map/ppermute | solution.py:309
  95.5 3.4 %collective-permute-start.2 = (bf16[384,128]{1,0:T(8,128)(2,1)}, bf16[384,128]{1,0:T(8,128)(2,1)}, u32[]{:S(2)}, u32[]{:S(2)}) collective-permute-start(bf16[384,128]{1,0:T(8,128)(2,1)} %get-tuple-element.28), channel_id=1, source_target_pairs={{0,3},{1,0},{2,1},{3,2},{4,7},{5,4},{6,5},{7,6},{8,11},{9,8},{10,9... | collective-permute-start | bytes 294920 | tf_op jit(solution)/shard_map/ppermute | solution.py:309
  98.9 3.5 %collective-permute-start.1 = (bf16[384,128]{1,0:T(8,128)(2,1)}, bf16[384,128]{1,0:T(8,128)(2,1)}, u32[]{:S(2)}, u32[]{:S(2)}) collective-permute-start(bf16[384,128]{1,0:T(8,128)(2,1)} %get-tuple-element.29), channel_id=1, source_target_pairs={{0,2},{1,3},{2,0},{3,1},{4,6},{5,7},{6,4},{7,5},{8,10},{9,11},{10,... | collective-permute-start | bytes 294920 | tf_op jit(solution)/shard_map/ppermute | solution.py:309
  103.0 3.3 %collective-permute-done.1 = bf16[384,128]{1,0:T(8,128)(2,1)} collective-permute-done((bf16[384,128]{1,0:T(8,128)(2,1)}, bf16[384,128]{1,0:T(8,128)(2,1)}, u32[]{:S(2)}, u32[]{:S(2)}) %collective-permute-start.1) | collective-permute-done | bytes 98336 | tf_op jit(solution)/shard_map/ppermute | solution.py:309
  106.3 1.0 fusion.2
  107.4 6.2 %all-to-all-done.2.arrived_ref = bf16[32,32,128]{2,1,0:T(8,128)(2,1)S(1)} async-done(((bf16[32,32,128]{2,1,0:T(8,128)(2,1)}), bf16[32,32,128]{2,1,0:T(8,128)(2,1)S(1)}, u32[]{:S(2)}, u32[]{:S(2)}) %all-to-all-start.2) | async-done | bytes 262176 | tf_op jit(solution)/shard_map/all_to_all | solution.py:294
  113.6 1.3 shard_map.161
  114.9 7.6 %all-to-all-start.3 = ((bf16[32,80,128]{2,1,0:T(8,128)(2,1)}), bf16[32,80,128]{2,1,0:T(8,128)(2,1)S(1)}, u32[]{:S(2)}, u32[]{:S(2)}) async-start(bf16[32,80,128]{2,1,0:T(8,128)(2,1)} %get-tuple-element.22), calls=%async_computation.3 | async-start | bytes 1310720 | tf_op jit(solution)/shard_map/all_to_all | solution.py:294
  122.5 10.2 %all-gather = bf16[960,128]{1,0:T(8,128)(2,1)S(1)} all-gather(bf16[240,128]{1,0:T(8,128)(2,1)S(1)} %get-tuple-element.26), channel_id=2, replica_groups=mesh['pipe'=4,'sp_0'=16,'sp_1'=2,'dp'=4] {'dp'}, dimensions={0}, use_global_device_ids=true | all-gather | bytes 307200 | tf_op jit(solution)/shard_map/all_gather | solution.py:329
  132.8 4.1 %collective-permute-start.5 = (bf16[120,128]{1,0:T(8,128)(2,1)S(1)}, bf16[120,128]{1,0:T(8,128)(2,1)S(1)}, u32[]{:S(2)}, u32[]{:S(2)}) collective-permute-start(bf16[120,128]{1,0:T(8,128)(2,1)S(1)} %dynamic-slice_bitcast_fusion.3), channel_id=1, source_target_pairs={{0,4},{4,0},{1,5},{5,1},{2,6},{6,2},{3,7},{7,3},{8,12},{12,8},{9,1... | collective-permute-start | bytes 92168 | tf_op jit(solution)/shard_map/ppermute | solution.py:309
  136.9 0.8 collective-permute-done.5
  137.8 36.4 %all-gather.1 = bf16[1920,128]{1,0:T(8,128)(2,1)S(1)} all-gather(bf16[120,128]{1,0:T(8,128)(2,1)S(1)} %fusion.3), channel_id=3, replica_groups=mesh['pipe'=4,'sp_0'=16,'sp_1'=2,'dp'=4] {'sp_0'}, dimensions={0}, use_global_device_ids=true | all-gather | bytes 522240 | tf_op jit(solution)/shard_map/all_gather | solution.py:331
  174.9 16.5 %all-to-all-start.4 = ((bf16[32,16,128]{2,1,0:T(8,128)(2,1)}), bf16[32,16,128]{2,1,0:T(8,128)(2,1)S(1)}, u32[]{:S(2)}, u32[]{:S(2)}) async-start(bf16[32,16,128]{2,1,0:T(8,128)(2,1)} %shard_map.164), calls=%async_computation.4 | async-start | bytes 262144 | tf_op jit(solution)/shard_map/all_to_all | solution.py:294
  191.5 2.1 %collective-permute-start.6 = (f32[120,128]{1,0:T(8,128)S(1)}, f32[120,128]{1,0:T(8,128)S(1)}, u32[]{:S(2)}, u32[]{:S(2)}) collective-permute-start(f32[120,128]{1,0:T(8,128)S(1)} %convert_reduce_fusion), channel_id=1, source_target_pairs={{0,4},{4,0},{1,5},{5,1},{2,6},{6,2},{3,7},{7,3},{8,12},{12,8},{9,1... | collective-permute-start | bytes 184328 | tf_op jit(solution)/shard_map/ppermute | solution.py:309
  193.7 2.2 %shard_map.162 = bf16[4,240,128]{2,1,0:T(8,128)(2,1)S(1)} custom-call(bf16[4,240,128]{2,1,0:T(8,128)(2,1)S(1)} %bitcast.50, bf16[32,80,128]{2,1,0:T(8,128)(2,1)S(1)} %all-to-all-done.3.values_ref.coeffs_ref.arrived_ref, bf16[240,256]{1,0:T(8,128)(2,1)S(1)} %copy-done.9, bf16[128,768]{1,0:T(8,128)(2,1)S(1)} %bitcast.56, bf16[768,128]{1,0:T(8,128)(2,1)S(1)} %bitcast.58, ...), custom_call_target="tpu_custom_call" | custom-call | flops 440401920 | bytes 1662992 | tf_op jit(solution)/shard_map/pallas_call | solution.py:272
  195.9 3.1 %collective-permute-start.3 = (bf16[1,1,4,240,128]{4,3,2,1,0:T(8,128)(2,1)S(1)}, bf16[1,1,4,240,128]{4,3,2,1,0:T(8,128)(2,1)S(1)}, u32[]{:S(2)}, u32[]{:S(2)}) collective-permute-start(bf16[1,1,4,240,128]{4,3,2,1,0:T(8,128)(2,1)S(1)} %bitcast.53), channel_id=1, source_target_pairs={{0,128},{128,256},{256,384},{1,129},{129,257},{257,385},{2,130},{1... | collective-permute-start | bytes 737288 | tf_op jit(solution)/shard_map/ppermute | solution.py:304
  199.1 0.8 shard_map.163
  199.9 1.3 collective-permute-start.4
  201.9 2.2 %collective-permute-done.3 = bf16[1,1,4,240,128]{4,3,2,1,0:T(8,128)(2,1)S(1)} collective-permute-done((bf16[1,1,4,240,128]{4,3,2,1,0:T(8,128)(2,1)S(1)}, bf16[1,1,4,240,128]{4,3,2,1,0:T(8,128)(2,1)S(1)}, u32[]{:S(2)}, u32[]{:S(2)}) %collective-permute-start.3) | collective-permute-done | bytes 245792 | tf_op jit(solution)/shard_map/ppermute | solution.py:304
  204.1 4.6 %collective-permute-done.4 = bf16[1,1,4,240,128]{4,3,2,1,0:T(8,128)(2,1)S(1)} collective-permute-done((bf16[1,1,4,240,128]{4,3,2,1,0:T(8,128)(2,1)S(1)}, bf16[1,1,4,240,128]{4,3,2,1,0:T(8,128)(2,1)S(1)}, u32[]{:S(2)}, u32[]{:S(2)}) %collective-permute-start.4) | collective-permute-done | bytes 245792 | tf_op jit(solution)/shard_map/ppermute | solution.py:304
  (50 shorter events, 6.5 us)
Async XLA Ops:
  0.6 0.9 copy-start.2
  1.5 0.9 copy-start.4
  3.5 18.9 %copy-start.1 = (bf16[1,1,4,240,128]{4,3,2,1,0:T(8,128)(2,1)S(1)}, bf16[1,1,4,240,128]{4,3,2,1,0:T(8,128)(2,1)}, u32[]{:S(2)}) copy-start(bf16[1,1,4,240,128]{4,3,2,1,0:T(8,128)(2,1)} %param.12) | copy-start | bytes 737284
  3.5 18.9 %copy-start.3 = (bf16[256,240]{1,0:T(8,128)(2,1)S(1)}, bf16[256,240]{1,0:T(8,128)(2,1)}, u32[]{:S(2)}) copy-start(bf16[256,240]{1,0:T(8,128)(2,1)} %constant.109.clone.forward_ref) | copy-start | bytes 368644
  3.5 38.9 %all-to-all-start = ((bf16[32,32,128]{2,1,0:T(8,128)(2,1)}), bf16[32,32,128]{2,1,0:T(8,128)(2,1)S(1)}, u32[]{:S(2)}, u32[]{:S(2)}) async-start(bf16[32,32,128]{2,1,0:T(8,128)(2,1)} %shard_map.155), calls=%async_computation | async-start | bytes 524288 | tf_op jit(solution)/shard_map/all_to_all | solution.py:294
  20.4 0.7 copy-start.13
  22.4 20.0 %copy-start = (f32[1,2,120,128]{3,2,1,0:T(8,128)S(1)}, f32[1,2,120,128]{3,2,1,0:T(8,128)}, u32[]{:S(2)}) copy-start(f32[1,2,120,128]{3,2,1,0:T(8,128)} %param.17) | copy-start | bytes 368644
  43.6 38.3 %copy-start.5 = (bf16[1,1,4,240,128]{4,3,2,1,0:T(8,128)(2,1)S(1)}, bf16[1,1,4,240,128]{4,3,2,1,0:T(8,128)(2,1)}, u32[]{:S(2)}) copy-start(bf16[1,1,4,240,128]{4,3,2,1,0:T(8,128)(2,1)} %param.13) | copy-start | bytes 737284
  43.6 38.3 %copy-start.6 = (bf16[1,128,768]{2,1,0:T(8,128)(2,1)S(1)}, bf16[1,128,768]{2,1,0:T(8,128)(2,1)}, u32[]{:S(2)}) copy-start(bf16[1,128,768]{2,1,0:T(8,128)(2,1)} %param.15) | copy-start | bytes 589828
  43.6 38.3 %copy-start.7 = (bf16[1,768,128]{2,1,0:T(8,128)(2,1)S(1)}, bf16[1,768,128]{2,1,0:T(8,128)(2,1)}, u32[]{:S(2)}) copy-start(bf16[1,768,128]{2,1,0:T(8,128)(2,1)} %param.16) | copy-start | bytes 589828
  43.6 38.3 %copy-start.8 = (bf16[240,256]{1,0:T(8,128)(2,1)S(1)}, bf16[240,256]{1,0:T(8,128)(2,1)}, u32[]{:S(2)}) copy-start(bf16[240,256]{1,0:T(8,128)(2,1)} %constant.110.clone.inverse_ref) | copy-start | bytes 368644
  43.6 38.3 %copy-start.12 = (bf16[256,240]{1,0:T(8,128)(2,1)S(1)}, bf16[256,240]{1,0:T(8,128)(2,1)}, u32[]{:S(2)}) copy-start(bf16[256,240]{1,0:T(8,128)(2,1)} %constant.111.clone.inverse_t_ref) | copy-start | bytes 368644
  43.7 38.2 %all-to-all-start.1 = ((bf16[32,64,128]{2,1,0:T(8,128)(2,1)}), bf16[32,64,128]{2,1,0:T(8,128)(2,1)S(1)}, u32[]{:S(2)}, u32[]{:S(2)}) async-start(bf16[32,64,128]{2,1,0:T(8,128)(2,1)} %get-tuple-element.18), calls=%async_computation.1 | async-start | bytes 1048576 | tf_op jit(solution)/shard_map/all_to_all | solution.py:294
  81.9 0.9 copy-start.11
  87.2 26.3 %all-to-all-start.2 = ((bf16[32,32,128]{2,1,0:T(8,128)(2,1)}), bf16[32,32,128]{2,1,0:T(8,128)(2,1)S(1)}, u32[]{:S(2)}, u32[]{:S(2)}) async-start(bf16[32,32,128]{2,1,0:T(8,128)(2,1)} %get-tuple-element.19), calls=%async_computation.2 | async-start | bytes 524288 | tf_op jit(solution)/shard_map/all_to_all | solution.py:294
  92.3 10.6 %collective-permute-start = (bf16[384,128]{1,0:T(8,128)(2,1)}, bf16[384,128]{1,0:T(8,128)(2,1)}, u32[]{:S(2)}, u32[]{:S(2)}) collective-permute-start(bf16[384,128]{1,0:T(8,128)(2,1)} %get-tuple-element.27), channel_id=1, source_target_pairs={{0,1},{1,2},{2,3},{3,0},{4,5},{5,6},{6,7},{7,4},{8,9},{9,10},{10,1... | collective-permute-start | bytes 294920 | tf_op jit(solution)/shard_map/ppermute | solution.py:309
  95.5 7.4 %collective-permute-start.2 = (bf16[384,128]{1,0:T(8,128)(2,1)}, bf16[384,128]{1,0:T(8,128)(2,1)}, u32[]{:S(2)}, u32[]{:S(2)}) collective-permute-start(bf16[384,128]{1,0:T(8,128)(2,1)} %get-tuple-element.28), channel_id=1, source_target_pairs={{0,3},{1,0},{2,1},{3,2},{4,7},{5,4},{6,5},{7,6},{8,11},{9,8},{10,9... | collective-permute-start | bytes 294920 | tf_op jit(solution)/shard_map/ppermute | solution.py:309
  98.9 7.4 %collective-permute-start.1 = (bf16[384,128]{1,0:T(8,128)(2,1)}, bf16[384,128]{1,0:T(8,128)(2,1)}, u32[]{:S(2)}, u32[]{:S(2)}) collective-permute-start(bf16[384,128]{1,0:T(8,128)(2,1)} %get-tuple-element.29), channel_id=1, source_target_pairs={{0,2},{1,3},{2,0},{3,1},{4,6},{5,7},{6,4},{7,5},{8,10},{9,11},{10,... | collective-permute-start | bytes 294920 | tf_op jit(solution)/shard_map/ppermute | solution.py:309
  114.9 59.3 %all-to-all-start.3 = ((bf16[32,80,128]{2,1,0:T(8,128)(2,1)}), bf16[32,80,128]{2,1,0:T(8,128)(2,1)S(1)}, u32[]{:S(2)}, u32[]{:S(2)}) async-start(bf16[32,80,128]{2,1,0:T(8,128)(2,1)} %get-tuple-element.22), calls=%async_computation.3 | async-start | bytes 1310720 | tf_op jit(solution)/shard_map/all_to_all | solution.py:294
  132.8 5.0 %collective-permute-start.5 = (bf16[120,128]{1,0:T(8,128)(2,1)S(1)}, bf16[120,128]{1,0:T(8,128)(2,1)S(1)}, u32[]{:S(2)}, u32[]{:S(2)}) collective-permute-start(bf16[120,128]{1,0:T(8,128)(2,1)S(1)} %dynamic-slice_bitcast_fusion.3), channel_id=1, source_target_pairs={{0,4},{4,0},{1,5},{5,1},{2,6},{6,2},{3,7},{7,3},{8,12},{12,8},{9,1... | collective-permute-start | bytes 92168 | tf_op jit(solution)/shard_map/ppermute | solution.py:309
  174.9 33.8 %all-to-all-start.4 = ((bf16[32,16,128]{2,1,0:T(8,128)(2,1)}), bf16[32,16,128]{2,1,0:T(8,128)(2,1)S(1)}, u32[]{:S(2)}, u32[]{:S(2)}) async-start(bf16[32,16,128]{2,1,0:T(8,128)(2,1)} %shard_map.164), calls=%async_computation.4 | async-start | bytes 262144 | tf_op jit(solution)/shard_map/all_to_all | solution.py:294
  191.5 2.3 %copy-start.9 = (bf16[240,256]{1,0:T(8,128)(2,1)S(1)}, bf16[240,256]{1,0:T(8,128)(2,1)}, u32[]{:S(2)}) copy-start(bf16[240,256]{1,0:T(8,128)(2,1)} %constant.110.clone.inverse_ref) | copy-start | bytes 368644
  191.5 9.6 %collective-permute-start.6 = (f32[120,128]{1,0:T(8,128)S(1)}, f32[120,128]{1,0:T(8,128)S(1)}, u32[]{:S(2)}, u32[]{:S(2)}) collective-permute-start(f32[120,128]{1,0:T(8,128)S(1)} %convert_reduce_fusion), channel_id=1, source_target_pairs={{0,4},{4,0},{1,5},{5,1},{2,6},{6,2},{3,7},{7,3},{8,12},{12,8},{9,1... | collective-permute-start | bytes 184328 | tf_op jit(solution)/shard_map/ppermute | solution.py:309
  193.7 5.3 %copy-start.10 = (bf16[240,256]{1,0:T(8,128)(2,1)S(1)}, bf16[240,256]{1,0:T(8,128)(2,1)}, u32[]{:S(2)}) copy-start(bf16[240,256]{1,0:T(8,128)(2,1)} %constant.108.clone.forward_ref) | copy-start | bytes 368644
  195.9 8.2 %collective-permute-start.3 = (bf16[1,1,4,240,128]{4,3,2,1,0:T(8,128)(2,1)S(1)}, bf16[1,1,4,240,128]{4,3,2,1,0:T(8,128)(2,1)S(1)}, u32[]{:S(2)}, u32[]{:S(2)}) collective-permute-start(bf16[1,1,4,240,128]{4,3,2,1,0:T(8,128)(2,1)S(1)} %bitcast.53), channel_id=1, source_target_pairs={{0,128},{128,256},{256,384},{1,129},{129,257},{257,385},{2,130},{1... | collective-permute-start | bytes 737288 | tf_op jit(solution)/shard_map/ppermute | solution.py:304
  199.9 8.8 %collective-permute-start.4 = (bf16[1,1,4,240,128]{4,3,2,1,0:T(8,128)(2,1)S(1)}, bf16[1,1,4,240,128]{4,3,2,1,0:T(8,128)(2,1)S(1)}, u32[]{:S(2)}, u32[]{:S(2)}) collective-permute-start(bf16[1,1,4,240,128]{4,3,2,1,0:T(8,128)(2,1)S(1)} %bitcast.54), channel_id=1, source_target_pairs={{128,0},{256,128},{384,256},{129,1},{257,129},{385,257},{130,2},{2... | collective-permute-start | bytes 737288 | tf_op jit(solution)/shard_map/ppermute | solution.py:304

commit v4 on v3

--- a/solution.py
+++ b/solution.py
@@ -151,12 +151,10 @@
     beside_ref,
     shares_ref,
     out_ref,
-    grad_ref,
     came_ref,
     goes_ref,
 ):
     out_ref[:, 32:64, :] = beside_ref[...]
-    out_ref[:, 64:, :] = shares_ref[...]
     came_ref[...] = arrived_ref[...].reshape(LANES * 8, CH).astype(F32)
     real, imag = padded_filter(filt_ref)
     total_real = jnp.zeros((LANES, CH), F32)
@@ -176,7 +174,9 @@
         for r in range(2):
             goes_ref[pl.ds(r * ROWS + t, LANES, stride=8), :] = coeffs[:, r * CH : (r + 1) * CH]
     out_ref[:, :32, :] = goes_ref[...].reshape(PEERS, 32, CH).astype(BF16)
-    grad_ref[...] = jnp.concatenate([total_real[:NLAT], total_imag[:NLAT]], axis=0).astype(BF16)
+    filter_part = jnp.concatenate([total_real, total_imag], axis=0).reshape(PEERS, 8, CH)
+    sums = jnp.concatenate([shares_ref[...].astype(F32), filter_part], axis=1)
+    out_ref[:, 64:, :] = sums.astype(BF16)
 
 
 def live(cycle_ref, j):
@@ -252,16 +252,25 @@
             out_ref[j] = (total * live(cycle_ref, j)).astype(BF16)
 
 
-def share_piece_kernel(arrived_ref, out_ref):
-    piece = arrived_ref[:, 64:, :].astype(F32).sum(axis=0).astype(BF16)
-    out_ref[...] = jnp.broadcast_to(piece[None], out_ref.shape)
-
-
-def share_result_kernel(pieces_ref, expand_ref, reduce_ref):
+def piece_kernel(arrived_ref, share_ref, filter_ref):
+    piece = arrived_ref[:, 64:, :].astype(F32).sum(axis=0)
+    share_ref[...] = piece[:16]
+    filter_ref[...] = jnp.broadcast_to(piece[16:][None], filter_ref.shape)
+
+
+def spread_kernel(share_ref, filter_ref, out_ref):
+    piece = jnp.concatenate([share_ref[...], filter_ref[...].sum(axis=0)], axis=0)
+    out_ref[...] = jnp.broadcast_to(piece[None], out_ref.shape).astype(BF16)
+
+
+def result_kernel(pieces_ref, expand_ref, reduce_ref, filter_ref):
     half = PEERS // 2
     for p in range(PEERS):
-        target = expand_ref if p < half else reduce_ref
-        target[(p % half) * 12 : (p % half) * 12 + 12, :] = pieces_ref[p].astype(F32)[:12]
+        side, at = divmod(p, half)
+        piece = pieces_ref[p].astype(F32)
+        (reduce_ref if side else expand_ref)[at * 12 : at * 12 + 12, :] = piece[:12]
+        if at < NLAT // 8:
+            filter_ref[side, at * 8 : at * 8 + 8, :] = piece[16:]
 
 
 def call(kernel, outs, args, scratch=(), flops=0, transcendentals=0, smem=()):
@@ -283,8 +292,7 @@
 
 
 PAIRED = jax.ShapeDtypeStruct((PEERS, 64, CH), BF16)
-TRIPLE = jax.ShapeDtypeStruct((PEERS, 80, CH), BF16)
-SHARES = jax.ShapeDtypeStruct((PEERS, 16, CH), BF16)
+TRIPLE = jax.ShapeDtypeStruct((PEERS, 88, CH), BF16)
 BLOCKS = jax.ShapeDtypeStruct((PEERS, 32, CH), BF16)
 TOKENS = jax.ShapeDtypeStruct((ROWS, NLON, CH), BF16)
 SPECTRAL_SCRATCH = (pltpu.VMEM((LANES * 8, CH), F32), pltpu.VMEM((LANES * 8, CH), F32))
@@ -292,10 +300,6 @@
 
 def exchange(blocks, axes):
     return lax.all_to_all(blocks, axes, split_axis=0, concat_axis=0, tiled=True)
-
-
-def total(blocks):
-    return blocks.astype(F32).sum(axis=0)
 
 
 def from_behind(block, axis, distance):
@@ -323,15 +327,6 @@
 def share_blocks_of(shares):
     own = scattered_total(shares, "dp").astype(BF16).reshape(PEERS, 12, CH)
     return jnp.pad(own, ((0, 0), (0, 4), (0, 0)))
-
-
-def filter_total(part):
-    over_dp = total(lax.all_gather(part, "dp")).astype(BF16)
-    half = scattered_total(over_dp.reshape(2, NLAT, CH), "sp_1").astype(BF16)
-    mine = total(lax.all_gather(half, "sp_0"))
-    other = around(mine, "sp_1", 1)
-    first = lax.axis_index("sp_1") == 0
-    return jnp.stack([jnp.where(first, mine, other), jnp.where(first, other, mine)])
 
 
 def on_device(
@@ -412,16 +407,23 @@
     )[0]
     share_blocks = share_blocks_of(shares)
 
-    coeffs_fresh, filter_part = call(
+    coeffs_fresh = call(
         spectral_back_kernel,
-        [TRIPLE, jax.ShapeDtypeStruct((2 * NLAT, CH), BF16)],
+        [TRIPLE],
         [grads_at_orders, spectra, ana, syn, filt, fresh_values, share_blocks],
         SPECTRAL_SCRATCH,
         flops=leg,
-    )
+    )[0]
     coeffs_fresh = exchange(coeffs_fresh, SP)
-    filter_grad = filter_total(filter_part)
-    pieces = call(share_piece_kernel, [SHARES], [coeffs_fresh])[0]
+    share, filter_piece = call(
+        piece_kernel,
+        [jax.ShapeDtypeStruct((16, CH), F32), jax.ShapeDtypeStruct((4, 8, CH), F32)],
+        [coeffs_fresh],
+    )
+    filter_piece = exchange(filter_piece, "dp")
+    pieces = call(
+        spread_kernel, [jax.ShapeDtypeStruct((PEERS, 24, CH), BF16)], [share, filter_piece]
+    )[0]
     pieces = exchange(pieces, SP)
     input_grad = call(
         input_grad_kernel,
@@ -441,7 +443,9 @@
     )[0]
     next_input = from_behind(block[None, None], "pipe", 1)
     part = jax.ShapeDtypeStruct((HID // 4, CH), F32)
-    expand_grad, reduce_grad = call(share_result_kernel, [part, part], [pieces])
+    expand_grad, reduce_grad, filter_grad = call(
+        result_kernel, [part, part, jax.ShapeDtypeStruct((2, NLAT, CH), F32)], [pieces]
+    )
     return (next_input, sent_back, expand_grad.T[None], reduce_grad[None], filter_grad[None])
 
 

time: 212 us -> 198 us (0.934)
  starting transfers between devices: 70.8 us -> 46 us
  blocking collectives: 46.7 us -> 56.2 us
  waiting for transfers between devices: 70.3 us -> 74 us
    all_to_all x0 -> x2, blocking collectives: none -> 56.2 us  [exchange(): return lax.all_to_all(blocks, axes, split_axis=0, concat_axis=0, tiled=True)]
    all_gather x2 -> x0, blocking collectives: 46.7 us -> none  [the longest x1 36.4 us: filter_total(): mine = total(lax.all_gather(half, 'sp_0'))]
    all_to_all x5 -> x4, starting transfers between devices: 50 us -> 31.5 us  [exchange(): return lax.all_to_all(blocks, axes, split_axis=0, concat_axis=0, tiled=True)]
    ppermute x5 -> x3, starting transfers between devices: 16.4 us -> 10.1 us  [around(): lax.ppermute(block, axis, [(i, (i + distance) % count) for i in range(cou...]
    all_to_all x5 -> x4, waiting for transfers between devices: 59.3 us -> 63.2 us  [exchange(): return lax.all_to_all(blocks, axes, split_axis=0, concat_axis=0, tiled=True)]
    pallas_call x11 -> x12, Pallas kernels: 13.6 us -> 12.9 us  [call(): pl.pallas_call(kernel, out_shape=outs, in_specs=specs, out_specs=[pl.Bloc...]
  transfers between devices with their start and end apart: 12 -> 9, of which waited for: 7 -> 7; matrix products, arithmetic and copies ran while one was open for 2% -> 1% of each run, Pallas kernels for 2% -> 2%
where the time goes in v4:
time: 198 us
  waiting for transfers between devices  74 us (37%)
  blocking collectives  56.2 us (28%)
  starting transfers between devices  46 us (23%)
  Pallas kernels  12.9 us (7%)
  local copies, waits for them, and re-layouts  6.43 us (3%)
    all_to_all x4, waiting for transfers between devices, exchange(): return lax.all_to_all(blocks, axes, split_axis=0, concat_axis=0, tiled=True)  63.2 us
    all_to_all x2, blocking collectives, exchange(): return lax.all_to_all(blocks, axes, split_axis=0, concat_axis=0, tiled=True)  56.2 us
    all_to_all x4, starting transfers between devices, exchange(): return lax.all_to_all(blocks, axes, split_axis=0, concat_axis=0, tiled=True)  31.5 us
    pallas_call x12, Pallas kernels, call(): pl.pallas_call(kernel, out_shape=outs, in_specs=specs, out_specs=[pl.Bloc...  12.9 us
    ppermute x3, starting transfers between devices, around(): lax.ppermute(block, axis, [(i, (i + distance) % count) for i in range(cou...  10.1 us
    ppermute x2, waiting for transfers between devices, from_behind(): return lax.ppermute(block, axis, route)  7.47 us
    unnamed x30, local copies, waits for them, and re-layouts  4.86 us
    ppermute x2, starting transfers between devices, from_behind(): return lax.ppermute(block, axis, route)  4.42 us
  transfers between devices with their start and end apart: 9, of which 7 were waited for; matrix products, arithmetic and copies ran while one was open for 1% of the time, Pallas kernels for 2%

profile of v4, /device:TPU:1, one launch (start us, length us, event | category | flops | bytes accessed | tf_op | source)
XLA Modules:
  0.0 197.6 jit_solution(5373033869914958376)
XLA Ops:
  0.6 0.9 copy-done.2
  1.5 0.9 copy-done.4
  2.5 1.0 shard_map.155
  3.5 16.9 %all-to-all-start = ((bf16[32,32,128]{2,1,0:T(8,128)(2,1)}), bf16[32,32,128]{2,1,0:T(8,128)(2,1)S(1)}, u32[]{:S(2)}, u32[]{:S(2)}) async-start(bf16[32,32,128]{2,1,0:T(8,128)(2,1)} %shard_map.155), calls=%async_computation | async-start | bytes 524288 | tf_op jit(solution)/shard_map/all_to_all | solution.py:302
  21.1 0.7 dynamic-slice_bitcast_fusion.3.order_ref
  22.7 19.7 %all-to-all-done.arrived_ref = bf16[32,32,128]{2,1,0:T(8,128)(2,1)S(1)} async-done(((bf16[32,32,128]{2,1,0:T(8,128)(2,1)}), bf16[32,32,128]{2,1,0:T(8,128)(2,1)S(1)}, u32[]{:S(2)}, u32[]{:S(2)}) %all-to-all-start) | async-done | bytes 262176 | tf_op jit(solution)/shard_map/all_to_all | solution.py:302
  42.4 1.3 shard_map.158
  43.7 4.7 %all-to-all-start.1 = ((bf16[32,64,128]{2,1,0:T(8,128)(2,1)}), bf16[32,64,128]{2,1,0:T(8,128)(2,1)S(1)}, u32[]{:S(2)}, u32[]{:S(2)}) async-start(bf16[32,64,128]{2,1,0:T(8,128)(2,1)} %get-tuple-element.19), calls=%async_computation.1 | async-start | bytes 1048576 | tf_op jit(solution)/shard_map/all_to_all | solution.py:302
  48.4 33.5 %all-to-all-done.1.values_ref.arrived_ref = bf16[32,64,128]{2,1,0:T(8,128)(2,1)S(1)} async-done(((bf16[32,64,128]{2,1,0:T(8,128)(2,1)}), bf16[32,64,128]{2,1,0:T(8,128)(2,1)S(1)}, u32[]{:S(2)}, u32[]{:S(2)}) %all-to-all-start.1) | async-done | bytes 524320 | tf_op jit(solution)/shard_map/all_to_all | solution.py:302
  81.9 0.9 copy-done.11
  82.9 4.3 %shard_map.159 = (bf16[32,32,128]{2,1,0:T(8,128)(2,1)}, f32[4,240,128]{2,1,0:T(8,128)S(1)}, bf16[4,384,128]{2,1,0:T(8,128)(2,1)S(1)}) custom-call(bf16[4,240,128]{2,1,0:T(8,128)(2,1)S(1)} %bitcast.39, bf16[32,64,128]{2,1,0:T(8,128)(2,1)S(1)} %all-to-all-done.1.values_ref.arrived_ref, bf16[4,240,128]{2,1,0:T(8,128)(2,1)S(1)} %bitcast.45, ...), custom_call_target="tpu_custom_call" | custom-call | flops 1069547520 | bytes 2801680 | tf_op jit(solution)/shard_map/pallas_call | solution.py:281
  87.2 4.3 %all-to-all-start.2 = ((bf16[32,32,128]{2,1,0:T(8,128)(2,1)}), bf16[32,32,128]{2,1,0:T(8,128)(2,1)S(1)}, u32[]{:S(2)}, u32[]{:S(2)}) async-start(bf16[32,32,128]{2,1,0:T(8,128)(2,1)} %get-tuple-element.20), calls=%async_computation.2 | async-start | bytes 524288 | tf_op jit(solution)/shard_map/all_to_all | solution.py:302
  91.6 0.7 dynamic-slice_bitcast_fusion.2
  92.3 3.2 %collective-permute-start = (bf16[384,128]{1,0:T(8,128)(2,1)}, bf16[384,128]{1,0:T(8,128)(2,1)}, u32[]{:S(2)}, u32[]{:S(2)}) collective-permute-start(bf16[384,128]{1,0:T(8,128)(2,1)} %get-tuple-element.29), channel_id=1, source_target_pairs={{0,1},{1,2},{2,3},{3,0},{4,5},{5,6},{6,7},{7,4},{8,9},{9,10},{10,1... | collective-permute-start | bytes 294920 | tf_op jit(solution)/shard_map/ppermute | solution.py:313
  95.5 3.4 %collective-permute-start.2 = (bf16[384,128]{1,0:T(8,128)(2,1)}, bf16[384,128]{1,0:T(8,128)(2,1)}, u32[]{:S(2)}, u32[]{:S(2)}) collective-permute-start(bf16[384,128]{1,0:T(8,128)(2,1)} %get-tuple-element.30), channel_id=1, source_target_pairs={{0,3},{1,0},{2,1},{3,2},{4,7},{5,4},{6,5},{7,6},{8,11},{9,8},{10,9... | collective-permute-start | bytes 294920 | tf_op jit(solution)/shard_map/ppermute | solution.py:313
  98.9 3.5 %collective-permute-start.1 = (bf16[384,128]{1,0:T(8,128)(2,1)}, bf16[384,128]{1,0:T(8,128)(2,1)}, u32[]{:S(2)}, u32[]{:S(2)}) collective-permute-start(bf16[384,128]{1,0:T(8,128)(2,1)} %get-tuple-element.31), channel_id=1, source_target_pairs={{0,2},{1,3},{2,0},{3,1},{4,6},{5,7},{6,4},{7,5},{8,10},{9,11},{10,... | collective-permute-start | bytes 294920 | tf_op jit(solution)/shard_map/ppermute | solution.py:313
  103.0 3.3 %collective-permute-done.1 = bf16[384,128]{1,0:T(8,128)(2,1)} collective-permute-done((bf16[384,128]{1,0:T(8,128)(2,1)}, bf16[384,128]{1,0:T(8,128)(2,1)}, u32[]{:S(2)}, u32[]{:S(2)}) %collective-permute-start.1) | collective-permute-done | bytes 98336 | tf_op jit(solution)/shard_map/ppermute | solution.py:313
  106.3 1.0 fusion.2
  107.4 6.2 %all-to-all-done.2.arrived_ref = bf16[32,32,128]{2,1,0:T(8,128)(2,1)S(1)} async-done(((bf16[32,32,128]{2,1,0:T(8,128)(2,1)}), bf16[32,32,128]{2,1,0:T(8,128)(2,1)S(1)}, u32[]{:S(2)}, u32[]{:S(2)}) %all-to-all-start.2) | async-done | bytes 262176 | tf_op jit(solution)/shard_map/all_to_all | solution.py:302
  114.1 49.2 %all_to_all.30.values_ref.coeffs_ref.arrived_ref = bf16[32,88,128]{2,1,0:T(8,128)(2,1)S(1)} all-to-all(bf16[32,88,128]{2,1,0:T(8,128)(2,1)S(1)} %shard_map.161), channel_id=1, replica_groups=mesh['pipe'=4,'sp_0'=16,'sp_1'=2,'dp'=4] {'sp_0','sp_1'}, dimensions={0} | all-to-all | bytes 1441792 | tf_op jit(solution)/shard_map/all_to_all | solution.py:302
  163.4 7.0 %all_to_all.31.filter_ref = f32[4,8,128]{2,1,0:T(8,128)S(1)} all-to-all(f32[4,8,128]{2,1,0:T(8,128)S(1)} %get-tuple-element.25), channel_id=1, replica_groups=mesh['pipe'=4,'sp_0'=16,'sp_1'=2,'dp'=4] {'dp'}, dimensions={0} | all-to-all | bytes 32768 | tf_op jit(solution)/shard_map/all_to_all | solution.py:302
  171.0 5.6 %all-to-all-start.5 = ((bf16[32,24,128]{2,1,0:T(8,128)(2,1)}), bf16[32,24,128]{2,1,0:T(8,128)(2,1)S(1)}, u32[]{:S(2)}, u32[]{:S(2)}) async-start(bf16[32,24,128]{2,1,0:T(8,128)(2,1)} %shard_map.165), calls=%async_computation.5 | async-start | bytes 393216 | tf_op jit(solution)/shard_map/all_to_all | solution.py:302
  176.7 2.2 %shard_map.162 = bf16[4,240,128]{2,1,0:T(8,128)(2,1)S(1)} custom-call(bf16[4,240,128]{2,1,0:T(8,128)(2,1)S(1)} %bitcast.36, bf16[32,88,128]{2,1,0:T(8,128)(2,1)S(1)} %all_to_all.30.values_ref.coeffs_ref.arrived_ref, bf16[240,256]{1,0:T(8,128)(2,1)S(1)} %copy-done.10, bf16[128,768]{1,0:T(8,128)(2,1)S(1)} %bitcast.42, bf16[768,128]{1,0:T(8,128)(2,1)S(1)} %bitcast.44, ...), custom_call_target="tpu_custom_call" | custom-call | flops 440401920 | bytes 1728528 | tf_op jit(solution)/shard_map/pallas_call | solution.py:281
  178.8 3.1 %collective-permute-start.3 = (bf16[1,1,4,240,128]{4,3,2,1,0:T(8,128)(2,1)S(1)}, bf16[1,1,4,240,128]{4,3,2,1,0:T(8,128)(2,1)S(1)}, u32[]{:S(2)}, u32[]{:S(2)}) collective-permute-start(bf16[1,1,4,240,128]{4,3,2,1,0:T(8,128)(2,1)S(1)} %bitcast.37), channel_id=1, source_target_pairs={{0,128},{128,256},{256,384},{1,129},{129,257},{257,385},{2,130},{1... | collective-permute-start | bytes 737288 | tf_op jit(solution)/shard_map/ppermute | solution.py:308
  182.0 0.8 shard_map.163
  182.8 1.3 collective-permute-start.4
  184.1 2.8 %collective-permute-done.3 = bf16[1,1,4,240,128]{4,3,2,1,0:T(8,128)(2,1)S(1)} collective-permute-done((bf16[1,1,4,240,128]{4,3,2,1,0:T(8,128)(2,1)S(1)}, bf16[1,1,4,240,128]{4,3,2,1,0:T(8,128)(2,1)S(1)}, u32[]{:S(2)}, u32[]{:S(2)}) %collective-permute-start.3) | collective-permute-done | bytes 245792 | tf_op jit(solution)/shard_map/ppermute | solution.py:308
  186.9 4.6 %collective-permute-done.4 = bf16[1,1,4,240,128]{4,3,2,1,0:T(8,128)(2,1)S(1)} collective-permute-done((bf16[1,1,4,240,128]{4,3,2,1,0:T(8,128)(2,1)S(1)}, bf16[1,1,4,240,128]{4,3,2,1,0:T(8,128)(2,1)S(1)}, u32[]{:S(2)}, u32[]{:S(2)}) %collective-permute-start.4) | collective-permute-done | bytes 245792 | tf_op jit(solution)/shard_map/ppermute | solution.py:308
  191.6 3.9 %all-to-all-done.5.pieces_ref = bf16[32,24,128]{2,1,0:T(8,128)(2,1)S(1)} async-done(((bf16[32,24,128]{2,1,0:T(8,128)(2,1)}), bf16[32,24,128]{2,1,0:T(8,128)(2,1)S(1)}, u32[]{:S(2)}, u32[]{:S(2)}) %all-to-all-start.5) | async-done | bytes 196640 | tf_op jit(solution)/shard_map/all_to_all | solution.py:302
  195.5 0.7 shard_map.166
  196.2 0.7 copy.19
  196.9 0.7 copy.20
  (39 shorter events, 3.5 us)
Async XLA Ops:
  0.6 0.9 copy-start.2
  1.5 0.9 copy-start.4
  3.5 18.9 %copy-start.1 = (bf16[1,1,4,240,128]{4,3,2,1,0:T(8,128)(2,1)S(1)}, bf16[1,1,4,240,128]{4,3,2,1,0:T(8,128)(2,1)}, u32[]{:S(2)}) copy-start(bf16[1,1,4,240,128]{4,3,2,1,0:T(8,128)(2,1)} %param.12) | copy-start | bytes 737284
  3.5 18.9 %copy-start.3 = (bf16[256,240]{1,0:T(8,128)(2,1)S(1)}, bf16[256,240]{1,0:T(8,128)(2,1)}, u32[]{:S(2)}) copy-start(bf16[256,240]{1,0:T(8,128)(2,1)} %constant.90.clone.forward_ref) | copy-start | bytes 368644
  3.5 38.9 %all-to-all-start = ((bf16[32,32,128]{2,1,0:T(8,128)(2,1)}), bf16[32,32,128]{2,1,0:T(8,128)(2,1)S(1)}, u32[]{:S(2)}, u32[]{:S(2)}) async-start(bf16[32,32,128]{2,1,0:T(8,128)(2,1)} %shard_map.155), calls=%async_computation | async-start | bytes 524288 | tf_op jit(solution)/shard_map/all_to_all | solution.py:302
  20.4 0.7 copy-start.13
  22.4 20.0 %copy-start = (f32[1,2,120,128]{3,2,1,0:T(8,128)S(1)}, f32[1,2,120,128]{3,2,1,0:T(8,128)}, u32[]{:S(2)}) copy-start(f32[1,2,120,128]{3,2,1,0:T(8,128)} %param.17) | copy-start | bytes 368644
  43.6 38.3 %copy-start.5 = (bf16[1,1,4,240,128]{4,3,2,1,0:T(8,128)(2,1)S(1)}, bf16[1,1,4,240,128]{4,3,2,1,0:T(8,128)(2,1)}, u32[]{:S(2)}) copy-start(bf16[1,1,4,240,128]{4,3,2,1,0:T(8,128)(2,1)} %param.13) | copy-start | bytes 737284
  43.6 38.3 %copy-start.6 = (bf16[1,128,768]{2,1,0:T(8,128)(2,1)S(1)}, bf16[1,128,768]{2,1,0:T(8,128)(2,1)}, u32[]{:S(2)}) copy-start(bf16[1,128,768]{2,1,0:T(8,128)(2,1)} %param.15) | copy-start | bytes 589828
  43.6 38.3 %copy-start.7 = (bf16[1,768,128]{2,1,0:T(8,128)(2,1)S(1)}, bf16[1,768,128]{2,1,0:T(8,128)(2,1)}, u32[]{:S(2)}) copy-start(bf16[1,768,128]{2,1,0:T(8,128)(2,1)} %param.16) | copy-start | bytes 589828
  43.6 38.3 %copy-start.9 = (bf16[240,256]{1,0:T(8,128)(2,1)S(1)}, bf16[240,256]{1,0:T(8,128)(2,1)}, u32[]{:S(2)}) copy-start(bf16[240,256]{1,0:T(8,128)(2,1)} %constant.91.clone.inverse_ref) | copy-start | bytes 368644
  43.7 38.3 %copy-start.12 = (bf16[256,240]{1,0:T(8,128)(2,1)S(1)}, bf16[256,240]{1,0:T(8,128)(2,1)}, u32[]{:S(2)}) copy-start(bf16[256,240]{1,0:T(8,128)(2,1)} %constant.92.clone.inverse_t_ref) | copy-start | bytes 368644
  43.7 38.2 %all-to-all-start.1 = ((bf16[32,64,128]{2,1,0:T(8,128)(2,1)}), bf16[32,64,128]{2,1,0:T(8,128)(2,1)S(1)}, u32[]{:S(2)}, u32[]{:S(2)}) async-start(bf16[32,64,128]{2,1,0:T(8,128)(2,1)} %get-tuple-element.19), calls=%async_computation.1 | async-start | bytes 1048576 | tf_op jit(solution)/shard_map/all_to_all | solution.py:302
  81.9 0.9 copy-start.11
  87.2 26.3 %all-to-all-start.2 = ((bf16[32,32,128]{2,1,0:T(8,128)(2,1)}), bf16[32,32,128]{2,1,0:T(8,128)(2,1)S(1)}, u32[]{:S(2)}, u32[]{:S(2)}) async-start(bf16[32,32,128]{2,1,0:T(8,128)(2,1)} %get-tuple-element.20), calls=%async_computation.2 | async-start | bytes 524288 | tf_op jit(solution)/shard_map/all_to_all | solution.py:302
  92.3 10.6 %collective-permute-start = (bf16[384,128]{1,0:T(8,128)(2,1)}, bf16[384,128]{1,0:T(8,128)(2,1)}, u32[]{:S(2)}, u32[]{:S(2)}) collective-permute-start(bf16[384,128]{1,0:T(8,128)(2,1)} %get-tuple-element.29), channel_id=1, source_target_pairs={{0,1},{1,2},{2,3},{3,0},{4,5},{5,6},{6,7},{7,4},{8,9},{9,10},{10,1... | collective-permute-start | bytes 294920 | tf_op jit(solution)/shard_map/ppermute | solution.py:313
  95.5 7.4 %collective-permute-start.2 = (bf16[384,128]{1,0:T(8,128)(2,1)}, bf16[384,128]{1,0:T(8,128)(2,1)}, u32[]{:S(2)}, u32[]{:S(2)}) collective-permute-start(bf16[384,128]{1,0:T(8,128)(2,1)} %get-tuple-element.30), channel_id=1, source_target_pairs={{0,3},{1,0},{2,1},{3,2},{4,7},{5,4},{6,5},{7,6},{8,11},{9,8},{10,9... | collective-permute-start | bytes 294920 | tf_op jit(solution)/shard_map/ppermute | solution.py:313
  98.9 7.4 %collective-permute-start.1 = (bf16[384,128]{1,0:T(8,128)(2,1)}, bf16[384,128]{1,0:T(8,128)(2,1)}, u32[]{:S(2)}, u32[]{:S(2)}) collective-permute-start(bf16[384,128]{1,0:T(8,128)(2,1)} %get-tuple-element.31), channel_id=1, source_target_pairs={{0,2},{1,3},{2,0},{3,1},{4,6},{5,7},{6,4},{7,5},{8,10},{9,11},{10,... | collective-permute-start | bytes 294920 | tf_op jit(solution)/shard_map/ppermute | solution.py:313
  171.0 5.6 %copy-start.10 = (bf16[240,256]{1,0:T(8,128)(2,1)S(1)}, bf16[240,256]{1,0:T(8,128)(2,1)}, u32[]{:S(2)}) copy-start(bf16[240,256]{1,0:T(8,128)(2,1)} %constant.91.clone.inverse_ref) | copy-start | bytes 368644
  171.0 24.4 %all-to-all-start.5 = ((bf16[32,24,128]{2,1,0:T(8,128)(2,1)}), bf16[32,24,128]{2,1,0:T(8,128)(2,1)S(1)}, u32[]{:S(2)}, u32[]{:S(2)}) async-start(bf16[32,24,128]{2,1,0:T(8,128)(2,1)} %shard_map.165), calls=%async_computation.5 | async-start | bytes 393216 | tf_op jit(solution)/shard_map/all_to_all | solution.py:302
  176.6 5.3 %copy-start.8 = (bf16[240,256]{1,0:T(8,128)(2,1)S(1)}, bf16[240,256]{1,0:T(8,128)(2,1)}, u32[]{:S(2)}) copy-start(bf16[240,256]{1,0:T(8,128)(2,1)} %constant.89.clone.forward_ref) | copy-start | bytes 368644
  178.8 8.1 %collective-permute-start.3 = (bf16[1,1,4,240,128]{4,3,2,1,0:T(8,128)(2,1)S(1)}, bf16[1,1,4,240,128]{4,3,2,1,0:T(8,128)(2,1)S(1)}, u32[]{:S(2)}, u32[]{:S(2)}) collective-permute-start(bf16[1,1,4,240,128]{4,3,2,1,0:T(8,128)(2,1)S(1)} %bitcast.37), channel_id=1, source_target_pairs={{0,128},{128,256},{256,384},{1,129},{129,257},{257,385},{2,130},{1... | collective-permute-start | bytes 737288 | tf_op jit(solution)/shard_map/ppermute | solution.py:308
  182.8 8.8 %collective-permute-start.4 = (bf16[1,1,4,240,128]{4,3,2,1,0:T(8,128)(2,1)S(1)}, bf16[1,1,4,240,128]{4,3,2,1,0:T(8,128)(2,1)S(1)}, u32[]{:S(2)}, u32[]{:S(2)}) collective-permute-start(bf16[1,1,4,240,128]{4,3,2,1,0:T(8,128)(2,1)S(1)} %bitcast.40), channel_id=1, source_target_pairs={{128,0},{256,128},{384,256},{129,1},{257,129},{385,257},{130,2},{2... | collective-permute-start | bytes 737288 | tf_op jit(solution)/shard_map/ppermute | solution.py:308

commit v5 on v4

--- a/solution.py
+++ b/solution.py
@@ -206,7 +206,6 @@
     cycle_ref,
     out_ref,
     grad_mixed_ref,
-    shares_ref,
     mixed_ref,
     masked_ref,
     hidden_ref,
@@ -235,12 +234,15 @@
             grad_mixed_ref[j] = grad_mixed
             grad_values.append(matmul(inverse_t_ref[...], grad_mixed.astype(BF16)))
         to_blocks(out_ref, half, grad_values)
-    expand_grad = matmul(grad_pre_ref[...], mixed_ref[...], ((0,), (0,))).astype(BF16)
-    reduce_grad = matmul(hidden_ref[...], masked_ref[...], ((0,), (0,))).astype(BF16)
-    part = HID // 4
-    for d in range(4):
-        shares_ref[d, :part, :] = expand_grad[d * part : (d + 1) * part]
-        shares_ref[d, part:, :] = reduce_grad[d * part : (d + 1) * part]
+
+
+def weight_grads_kernel(mixed_ref, masked_ref, hidden_ref, grad_pre_ref, out_ref):
+    quarter = HID // 4
+    pairs = ((grad_pre_ref, mixed_ref), (hidden_ref, masked_ref))
+    for side, (wide_ref, narrow_ref) in enumerate(pairs):
+        grad = matmul(wide_ref[...], narrow_ref[...], ((0,), (0,))).astype(BF16)
+        for d in range(4):
+            out_ref[side, d] = grad[d * quarter : (d + 1) * quarter]
 
 
 def input_grad_kernel(coeffs_ref, grad_mixed_ref, forward_ref, cycle_ref, out_ref):
@@ -253,22 +255,39 @@
 
 
 def piece_kernel(arrived_ref, share_ref, filter_ref):
-    piece = arrived_ref[:, 64:, :].astype(F32).sum(axis=0)
-    share_ref[...] = piece[:16]
-    filter_ref[...] = jnp.broadcast_to(piece[16:][None], filter_ref.shape)
+    came = arrived_ref[:, 64:, :].astype(F32).reshape(PEERS // 2, 2, 16, CH)
+    sums = came.sum(axis=0)
+    share_ref[0] = sums[0, :8]
+    share_ref[1] = sums[1, :8]
+    filter_ref[...] = jnp.broadcast_to((sums[0, 8:] + sums[1, 8:])[None], filter_ref.shape)
 
 
 def spread_kernel(share_ref, filter_ref, out_ref):
-    piece = jnp.concatenate([share_ref[...], filter_ref[...].sum(axis=0)], axis=0)
+    piece = jnp.concatenate([share_ref[0], share_ref[1], filter_ref[...].sum(axis=0)], axis=0)
     out_ref[...] = jnp.broadcast_to(piece[None], out_ref.shape).astype(BF16)
 
 
-def result_kernel(pieces_ref, expand_ref, reduce_ref, filter_ref):
-    half = PEERS // 2
+def result_kernel(
+    pieces_ref,
+    other_ref,
+    core_ref,
+    next_ref,
+    back_ref,
+    expand_ref,
+    reduce_ref,
+    filter_ref,
+    next_out_ref,
+    back_out_ref,
+):
+    next_out_ref[...] = next_ref[...]
+    back_out_ref[...] = back_ref[...]
+    first = core_ref[0] == 0
     for p in range(PEERS):
-        side, at = divmod(p, half)
-        piece = pieces_ref[p].astype(F32)
-        (reduce_ref if side else expand_ref)[at * 12 : at * 12 + 12, :] = piece[:12]
+        mine, other = pieces_ref[p // 2].astype(F32), other_ref[p // 2].astype(F32)
+        piece = jnp.where(first, mine, other) if p % 2 == 0 else jnp.where(first, other, mine)
+        expand_ref[p * 6 : p * 6 + 6, :] = piece[:6]
+        reduce_ref[p * 6 : p * 6 + 6, :] = piece[8:14]
+        side, at = divmod(p, PEERS // 2)
         if at < NLAT // 8:
             filter_ref[side, at * 8 : at * 8 + 8, :] = piece[16:]
 
@@ -292,10 +311,13 @@
 
 
 PAIRED = jax.ShapeDtypeStruct((PEERS, 64, CH), BF16)
-TRIPLE = jax.ShapeDtypeStruct((PEERS, 88, CH), BF16)
+TRIPLE = jax.ShapeDtypeStruct((PEERS, 80, CH), BF16)
 BLOCKS = jax.ShapeDtypeStruct((PEERS, 32, CH), BF16)
 TOKENS = jax.ShapeDtypeStruct((ROWS, NLON, CH), BF16)
 SPECTRAL_SCRATCH = (pltpu.VMEM((LANES * 8, CH), F32), pltpu.VMEM((LANES * 8, CH), F32))
+
+
+CORE_SWAP = [(0, 1), (1, 0)]
 
 
 def exchange(blocks, axes):
@@ -308,6 +330,13 @@
     return lax.ppermute(block, axis, route)
 
 
+def halved(blocks, axis, route, kept):
+    mine = lax.dynamic_index_in_dim(blocks, kept, 0, keepdims=False)
+    sent = lax.dynamic_index_in_dim(blocks, 1 - kept, 0, keepdims=False)
+    came = lax.ppermute(sent, axis, route)
+    return (mine.astype(F32) + came.astype(F32)).astype(BF16)
+
+
 def around(block, axis, distance):
     count = lax.axis_size(axis)
     return lax.ppermute(block, axis, [(i, (i + distance) % count) for i in range(count)])
@@ -325,8 +354,9 @@
 
 
 def share_blocks_of(shares):
-    own = scattered_total(shares, "dp").astype(BF16).reshape(PEERS, 12, CH)
-    return jnp.pad(own, ((0, 0), (0, 4), (0, 0)))
+    kept = halved(shares, "sp_1", CORE_SWAP, lax.axis_index("sp_1"))
+    kept = scattered_total(kept, "dp").astype(BF16)
+    return jnp.pad(kept.reshape(PEERS, 6, CH), ((0, 0), (0, 2), (0, 0)))
 
 
 def on_device(
@@ -383,27 +413,25 @@
     )
     values_fresh = exchange(values_fresh, SP)
 
-    grad_values, grad_mixed, shares = call(
+    narrow = jax.ShapeDtypeStruct((ROWS * NLON, CH), BF16)
+    wide = jax.ShapeDtypeStruct((ROWS * NLON, HID), BF16)
+    grad_values, grad_mixed, *grad_operands = call(
         mlp_back_kernel,
-        [
-            BLOCKS,
-            jax.ShapeDtypeStruct((ROWS, NLON, CH), F32),
-            jax.ShapeDtypeStruct((4, 2 * HID // 4, CH), BF16),
-        ],
+        [BLOCKS, jax.ShapeDtypeStruct((ROWS, NLON, CH), F32), narrow, narrow, wide, wide],
         [saved, values_fresh, cotangent, inverse, inverse_t, expand, contract, own_cycles],
-        [
-            pltpu.VMEM((ROWS * NLON, CH), BF16),
-            pltpu.VMEM((ROWS * NLON, CH), BF16),
-            pltpu.VMEM((ROWS * NLON, HID), BF16),
-            pltpu.VMEM((ROWS * NLON, HID), BF16),
-        ],
-        flops=5 * mlp + 2 * dft,
+        flops=3 * mlp + 2 * dft,
         transcendentals=2 * ROWS * NLON * HID,
         smem=(7,),
     )
     grads_at_orders = exchange(grad_values, SP)
     fresh_values = call(
         fresh_spectral_kernel, [BLOCKS], [values_fresh, ana, syn, filt], SPECTRAL_SCRATCH, flops=leg
+    )[0]
+    shares = call(
+        weight_grads_kernel,
+        [jax.ShapeDtypeStruct((2, 4, HID // 4, CH), BF16)],
+        grad_operands,
+        flops=2 * mlp,
     )[0]
     share_blocks = share_blocks_of(shares)
 
@@ -417,14 +445,10 @@
     coeffs_fresh = exchange(coeffs_fresh, SP)
     share, filter_piece = call(
         piece_kernel,
-        [jax.ShapeDtypeStruct((16, CH), F32), jax.ShapeDtypeStruct((4, 8, CH), F32)],
+        [jax.ShapeDtypeStruct((2, 8, CH), F32), jax.ShapeDtypeStruct((4, 8, CH), F32)],
         [coeffs_fresh],
     )
     filter_piece = exchange(filter_piece, "dp")
-    pieces = call(
-        spread_kernel, [jax.ShapeDtypeStruct((PEERS, 24, CH), BF16)], [share, filter_piece]
-    )[0]
-    pieces = exchange(pieces, SP)
     input_grad = call(
         input_grad_kernel,
         [TOKENS],
@@ -432,7 +456,13 @@
         flops=dft,
         smem=(3,),
     )[0]
-    sent_back = from_behind(input_grad[None, None], "pipe", -1)
+    filter_piece, _ = lax.optimization_barrier((filter_piece, input_grad))
+    pieces = call(
+        spread_kernel, [jax.ShapeDtypeStruct((PEERS // 2, 24, CH), BF16)], [share, filter_piece]
+    )[0]
+    pieces = exchange(pieces, "sp_0")
+    other_pieces = lax.ppermute(pieces, "sp_1", CORE_SWAP)
+    sent_back = from_behind(input_grad, "pipe", -1)
     block = call(
         mlp_kernel,
         [TOKENS],
@@ -441,12 +471,22 @@
         transcendentals=ROWS * NLON * HID,
         smem=(5,),
     )[0]
-    next_input = from_behind(block[None, None], "pipe", 1)
+    next_input = from_behind(block, "pipe", 1)
     part = jax.ShapeDtypeStruct((HID // 4, CH), F32)
-    expand_grad, reduce_grad, filter_grad = call(
-        result_kernel, [part, part, jax.ShapeDtypeStruct((2, NLAT, CH), F32)], [pieces]
-    )
-    return (next_input, sent_back, expand_grad.T[None], reduce_grad[None], filter_grad[None])
+    core = lax.axis_index("sp_1").astype(jnp.int32)[None]
+    expand_grad, reduce_grad, filter_grad, next_input, sent_back = call(
+        result_kernel,
+        [part, part, jax.ShapeDtypeStruct((2, NLAT, CH), F32), TOKENS, TOKENS],
+        [pieces, other_pieces, core, next_input, sent_back],
+        smem=(2,),
+    )
+    return (
+        next_input[None, None],
+        sent_back[None, None],
+        expand_grad.T[None],
+        reduce_grad[None],
+        filter_grad[None],
+    )
 
 
 def solution(mesh):

time: 198 us -> 204 us (1.030)
  waiting for transfers between devices: 74 us -> 64.4 us
  local copies, waits for them, and re-layouts: 6.43 us -> 15.1 us
  starting transfers between devices: 46 us -> 54.3 us
  blocking collectives: 56.2 us -> 51.9 us
    unnamed x30 -> x50, local copies, waits for them, and re-layouts: 4.86 us -> 14.3 us
    ppermute x2, waiting for transfers between devices: 7.47 us -> 0.01 us  [from_behind(): return lax.ppermute(block, axis, route)]
    ppermute x0 -> x2, starting transfers between devices: none -> 7.31 us  [the longest x1 4.92 us: on_device(): other_pieces = lax.ppermute(pieces, 'sp_1', CORE_SWAP)]
    all_to_all x2 -> x1, blocking collectives: 56.2 us -> 51.9 us  [exchange(): return lax.all_to_all(blocks, axes, split_axis=0, concat_axis=0, tiled=True)]
    all_to_all x4 -> x5, waiting for transfers between devices: 63.2 us -> 59.9 us  [exchange(): return lax.all_to_all(blocks, axes, split_axis=0, concat_axis=0, tiled=True)]
    pallas_call x12 -> x13, Pallas kernels: 12.9 us -> 14.6 us  [call(): pl.pallas_call(kernel, out_shape=outs, in_specs=specs, out_specs=[pl.Bloc...]
    all_to_all x4 -> x5, starting transfers between devices: 31.5 us -> 32.5 us  [exchange(): return lax.all_to_all(blocks, axes, split_axis=0, concat_axis=0, tiled=True)]
  transfers between devices with their start and end apart: 9 -> 12, of which waited for: 7 -> 8; matrix products, arithmetic and copies ran while one was open for 1% -> 1% of each run, Pallas kernels for 2% -> 3%
where the time goes in v5:
time: 204 us; the launch traced here: 203 us
  waiting for transfers between devices  64.4 us (32%)
  starting transfers between devices  54.3 us (27%)
  blocking collectives  51.9 us (25%)
  local copies, waits for them, and re-layouts  15.1 us (7%)
  Pallas kernels  14.6 us (7%)
    all_to_all x5, waiting for transfers between devices, exchange(): return lax.all_to_all(blocks, axes, split_axis=0, concat_axis=0, tiled=True)  59.9 us
    all_to_all x1, blocking collectives, exchange(): return lax.all_to_all(blocks, axes, split_axis=0, concat_axis=0, tiled=True)  51.9 us
    all_to_all x5, starting transfers between devices, exchange(): return lax.all_to_all(blocks, axes, split_axis=0, concat_axis=0, tiled=True)  32.5 us
    pallas_call x13, Pallas kernels, call(): pl.pallas_call(kernel, out_shape=outs, in_specs=specs, out_specs=[pl.Bloc...  14.6 us
    unnamed x50, local copies, waits for them, and re-layouts  14.3 us
    ppermute x3, starting transfers between devices, around(): lax.ppermute(block, axis, [(i, (i + distance) % count) for i in range(cou...  10.1 us
    ppermute x1, starting transfers between devices, on_device(): other_pieces = lax.ppermute(pieces, 'sp_1', CORE_SWAP)  4.92 us
    ppermute x2, starting transfers between devices, from_behind(): return lax.ppermute(block, axis, route)  4.43 us
  transfers between devices with their start and end apart: 12, of which 8 were waited for; matrix products, arithmetic and copies ran while one was open for 1% of the time, Pallas kernels for 3%

profile of v5, /device:TPU:1, one launch (start us, length us, event | category | flops | bytes accessed | tf_op | source)
XLA Modules:
  0.0 202.9 jit_solution(6132276147237630817)
XLA Ops:
  1.6 0.9 copy-done.9
  2.5 1.0 shard_map.155
  3.5 16.9 %all-to-all-start = ((bf16[32,32,128]{2,1,0:T(8,128)(2,1)}), bf16[32,32,128]{2,1,0:T(8,128)(2,1)S(1)}, u32[]{:S(2)}, u32[]{:S(2)}) async-start(bf16[32,32,128]{2,1,0:T(8,128)(2,1)} %shard_map.155), calls=%async_computation | async-start | bytes 524288 | tf_op jit(solution)/shard_map/all_to_all | solution.py:324
  23.2 0.9 copy-done.3
  25.3 17.1 %all-to-all-done.arrived_ref = bf16[32,32,128]{2,1,0:T(8,128)(2,1)S(1)} async-done(((bf16[32,32,128]{2,1,0:T(8,128)(2,1)}), bf16[32,32,128]{2,1,0:T(8,128)(2,1)S(1)}, u32[]{:S(2)}, u32[]{:S(2)}) %all-to-all-start) | async-done | bytes 262176 | tf_op jit(solution)/shard_map/all_to_all | solution.py:324
  42.4 1.3 shard_map.158
  44.5 4.5 %all-to-all-start.1 = ((bf16[32,64,128]{2,1,0:T(8,128)(2,1)}), bf16[32,64,128]{2,1,0:T(8,128)(2,1)S(1)}, u32[]{:S(2)}, u32[]{:S(2)}) async-start(bf16[32,64,128]{2,1,0:T(8,128)(2,1)} %get-tuple-element.25), calls=%async_computation.1 | async-start | bytes 1048576 | tf_op jit(solution)/shard_map/all_to_all | solution.py:324
  49.1 33.5 %all-to-all-done.1.values_ref.arrived_ref = bf16[32,64,128]{2,1,0:T(8,128)(2,1)S(1)} async-done(((bf16[32,64,128]{2,1,0:T(8,128)(2,1)}), bf16[32,64,128]{2,1,0:T(8,128)(2,1)S(1)}, u32[]{:S(2)}, u32[]{:S(2)}) %all-to-all-start.1) | async-done | bytes 524320 | tf_op jit(solution)/shard_map/all_to_all | solution.py:324
  85.4 0.9 copy-done.22
  87.2 4.2 %shard_map.159 = (bf16[32,32,128]{2,1,0:T(8,128)(2,1)}, f32[4,240,128]{2,1,0:T(8,128)S(1)}, bf16[960,128]{1,0:T(8,128)(2,1)S(1)}, bf16[960,128]{1,0:T(8,128)(2,1...) custom-call(bf16[4,240,128]{2,1,0:T(8,128)(2,1)S(1)} %bitcast.44, ...), custom_call_target="tpu_custom_call" | custom-call | flops 692060160 | bytes 5849104 | tf_op jit(solution)/shard_map/pallas_call | solution.py:300
  91.5 1.1 copy-done
  93.3 4.3 %all-to-all-start.2 = ((bf16[32,32,128]{2,1,0:T(8,128)(2,1)}), bf16[32,32,128]{2,1,0:T(8,128)(2,1)S(1)}, u32[]{:S(2)}, u32[]{:S(2)}) async-start(bf16[32,32,128]{2,1,0:T(8,128)(2,1)} %get-tuple-element.26), calls=%async_computation.2 | async-start | bytes 524288 | tf_op jit(solution)/shard_map/all_to_all | solution.py:324
  97.6 1.4 copy-done.1
  99.0 0.9 copy-done.12
  99.9 0.9 copy-done.14
  100.9 1.0 shard_map.161
  102.0 2.4 %collective-permute-start = (bf16[4,192,128]{2,1,0:T(8,128)(2,1)S(1)}, bf16[4,192,128]{2,1,0:T(8,128)(2,1)S(1)}, u32[]{:S(2)}, u32[]{:S(2)}) collective-permute-start(bf16[4,192,128]{2,1,0:T(8,128)(2,1)S(1)} %dynamic-slice_bitcast_fusion), channel_id=1, source_target_pairs={{0,4},{4,0},{1,5},{5,1},{2,6},{6,2},{3,7},{7,3},{8,12},{12,8},{9,1... | collective-permute-start | bytes 589832 | tf_op jit(solution)/shard_map/ppermute | solution.py:336
  104.4 1.0 collective-permute-done
  105.5 3.2 %collective-permute-start.1 = (bf16[192,128]{1,0:T(8,128)(2,1)S(1)}, bf16[192,128]{1,0:T(8,128)(2,1)S(1)}, u32[]{:S(2)}, u32[]{:S(2)}) collective-permute-start(bf16[192,128]{1,0:T(8,128)(2,1)S(1)} %get-tuple-element.41), channel_id=1, source_target_pairs={{0,1},{1,2},{2,3},{3,0},{4,5},{5,6},{6,7},{7,4},{8,9},{9,10},{10,1... | collective-permute-start | bytes 147464 | tf_op jit(solution)/shard_map/ppermute | solution.py:342
  108.7 3.4 %collective-permute-start.3 = (bf16[192,128]{1,0:T(8,128)(2,1)S(1)}, bf16[192,128]{1,0:T(8,128)(2,1)S(1)}, u32[]{:S(2)}, u32[]{:S(2)}) collective-permute-start(bf16[192,128]{1,0:T(8,128)(2,1)S(1)} %get-tuple-element.42), channel_id=1, source_target_pairs={{0,3},{1,0},{2,1},{3,2},{4,7},{5,4},{6,5},{7,6},{8,11},{9,8},{10,9... | collective-permute-start | bytes 147464 | tf_op jit(solution)/shard_map/ppermute | solution.py:342
  112.1 3.5 %collective-permute-start.2 = (bf16[192,128]{1,0:T(8,128)(2,1)S(1)}, bf16[192,128]{1,0:T(8,128)(2,1)S(1)}, u32[]{:S(2)}, u32[]{:S(2)}) collective-permute-start(bf16[192,128]{1,0:T(8,128)(2,1)S(1)} %get-tuple-element.43), channel_id=1, source_target_pairs={{0,2},{1,3},{2,0},{3,1},{4,6},{5,7},{6,4},{7,5},{8,10},{9,11},{10,... | collective-permute-start | bytes 147464 | tf_op jit(solution)/shard_map/ppermute | solution.py:342
  116.2 2.6 %collective-permute-done.2 = bf16[192,128]{1,0:T(8,128)(2,1)S(1)} collective-permute-done((bf16[192,128]{1,0:T(8,128)(2,1)S(1)}, bf16[192,128]{1,0:T(8,128)(2,1)S(1)}, u32[]{:S(2)}, u32[]{:S(2)}) %collective-permute-start.2) | collective-permute-done | bytes 49184 | tf_op jit(solution)/shard_map/ppermute | solution.py:342
  120.1 51.9 %all_to_all.30.arrived_ref.coeffs_ref.values_ref = bf16[32,80,128]{2,1,0:T(8,128)(2,1)S(1)} all-to-all(bf16[32,80,128]{2,1,0:T(8,128)(2,1)S(1)} %shard_map.162), channel_id=1, replica_groups=mesh['pipe'=4,'sp_0'=16,'sp_1'=2,'dp'=4] {'sp_0','sp_1'}, dimensions={0} | all-to-all | bytes 1310720 | tf_op jit(solution)/shard_map/all_to_all | solution.py:324
  172.6 3.3 %all-to-all-start.4 = ((f32[4,8,128]{2,1,0:T(8,128)}), f32[4,8,128]{2,1,0:T(8,128)S(1)}, u32[]{:S(2)}, u32[]{:S(2)}) async-start(f32[4,8,128]{2,1,0:T(8,128)} %get-tuple-element.33), calls=%async_computation.4 | async-start | bytes 32768 | tf_op jit(solution)/shard_map/all_to_all | solution.py:324
  176.7 3.3 %all-to-all-done.4.filter_ref = f32[4,8,128]{2,1,0:T(8,128)S(1)} async-done(((f32[4,8,128]{2,1,0:T(8,128)}), f32[4,8,128]{2,1,0:T(8,128)S(1)}, u32[]{:S(2)}, u32[]{:S(2)}) %all-to-all-start.4) | async-done | bytes 16416 | tf_op jit(solution)/shard_map/all_to_all | solution.py:324
  180.7 3.5 %all-to-all-start.5 = ((bf16[16,24,128]{2,1,0:T(8,128)(2,1)}), bf16[16,24,128]{2,1,0:T(8,128)(2,1)S(1)}, u32[]{:S(2)}, u32[]{:S(2)}) async-start(bf16[16,24,128]{2,1,0:T(8,128)(2,1)} %shard_map.165), calls=%async_computation.5 | async-start | bytes 196608 | tf_op jit(solution)/shard_map/all_to_all | solution.py:324
  184.3 2.2 %shard_map.166 = bf16[4,240,128]{2,1,0:T(8,128)(2,1)S(1)} custom-call(bf16[4,240,128]{2,1,0:T(8,128)(2,1)S(1)} %bitcast.42, bf16[32,80,128]{2,1,0:T(8,128)(2,1)S(1)} %all_to_all.30.arrived_ref.coeffs_ref.values_ref, bf16[240,256]{1,0:T(8,128)(2,1)S(1)} %copy-done.20, bf16[128,768]{1,0:T(8,128)(2,1)S(1)} %bitcast.46, bf16[768,128]{1,0:T(8,128)(2,1)S(1)} %bitcast.48, ...), custom_call_target="tpu_custom_call" | custom-call | flops 440401920 | bytes 1662992 | tf_op jit(solution)/shard_map/pallas_call | solution.py:300
  186.5 3.1 %collective-permute-start.5 = (bf16[4,240,128]{2,1,0:T(8,128)(2,1)S(1)}, bf16[4,240,128]{2,1,0:T(8,128)(2,1)S(1)}, u32[]{:S(2)}, u32[]{:S(2)}) collective-permute-start(bf16[4,240,128]{2,1,0:T(8,128)(2,1)S(1)} %shard_map.166), channel_id=1, source_target_pairs={{0,128},{128,256},{256,384},{1,129},{129,257},{257,385},{2,130},{1... | collective-permute-start | bytes 737288 | tf_op jit(solution)/shard_map/ppermute | solution.py:330
  189.6 1.3 collective-permute-start.6
  190.9 5.2 %all-to-all-done.5.pieces_ref = bf16[16,24,128]{2,1,0:T(8,128)(2,1)S(1)} async-done(((bf16[16,24,128]{2,1,0:T(8,128)(2,1)}), bf16[16,24,128]{2,1,0:T(8,128)(2,1)S(1)}, u32[]{:S(2)}, u32[]{:S(2)}) %all-to-all-start.5) | async-done | bytes 98336 | tf_op jit(solution)/shard_map/all_to_all | solution.py:324
  196.1 4.9 %collective-permute-start.4 = (bf16[16,24,128]{2,1,0:T(8,128)(2,1)S(1)}, bf16[16,24,128]{2,1,0:T(8,128)(2,1)S(1)}, u32[]{:S(2)}, u32[]{:S(2)}) collective-permute-start(bf16[16,24,128]{2,1,0:T(8,128)(2,1)S(1)} %all-to-all-done.5.pieces_ref), channel_id=1, source_target_pairs={{0,4},{4,0},{1,5},{5,1},{2,6},{6,2},{3,7},{7,3},{8,12},{12,8},{9,1... | collective-permute-start | bytes 294920 | tf_op jit(solution)/shard_map/ppermute | solution.py:464
  201.9 0.9 shard_map.167
  (67 shorter events, 15.1 us)
Async XLA Ops:
  0.6 41.8 %copy-start.2 = (f32[1,2,120,128]{3,2,1,0:T(8,128)S(1)}, f32[1,2,120,128]{3,2,1,0:T(8,128)}, u32[]{:S(2)}) copy-start(f32[1,2,120,128]{3,2,1,0:T(8,128)} %param.17) | copy-start | bytes 368644
  0.6 0.9 copy-start.5
  1.6 0.9 copy-start.9
  3.5 79.1 %copy-start.10 = (bf16[1,1,4,240,128]{4,3,2,1,0:T(8,128)(2,1)S(1)}, bf16[1,1,4,240,128]{4,3,2,1,0:T(8,128)(2,1)}, u32[]{:S(2)}) copy-start(bf16[1,1,4,240,128]{4,3,2,1,0:T(8,128)(2,1)} %param.13) | copy-start | bytes 737284
  3.5 38.9 %all-to-all-start = ((bf16[32,32,128]{2,1,0:T(8,128)(2,1)}), bf16[32,32,128]{2,1,0:T(8,128)(2,1)S(1)}, u32[]{:S(2)}, u32[]{:S(2)}) async-start(bf16[32,32,128]{2,1,0:T(8,128)(2,1)} %shard_map.155), calls=%async_computation | async-start | bytes 524288 | tf_op jit(solution)/shard_map/all_to_all | solution.py:324
  20.4 28.6 %copy-start.24 = (s32[128]{0:T(128)S(1)}, s32[128]{0:T(128)}, u32[]{:S(2)}) copy-start(s32[128]{0:T(128)} %param.18) | copy-start | bytes 1540
  23.2 0.9 copy-start.3
  44.5 38.1 %all-to-all-start.1 = ((bf16[32,64,128]{2,1,0:T(8,128)(2,1)}), bf16[32,64,128]{2,1,0:T(8,128)(2,1)S(1)}, u32[]{:S(2)}, u32[]{:S(2)}) async-start(bf16[32,64,128]{2,1,0:T(8,128)(2,1)} %get-tuple-element.25), calls=%async_computation.1 | async-start | bytes 1048576 | tf_op jit(solution)/shard_map/all_to_all | solution.py:324
  82.6 0.9 copy-start.15
  83.5 0.9 copy-start.17
  85.4 0.9 copy-start.22
  91.4 1.1 copy-start
  93.3 4.3 %copy-start.11 = (bf16[960,128]{1,0:T(8,128)(2,1)}, bf16[960,128]{1,0:T(8,128)(2,1)S(1)}, u32[]{:S(2)}) copy-start(bf16[960,128]{1,0:T(8,128)(2,1)S(1)} %get-tuple-element.28.mixed_ref) | copy-start | bytes 737284
  93.3 26.3 %all-to-all-start.2 = ((bf16[32,32,128]{2,1,0:T(8,128)(2,1)}), bf16[32,32,128]{2,1,0:T(8,128)(2,1)S(1)}, u32[]{:S(2)}, u32[]{:S(2)}) async-start(bf16[32,32,128]{2,1,0:T(8,128)(2,1)} %get-tuple-element.26), calls=%async_computation.2 | async-start | bytes 524288 | tf_op jit(solution)/shard_map/all_to_all | solution.py:324
  97.6 1.4 copy-start.1
  99.0 0.9 copy-start.12
  99.9 0.9 copy-start.14
  101.9 17.7 %copy-start.8 = (f32[4,128,256]{2,1,0:T(8,128)S(1)}, f32[4,128,256]{2,1,0:T(8,128)}, u32[]{:S(2)}) copy-start(f32[4,128,256]{2,1,0:T(8,128)} %copy-done.7) | copy-start | bytes 1572868
  102.0 3.5 %collective-permute-start = (bf16[4,192,128]{2,1,0:T(8,128)(2,1)S(1)}, bf16[4,192,128]{2,1,0:T(8,128)(2,1)S(1)}, u32[]{:S(2)}, u32[]{:S(2)}) collective-permute-start(bf16[4,192,128]{2,1,0:T(8,128)(2,1)S(1)} %dynamic-slice_bitcast_fusion), channel_id=1, source_target_pairs={{0,4},{4,0},{1,5},{5,1},{2,6},{6,2},{3,7},{7,3},{8,12},{12,8},{9,1... | collective-permute-start | bytes 589832 | tf_op jit(solution)/shard_map/ppermute | solution.py:336
  105.5 10.6 %collective-permute-start.1 = (bf16[192,128]{1,0:T(8,128)(2,1)S(1)}, bf16[192,128]{1,0:T(8,128)(2,1)S(1)}, u32[]{:S(2)}, u32[]{:S(2)}) collective-permute-start(bf16[192,128]{1,0:T(8,128)(2,1)S(1)} %get-tuple-element.41), channel_id=1, source_target_pairs={{0,1},{1,2},{2,3},{3,0},{4,5},{5,6},{6,7},{7,4},{8,9},{9,10},{10,1... | collective-permute-start | bytes 147464 | tf_op jit(solution)/shard_map/ppermute | solution.py:342
  108.7 7.4 %collective-permute-start.3 = (bf16[192,128]{1,0:T(8,128)(2,1)S(1)}, bf16[192,128]{1,0:T(8,128)(2,1)S(1)}, u32[]{:S(2)}, u32[]{:S(2)}) collective-permute-start(bf16[192,128]{1,0:T(8,128)(2,1)S(1)} %get-tuple-element.42), channel_id=1, source_target_pairs={{0,3},{1,0},{2,1},{3,2},{4,7},{5,4},{6,5},{7,6},{8,11},{9,8},{10,9... | collective-permute-start | bytes 147464 | tf_op jit(solution)/shard_map/ppermute | solution.py:342
  112.1 6.6 %collective-permute-start.2 = (bf16[192,128]{1,0:T(8,128)(2,1)S(1)}, bf16[192,128]{1,0:T(8,128)(2,1)S(1)}, u32[]{:S(2)}, u32[]{:S(2)}) collective-permute-start(bf16[192,128]{1,0:T(8,128)(2,1)S(1)} %get-tuple-element.43), channel_id=1, source_target_pairs={{0,2},{1,3},{2,0},{3,1},{4,6},{5,7},{6,4},{7,5},{8,10},{9,11},{10,... | collective-permute-start | bytes 147464 | tf_op jit(solution)/shard_map/ppermute | solution.py:342
  120.1 55.8 %copy-start.21 = (bf16[240,256]{1,0:T(8,128)(2,1)S(1)}, bf16[240,256]{1,0:T(8,128)(2,1)}, u32[]{:S(2)}) copy-start(bf16[240,256]{1,0:T(8,128)(2,1)} %constant.96.clone.forward_ref) | copy-start | bytes 368644
  172.0 12.2 %copy-start.4 = (bf16[1,1,4,240,128]{4,3,2,1,0:T(8,128)(2,1)S(1)}, bf16[1,1,4,240,128]{4,3,2,1,0:T(8,128)(2,1)}, u32[]{:S(2)}) copy-start(bf16[1,1,4,240,128]{4,3,2,1,0:T(8,128)(2,1)} %param.12) | copy-start | bytes 737284
  172.0 12.3 %copy-start.16 = (bf16[1,128,768]{2,1,0:T(8,128)(2,1)S(1)}, bf16[1,128,768]{2,1,0:T(8,128)(2,1)}, u32[]{:S(2)}) copy-start(bf16[1,128,768]{2,1,0:T(8,128)(2,1)} %param.15) | copy-start | bytes 589828
  172.0 12.3 %copy-start.18 = (bf16[1,768,128]{2,1,0:T(8,128)(2,1)S(1)}, bf16[1,768,128]{2,1,0:T(8,128)(2,1)}, u32[]{:S(2)}) copy-start(bf16[1,768,128]{2,1,0:T(8,128)(2,1)} %param.16) | copy-start | bytes 589828
  172.0 12.3 %copy-start.20 = (bf16[240,256]{1,0:T(8,128)(2,1)S(1)}, bf16[240,256]{1,0:T(8,128)(2,1)}, u32[]{:S(2)}) copy-start(bf16[240,256]{1,0:T(8,128)(2,1)} %constant.98.clone.inverse_ref) | copy-start | bytes 368644
  172.6 7.4 %all-to-all-start.4 = ((f32[4,8,128]{2,1,0:T(8,128)}), f32[4,8,128]{2,1,0:T(8,128)S(1)}, u32[]{:S(2)}, u32[]{:S(2)}) async-start(f32[4,8,128]{2,1,0:T(8,128)} %get-tuple-element.33), calls=%async_computation.4 | async-start | bytes 32768 | tf_op jit(solution)/shard_map/all_to_all | solution.py:324
  180.7 15.3 %all-to-all-start.5 = ((bf16[16,24,128]{2,1,0:T(8,128)(2,1)}), bf16[16,24,128]{2,1,0:T(8,128)(2,1)S(1)}, u32[]{:S(2)}, u32[]{:S(2)}) async-start(bf16[16,24,128]{2,1,0:T(8,128)(2,1)} %shard_map.165), calls=%async_computation.5 | async-start | bytes 196608 | tf_op jit(solution)/shard_map/all_to_all | solution.py:324
  186.5 14.5 %collective-permute-start.5 = (bf16[4,240,128]{2,1,0:T(8,128)(2,1)S(1)}, bf16[4,240,128]{2,1,0:T(8,128)(2,1)S(1)}, u32[]{:S(2)}, u32[]{:S(2)}) collective-permute-start(bf16[4,240,128]{2,1,0:T(8,128)(2,1)S(1)} %shard_map.166), channel_id=1, source_target_pairs={{0,128},{128,256},{256,384},{1,129},{129,257},{257,385},{2,130},{1... | collective-permute-start | bytes 737288 | tf_op jit(solution)/shard_map/ppermute | solution.py:330
  189.6 11.4 %collective-permute-start.6 = (bf16[4,240,128]{2,1,0:T(8,128)(2,1)S(1)}, bf16[4,240,128]{2,1,0:T(8,128)(2,1)S(1)}, u32[]{:S(2)}, u32[]{:S(2)}) collective-permute-start(bf16[4,240,128]{2,1,0:T(8,128)(2,1)S(1)} %shard_map.164), channel_id=1, source_target_pairs={{128,0},{256,128},{384,256},{129,1},{257,129},{385,257},{130,2},{2... | collective-permute-start | bytes 737288 | tf_op jit(solution)/shard_map/ppermute | solution.py:330
  196.1 5.9 %collective-permute-start.4 = (bf16[16,24,128]{2,1,0:T(8,128)(2,1)S(1)}, bf16[16,24,128]{2,1,0:T(8,128)(2,1)S(1)}, u32[]{:S(2)}, u32[]{:S(2)}) collective-permute-start(bf16[16,24,128]{2,1,0:T(8,128)(2,1)S(1)} %all-to-all-done.5.pieces_ref), channel_id=1, source_target_pairs={{0,4},{4,0},{1,5},{5,1},{2,6},{6,2},{3,7},{7,3},{8,12},{12,8},{9,1... | collective-permute-start | bytes 294920 | tf_op jit(solution)/shard_map/ppermute | solution.py:464
  (5 other events, 4.2 us)

commit v6 on v5

--- a/solution.py
+++ b/solution.py
@@ -16,6 +16,7 @@
 HID = 768
 ROWS = 4
 PEERS = 32
+VMEM_LIMIT = 16 * 1024 * 1024
 LANES = 128
 SP = ("sp_0", "sp_1")
 
@@ -101,7 +102,27 @@
     return lax.dot_general(left, right, (dims, ((), ())), preferred_element_type=F32)
 
 
-def coeffs_kernel(x_ref, forward_ref, out_ref):
+def fetch(source, target, sem):
+    copy = pltpu.make_async_copy(source, target, sem)
+    copy.start()
+    return copy
+
+
+def saved_coeffs_kernel(x_hbm, forward_hbm, out_ref, x_ref, forward_ref, sems):
+    table = fetch(forward_hbm, forward_ref, sems.at[ROWS])
+    cycles = [fetch(x_hbm.at[j], x_ref.at[j], sems.at[j]) for j in range(ROWS)]
+    table.wait()
+    for half in range(2):
+        cycles[2 * half].wait()
+        cycles[2 * half + 1].wait()
+        to_blocks(out_ref, half, [matmul(forward_ref[...], x_ref[2 * half + h]) for h in range(2)])
+
+
+def fresh_coeffs_kernel(x_ref, forward_ref, *rest):
+    count = len(rest) // 2
+    out_ref = rest[count]
+    for source, target in zip(rest[:count], rest[count + 1 :]):
+        target[...] = source[...]
     for half in range(2):
         to_blocks(out_ref, half, [matmul(forward_ref[...], x_ref[2 * half + h]) for h in range(2)])
 
@@ -136,10 +157,13 @@
     out_ref[:, :32, :] = goes_ref[...].reshape(PEERS, 32, CH).astype(BF16)
 
 
-def fresh_spectral_kernel(arrived_ref, ana_ref, syn_ref, filt_ref, out_ref, came_ref, goes_ref):
+def fresh_spectral_kernel(
+    arrived_ref, ana_ref, syn_ref, filt_ref, beside_ref, out_ref, came_ref, goes_ref
+):
+    out_ref[:, :32, :] = beside_ref[...]
     came_ref[...] = arrived_ref[:, 32:, :].reshape(LANES * 8, CH).astype(F32)
     spectral(came_ref, goes_ref, ana_ref, syn_ref, filt_ref)
-    out_ref[...] = goes_ref[...].reshape(PEERS, 32, CH).astype(BF16)
+    out_ref[:, 32:, :] = goes_ref[...].reshape(PEERS, 32, CH).astype(BF16)
 
 
 def spectral_back_kernel(
@@ -148,14 +172,12 @@
     ana_ref,
     syn_ref,
     filt_ref,
-    beside_ref,
     shares_ref,
     out_ref,
     came_ref,
     goes_ref,
 ):
-    out_ref[:, 32:64, :] = beside_ref[...]
-    came_ref[...] = arrived_ref[...].reshape(LANES * 8, CH).astype(F32)
+    came_ref[...] = arrived_ref[:, :32, :].reshape(LANES * 8, CH).astype(F32)
     real, imag = padded_filter(filt_ref)
     total_real = jnp.zeros((LANES, CH), F32)
     total_imag = jnp.zeros((LANES, CH), F32)
@@ -176,7 +198,7 @@
     out_ref[:, :32, :] = goes_ref[...].reshape(PEERS, 32, CH).astype(BF16)
     filter_part = jnp.concatenate([total_real, total_imag], axis=0).reshape(PEERS, 8, CH)
     sums = jnp.concatenate([shares_ref[...].astype(F32), filter_part], axis=1)
-    out_ref[:, 64:, :] = sums.astype(BF16)
+    out_ref[:, 32:, :] = sums.astype(BF16)
 
 
 def live(cycle_ref, j):
@@ -206,6 +228,7 @@
     cycle_ref,
     out_ref,
     grad_mixed_ref,
+    shares_ref,
     mixed_ref,
     masked_ref,
     hidden_ref,
@@ -234,15 +257,12 @@
             grad_mixed_ref[j] = grad_mixed
             grad_values.append(matmul(inverse_t_ref[...], grad_mixed.astype(BF16)))
         to_blocks(out_ref, half, grad_values)
-
-
-def weight_grads_kernel(mixed_ref, masked_ref, hidden_ref, grad_pre_ref, out_ref):
     quarter = HID // 4
     pairs = ((grad_pre_ref, mixed_ref), (hidden_ref, masked_ref))
     for side, (wide_ref, narrow_ref) in enumerate(pairs):
         grad = matmul(wide_ref[...], narrow_ref[...], ((0,), (0,))).astype(BF16)
         for d in range(4):
-            out_ref[side, d] = grad[d * quarter : (d + 1) * quarter]
+            shares_ref[side, d] = grad[d * quarter : (d + 1) * quarter]
 
 
 def input_grad_kernel(coeffs_ref, grad_mixed_ref, forward_ref, cycle_ref, out_ref):
@@ -255,7 +275,7 @@
 
 
 def piece_kernel(arrived_ref, share_ref, filter_ref):
-    came = arrived_ref[:, 64:, :].astype(F32).reshape(PEERS // 2, 2, 16, CH)
+    came = arrived_ref[:, 32:, :].astype(F32).reshape(PEERS // 2, 2, 16, CH)
     sums = came.sum(axis=0)
     share_ref[0] = sums[0, :8]
     share_ref[1] = sums[1, :8]
@@ -292,10 +312,11 @@
             filter_ref[side, at * 8 : at * 8 + 8, :] = piece[16:]
 
 
-def call(kernel, outs, args, scratch=(), flops=0, transcendentals=0, smem=()):
-    specs = [
-        pl.BlockSpec(memory_space=pltpu.SMEM if n in smem else pltpu.VMEM) for n in range(len(args))
-    ]
+def call(
+    kernel, outs, args, scratch=(), flops=0, transcendentals=0, smem=(), hbm=(), limit=VMEM_LIMIT
+):
+    places = {n: pltpu.SMEM for n in smem} | {n: pl.ANY for n in hbm}
+    specs = [pl.BlockSpec(memory_space=places.get(n, pltpu.VMEM)) for n in range(len(args))]
     moved = sum(a.size * a.dtype.itemsize for a in (*args, *outs))
     return pl.pallas_call(
         kernel,
@@ -303,7 +324,7 @@
         in_specs=specs,
         out_specs=[pl.BlockSpec(memory_space=pltpu.VMEM)] * len(outs),
         scratch_shapes=list(scratch),
-        compiler_params=pltpu.CompilerParams(vmem_limit_bytes=24 * 1024 * 1024),
+        compiler_params=pltpu.CompilerParams(vmem_limit_bytes=limit),
         cost_estimate=pl.CostEstimate(
             flops=flops, bytes_accessed=moved, transcendentals=transcendentals
         ),
@@ -311,7 +332,7 @@
 
 
 PAIRED = jax.ShapeDtypeStruct((PEERS, 64, CH), BF16)
-TRIPLE = jax.ShapeDtypeStruct((PEERS, 80, CH), BF16)
+SUMMED = jax.ShapeDtypeStruct((PEERS, 48, CH), BF16)
 BLOCKS = jax.ShapeDtypeStruct((PEERS, 32, CH), BF16)
 TOKENS = jax.ShapeDtypeStruct((ROWS, NLON, CH), BF16)
 SPECTRAL_SCRATCH = (pltpu.VMEM((LANES * 8, CH), F32), pltpu.VMEM((LANES * 8, CH), F32))
@@ -383,9 +404,27 @@
     leg = 2 * 16 * 128 * 128 * CH
     mlp = 2 * ROWS * NLON * CH * HID
 
-    saved_blocks = call(coeffs_kernel, [BLOCKS], [saved, forward_t], flops=dft)[0]
+    saved_blocks = call(
+        saved_coeffs_kernel,
+        [BLOCKS],
+        [saved, forward_t],
+        (
+            pltpu.VMEM((ROWS, NLON, CH), BF16),
+            pltpu.VMEM((256, NLON), BF16),
+            pltpu.SemaphoreType.DMA((ROWS + 1,)),
+        ),
+        flops=dft,
+        hbm=(0, 1),
+        limit=60 * 1024 * 1024,
+    )[0]
     saved_at_orders = exchange(saved_blocks, SP)
-    fresh_blocks = call(coeffs_kernel, [BLOCKS], [fresh, forward_t], flops=dft)[0]
+    kept = [inverse, inverse_t, expand, contract]
+    fresh_blocks, inverse, inverse_t, expand, contract = call(
+        fresh_coeffs_kernel,
+        [BLOCKS] + [jax.ShapeDtypeStruct(k.shape, BF16) for k in kept],
+        [fresh, forward_t, *kept],
+        flops=dft,
+    )
 
     lat_live = (cycle_table < NLAT).astype(F32)
     colatitude = math.pi * (jnp.minimum(cycle_table, NLAT - 1).astype(F32) + 0.5) / NLAT
@@ -413,46 +452,59 @@
     )
     values_fresh = exchange(values_fresh, SP)
 
-    narrow = jax.ShapeDtypeStruct((ROWS * NLON, CH), BF16)
-    wide = jax.ShapeDtypeStruct((ROWS * NLON, HID), BF16)
-    grad_values, grad_mixed, *grad_operands = call(
+    narrow = pltpu.VMEM((ROWS * NLON, CH), BF16)
+    wide = pltpu.VMEM((ROWS * NLON, HID), BF16)
+    grad_values, grad_mixed, shares = call(
         mlp_back_kernel,
-        [BLOCKS, jax.ShapeDtypeStruct((ROWS, NLON, CH), F32), narrow, narrow, wide, wide],
+        [
+            BLOCKS,
+            jax.ShapeDtypeStruct((ROWS, NLON, CH), F32),
+            jax.ShapeDtypeStruct((2, 4, HID // 4, CH), BF16),
+        ],
         [saved, values_fresh, cotangent, inverse, inverse_t, expand, contract, own_cycles],
-        flops=3 * mlp + 2 * dft,
+        [narrow, narrow, wide, wide],
+        flops=5 * mlp + 2 * dft,
         transcendentals=2 * ROWS * NLON * HID,
         smem=(7,),
     )
-    grads_at_orders = exchange(grad_values, SP)
-    fresh_values = call(
-        fresh_spectral_kernel, [BLOCKS], [values_fresh, ana, syn, filt], SPECTRAL_SCRATCH, flops=leg
-    )[0]
-    shares = call(
-        weight_grads_kernel,
-        [jax.ShapeDtypeStruct((2, 4, HID // 4, CH), BF16)],
-        grad_operands,
-        flops=2 * mlp,
-    )[0]
-    share_blocks = share_blocks_of(shares)
-
-    coeffs_fresh = call(
-        spectral_back_kernel,
-        [TRIPLE],
-        [grads_at_orders, spectra, ana, syn, filt, fresh_values, share_blocks],
+    grads_fresh = call(
+        fresh_spectral_kernel,
+        [PAIRED],
+        [values_fresh, ana, syn, filt, grad_values],
         SPECTRAL_SCRATCH,
         flops=leg,
     )[0]
-    coeffs_fresh = exchange(coeffs_fresh, SP)
+    grads_fresh = exchange(grads_fresh, SP)
+    share_blocks = share_blocks_of(shares)
+
+    block = call(
+        mlp_kernel,
+        [TOKENS],
+        [fresh, grads_fresh, inverse, expand, contract, own_cycles],
+        flops=2 * mlp + dft,
+        transcendentals=ROWS * NLON * HID,
+        smem=(5,),
+    )[0]
+    next_input = from_behind(block, "pipe", 1)
+    coeffs_summed = call(
+        spectral_back_kernel,
+        [SUMMED],
+        [grads_fresh, spectra, ana, syn, filt, share_blocks],
+        SPECTRAL_SCRATCH,
+        flops=leg,
+    )[0]
+    coeffs_summed = exchange(coeffs_summed, SP)
+    coeffs_summed, next_input = lax.optimization_barrier((coeffs_summed, next_input))
     share, filter_piece = call(
         piece_kernel,
         [jax.ShapeDtypeStruct((2, 8, CH), F32), jax.ShapeDtypeStruct((4, 8, CH), F32)],
-        [coeffs_fresh],
+        [coeffs_summed],
     )
     filter_piece = exchange(filter_piece, "dp")
     input_grad = call(
         input_grad_kernel,
         [TOKENS],
-        [coeffs_fresh, grad_mixed, forward, own_cycles],
+        [coeffs_summed, grad_mixed, forward, own_cycles],
         flops=dft,
         smem=(3,),
     )[0]
@@ -463,15 +515,6 @@
     pieces = exchange(pieces, "sp_0")
     other_pieces = lax.ppermute(pieces, "sp_1", CORE_SWAP)
     sent_back = from_behind(input_grad, "pipe", -1)
-    block = call(
-        mlp_kernel,
-        [TOKENS],
-        [fresh, coeffs_fresh, inverse, expand, contract, own_cycles],
-        flops=2 * mlp + dft,
-        transcendentals=ROWS * NLON * HID,
-        smem=(5,),
-    )[0]
-    next_input = from_behind(block, "pipe", 1)
     part = jax.ShapeDtypeStruct((HID // 4, CH), F32)
     core = lax.axis_index("sp_1").astype(jnp.int32)[None]
     expand_grad, reduce_grad, filter_grad, next_input, sent_back = call(

time: 204 us -> 193 us (0.946)
  blocking collectives: 51.9 us -> 0 us
  waiting for transfers between devices: 64.4 us -> 111 us
  local copies, waits for them, and re-layouts: 15.1 us -> 2.52 us
  starting transfers between devices: 54.3 us -> 61 us
    all_to_all x1 -> x0, blocking collectives: 51.9 us -> none  [exchange(): return lax.all_to_all(blocks, axes, split_axis=0, concat_axis=0, tiled=True)]
    all_to_all x5 -> x6, waiting for transfers between devices: 59.9 us -> 102 us  [exchange(): return lax.all_to_all(blocks, axes, split_axis=0, concat_axis=0, tiled=True)]
    unnamed x50 -> x34, local copies, waits for them, and re-layouts: 14.3 us -> 1.64 us
    all_to_all x5 -> x6, starting transfers between devices: 32.5 us -> 38.1 us  [exchange(): return lax.all_to_all(blocks, axes, split_axis=0, concat_axis=0, tiled=True)]
    ppermute x2, waiting for transfers between devices: 0.01 us -> 4.96 us  [from_behind(): return lax.ppermute(block, axis, route)]
    pallas_call x13 -> x12, Pallas kernels: 14.6 us -> 16.4 us  [call(): pl.pallas_call(kernel, out_shape=outs, in_specs=specs, out_specs=[pl.Bloc...]
  transfers between devices with their start and end apart: 12 -> 13, of which waited for: 8 -> 10; matrix products, arithmetic and copies ran while one was open for 1% -> 1% of each run, Pallas kernels for 3% -> 2%
where the time goes in v6:
time: 193 us; the launch traced here: 192 us
  waiting for transfers between devices  111 us (58%)
  starting transfers between devices  61 us (32%)
  Pallas kernels  16.4 us (8%)
  local copies, waits for them, and re-layouts  2.52 us (1%)
    all_to_all x6, waiting for transfers between devices, exchange(): return lax.all_to_all(blocks, axes, split_axis=0, concat_axis=0, tiled=True)  102 us
    all_to_all x6, starting transfers between devices, exchange(): return lax.all_to_all(blocks, axes, split_axis=0, concat_axis=0, tiled=True)  38.1 us
    pallas_call x12, Pallas kernels, call(): pl.pallas_call(kernel, out_shape=outs, in_specs=specs, out_specs=[pl.Bloc...  16.4 us
    ppermute x3, starting transfers between devices, around(): lax.ppermute(block, axis, [(i, (i + distance) % count) for i in range(cou...  10.7 us
    ppermute x1, starting transfers between devices, on_device(): other_pieces = lax.ppermute(pieces, 'sp_1', CORE_SWAP)  5.43 us
    ppermute x2, waiting for transfers between devices, from_behind(): return lax.ppermute(block, axis, route)  4.96 us
    ppermute x2, starting transfers between devices, from_behind(): return lax.ppermute(block, axis, route)  4.55 us
  transfers between devices with their start and end apart: 13, of which 10 were waited for; matrix products, arithmetic and copies ran while one was open for 1% of the time, Pallas kernels for 2%

profile of v6, /device:TPU:1, one launch (start us, length us, event | category | flops | bytes accessed | tf_op | source)
XLA Modules:
  0.0 191.7 jit_solution(14965556805284810295)
XLA Ops:
  0.7 2.2 %shard_map.155 = bf16[32,32,128]{2,1,0:T(8,128)(2,1)} custom-call(bf16[4,240,128]{2,1,0:T(8,128)(2,1)} %bitcast.41, bf16[256,240]{1,0:T(8,128)(2,1)} %constant.97.clone.forward_hbm.forward_ref), custom_call_target="tpu_custom_call" | custom-call | flops 62914560 | bytes 630784 | tf_op jit(solution)/shard_map/pallas_call | solution.py:321
  2.9 16.9 %all-to-all-start = ((bf16[32,32,128]{2,1,0:T(8,128)(2,1)}), bf16[32,32,128]{2,1,0:T(8,128)(2,1)S(1)}, u32[]{:S(2)}, u32[]{:S(2)}) async-start(bf16[32,32,128]{2,1,0:T(8,128)(2,1)} %shard_map.155), calls=%async_computation | async-start | bytes 524288 | tf_op jit(solution)/shard_map/all_to_all | solution.py:345
  22.3 19.5 %all-to-all-done.arrived_ref = bf16[32,32,128]{2,1,0:T(8,128)(2,1)S(1)} async-done(((bf16[32,32,128]{2,1,0:T(8,128)(2,1)}), bf16[32,32,128]{2,1,0:T(8,128)(2,1)S(1)}, u32[]{:S(2)}, u32[]{:S(2)}) %all-to-all-start) | async-done | bytes 262176 | tf_op jit(solution)/shard_map/all_to_all | solution.py:345
  41.8 1.3 shard_map.158
  43.1 4.7 %all-to-all-start.1 = ((bf16[32,64,128]{2,1,0:T(8,128)(2,1)}), bf16[32,64,128]{2,1,0:T(8,128)(2,1)S(1)}, u32[]{:S(2)}, u32[]{:S(2)}) async-start(bf16[32,64,128]{2,1,0:T(8,128)(2,1)} %get-tuple-element.30), calls=%async_computation.1 | async-start | bytes 1048576 | tf_op jit(solution)/shard_map/all_to_all | solution.py:345
  47.9 33.5 %all-to-all-done.1.values_ref.arrived_ref = bf16[32,64,128]{2,1,0:T(8,128)(2,1)S(1)} async-done(((bf16[32,64,128]{2,1,0:T(8,128)(2,1)}), bf16[32,64,128]{2,1,0:T(8,128)(2,1)S(1)}, u32[]{:S(2)}, u32[]{:S(2)}) %all-to-all-start.1) | async-done | bytes 524320 | tf_op jit(solution)/shard_map/all_to_all | solution.py:345
  81.3 0.9 copy-done.11
  82.3 4.3 %shard_map.159 = (bf16[32,32,128]{2,1,0:T(8,128)(2,1)S(1)}, f32[4,240,128]{2,1,0:T(8,128)S(1)}, bf16[2,4,192,128]{3,2,1,0:T(8,128)(2,1)S(1)}) custom-call(bf16[4,240,128]{2,1,0:T(8,128)(2,1)S(1)} %bitcast.42, bf16[32,64,128]{2,1,0:T(8,128)(2,1)S(1)} %all-to-all-done.1.values_ref.arrived_ref, bf16[4,240,128]{2,1,0:T(8,128)(2,1)S(1)} %bitcast.47, ...), custom_call_target="tpu_custom_call" | custom-call | flops 1069547520 | bytes 2801680 | tf_op jit(solution)/shard_map/pallas_call | solution.py:321
  86.5 1.3 shard_map.160
  87.8 4.3 %all-to-all-start.2 = ((bf16[32,64,128]{2,1,0:T(8,128)(2,1)}), bf16[32,64,128]{2,1,0:T(8,128)(2,1)S(1)}, u32[]{:S(2)}, u32[]{:S(2)}) async-start(bf16[32,64,128]{2,1,0:T(8,128)(2,1)} %shard_map.160), calls=%async_computation.2 | async-start | bytes 1048576 | tf_op jit(solution)/shard_map/all_to_all | solution.py:345
  92.2 2.3 %collective-permute-start = (bf16[4,192,128]{2,1,0:T(8,128)(2,1)S(1)}, bf16[4,192,128]{2,1,0:T(8,128)(2,1)S(1)}, u32[]{:S(2)}, u32[]{:S(2)}) collective-permute-start(bf16[4,192,128]{2,1,0:T(8,128)(2,1)S(1)} %dynamic-slice_bitcast_fusion), channel_id=1, source_target_pairs={{0,4},{4,0},{1,5},{5,1},{2,6},{6,2},{3,7},{7,3},{8,12},{12,8},{9,1... | collective-permute-start | bytes 589832 | tf_op jit(solution)/shard_map/ppermute | solution.py:357
  94.5 1.0 collective-permute-done
  95.6 3.2 %collective-permute-start.1 = (bf16[192,128]{1,0:T(8,128)(2,1)S(1)}, bf16[192,128]{1,0:T(8,128)(2,1)S(1)}, u32[]{:S(2)}, u32[]{:S(2)}) collective-permute-start(bf16[192,128]{1,0:T(8,128)(2,1)S(1)} %get-tuple-element.49), channel_id=1, source_target_pairs={{0,1},{1,2},{2,3},{3,0},{4,5},{5,6},{6,7},{7,4},{8,9},{9,10},{10,1... | collective-permute-start | bytes 147464 | tf_op jit(solution)/shard_map/ppermute | solution.py:363
  98.9 4.5 %collective-permute-start.2 = (bf16[192,128]{1,0:T(8,128)(2,1)S(1)}, bf16[192,128]{1,0:T(8,128)(2,1)S(1)}, u32[]{:S(2)}, u32[]{:S(2)}) collective-permute-start(bf16[192,128]{1,0:T(8,128)(2,1)S(1)} %get-tuple-element.51), channel_id=1, source_target_pairs={{0,2},{1,3},{2,0},{3,1},{4,6},{5,7},{6,4},{7,5},{8,10},{9,11},{10,... | collective-permute-start | bytes 147464 | tf_op jit(solution)/shard_map/ppermute | solution.py:363
  103.4 3.0 %collective-permute-start.3 = (bf16[192,128]{1,0:T(8,128)(2,1)S(1)}, bf16[192,128]{1,0:T(8,128)(2,1)S(1)}, u32[]{:S(2)}, u32[]{:S(2)}) collective-permute-start(bf16[192,128]{1,0:T(8,128)(2,1)S(1)} %get-tuple-element.50), channel_id=1, source_target_pairs={{0,3},{1,0},{2,1},{3,2},{4,7},{5,4},{6,5},{7,6},{8,11},{9,8},{10,9... | collective-permute-start | bytes 147464 | tf_op jit(solution)/shard_map/ppermute | solution.py:363
  106.4 2.1 %collective-permute-done.3 = bf16[192,128]{1,0:T(8,128)(2,1)S(1)} collective-permute-done((bf16[192,128]{1,0:T(8,128)(2,1)S(1)}, bf16[192,128]{1,0:T(8,128)(2,1)S(1)}, u32[]{:S(2)}, u32[]{:S(2)}) %collective-permute-start.3) | collective-permute-done | bytes 49184 | tf_op jit(solution)/shard_map/ppermute | solution.py:363
  108.6 17.1 %all-to-all-done.2.arrived_ref.values_ref = bf16[32,64,128]{2,1,0:T(8,128)(2,1)S(1)} async-done(((bf16[32,64,128]{2,1,0:T(8,128)(2,1)}), bf16[32,64,128]{2,1,0:T(8,128)(2,1)S(1)}, u32[]{:S(2)}, u32[]{:S(2)}) %all-to-all-start.2) | async-done | bytes 524320 | tf_op jit(solution)/shard_map/all_to_all | solution.py:345
  125.7 1.2 shard_map.161
  127.0 4.5 %all-to-all-start.3 = ((bf16[32,48,128]{2,1,0:T(8,128)(2,1)}), bf16[32,48,128]{2,1,0:T(8,128)(2,1)S(1)}, u32[]{:S(2)}, u32[]{:S(2)}) async-start(bf16[32,48,128]{2,1,0:T(8,128)(2,1)} %shard_map.161), calls=%async_computation.3 | async-start | bytes 786432 | tf_op jit(solution)/shard_map/all_to_all | solution.py:345
  131.5 2.2 %shard_map.162 = bf16[4,240,128]{2,1,0:T(8,128)(2,1)S(1)} custom-call(bf16[4,240,128]{2,1,0:T(8,128)(2,1)S(1)} %bitcast.44, bf16[32,64,128]{2,1,0:T(8,128)(2,1)S(1)} %all-to-all-done.2.arrived_ref.values_ref, bf16[240,256]{1,0:T(8,128)(2,1)S(1)} %copy-done.15, bf16[128,768]{1,0:T(8,128)(2,1)S(1)} %get-tuple-element.33.expand_ref, ...), custom_call_target="tpu_custom_call" | custom-call | flops 440401920 | bytes 1531920 | tf_op jit(solution)/shard_map/pallas_call | solution.py:321
  133.7 3.3 %collective-permute-start.4 = (bf16[4,240,128]{2,1,0:T(8,128)(2,1)S(1)}, bf16[4,240,128]{2,1,0:T(8,128)(2,1)S(1)}, u32[]{:S(2)}, u32[]{:S(2)}) collective-permute-start(bf16[4,240,128]{2,1,0:T(8,128)(2,1)S(1)} %shard_map.162), channel_id=1, source_target_pairs={{0,128},{128,256},{256,384},{1,129},{129,257},{257,385},{2,130},{1... | collective-permute-start | bytes 737288 | tf_op jit(solution)/shard_map/ppermute | solution.py:351
  136.9 5.0 %collective-permute-done.4.next_ref = bf16[4,240,128]{2,1,0:T(8,128)(2,1)S(1)} collective-permute-done((bf16[4,240,128]{2,1,0:T(8,128)(2,1)S(1)}, bf16[4,240,128]{2,1,0:T(8,128)(2,1)S(1)}, u32[]{:S(2)}, u32[]{:S(2)}) %collective-permute-start.4) | collective-permute-done | bytes 245792 | tf_op jit(solution)/shard_map/ppermute | solution.py:351
  141.9 17.6 %all-to-all-done.3.arrived_ref.coeffs_ref = bf16[32,48,128]{2,1,0:T(8,128)(2,1)S(1)} async-done(((bf16[32,48,128]{2,1,0:T(8,128)(2,1)}), bf16[32,48,128]{2,1,0:T(8,128)(2,1)S(1)}, u32[]{:S(2)}, u32[]{:S(2)}) %all-to-all-start.3) | async-done | bytes 393248 | tf_op jit(solution)/shard_map/all_to_all | solution.py:345
  160.1 4.2 %all-to-all-start.4 = ((f32[4,8,128]{2,1,0:T(8,128)}), f32[4,8,128]{2,1,0:T(8,128)S(1)}, u32[]{:S(2)}, u32[]{:S(2)}) async-start(f32[4,8,128]{2,1,0:T(8,128)} %get-tuple-element.40), calls=%async_computation.4 | async-start | bytes 32768 | tf_op jit(solution)/shard_map/all_to_all | solution.py:345
  164.3 0.8 shard_map.164
  165.1 3.4 %all-to-all-done.4.filter_ref = f32[4,8,128]{2,1,0:T(8,128)S(1)} async-done(((f32[4,8,128]{2,1,0:T(8,128)}), f32[4,8,128]{2,1,0:T(8,128)S(1)}, u32[]{:S(2)}, u32[]{:S(2)}) %all-to-all-start.4) | async-done | bytes 16416 | tf_op jit(solution)/shard_map/all_to_all | solution.py:345
  169.1 3.5 %all-to-all-start.5 = ((bf16[16,24,128]{2,1,0:T(8,128)(2,1)}), bf16[16,24,128]{2,1,0:T(8,128)(2,1)S(1)}, u32[]{:S(2)}, u32[]{:S(2)}) async-start(bf16[16,24,128]{2,1,0:T(8,128)(2,1)} %shard_map.165), calls=%async_computation.5 | async-start | bytes 196608 | tf_op jit(solution)/shard_map/all_to_all | solution.py:345
  172.7 1.3 collective-permute-start.6
  174.0 10.4 %all-to-all-done.5.pieces_ref = bf16[16,24,128]{2,1,0:T(8,128)(2,1)S(1)} async-done(((bf16[16,24,128]{2,1,0:T(8,128)(2,1)}), bf16[16,24,128]{2,1,0:T(8,128)(2,1)S(1)}, u32[]{:S(2)}, u32[]{:S(2)}) %all-to-all-start.5) | async-done | bytes 98336 | tf_op jit(solution)/shard_map/all_to_all | solution.py:345
  184.4 5.4 %collective-permute-start.5 = (bf16[16,24,128]{2,1,0:T(8,128)(2,1)S(1)}, bf16[16,24,128]{2,1,0:T(8,128)(2,1)S(1)}, u32[]{:S(2)}, u32[]{:S(2)}) collective-permute-start(bf16[16,24,128]{2,1,0:T(8,128)(2,1)S(1)} %all-to-all-done.5.pieces_ref), channel_id=1, source_target_pairs={{0,4},{4,0},{1,5},{5,1},{2,6},{6,2},{3,7},{7,3},{8,12},{12,8},{9,1... | collective-permute-start | bytes 294920 | tf_op jit(solution)/shard_map/ppermute | solution.py:516
  189.9 0.9 collective-permute-done.5.other_ref
  190.8 0.9 shard_map.166
  (51 shorter events, 3.9 us)
Async XLA Ops:
  0.6 19.2 %copy-start.16 = (s32[128]{0:T(128)S(1)}, s32[128]{0:T(128)}, u32[]{:S(2)}) copy-start(s32[128]{0:T(128)} %param.18) | copy-start | bytes 1540
  0.6 20.5 %copy-start.5 = (bf16[1,768,128]{2,1,0:T(8,128)(2,1)S(1)}, bf16[1,768,128]{2,1,0:T(8,128)(2,1)}, u32[]{:S(2)}) copy-start(bf16[1,768,128]{2,1,0:T(8,128)(2,1)} %param.16) | copy-start | bytes 589828
  0.7 20.5 %copy-start.6 = (bf16[256,240]{1,0:T(8,128)(2,1)S(1)}, bf16[256,240]{1,0:T(8,128)(2,1)}, u32[]{:S(2)}) copy-start(bf16[256,240]{1,0:T(8,128)(2,1)} %constant.99.clone.rest_1_) | copy-start | bytes 368644
  0.7 20.5 %copy-start.8 = (bf16[240,256]{1,0:T(8,128)(2,1)S(1)}, bf16[240,256]{1,0:T(8,128)(2,1)}, u32[]{:S(2)}) copy-start(bf16[240,256]{1,0:T(8,128)(2,1)} %constant.98.clone.rest_0_) | copy-start | bytes 368644
  2.9 18.3 %copy-start.1 = (bf16[256,240]{1,0:T(8,128)(2,1)S(1)}, bf16[256,240]{1,0:T(8,128)(2,1)}, u32[]{:S(2)}) copy-start(bf16[256,240]{1,0:T(8,128)(2,1)} %constant.97.clone.forward_hbm.forward_ref) | copy-start | bytes 368644
  2.9 18.3 %copy-start.3 = (bf16[1,1,4,240,128]{4,3,2,1,0:T(8,128)(2,1)S(1)}, bf16[1,1,4,240,128]{4,3,2,1,0:T(8,128)(2,1)}, u32[]{:S(2)}) copy-start(bf16[1,1,4,240,128]{4,3,2,1,0:T(8,128)(2,1)} %param.12) | copy-start | bytes 737284
  2.9 18.3 %copy-start.4 = (bf16[1,128,768]{2,1,0:T(8,128)(2,1)S(1)}, bf16[1,128,768]{2,1,0:T(8,128)(2,1)}, u32[]{:S(2)}) copy-start(bf16[1,128,768]{2,1,0:T(8,128)(2,1)} %param.15) | copy-start | bytes 589828
  2.9 38.9 %all-to-all-start = ((bf16[32,32,128]{2,1,0:T(8,128)(2,1)}), bf16[32,32,128]{2,1,0:T(8,128)(2,1)S(1)}, u32[]{:S(2)}, u32[]{:S(2)}) async-start(bf16[32,32,128]{2,1,0:T(8,128)(2,1)} %shard_map.155), calls=%async_computation | async-start | bytes 524288 | tf_op jit(solution)/shard_map/all_to_all | solution.py:345
  21.2 20.6 %copy-start = (f32[1,2,120,128]{3,2,1,0:T(8,128)S(1)}, f32[1,2,120,128]{3,2,1,0:T(8,128)}, u32[]{:S(2)}) copy-start(f32[1,2,120,128]{3,2,1,0:T(8,128)} %param.17) | copy-start | bytes 368644
  21.6 0.7 copy-start.13
  22.2 20.8 %copy-start.10 = (bf16[768,128]{1,0:T(8,128)(2,1)}, bf16[768,128]{1,0:T(8,128)(2,1)S(1)}, u32[]{:S(2)}) copy-start(bf16[768,128]{1,0:T(8,128)(2,1)S(1)} %get-tuple-element.34.reduce_ref) | copy-start | bytes 589828
  43.1 38.2 %copy-start.2 = (bf16[1,1,4,240,128]{4,3,2,1,0:T(8,128)(2,1)S(1)}, bf16[1,1,4,240,128]{4,3,2,1,0:T(8,128)(2,1)}, u32[]{:S(2)}) copy-start(bf16[1,1,4,240,128]{4,3,2,1,0:T(8,128)(2,1)} %param.13) | copy-start | bytes 737284
  43.1 38.2 %copy-start.9 = (bf16[1,1,4,240,128]{4,3,2,1,0:T(8,128)(2,1)S(1)}, bf16[1,1,4,240,128]{4,3,2,1,0:T(8,128)(2,1)}, u32[]{:S(2)}) copy-start(bf16[1,1,4,240,128]{4,3,2,1,0:T(8,128)(2,1)} %param.14) | copy-start | bytes 737284
  43.1 38.2 %copy-start.14 = (bf16[240,256]{1,0:T(8,128)(2,1)S(1)}, bf16[240,256]{1,0:T(8,128)(2,1)}, u32[]{:S(2)}) copy-start(bf16[240,256]{1,0:T(8,128)(2,1)} %copy-done.13) | copy-start | bytes 368644
  43.1 38.2 %all-to-all-start.1 = ((bf16[32,64,128]{2,1,0:T(8,128)(2,1)}), bf16[32,64,128]{2,1,0:T(8,128)(2,1)S(1)}, u32[]{:S(2)}, u32[]{:S(2)}) async-start(bf16[32,64,128]{2,1,0:T(8,128)(2,1)} %get-tuple-element.30), calls=%async_computation.1 | async-start | bytes 1048576 | tf_op jit(solution)/shard_map/all_to_all | solution.py:345
  81.3 0.9 copy-start.11
  87.8 37.9 %all-to-all-start.2 = ((bf16[32,64,128]{2,1,0:T(8,128)(2,1)}), bf16[32,64,128]{2,1,0:T(8,128)(2,1)S(1)}, u32[]{:S(2)}, u32[]{:S(2)}) async-start(bf16[32,64,128]{2,1,0:T(8,128)(2,1)} %shard_map.160), calls=%async_computation.2 | async-start | bytes 1048576 | tf_op jit(solution)/shard_map/all_to_all | solution.py:345
  92.2 3.3 %collective-permute-start = (bf16[4,192,128]{2,1,0:T(8,128)(2,1)S(1)}, bf16[4,192,128]{2,1,0:T(8,128)(2,1)S(1)}, u32[]{:S(2)}, u32[]{:S(2)}) collective-permute-start(bf16[4,192,128]{2,1,0:T(8,128)(2,1)S(1)} %dynamic-slice_bitcast_fusion), channel_id=1, source_target_pairs={{0,4},{4,0},{1,5},{5,1},{2,6},{6,2},{3,7},{7,3},{8,12},{12,8},{9,1... | collective-permute-start | bytes 589832 | tf_op jit(solution)/shard_map/ppermute | solution.py:357
  95.6 10.7 %collective-permute-start.1 = (bf16[192,128]{1,0:T(8,128)(2,1)S(1)}, bf16[192,128]{1,0:T(8,128)(2,1)S(1)}, u32[]{:S(2)}, u32[]{:S(2)}) collective-permute-start(bf16[192,128]{1,0:T(8,128)(2,1)S(1)} %get-tuple-element.49), channel_id=1, source_target_pairs={{0,1},{1,2},{2,3},{3,0},{4,5},{5,6},{6,7},{7,4},{8,9},{9,10},{10,1... | collective-permute-start | bytes 147464 | tf_op jit(solution)/shard_map/ppermute | solution.py:363
  98.9 7.5 %collective-permute-start.2 = (bf16[192,128]{1,0:T(8,128)(2,1)S(1)}, bf16[192,128]{1,0:T(8,128)(2,1)S(1)}, u32[]{:S(2)}, u32[]{:S(2)}) collective-permute-start(bf16[192,128]{1,0:T(8,128)(2,1)S(1)} %get-tuple-element.51), channel_id=1, source_target_pairs={{0,2},{1,3},{2,0},{3,1},{4,6},{5,7},{6,4},{7,5},{8,10},{9,11},{10,... | collective-permute-start | bytes 147464 | tf_op jit(solution)/shard_map/ppermute | solution.py:363
  103.4 5.1 %collective-permute-start.3 = (bf16[192,128]{1,0:T(8,128)(2,1)S(1)}, bf16[192,128]{1,0:T(8,128)(2,1)S(1)}, u32[]{:S(2)}, u32[]{:S(2)}) collective-permute-start(bf16[192,128]{1,0:T(8,128)(2,1)S(1)} %get-tuple-element.50), channel_id=1, source_target_pairs={{0,3},{1,0},{2,1},{3,2},{4,7},{5,4},{6,5},{7,6},{8,11},{9,8},{10,9... | collective-permute-start | bytes 147464 | tf_op jit(solution)/shard_map/ppermute | solution.py:363
  127.0 4.5 %copy-start.12 = (bf16[768,128]{1,0:T(8,128)(2,1)S(1)}, bf16[768,128]{1,0:T(8,128)(2,1)}, u32[]{:S(2)}) copy-start(bf16[768,128]{1,0:T(8,128)(2,1)} %copy-done.10) | copy-start | bytes 589828
  127.0 4.5 %copy-start.15 = (bf16[240,256]{1,0:T(8,128)(2,1)S(1)}, bf16[240,256]{1,0:T(8,128)(2,1)}, u32[]{:S(2)}) copy-start(bf16[240,256]{1,0:T(8,128)(2,1)} %copy-done.13) | copy-start | bytes 368644
  127.0 32.5 %all-to-all-start.3 = ((bf16[32,48,128]{2,1,0:T(8,128)(2,1)}), bf16[32,48,128]{2,1,0:T(8,128)(2,1)S(1)}, u32[]{:S(2)}, u32[]{:S(2)}) async-start(bf16[32,48,128]{2,1,0:T(8,128)(2,1)} %shard_map.161), calls=%async_computation.3 | async-start | bytes 786432 | tf_op jit(solution)/shard_map/all_to_all | solution.py:345
  133.7 30.6 %copy-start.7 = (bf16[240,256]{1,0:T(8,128)(2,1)S(1)}, bf16[240,256]{1,0:T(8,128)(2,1)}, u32[]{:S(2)}) copy-start(bf16[240,256]{1,0:T(8,128)(2,1)} %constant.96.clone.forward_ref) | copy-start | bytes 368644
  133.7 8.2 %collective-permute-start.4 = (bf16[4,240,128]{2,1,0:T(8,128)(2,1)S(1)}, bf16[4,240,128]{2,1,0:T(8,128)(2,1)S(1)}, u32[]{:S(2)}, u32[]{:S(2)}) collective-permute-start(bf16[4,240,128]{2,1,0:T(8,128)(2,1)S(1)} %shard_map.162), channel_id=1, source_target_pairs={{0,128},{128,256},{256,384},{1,129},{129,257},{257,385},{2,130},{1... | collective-permute-start | bytes 737288 | tf_op jit(solution)/shard_map/ppermute | solution.py:351
  160.1 8.4 %all-to-all-start.4 = ((f32[4,8,128]{2,1,0:T(8,128)}), f32[4,8,128]{2,1,0:T(8,128)S(1)}, u32[]{:S(2)}, u32[]{:S(2)}) async-start(f32[4,8,128]{2,1,0:T(8,128)} %get-tuple-element.40), calls=%async_computation.4 | async-start | bytes 32768 | tf_op jit(solution)/shard_map/all_to_all | solution.py:345
  169.1 15.3 %all-to-all-start.5 = ((bf16[16,24,128]{2,1,0:T(8,128)(2,1)}), bf16[16,24,128]{2,1,0:T(8,128)(2,1)S(1)}, u32[]{:S(2)}, u32[]{:S(2)}) async-start(bf16[16,24,128]{2,1,0:T(8,128)(2,1)} %shard_map.165), calls=%async_computation.5 | async-start | bytes 196608 | tf_op jit(solution)/shard_map/all_to_all | solution.py:345
  172.7 17.2 %collective-permute-start.6 = (bf16[4,240,128]{2,1,0:T(8,128)(2,1)S(1)}, bf16[4,240,128]{2,1,0:T(8,128)(2,1)S(1)}, u32[]{:S(2)}, u32[]{:S(2)}) collective-permute-start(bf16[4,240,128]{2,1,0:T(8,128)(2,1)S(1)} %shard_map.164), channel_id=1, source_target_pairs={{128,0},{256,128},{384,256},{129,1},{257,129},{385,257},{130,2},{2... | collective-permute-start | bytes 737288 | tf_op jit(solution)/shard_map/ppermute | solution.py:351
  184.4 6.4 %collective-permute-start.5 = (bf16[16,24,128]{2,1,0:T(8,128)(2,1)S(1)}, bf16[16,24,128]{2,1,0:T(8,128)(2,1)S(1)}, u32[]{:S(2)}, u32[]{:S(2)}) collective-permute-start(bf16[16,24,128]{2,1,0:T(8,128)(2,1)S(1)} %all-to-all-done.5.pieces_ref), channel_id=1, source_target_pairs={{0,4},{4,0},{1,5},{5,1},{2,6},{6,2},{3,7},{7,3},{8,12},{12,8},{9,1... | collective-permute-start | bytes 294920 | tf_op jit(solution)/shard_map/ppermute | solution.py:516

commit v7 on v6

--- a/solution.py
+++ b/solution.py
@@ -274,22 +274,22 @@
             out_ref[j] = (total * live(cycle_ref, j)).astype(BF16)
 
 
-def piece_kernel(arrived_ref, share_ref, filter_ref):
+def piece_kernel(arrived_ref, out_ref):
     came = arrived_ref[:, 32:, :].astype(F32).reshape(PEERS // 2, 2, 16, CH)
     sums = came.sum(axis=0)
-    share_ref[0] = sums[0, :8]
-    share_ref[1] = sums[1, :8]
-    filter_ref[...] = jnp.broadcast_to((sums[0, 8:] + sums[1, 8:])[None], filter_ref.shape)
-
-
-def spread_kernel(share_ref, filter_ref, out_ref):
-    piece = jnp.concatenate([share_ref[0], share_ref[1], filter_ref[...].sum(axis=0)], axis=0)
+    piece = jnp.concatenate([sums[0, :8], sums[1, :8], sums[0, 8:] + sums[1, 8:]], axis=0)
     out_ref[...] = jnp.broadcast_to(piece[None], out_ref.shape).astype(BF16)
+
+
+def filter_rows_kernel(pieces_ref, out_ref):
+    rows = pieces_ref[...].astype(F32)[:, 16:].reshape(128, CH).astype(BF16)
+    out_ref[...] = jnp.broadcast_to(rows[None], out_ref.shape)
 
 
 def result_kernel(
     pieces_ref,
     other_ref,
+    filter_rows_ref,
     core_ref,
     next_ref,
     back_ref,
@@ -302,6 +302,7 @@
     next_out_ref[...] = next_ref[...]
     back_out_ref[...] = back_ref[...]
     first = core_ref[0] == 0
+    filters = [filter_rows_ref[4 * c : 4 * c + 4].astype(F32).sum(axis=0) for c in range(2)]
     for p in range(PEERS):
         mine, other = pieces_ref[p // 2].astype(F32), other_ref[p // 2].astype(F32)
         piece = jnp.where(first, mine, other) if p % 2 == 0 else jnp.where(first, other, mine)
@@ -309,7 +310,8 @@
         reduce_ref[p * 6 : p * 6 + 6, :] = piece[8:14]
         side, at = divmod(p, PEERS // 2)
         if at < NLAT // 8:
-            filter_ref[side, at * 8 : at * 8 + 8, :] = piece[16:]
+            rows = filters[p % 2][p // 2 * 8 : p // 2 * 8 + 8]
+            filter_ref[side, at * 8 : at * 8 + 8, :] = rows
 
 
 def call(
@@ -495,12 +497,15 @@
     )[0]
     coeffs_summed = exchange(coeffs_summed, SP)
     coeffs_summed, next_input = lax.optimization_barrier((coeffs_summed, next_input))
-    share, filter_piece = call(
-        piece_kernel,
-        [jax.ShapeDtypeStruct((2, 8, CH), F32), jax.ShapeDtypeStruct((4, 8, CH), F32)],
-        [coeffs_summed],
-    )
-    filter_piece = exchange(filter_piece, "dp")
+    pieces = call(
+        piece_kernel, [jax.ShapeDtypeStruct((PEERS // 2, 24, CH), BF16)], [coeffs_summed]
+    )[0]
+    pieces = exchange(pieces, "sp_0")
+    filter_rows = call(
+        filter_rows_kernel, [jax.ShapeDtypeStruct((8, 128, CH), BF16)], [pieces]
+    )[0]
+    filter_rows = exchange(filter_rows, ("sp_1", "dp"))
+    other_pieces = lax.ppermute(pieces, "sp_1", CORE_SWAP)
     input_grad = call(
         input_grad_kernel,
         [TOKENS],
@@ -508,20 +513,14 @@
         flops=dft,
         smem=(3,),
     )[0]
-    filter_piece, _ = lax.optimization_barrier((filter_piece, input_grad))
-    pieces = call(
-        spread_kernel, [jax.ShapeDtypeStruct((PEERS // 2, 24, CH), BF16)], [share, filter_piece]
-    )[0]
-    pieces = exchange(pieces, "sp_0")
-    other_pieces = lax.ppermute(pieces, "sp_1", CORE_SWAP)
     sent_back = from_behind(input_grad, "pipe", -1)
     part = jax.ShapeDtypeStruct((HID // 4, CH), F32)
     core = lax.axis_index("sp_1").astype(jnp.int32)[None]
     expand_grad, reduce_grad, filter_grad, next_input, sent_back = call(
         result_kernel,
         [part, part, jax.ShapeDtypeStruct((2, NLAT, CH), F32), TOKENS, TOKENS],
-        [pieces, other_pieces, core, next_input, sent_back],
-        smem=(2,),
+        [pieces, other_pieces, filter_rows, core, next_input, sent_back],
+        smem=(3,),
     )
     return (
         next_input[None, None],

time: 193 us -> 192 us (level)
    ppermute x1, starting transfers between devices: 5.43 us -> 1.91 us  [on_device(): other_pieces = lax.ppermute(pieces, 'sp_1', CORE_SWAP)]
    all_to_all x6, starting transfers between devices: 38.1 us -> 41.2 us  [exchange(): return lax.all_to_all(blocks, axes, split_axis=0, concat_axis=0, tiled=True)]
where the time goes in v7:
time: 192 us; the launch traced here: 191 us
  waiting for transfers between devices  110 us (57%)
  starting transfers between devices  60.5 us (32%)
  Pallas kernels  16.5 us (9%)
  local copies, waits for them, and re-layouts  2.51 us (1%)
    all_to_all x6, waiting for transfers between devices, exchange(): return lax.all_to_all(blocks, axes, split_axis=0, concat_axis=0, tiled=True)  101 us
    all_to_all x6, starting transfers between devices, exchange(): return lax.all_to_all(blocks, axes, split_axis=0, concat_axis=0, tiled=True)  41.2 us
    pallas_call x12, Pallas kernels, call(): pl.pallas_call(kernel, out_shape=outs, in_specs=specs, out_specs=[pl.Bloc...  16.5 us
    ppermute x3, starting transfers between devices, around(): lax.ppermute(block, axis, [(i, (i + distance) % count) for i in range(cou...  10.7 us
    ppermute x2, waiting for transfers between devices, from_behind(): return lax.ppermute(block, axis, route)  4.96 us
    ppermute x2, starting transfers between devices, from_behind(): return lax.ppermute(block, axis, route)  4.42 us
  transfers between devices with their start and end apart: 13, of which 10 were waited for; matrix products, arithmetic and copies ran while one was open for 1% of the time, Pallas kernels for 2%

profile of v7, /device:TPU:1, one launch (start us, length us, event | category | flops | bytes accessed | tf_op | source)
XLA Modules:
  0.0 191.0 jit_solution(15748125528752725959)
XLA Ops:
  0.7 2.2 %shard_map.155 = bf16[32,32,128]{2,1,0:T(8,128)(2,1)} custom-call(bf16[4,240,128]{2,1,0:T(8,128)(2,1)} %bitcast.41, bf16[256,240]{1,0:T(8,128)(2,1)} %constant.97.clone.forward_hbm.forward_ref), custom_call_target="tpu_custom_call" | custom-call | flops 62914560 | bytes 630784 | tf_op jit(solution)/shard_map/pallas_call | solution.py:323
  2.9 16.9 %all-to-all-start = ((bf16[32,32,128]{2,1,0:T(8,128)(2,1)}), bf16[32,32,128]{2,1,0:T(8,128)(2,1)S(1)}, u32[]{:S(2)}, u32[]{:S(2)}) async-start(bf16[32,32,128]{2,1,0:T(8,128)(2,1)} %shard_map.155), calls=%async_computation | async-start | bytes 524288 | tf_op jit(solution)/shard_map/all_to_all | solution.py:347
  22.2 19.5 %all-to-all-done.arrived_ref = bf16[32,32,128]{2,1,0:T(8,128)(2,1)S(1)} async-done(((bf16[32,32,128]{2,1,0:T(8,128)(2,1)}), bf16[32,32,128]{2,1,0:T(8,128)(2,1)S(1)}, u32[]{:S(2)}, u32[]{:S(2)}) %all-to-all-start) | async-done | bytes 262176 | tf_op jit(solution)/shard_map/all_to_all | solution.py:347
  41.8 1.3 shard_map.158
  43.1 4.7 %all-to-all-start.1 = ((bf16[32,64,128]{2,1,0:T(8,128)(2,1)}), bf16[32,64,128]{2,1,0:T(8,128)(2,1)S(1)}, u32[]{:S(2)}, u32[]{:S(2)}) async-start(bf16[32,64,128]{2,1,0:T(8,128)(2,1)} %get-tuple-element.27), calls=%async_computation.1 | async-start | bytes 1048576 | tf_op jit(solution)/shard_map/all_to_all | solution.py:347
  47.8 33.5 %all-to-all-done.1.values_ref.arrived_ref = bf16[32,64,128]{2,1,0:T(8,128)(2,1)S(1)} async-done(((bf16[32,64,128]{2,1,0:T(8,128)(2,1)}), bf16[32,64,128]{2,1,0:T(8,128)(2,1)S(1)}, u32[]{:S(2)}, u32[]{:S(2)}) %all-to-all-start.1) | async-done | bytes 524320 | tf_op jit(solution)/shard_map/all_to_all | solution.py:347
  81.3 0.9 copy-done.11
  82.2 4.3 %shard_map.159 = (bf16[32,32,128]{2,1,0:T(8,128)(2,1)S(1)}, f32[4,240,128]{2,1,0:T(8,128)S(1)}, bf16[2,4,192,128]{3,2,1,0:T(8,128)(2,1)S(1)}) custom-call(bf16[4,240,128]{2,1,0:T(8,128)(2,1)S(1)} %bitcast.42, bf16[32,64,128]{2,1,0:T(8,128)(2,1)S(1)} %all-to-all-done.1.values_ref.arrived_ref, bf16[4,240,128]{2,1,0:T(8,128)(2,1)S(1)} %bitcast.47, ...), custom_call_target="tpu_custom_call" | custom-call | flops 1069547520 | bytes 2801680 | tf_op jit(solution)/shard_map/pallas_call | solution.py:323
  86.5 1.3 shard_map.160
  87.8 4.3 %all-to-all-start.2 = ((bf16[32,64,128]{2,1,0:T(8,128)(2,1)}), bf16[32,64,128]{2,1,0:T(8,128)(2,1)S(1)}, u32[]{:S(2)}, u32[]{:S(2)}) async-start(bf16[32,64,128]{2,1,0:T(8,128)(2,1)} %shard_map.160), calls=%async_computation.2 | async-start | bytes 1048576 | tf_op jit(solution)/shard_map/all_to_all | solution.py:347
  92.2 2.3 %collective-permute-start = (bf16[4,192,128]{2,1,0:T(8,128)(2,1)S(1)}, bf16[4,192,128]{2,1,0:T(8,128)(2,1)S(1)}, u32[]{:S(2)}, u32[]{:S(2)}) collective-permute-start(bf16[4,192,128]{2,1,0:T(8,128)(2,1)S(1)} %dynamic-slice_bitcast_fusion), channel_id=1, source_target_pairs={{0,4},{4,0},{1,5},{5,1},{2,6},{6,2},{3,7},{7,3},{8,12},{12,8},{9,1... | collective-permute-start | bytes 589832 | tf_op jit(solution)/shard_map/ppermute | solution.py:359
  94.5 1.0 collective-permute-done
  95.6 3.2 %collective-permute-start.1 = (bf16[192,128]{1,0:T(8,128)(2,1)S(1)}, bf16[192,128]{1,0:T(8,128)(2,1)S(1)}, u32[]{:S(2)}, u32[]{:S(2)}) collective-permute-start(bf16[192,128]{1,0:T(8,128)(2,1)S(1)} %get-tuple-element.43), channel_id=1, source_target_pairs={{0,1},{1,2},{2,3},{3,0},{4,5},{5,6},{6,7},{7,4},{8,9},{9,10},{10,1... | collective-permute-start | bytes 147464 | tf_op jit(solution)/shard_map/ppermute | solution.py:365
  98.8 4.5 %collective-permute-start.2 = (bf16[192,128]{1,0:T(8,128)(2,1)S(1)}, bf16[192,128]{1,0:T(8,128)(2,1)S(1)}, u32[]{:S(2)}, u32[]{:S(2)}) collective-permute-start(bf16[192,128]{1,0:T(8,128)(2,1)S(1)} %get-tuple-element.45), channel_id=1, source_target_pairs={{0,2},{1,3},{2,0},{3,1},{4,6},{5,7},{6,4},{7,5},{8,10},{9,11},{10,... | collective-permute-start | bytes 147464 | tf_op jit(solution)/shard_map/ppermute | solution.py:365
  103.4 3.0 %collective-permute-start.3 = (bf16[192,128]{1,0:T(8,128)(2,1)S(1)}, bf16[192,128]{1,0:T(8,128)(2,1)S(1)}, u32[]{:S(2)}, u32[]{:S(2)}) collective-permute-start(bf16[192,128]{1,0:T(8,128)(2,1)S(1)} %get-tuple-element.44), channel_id=1, source_target_pairs={{0,3},{1,0},{2,1},{3,2},{4,7},{5,4},{6,5},{7,6},{8,11},{9,8},{10,9... | collective-permute-start | bytes 147464 | tf_op jit(solution)/shard_map/ppermute | solution.py:365
  106.4 2.1 %collective-permute-done.3 = bf16[192,128]{1,0:T(8,128)(2,1)S(1)} collective-permute-done((bf16[192,128]{1,0:T(8,128)(2,1)S(1)}, bf16[192,128]{1,0:T(8,128)(2,1)S(1)}, u32[]{:S(2)}, u32[]{:S(2)}) %collective-permute-start.3) | collective-permute-done | bytes 49184 | tf_op jit(solution)/shard_map/ppermute | solution.py:365
  108.6 17.1 %all-to-all-done.2.arrived_ref.values_ref = bf16[32,64,128]{2,1,0:T(8,128)(2,1)S(1)} async-done(((bf16[32,64,128]{2,1,0:T(8,128)(2,1)}), bf16[32,64,128]{2,1,0:T(8,128)(2,1)S(1)}, u32[]{:S(2)}, u32[]{:S(2)}) %all-to-all-start.2) | async-done | bytes 524320 | tf_op jit(solution)/shard_map/all_to_all | solution.py:347
  125.7 1.2 shard_map.161
  127.0 4.5 %all-to-all-start.3 = ((bf16[32,48,128]{2,1,0:T(8,128)(2,1)}), bf16[32,48,128]{2,1,0:T(8,128)(2,1)S(1)}, u32[]{:S(2)}, u32[]{:S(2)}) async-start(bf16[32,48,128]{2,1,0:T(8,128)(2,1)} %shard_map.161), calls=%async_computation.3 | async-start | bytes 786432 | tf_op jit(solution)/shard_map/all_to_all | solution.py:347
  131.5 2.2 %shard_map.162 = bf16[4,240,128]{2,1,0:T(8,128)(2,1)S(1)} custom-call(bf16[4,240,128]{2,1,0:T(8,128)(2,1)S(1)} %bitcast.44, bf16[32,64,128]{2,1,0:T(8,128)(2,1)S(1)} %all-to-all-done.2.arrived_ref.values_ref, bf16[240,256]{1,0:T(8,128)(2,1)S(1)} %copy-done.15, bf16[128,768]{1,0:T(8,128)(2,1)S(1)} %get-tuple-element.30.expand_ref, ...), custom_call_target="tpu_custom_call" | custom-call | flops 440401920 | bytes 1531920 | tf_op jit(solution)/shard_map/pallas_call | solution.py:323
  133.6 3.1 %collective-permute-start.4 = (bf16[4,240,128]{2,1,0:T(8,128)(2,1)S(1)}, bf16[4,240,128]{2,1,0:T(8,128)(2,1)S(1)}, u32[]{:S(2)}, u32[]{:S(2)}) collective-permute-start(bf16[4,240,128]{2,1,0:T(8,128)(2,1)S(1)} %shard_map.162), channel_id=1, source_target_pairs={{0,128},{128,256},{256,384},{1,129},{129,257},{257,385},{2,130},{1... | collective-permute-start | bytes 737288 | tf_op jit(solution)/shard_map/ppermute | solution.py:353
  136.8 5.0 %collective-permute-done.4.next_ref = bf16[4,240,128]{2,1,0:T(8,128)(2,1)S(1)} collective-permute-done((bf16[4,240,128]{2,1,0:T(8,128)(2,1)S(1)}, bf16[4,240,128]{2,1,0:T(8,128)(2,1)S(1)}, u32[]{:S(2)}, u32[]{:S(2)}) %collective-permute-start.4) | collective-permute-done | bytes 245792 | tf_op jit(solution)/shard_map/ppermute | solution.py:353
  141.7 17.7 %all-to-all-done.3.arrived_ref.coeffs_ref = bf16[32,48,128]{2,1,0:T(8,128)(2,1)S(1)} async-done(((bf16[32,48,128]{2,1,0:T(8,128)(2,1)}), bf16[32,48,128]{2,1,0:T(8,128)(2,1)S(1)}, u32[]{:S(2)}, u32[]{:S(2)}) %all-to-all-start.3) | async-done | bytes 393248 | tf_op jit(solution)/shard_map/all_to_all | solution.py:347
  160.1 3.6 %all-to-all-start.4 = ((bf16[16,24,128]{2,1,0:T(8,128)(2,1)}), bf16[16,24,128]{2,1,0:T(8,128)(2,1)S(1)}, u32[]{:S(2)}, u32[]{:S(2)}) async-start(bf16[16,24,128]{2,1,0:T(8,128)(2,1)} %shard_map.163), calls=%async_computation.4 | async-start | bytes 196608 | tf_op jit(solution)/shard_map/all_to_all | solution.py:347
  163.8 0.8 shard_map.165
  164.6 1.3 collective-permute-start.6
  165.9 9.6 %all-to-all-done.4.pieces_ref = bf16[16,24,128]{2,1,0:T(8,128)(2,1)S(1)} async-done(((bf16[16,24,128]{2,1,0:T(8,128)(2,1)}), bf16[16,24,128]{2,1,0:T(8,128)(2,1)S(1)}, u32[]{:S(2)}, u32[]{:S(2)}) %all-to-all-start.4) | async-done | bytes 98336 | tf_op jit(solution)/shard_map/all_to_all | solution.py:347
  176.3 7.2 %all-to-all-start.5 = ((bf16[8,128,128]{2,1,0:T(8,128)(2,1)}), bf16[8,128,128]{2,1,0:T(8,128)(2,1)S(1)}, u32[]{:S(2)}, u32[]{:S(2)}) async-start(bf16[8,128,128]{2,1,0:T(8,128)(2,1)} %shard_map.164), calls=%async_computation.5 | async-start | bytes 524288 | tf_op jit(solution)/shard_map/all_to_all | solution.py:347
  183.5 1.9 collective-permute-start.5
  185.4 1.3 collective-permute-done.5.other_ref
  186.7 3.4 %all-to-all-done.5.filter_rows_ref = bf16[8,128,128]{2,1,0:T(8,128)(2,1)S(1)} async-done(((bf16[8,128,128]{2,1,0:T(8,128)(2,1)}), bf16[8,128,128]{2,1,0:T(8,128)(2,1)S(1)}, u32[]{:S(2)}, u32[]{:S(2)}) %all-to-all-start.5) | async-done | bytes 262176 | tf_op jit(solution)/shard_map/all_to_all | solution.py:347
  190.1 0.9 shard_map.166
  (51 shorter events, 4.1 us)
Async XLA Ops:
  0.6 19.2 %copy-start.16 = (s32[128]{0:T(128)S(1)}, s32[128]{0:T(128)}, u32[]{:S(2)}) copy-start(s32[128]{0:T(128)} %param.18) | copy-start | bytes 1540
  0.6 20.5 %copy-start.5 = (bf16[1,768,128]{2,1,0:T(8,128)(2,1)S(1)}, bf16[1,768,128]{2,1,0:T(8,128)(2,1)}, u32[]{:S(2)}) copy-start(bf16[1,768,128]{2,1,0:T(8,128)(2,1)} %param.16) | copy-start | bytes 589828
  0.7 20.5 %copy-start.6 = (bf16[256,240]{1,0:T(8,128)(2,1)S(1)}, bf16[256,240]{1,0:T(8,128)(2,1)}, u32[]{:S(2)}) copy-start(bf16[256,240]{1,0:T(8,128)(2,1)} %constant.99.clone.rest_1_) | copy-start | bytes 368644
  0.7 20.5 %copy-start.8 = (bf16[240,256]{1,0:T(8,128)(2,1)S(1)}, bf16[240,256]{1,0:T(8,128)(2,1)}, u32[]{:S(2)}) copy-start(bf16[240,256]{1,0:T(8,128)(2,1)} %constant.98.clone.rest_0_) | copy-start | bytes 368644
  2.9 18.3 %copy-start.1 = (bf16[256,240]{1,0:T(8,128)(2,1)S(1)}, bf16[256,240]{1,0:T(8,128)(2,1)}, u32[]{:S(2)}) copy-start(bf16[256,240]{1,0:T(8,128)(2,1)} %constant.97.clone.forward_hbm.forward_ref) | copy-start | bytes 368644
  2.9 18.3 %copy-start.3 = (bf16[1,1,4,240,128]{4,3,2,1,0:T(8,128)(2,1)S(1)}, bf16[1,1,4,240,128]{4,3,2,1,0:T(8,128)(2,1)}, u32[]{:S(2)}) copy-start(bf16[1,1,4,240,128]{4,3,2,1,0:T(8,128)(2,1)} %param.12) | copy-start | bytes 737284
  2.9 18.3 %copy-start.4 = (bf16[1,128,768]{2,1,0:T(8,128)(2,1)S(1)}, bf16[1,128,768]{2,1,0:T(8,128)(2,1)}, u32[]{:S(2)}) copy-start(bf16[1,128,768]{2,1,0:T(8,128)(2,1)} %param.15) | copy-start | bytes 589828
  2.9 38.9 %all-to-all-start = ((bf16[32,32,128]{2,1,0:T(8,128)(2,1)}), bf16[32,32,128]{2,1,0:T(8,128)(2,1)S(1)}, u32[]{:S(2)}, u32[]{:S(2)}) async-start(bf16[32,32,128]{2,1,0:T(8,128)(2,1)} %shard_map.155), calls=%async_computation | async-start | bytes 524288 | tf_op jit(solution)/shard_map/all_to_all | solution.py:347
  21.2 20.6 %copy-start = (f32[1,2,120,128]{3,2,1,0:T(8,128)S(1)}, f32[1,2,120,128]{3,2,1,0:T(8,128)}, u32[]{:S(2)}) copy-start(f32[1,2,120,128]{3,2,1,0:T(8,128)} %param.17) | copy-start | bytes 368644
  21.6 0.7 copy-start.13
  22.2 20.8 %copy-start.10 = (bf16[768,128]{1,0:T(8,128)(2,1)}, bf16[768,128]{1,0:T(8,128)(2,1)S(1)}, u32[]{:S(2)}) copy-start(bf16[768,128]{1,0:T(8,128)(2,1)S(1)} %get-tuple-element.31.reduce_ref) | copy-start | bytes 589828
  43.1 38.2 %copy-start.2 = (bf16[1,1,4,240,128]{4,3,2,1,0:T(8,128)(2,1)S(1)}, bf16[1,1,4,240,128]{4,3,2,1,0:T(8,128)(2,1)}, u32[]{:S(2)}) copy-start(bf16[1,1,4,240,128]{4,3,2,1,0:T(8,128)(2,1)} %param.13) | copy-start | bytes 737284
  43.1 38.2 %copy-start.9 = (bf16[1,1,4,240,128]{4,3,2,1,0:T(8,128)(2,1)S(1)}, bf16[1,1,4,240,128]{4,3,2,1,0:T(8,128)(2,1)}, u32[]{:S(2)}) copy-start(bf16[1,1,4,240,128]{4,3,2,1,0:T(8,128)(2,1)} %param.14) | copy-start | bytes 737284
  43.1 38.2 %copy-start.14 = (bf16[240,256]{1,0:T(8,128)(2,1)S(1)}, bf16[240,256]{1,0:T(8,128)(2,1)}, u32[]{:S(2)}) copy-start(bf16[240,256]{1,0:T(8,128)(2,1)} %copy-done.13) | copy-start | bytes 368644
  43.1 38.2 %all-to-all-start.1 = ((bf16[32,64,128]{2,1,0:T(8,128)(2,1)}), bf16[32,64,128]{2,1,0:T(8,128)(2,1)S(1)}, u32[]{:S(2)}, u32[]{:S(2)}) async-start(bf16[32,64,128]{2,1,0:T(8,128)(2,1)} %get-tuple-element.27), calls=%async_computation.1 | async-start | bytes 1048576 | tf_op jit(solution)/shard_map/all_to_all | solution.py:347
  81.3 0.9 copy-start.11
  87.8 37.9 %all-to-all-start.2 = ((bf16[32,64,128]{2,1,0:T(8,128)(2,1)}), bf16[32,64,128]{2,1,0:T(8,128)(2,1)S(1)}, u32[]{:S(2)}, u32[]{:S(2)}) async-start(bf16[32,64,128]{2,1,0:T(8,128)(2,1)} %shard_map.160), calls=%async_computation.2 | async-start | bytes 1048576 | tf_op jit(solution)/shard_map/all_to_all | solution.py:347
  92.2 3.3 %collective-permute-start = (bf16[4,192,128]{2,1,0:T(8,128)(2,1)S(1)}, bf16[4,192,128]{2,1,0:T(8,128)(2,1)S(1)}, u32[]{:S(2)}, u32[]{:S(2)}) collective-permute-start(bf16[4,192,128]{2,1,0:T(8,128)(2,1)S(1)} %dynamic-slice_bitcast_fusion), channel_id=1, source_target_pairs={{0,4},{4,0},{1,5},{5,1},{2,6},{6,2},{3,7},{7,3},{8,12},{12,8},{9,1... | collective-permute-start | bytes 589832 | tf_op jit(solution)/shard_map/ppermute | solution.py:359
  95.6 10.7 %collective-permute-start.1 = (bf16[192,128]{1,0:T(8,128)(2,1)S(1)}, bf16[192,128]{1,0:T(8,128)(2,1)S(1)}, u32[]{:S(2)}, u32[]{:S(2)}) collective-permute-start(bf16[192,128]{1,0:T(8,128)(2,1)S(1)} %get-tuple-element.43), channel_id=1, source_target_pairs={{0,1},{1,2},{2,3},{3,0},{4,5},{5,6},{6,7},{7,4},{8,9},{9,10},{10,1... | collective-permute-start | bytes 147464 | tf_op jit(solution)/shard_map/ppermute | solution.py:365
  98.8 7.5 %collective-permute-start.2 = (bf16[192,128]{1,0:T(8,128)(2,1)S(1)}, bf16[192,128]{1,0:T(8,128)(2,1)S(1)}, u32[]{:S(2)}, u32[]{:S(2)}) collective-permute-start(bf16[192,128]{1,0:T(8,128)(2,1)S(1)} %get-tuple-element.45), channel_id=1, source_target_pairs={{0,2},{1,3},{2,0},{3,1},{4,6},{5,7},{6,4},{7,5},{8,10},{9,11},{10,... | collective-permute-start | bytes 147464 | tf_op jit(solution)/shard_map/ppermute | solution.py:365
  103.4 5.1 %collective-permute-start.3 = (bf16[192,128]{1,0:T(8,128)(2,1)S(1)}, bf16[192,128]{1,0:T(8,128)(2,1)S(1)}, u32[]{:S(2)}, u32[]{:S(2)}) collective-permute-start(bf16[192,128]{1,0:T(8,128)(2,1)S(1)} %get-tuple-element.44), channel_id=1, source_target_pairs={{0,3},{1,0},{2,1},{3,2},{4,7},{5,4},{6,5},{7,6},{8,11},{9,8},{10,9... | collective-permute-start | bytes 147464 | tf_op jit(solution)/shard_map/ppermute | solution.py:365
  127.0 4.5 %copy-start.12 = (bf16[768,128]{1,0:T(8,128)(2,1)S(1)}, bf16[768,128]{1,0:T(8,128)(2,1)}, u32[]{:S(2)}) copy-start(bf16[768,128]{1,0:T(8,128)(2,1)} %copy-done.10) | copy-start | bytes 589828
  127.0 4.5 %copy-start.15 = (bf16[240,256]{1,0:T(8,128)(2,1)S(1)}, bf16[240,256]{1,0:T(8,128)(2,1)}, u32[]{:S(2)}) copy-start(bf16[240,256]{1,0:T(8,128)(2,1)} %copy-done.13) | copy-start | bytes 368644
  127.0 32.5 %all-to-all-start.3 = ((bf16[32,48,128]{2,1,0:T(8,128)(2,1)}), bf16[32,48,128]{2,1,0:T(8,128)(2,1)S(1)}, u32[]{:S(2)}, u32[]{:S(2)}) async-start(bf16[32,48,128]{2,1,0:T(8,128)(2,1)} %shard_map.161), calls=%async_computation.3 | async-start | bytes 786432 | tf_op jit(solution)/shard_map/all_to_all | solution.py:347
  133.6 8.1 %collective-permute-start.4 = (bf16[4,240,128]{2,1,0:T(8,128)(2,1)S(1)}, bf16[4,240,128]{2,1,0:T(8,128)(2,1)S(1)}, u32[]{:S(2)}, u32[]{:S(2)}) collective-permute-start(bf16[4,240,128]{2,1,0:T(8,128)(2,1)S(1)} %shard_map.162), channel_id=1, source_target_pairs={{0,128},{128,256},{256,384},{1,129},{129,257},{257,385},{2,130},{1... | collective-permute-start | bytes 737288 | tf_op jit(solution)/shard_map/ppermute | solution.py:353
  160.1 3.7 %copy-start.7 = (bf16[240,256]{1,0:T(8,128)(2,1)S(1)}, bf16[240,256]{1,0:T(8,128)(2,1)}, u32[]{:S(2)}) copy-start(bf16[240,256]{1,0:T(8,128)(2,1)} %constant.96.clone.forward_ref) | copy-start | bytes 368644
  160.1 15.4 %all-to-all-start.4 = ((bf16[16,24,128]{2,1,0:T(8,128)(2,1)}), bf16[16,24,128]{2,1,0:T(8,128)(2,1)S(1)}, u32[]{:S(2)}, u32[]{:S(2)}) async-start(bf16[16,24,128]{2,1,0:T(8,128)(2,1)} %shard_map.163), calls=%async_computation.4 | async-start | bytes 196608 | tf_op jit(solution)/shard_map/all_to_all | solution.py:347
  164.6 20.8 %collective-permute-start.6 = (bf16[4,240,128]{2,1,0:T(8,128)(2,1)S(1)}, bf16[4,240,128]{2,1,0:T(8,128)(2,1)S(1)}, u32[]{:S(2)}, u32[]{:S(2)}) collective-permute-start(bf16[4,240,128]{2,1,0:T(8,128)(2,1)S(1)} %shard_map.165), channel_id=1, source_target_pairs={{128,0},{256,128},{384,256},{129,1},{257,129},{385,257},{130,2},{2... | collective-permute-start | bytes 737288 | tf_op jit(solution)/shard_map/ppermute | solution.py:353
  176.3 13.8 %all-to-all-start.5 = ((bf16[8,128,128]{2,1,0:T(8,128)(2,1)}), bf16[8,128,128]{2,1,0:T(8,128)(2,1)S(1)}, u32[]{:S(2)}, u32[]{:S(2)}) async-start(bf16[8,128,128]{2,1,0:T(8,128)(2,1)} %shard_map.164), calls=%async_computation.5 | async-start | bytes 524288 | tf_op jit(solution)/shard_map/all_to_all | solution.py:347
  183.5 3.2 %collective-permute-start.5 = (bf16[16,24,128]{2,1,0:T(8,128)(2,1)S(1)}, bf16[16,24,128]{2,1,0:T(8,128)(2,1)S(1)}, u32[]{:S(2)}, u32[]{:S(2)}) collective-permute-start(bf16[16,24,128]{2,1,0:T(8,128)(2,1)S(1)} %all-to-all-done.4.pieces_ref), channel_id=1, source_target_pairs={{0,4},{4,0},{1,5},{5,1},{2,6},{6,2},{3,7},{7,3},{8,12},{12,8},{9,1... | collective-permute-start | bytes 294920 | tf_op jit(solution)/shard_map/ppermute | solution.py:508

commit v8 on v7

--- a/solution.py
+++ b/solution.py
@@ -59,6 +59,18 @@
             table[position, 1, row] = log_start
             table[position, 2, row] = float(slot < NLAT)
     return table
+
+
+def normal_and_density(u):
+    bell = jnp.exp(-0.5 * u * u)
+    t = 1.0 / (1.0 + (0.3275911 * ROOT_HALF) * jnp.abs(u))
+    series = (
+        (((0.5 * 1.061405429 * t - 0.5 * 1.453152027) * t + 0.5 * 1.421413741) * t - 0.5 * 0.284496736)
+        * t
+        + 0.5 * 0.254829592
+    )
+    below = series * t * bell
+    return jnp.where(u < 0.0, below, 1.0 - below), bell
 
 
 def tables_kernel(geo_ref, order_ref, ana_ref, syn_ref, work_ref):
@@ -212,7 +224,7 @@
             j = 2 * half + h
             mixed = x_ref[j].astype(F32) + matmul(inverse_ref[...], values[h])
             pre = matmul(mixed.astype(BF16), expand_ref[...])
-            hidden = (0.5 * pre * (1.0 + lax.erf(pre * ROOT_HALF))).astype(BF16)
+            hidden = (pre * normal_and_density(pre)[0]).astype(BF16)
             result = mixed + matmul(hidden, reduce_ref[...])
             out_ref[j] = (result * live(cycle_ref, j)).astype(BF16)
 
@@ -247,9 +259,9 @@
             mixed_ref[rows, :] = mixed_b
             masked_ref[rows, :] = masked
             pre = matmul(mixed_b, expand_ref[...])
-            normal = 0.5 * (1.0 + lax.erf(pre * ROOT_HALF))
+            normal, bell = normal_and_density(pre)
             hidden_ref[rows, :] = (pre * normal).astype(BF16)
-            slope = normal + pre * jnp.exp(-0.5 * pre * pre) * INV_ROOT_TAU
+            slope = normal + pre * bell * INV_ROOT_TAU
             grad_hidden = matmul(masked, reduce_ref[...], ((1,), (1,)))
             grad_pre = (grad_hidden * slope).astype(BF16)
             grad_pre_ref[rows, :] = grad_pre

time: 192 us -> 193 us (level)
  Pallas kernels: 16.5 us -> 19 us
    pallas_call x12, Pallas kernels: 16.5 us -> 19 us  [call(): pl.pallas_call(kernel, out_shape=outs, in_specs=specs, out_specs=[pl.Bloc...]
  transfers between devices with their start and end apart: 13 -> 13, of which waited for: 10 -> 10; matrix products, arithmetic and copies ran while one was open for 1% -> 1% of each run, Pallas kernels for 2% -> 3%
where the time goes in v8:
time: 193 us; the launch traced here: 192 us
  waiting for transfers between devices  109 us (56%)
  starting transfers between devices  60.6 us (31%)
  Pallas kernels  19 us (10%)
  local copies, waits for them, and re-layouts  2.51 us (1%)
    all_to_all x6, waiting for transfers between devices, exchange(): return lax.all_to_all(blocks, axes, split_axis=0, concat_axis=0, tiled=True)  99.6 us
    all_to_all x6, starting transfers between devices, exchange(): return lax.all_to_all(blocks, axes, split_axis=0, concat_axis=0, tiled=True)  41.3 us
    pallas_call x12, Pallas kernels, call(): pl.pallas_call(kernel, out_shape=outs, in_specs=specs, out_specs=[pl.Bloc...  19 us
    ppermute x3, starting transfers between devices, around(): lax.ppermute(block, axis, [(i, (i + distance) % count) for i in range(cou...  10.7 us
    ppermute x2, waiting for transfers between devices, from_behind(): return lax.ppermute(block, axis, route)  4.77 us
    ppermute x2, starting transfers between devices, from_behind(): return lax.ppermute(block, axis, route)  4.42 us
  transfers between devices with their start and end apart: 13, of which 10 were waited for; matrix products, arithmetic and copies ran while one was open for 1% of the time, Pallas kernels for 3%

profile of v8, /device:TPU:1, one launch (start us, length us, event | category | flops | bytes accessed | tf_op | source)
XLA Modules:
  0.0 192.1 jit_solution(15157677900113299734)
XLA Ops:
  0.7 2.2 %shard_map.155 = bf16[32,32,128]{2,1,0:T(8,128)(2,1)} custom-call(bf16[4,240,128]{2,1,0:T(8,128)(2,1)} %bitcast.41, bf16[256,240]{1,0:T(8,128)(2,1)} %constant.97.clone.forward_hbm.forward_ref), custom_call_target="tpu_custom_call" | custom-call | flops 62914560 | bytes 630784 | tf_op jit(solution)/shard_map/pallas_call | solution.py:335
  2.9 16.9 %all-to-all-start = ((bf16[32,32,128]{2,1,0:T(8,128)(2,1)}), bf16[32,32,128]{2,1,0:T(8,128)(2,1)S(1)}, u32[]{:S(2)}, u32[]{:S(2)}) async-start(bf16[32,32,128]{2,1,0:T(8,128)(2,1)} %shard_map.155), calls=%async_computation | async-start | bytes 524288 | tf_op jit(solution)/shard_map/all_to_all | solution.py:359
  22.2 19.5 %all-to-all-done.arrived_ref = bf16[32,32,128]{2,1,0:T(8,128)(2,1)S(1)} async-done(((bf16[32,32,128]{2,1,0:T(8,128)(2,1)}), bf16[32,32,128]{2,1,0:T(8,128)(2,1)S(1)}, u32[]{:S(2)}, u32[]{:S(2)}) %all-to-all-start) | async-done | bytes 262176 | tf_op jit(solution)/shard_map/all_to_all | solution.py:359
  41.8 1.3 shard_map.158
  43.1 4.7 %all-to-all-start.1 = ((bf16[32,64,128]{2,1,0:T(8,128)(2,1)}), bf16[32,64,128]{2,1,0:T(8,128)(2,1)S(1)}, u32[]{:S(2)}, u32[]{:S(2)}) async-start(bf16[32,64,128]{2,1,0:T(8,128)(2,1)} %get-tuple-element.27), calls=%async_computation.1 | async-start | bytes 1048576 | tf_op jit(solution)/shard_map/all_to_all | solution.py:359
  47.8 33.5 %all-to-all-done.1.values_ref.arrived_ref = bf16[32,64,128]{2,1,0:T(8,128)(2,1)S(1)} async-done(((bf16[32,64,128]{2,1,0:T(8,128)(2,1)}), bf16[32,64,128]{2,1,0:T(8,128)(2,1)S(1)}, u32[]{:S(2)}, u32[]{:S(2)}) %all-to-all-start.1) | async-done | bytes 524320 | tf_op jit(solution)/shard_map/all_to_all | solution.py:359
  81.3 0.9 copy-done.11
  82.2 5.4 %shard_map.159 = (bf16[32,32,128]{2,1,0:T(8,128)(2,1)S(1)}, f32[4,240,128]{2,1,0:T(8,128)S(1)}, bf16[2,4,192,128]{3,2,1,0:T(8,128)(2,1)S(1)}) custom-call(bf16[4,240,128]{2,1,0:T(8,128)(2,1)S(1)} %bitcast.42, bf16[32,64,128]{2,1,0:T(8,128)(2,1)S(1)} %all-to-all-done.1.values_ref.arrived_ref, bf16[4,240,128]{2,1,0:T(8,128)(2,1)S(1)} %bitcast.47, ...), custom_call_target="tpu_custom_call" | custom-call | flops 1069547520 | bytes 2801680 | tf_op jit(solution)/shard_map/pallas_call | solution.py:335
  87.7 1.3 shard_map.160
  89.0 4.3 %all-to-all-start.2 = ((bf16[32,64,128]{2,1,0:T(8,128)(2,1)}), bf16[32,64,128]{2,1,0:T(8,128)(2,1)S(1)}, u32[]{:S(2)}, u32[]{:S(2)}) async-start(bf16[32,64,128]{2,1,0:T(8,128)(2,1)} %shard_map.160), calls=%async_computation.2 | async-start | bytes 1048576 | tf_op jit(solution)/shard_map/all_to_all | solution.py:359
  93.3 2.3 %collective-permute-start = (bf16[4,192,128]{2,1,0:T(8,128)(2,1)S(1)}, bf16[4,192,128]{2,1,0:T(8,128)(2,1)S(1)}, u32[]{:S(2)}, u32[]{:S(2)}) collective-permute-start(bf16[4,192,128]{2,1,0:T(8,128)(2,1)S(1)} %dynamic-slice_bitcast_fusion), channel_id=1, source_target_pairs={{0,4},{4,0},{1,5},{5,1},{2,6},{6,2},{3,7},{7,3},{8,12},{12,8},{9,1... | collective-permute-start | bytes 589832 | tf_op jit(solution)/shard_map/ppermute | solution.py:371
  95.6 1.0 collective-permute-done
  96.8 3.2 %collective-permute-start.1 = (bf16[192,128]{1,0:T(8,128)(2,1)S(1)}, bf16[192,128]{1,0:T(8,128)(2,1)S(1)}, u32[]{:S(2)}, u32[]{:S(2)}) collective-permute-start(bf16[192,128]{1,0:T(8,128)(2,1)S(1)} %get-tuple-element.43), channel_id=1, source_target_pairs={{0,1},{1,2},{2,3},{3,0},{4,5},{5,6},{6,7},{7,4},{8,9},{9,10},{10,1... | collective-permute-start | bytes 147464 | tf_op jit(solution)/shard_map/ppermute | solution.py:377
  100.0 4.5 %collective-permute-start.2 = (bf16[192,128]{1,0:T(8,128)(2,1)S(1)}, bf16[192,128]{1,0:T(8,128)(2,1)S(1)}, u32[]{:S(2)}, u32[]{:S(2)}) collective-permute-start(bf16[192,128]{1,0:T(8,128)(2,1)S(1)} %get-tuple-element.45), channel_id=1, source_target_pairs={{0,2},{1,3},{2,0},{3,1},{4,6},{5,7},{6,4},{7,5},{8,10},{9,11},{10,... | collective-permute-start | bytes 147464 | tf_op jit(solution)/shard_map/ppermute | solution.py:377
  104.5 3.0 %collective-permute-start.3 = (bf16[192,128]{1,0:T(8,128)(2,1)S(1)}, bf16[192,128]{1,0:T(8,128)(2,1)S(1)}, u32[]{:S(2)}, u32[]{:S(2)}) collective-permute-start(bf16[192,128]{1,0:T(8,128)(2,1)S(1)} %get-tuple-element.44), channel_id=1, source_target_pairs={{0,3},{1,0},{2,1},{3,2},{4,7},{5,4},{6,5},{7,6},{8,11},{9,8},{10,9... | collective-permute-start | bytes 147464 | tf_op jit(solution)/shard_map/ppermute | solution.py:377
  107.5 2.1 %collective-permute-done.3 = bf16[192,128]{1,0:T(8,128)(2,1)S(1)} collective-permute-done((bf16[192,128]{1,0:T(8,128)(2,1)S(1)}, bf16[192,128]{1,0:T(8,128)(2,1)S(1)}, u32[]{:S(2)}, u32[]{:S(2)}) %collective-permute-start.3) | collective-permute-done | bytes 49184 | tf_op jit(solution)/shard_map/ppermute | solution.py:377
  109.7 17.1 %all-to-all-done.2.arrived_ref.values_ref = bf16[32,64,128]{2,1,0:T(8,128)(2,1)S(1)} async-done(((bf16[32,64,128]{2,1,0:T(8,128)(2,1)}), bf16[32,64,128]{2,1,0:T(8,128)(2,1)S(1)}, u32[]{:S(2)}, u32[]{:S(2)}) %all-to-all-start.2) | async-done | bytes 524320 | tf_op jit(solution)/shard_map/all_to_all | solution.py:359
  126.9 1.2 shard_map.161
  128.1 4.5 %all-to-all-start.3 = ((bf16[32,48,128]{2,1,0:T(8,128)(2,1)}), bf16[32,48,128]{2,1,0:T(8,128)(2,1)S(1)}, u32[]{:S(2)}, u32[]{:S(2)}) async-start(bf16[32,48,128]{2,1,0:T(8,128)(2,1)} %shard_map.161), calls=%async_computation.3 | async-start | bytes 786432 | tf_op jit(solution)/shard_map/all_to_all | solution.py:359
  132.6 3.6 %shard_map.162 = bf16[4,240,128]{2,1,0:T(8,128)(2,1)S(1)} custom-call(bf16[4,240,128]{2,1,0:T(8,128)(2,1)S(1)} %bitcast.44, bf16[32,64,128]{2,1,0:T(8,128)(2,1)S(1)} %all-to-all-done.2.arrived_ref.values_ref, bf16[240,256]{1,0:T(8,128)(2,1)S(1)} %copy-done.15, bf16[128,768]{1,0:T(8,128)(2,1)S(1)} %get-tuple-element.30.expand_ref, ...), custom_call_target="tpu_custom_call" | custom-call | flops 440401920 | bytes 1531920 | tf_op jit(solution)/shard_map/pallas_call | solution.py:335
  136.2 3.1 %collective-permute-start.4 = (bf16[4,240,128]{2,1,0:T(8,128)(2,1)S(1)}, bf16[4,240,128]{2,1,0:T(8,128)(2,1)S(1)}, u32[]{:S(2)}, u32[]{:S(2)}) collective-permute-start(bf16[4,240,128]{2,1,0:T(8,128)(2,1)S(1)} %shard_map.162), channel_id=1, source_target_pairs={{0,128},{128,256},{256,384},{1,129},{129,257},{257,385},{2,130},{1... | collective-permute-start | bytes 737288 | tf_op jit(solution)/shard_map/ppermute | solution.py:365
  139.4 4.8 %collective-permute-done.4.next_ref = bf16[4,240,128]{2,1,0:T(8,128)(2,1)S(1)} collective-permute-done((bf16[4,240,128]{2,1,0:T(8,128)(2,1)S(1)}, bf16[4,240,128]{2,1,0:T(8,128)(2,1)S(1)}, u32[]{:S(2)}, u32[]{:S(2)}) %collective-permute-start.4) | collective-permute-done | bytes 245792 | tf_op jit(solution)/shard_map/ppermute | solution.py:365
  144.1 16.5 %all-to-all-done.3.arrived_ref.coeffs_ref = bf16[32,48,128]{2,1,0:T(8,128)(2,1)S(1)} async-done(((bf16[32,48,128]{2,1,0:T(8,128)(2,1)}), bf16[32,48,128]{2,1,0:T(8,128)(2,1)S(1)}, u32[]{:S(2)}, u32[]{:S(2)}) %all-to-all-start.3) | async-done | bytes 393248 | tf_op jit(solution)/shard_map/all_to_all | solution.py:359
  161.3 3.6 %all-to-all-start.4 = ((bf16[16,24,128]{2,1,0:T(8,128)(2,1)}), bf16[16,24,128]{2,1,0:T(8,128)(2,1)S(1)}, u32[]{:S(2)}, u32[]{:S(2)}) async-start(bf16[16,24,128]{2,1,0:T(8,128)(2,1)} %shard_map.163), calls=%async_computation.4 | async-start | bytes 196608 | tf_op jit(solution)/shard_map/all_to_all | solution.py:359
  164.9 0.8 shard_map.165
  165.8 1.3 collective-permute-start.6
  167.1 9.6 %all-to-all-done.4.pieces_ref = bf16[16,24,128]{2,1,0:T(8,128)(2,1)S(1)} async-done(((bf16[16,24,128]{2,1,0:T(8,128)(2,1)}), bf16[16,24,128]{2,1,0:T(8,128)(2,1)S(1)}, u32[]{:S(2)}, u32[]{:S(2)}) %all-to-all-start.4) | async-done | bytes 98336 | tf_op jit(solution)/shard_map/all_to_all | solution.py:359
  177.4 7.2 %all-to-all-start.5 = ((bf16[8,128,128]{2,1,0:T(8,128)(2,1)}), bf16[8,128,128]{2,1,0:T(8,128)(2,1)S(1)}, u32[]{:S(2)}, u32[]{:S(2)}) async-start(bf16[8,128,128]{2,1,0:T(8,128)(2,1)} %shard_map.164), calls=%async_computation.5 | async-start | bytes 524288 | tf_op jit(solution)/shard_map/all_to_all | solution.py:359
  184.7 1.9 collective-permute-start.5
  186.6 1.3 collective-permute-done.5.other_ref
  187.8 3.4 %all-to-all-done.5.filter_rows_ref = bf16[8,128,128]{2,1,0:T(8,128)(2,1)S(1)} async-done(((bf16[8,128,128]{2,1,0:T(8,128)(2,1)}), bf16[8,128,128]{2,1,0:T(8,128)(2,1)S(1)}, u32[]{:S(2)}, u32[]{:S(2)}) %all-to-all-start.5) | async-done | bytes 262176 | tf_op jit(solution)/shard_map/all_to_all | solution.py:359
  191.2 0.9 shard_map.166
  (51 shorter events, 4.1 us)
Async XLA Ops:
  0.6 19.2 %copy-start.16 = (s32[128]{0:T(128)S(1)}, s32[128]{0:T(128)}, u32[]{:S(2)}) copy-start(s32[128]{0:T(128)} %param.18) | copy-start | bytes 1540
  0.6 20.5 %copy-start.5 = (bf16[1,768,128]{2,1,0:T(8,128)(2,1)S(1)}, bf16[1,768,128]{2,1,0:T(8,128)(2,1)}, u32[]{:S(2)}) copy-start(bf16[1,768,128]{2,1,0:T(8,128)(2,1)} %param.16) | copy-start | bytes 589828
  0.7 20.5 %copy-start.6 = (bf16[256,240]{1,0:T(8,128)(2,1)S(1)}, bf16[256,240]{1,0:T(8,128)(2,1)}, u32[]{:S(2)}) copy-start(bf16[256,240]{1,0:T(8,128)(2,1)} %constant.99.clone.rest_1_) | copy-start | bytes 368644
  0.7 20.5 %copy-start.8 = (bf16[240,256]{1,0:T(8,128)(2,1)S(1)}, bf16[240,256]{1,0:T(8,128)(2,1)}, u32[]{:S(2)}) copy-start(bf16[240,256]{1,0:T(8,128)(2,1)} %constant.98.clone.rest_0_) | copy-start | bytes 368644
  2.9 18.3 %copy-start.1 = (bf16[256,240]{1,0:T(8,128)(2,1)S(1)}, bf16[256,240]{1,0:T(8,128)(2,1)}, u32[]{:S(2)}) copy-start(bf16[256,240]{1,0:T(8,128)(2,1)} %constant.97.clone.forward_hbm.forward_ref) | copy-start | bytes 368644
  2.9 18.3 %copy-start.3 = (bf16[1,1,4,240,128]{4,3,2,1,0:T(8,128)(2,1)S(1)}, bf16[1,1,4,240,128]{4,3,2,1,0:T(8,128)(2,1)}, u32[]{:S(2)}) copy-start(bf16[1,1,4,240,128]{4,3,2,1,0:T(8,128)(2,1)} %param.12) | copy-start | bytes 737284
  2.9 18.3 %copy-start.4 = (bf16[1,128,768]{2,1,0:T(8,128)(2,1)S(1)}, bf16[1,128,768]{2,1,0:T(8,128)(2,1)}, u32[]{:S(2)}) copy-start(bf16[1,128,768]{2,1,0:T(8,128)(2,1)} %param.15) | copy-start | bytes 589828
  2.9 38.9 %all-to-all-start = ((bf16[32,32,128]{2,1,0:T(8,128)(2,1)}), bf16[32,32,128]{2,1,0:T(8,128)(2,1)S(1)}, u32[]{:S(2)}, u32[]{:S(2)}) async-start(bf16[32,32,128]{2,1,0:T(8,128)(2,1)} %shard_map.155), calls=%async_computation | async-start | bytes 524288 | tf_op jit(solution)/shard_map/all_to_all | solution.py:359
  21.2 20.6 %copy-start = (f32[1,2,120,128]{3,2,1,0:T(8,128)S(1)}, f32[1,2,120,128]{3,2,1,0:T(8,128)}, u32[]{:S(2)}) copy-start(f32[1,2,120,128]{3,2,1,0:T(8,128)} %param.17) | copy-start | bytes 368644
  21.6 0.7 copy-start.13
  22.2 20.8 %copy-start.10 = (bf16[768,128]{1,0:T(8,128)(2,1)}, bf16[768,128]{1,0:T(8,128)(2,1)S(1)}, u32[]{:S(2)}) copy-start(bf16[768,128]{1,0:T(8,128)(2,1)S(1)} %get-tuple-element.31.reduce_ref) | copy-start | bytes 589828
  43.1 38.2 %copy-start.2 = (bf16[1,1,4,240,128]{4,3,2,1,0:T(8,128)(2,1)S(1)}, bf16[1,1,4,240,128]{4,3,2,1,0:T(8,128)(2,1)}, u32[]{:S(2)}) copy-start(bf16[1,1,4,240,128]{4,3,2,1,0:T(8,128)(2,1)} %param.13) | copy-start | bytes 737284
  43.1 38.2 %copy-start.9 = (bf16[1,1,4,240,128]{4,3,2,1,0:T(8,128)(2,1)S(1)}, bf16[1,1,4,240,128]{4,3,2,1,0:T(8,128)(2,1)}, u32[]{:S(2)}) copy-start(bf16[1,1,4,240,128]{4,3,2,1,0:T(8,128)(2,1)} %param.14) | copy-start | bytes 737284
  43.1 38.2 %copy-start.14 = (bf16[240,256]{1,0:T(8,128)(2,1)S(1)}, bf16[240,256]{1,0:T(8,128)(2,1)}, u32[]{:S(2)}) copy-start(bf16[240,256]{1,0:T(8,128)(2,1)} %copy-done.13) | copy-start | bytes 368644
  43.1 38.2 %all-to-all-start.1 = ((bf16[32,64,128]{2,1,0:T(8,128)(2,1)}), bf16[32,64,128]{2,1,0:T(8,128)(2,1)S(1)}, u32[]{:S(2)}, u32[]{:S(2)}) async-start(bf16[32,64,128]{2,1,0:T(8,128)(2,1)} %get-tuple-element.27), calls=%async_computation.1 | async-start | bytes 1048576 | tf_op jit(solution)/shard_map/all_to_all | solution.py:359
  81.3 0.9 copy-start.11
  89.0 37.9 %all-to-all-start.2 = ((bf16[32,64,128]{2,1,0:T(8,128)(2,1)}), bf16[32,64,128]{2,1,0:T(8,128)(2,1)S(1)}, u32[]{:S(2)}, u32[]{:S(2)}) async-start(bf16[32,64,128]{2,1,0:T(8,128)(2,1)} %shard_map.160), calls=%async_computation.2 | async-start | bytes 1048576 | tf_op jit(solution)/shard_map/all_to_all | solution.py:359
  93.3 3.3 %collective-permute-start = (bf16[4,192,128]{2,1,0:T(8,128)(2,1)S(1)}, bf16[4,192,128]{2,1,0:T(8,128)(2,1)S(1)}, u32[]{:S(2)}, u32[]{:S(2)}) collective-permute-start(bf16[4,192,128]{2,1,0:T(8,128)(2,1)S(1)} %dynamic-slice_bitcast_fusion), channel_id=1, source_target_pairs={{0,4},{4,0},{1,5},{5,1},{2,6},{6,2},{3,7},{7,3},{8,12},{12,8},{9,1... | collective-permute-start | bytes 589832 | tf_op jit(solution)/shard_map/ppermute | solution.py:371
  96.8 10.8 %collective-permute-start.1 = (bf16[192,128]{1,0:T(8,128)(2,1)S(1)}, bf16[192,128]{1,0:T(8,128)(2,1)S(1)}, u32[]{:S(2)}, u32[]{:S(2)}) collective-permute-start(bf16[192,128]{1,0:T(8,128)(2,1)S(1)} %get-tuple-element.43), channel_id=1, source_target_pairs={{0,1},{1,2},{2,3},{3,0},{4,5},{5,6},{6,7},{7,4},{8,9},{9,10},{10,1... | collective-permute-start | bytes 147464 | tf_op jit(solution)/shard_map/ppermute | solution.py:377
  100.0 7.5 %collective-permute-start.2 = (bf16[192,128]{1,0:T(8,128)(2,1)S(1)}, bf16[192,128]{1,0:T(8,128)(2,1)S(1)}, u32[]{:S(2)}, u32[]{:S(2)}) collective-permute-start(bf16[192,128]{1,0:T(8,128)(2,1)S(1)} %get-tuple-element.45), channel_id=1, source_target_pairs={{0,2},{1,3},{2,0},{3,1},{4,6},{5,7},{6,4},{7,5},{8,10},{9,11},{10,... | collective-permute-start | bytes 147464 | tf_op jit(solution)/shard_map/ppermute | solution.py:377
  104.5 5.1 %collective-permute-start.3 = (bf16[192,128]{1,0:T(8,128)(2,1)S(1)}, bf16[192,128]{1,0:T(8,128)(2,1)S(1)}, u32[]{:S(2)}, u32[]{:S(2)}) collective-permute-start(bf16[192,128]{1,0:T(8,128)(2,1)S(1)} %get-tuple-element.44), channel_id=1, source_target_pairs={{0,3},{1,0},{2,1},{3,2},{4,7},{5,4},{6,5},{7,6},{8,11},{9,8},{10,9... | collective-permute-start | bytes 147464 | tf_op jit(solution)/shard_map/ppermute | solution.py:377
  128.1 4.5 %copy-start.12 = (bf16[768,128]{1,0:T(8,128)(2,1)S(1)}, bf16[768,128]{1,0:T(8,128)(2,1)}, u32[]{:S(2)}) copy-start(bf16[768,128]{1,0:T(8,128)(2,1)} %copy-done.10) | copy-start | bytes 589828
  128.1 4.5 %copy-start.15 = (bf16[240,256]{1,0:T(8,128)(2,1)S(1)}, bf16[240,256]{1,0:T(8,128)(2,1)}, u32[]{:S(2)}) copy-start(bf16[240,256]{1,0:T(8,128)(2,1)} %copy-done.13) | copy-start | bytes 368644
  128.1 32.5 %all-to-all-start.3 = ((bf16[32,48,128]{2,1,0:T(8,128)(2,1)}), bf16[32,48,128]{2,1,0:T(8,128)(2,1)S(1)}, u32[]{:S(2)}, u32[]{:S(2)}) async-start(bf16[32,48,128]{2,1,0:T(8,128)(2,1)} %shard_map.161), calls=%async_computation.3 | async-start | bytes 786432 | tf_op jit(solution)/shard_map/all_to_all | solution.py:359
  136.2 7.9 %collective-permute-start.4 = (bf16[4,240,128]{2,1,0:T(8,128)(2,1)S(1)}, bf16[4,240,128]{2,1,0:T(8,128)(2,1)S(1)}, u32[]{:S(2)}, u32[]{:S(2)}) collective-permute-start(bf16[4,240,128]{2,1,0:T(8,128)(2,1)S(1)} %shard_map.162), channel_id=1, source_target_pairs={{0,128},{128,256},{256,384},{1,129},{129,257},{257,385},{2,130},{1... | collective-permute-start | bytes 737288 | tf_op jit(solution)/shard_map/ppermute | solution.py:365
  161.3 3.7 %copy-start.7 = (bf16[240,256]{1,0:T(8,128)(2,1)S(1)}, bf16[240,256]{1,0:T(8,128)(2,1)}, u32[]{:S(2)}) copy-start(bf16[240,256]{1,0:T(8,128)(2,1)} %constant.96.clone.forward_ref) | copy-start | bytes 368644
  161.3 15.4 %all-to-all-start.4 = ((bf16[16,24,128]{2,1,0:T(8,128)(2,1)}), bf16[16,24,128]{2,1,0:T(8,128)(2,1)S(1)}, u32[]{:S(2)}, u32[]{:S(2)}) async-start(bf16[16,24,128]{2,1,0:T(8,128)(2,1)} %shard_map.163), calls=%async_computation.4 | async-start | bytes 196608 | tf_op jit(solution)/shard_map/all_to_all | solution.py:359
  165.8 20.8 %collective-permute-start.6 = (bf16[4,240,128]{2,1,0:T(8,128)(2,1)S(1)}, bf16[4,240,128]{2,1,0:T(8,128)(2,1)S(1)}, u32[]{:S(2)}, u32[]{:S(2)}) collective-permute-start(bf16[4,240,128]{2,1,0:T(8,128)(2,1)S(1)} %shard_map.165), channel_id=1, source_target_pairs={{128,0},{256,128},{384,256},{129,1},{257,129},{385,257},{130,2},{2... | collective-permute-start | bytes 737288 | tf_op jit(solution)/shard_map/ppermute | solution.py:365
  177.4 13.8 %all-to-all-start.5 = ((bf16[8,128,128]{2,1,0:T(8,128)(2,1)}), bf16[8,128,128]{2,1,0:T(8,128)(2,1)S(1)}, u32[]{:S(2)}, u32[]{:S(2)}) async-start(bf16[8,128,128]{2,1,0:T(8,128)(2,1)} %shard_map.164), calls=%async_computation.5 | async-start | bytes 524288 | tf_op jit(solution)/shard_map/all_to_all | solution.py:359
  184.7 3.2 %collective-permute-start.5 = (bf16[16,24,128]{2,1,0:T(8,128)(2,1)S(1)}, bf16[16,24,128]{2,1,0:T(8,128)(2,1)S(1)}, u32[]{:S(2)}, u32[]{:S(2)}) collective-permute-start(bf16[16,24,128]{2,1,0:T(8,128)(2,1)S(1)} %all-to-all-done.4.pieces_ref), channel_id=1, source_target_pairs={{0,4},{4,0},{1,5},{5,1},{2,6},{6,2},{3,7},{7,3},{8,12},{12,8},{9,1... | collective-permute-start | bytes 294920 | tf_op jit(solution)/shard_map/ppermute | solution.py:520

commit v9 on v7

--- a/solution.py
+++ b/solution.py
@@ -36,11 +36,12 @@
     factor = np.where(value == 0, 1.0, 2.0) * live / (2.0 * math.pi)
     inverse = np.stack([np.cos(phase) * factor, -np.sin(phase) * factor], axis=1)
 
-    def arranged(table):
-        table = table.reshape(NLON, 2, PEERS, ROWS).transpose(0, 2, 1, 3)
+    def arranged(table, places):
+        table = table.reshape(NLON, 2, PEERS, ROWS).transpose(0, *places)
         return table.reshape(NLON, 256).astype(np.float32).astype(jnp.bfloat16)
 
-    return arranged(forward), arranged(inverse)
+    saved, fresh = (2, 1, 3), (3, 1, 2)
+    return [arranged(table, places) for places in (saved, fresh) for table in (forward, inverse)]
 
 
 def order_constants():
@@ -119,12 +120,19 @@
 
 
 def fresh_coeffs_kernel(x_ref, forward_ref, *rest):
-    count = len(rest) // 2
-    out_ref = rest[count]
-    for source, target in zip(rest[:count], rest[count + 1 :]):
+    *rest, work_ref = rest
+    count = len(rest) // 2 - 1
+    own_ref, lent_ref = rest[count : count + 2]
+    for source, target in zip(rest[:count], rest[count + 2 :]):
         target[...] = source[...]
-    for half in range(2):
-        to_blocks(out_ref, half, [matmul(forward_ref[...], x_ref[2 * half + h]) for h in range(2)])
+    for j in range(ROWS):
+        coeffs = matmul(forward_ref[...], x_ref[j])
+        for place in range(8):
+            target = pl.ds(place // 2 * 256 + j * 2 + place % 2, PEERS, stride=8)
+            work_ref[target, :] = coeffs[place * PEERS : (place + 1) * PEERS]
+    groups = [work_ref[256 * u : 256 * u + 256, :].reshape(PEERS, 8, CH) for u in range(ROWS)]
+    own_ref[...] = jnp.concatenate(groups[:3], axis=1).astype(BF16)
+    lent_ref[...] = groups[3].astype(BF16)
 
 
 def padded_filter(filt_ref):
@@ -132,18 +140,20 @@
     return [jnp.concatenate([filt_ref[part], rest], axis=0) for part in range(2)]
 
 
-def spectral(came_ref, goes_ref, ana_ref, syn_ref, filt_ref, spectra_ref=None):
+def filter_step(spectra, real, imag):
+    first, second = spectra[:, :CH], spectra[:, CH:]
+    return jnp.concatenate(
+        [real * first - imag * second, real * second + imag * first], axis=1
+    ).astype(BF16)
+
+
+def spectral(came_ref, goes_ref, ana_ref, syn_ref, filt_ref, spectra_ref):
     real, imag = padded_filter(filt_ref)
     for t in range(ROWS):
         parts = [came_ref[pl.ds(r * ROWS + t, LANES, stride=8), :] for r in range(2)]
         spectra = matmul(ana_ref[t], jnp.concatenate(parts, axis=1).astype(BF16))
-        if spectra_ref is not None:
-            spectra_ref[t] = spectra
-        first, second = spectra[:, :CH], spectra[:, CH:]
-        filtered = jnp.concatenate(
-            [real * first - imag * second, real * second + imag * first], axis=1
-        ).astype(BF16)
-        values = matmul(syn_ref[t], filtered, ((0,), (0,)))
+        spectra_ref[t] = spectra
+        values = matmul(syn_ref[t], filter_step(spectra, real, imag), ((0,), (0,)))
         for r in range(2):
             goes_ref[pl.ds(r * ROWS + t, LANES, stride=8), :] = values[:, r * CH : (r + 1) * CH]
 
@@ -158,12 +168,35 @@
 
 
 def fresh_spectral_kernel(
-    arrived_ref, ana_ref, syn_ref, filt_ref, beside_ref, out_ref, came_ref, goes_ref
+    arrived_ref,
+    ana_ref,
+    syn_ref,
+    filt_ref,
+    lent_a_ref,
+    lent_b_ref,
+    lent_c_ref,
+    last_ref,
+    beside_ref,
+    out_ref,
+    came_ref,
+    goes_ref,
 ):
     out_ref[:, :32, :] = beside_ref[...]
-    came_ref[...] = arrived_ref[:, 32:, :].reshape(LANES * 8, CH).astype(F32)
-    spectral(came_ref, goes_ref, ana_ref, syn_ref, filt_ref)
-    out_ref[:, 32:, :] = goes_ref[...].reshape(PEERS, 32, CH).astype(BF16)
+    came = arrived_ref[:, 32:, :].astype(F32)
+    last = last_ref[0]
+    own = padded_filter(filt_ref)
+    for u, lent_ref in enumerate((lent_a_ref, lent_b_ref, lent_c_ref)):
+        came_ref[256 * u : 256 * u + 256, :] = came[:, 8 * u : 8 * u + 8].reshape(256, CH)
+        lent = padded_filter(lent_ref)
+        real, imag = [jnp.where(last == 1, lent[part], own[part]) for part in range(2)]
+        t = jnp.where(last == 1, 3, u)
+        parts = [came_ref[pl.ds(256 * u + r, LANES, stride=2), :] for r in range(2)]
+        spectra = matmul(ana_ref[t], jnp.concatenate(parts, axis=1).astype(BF16))
+        values = matmul(syn_ref[t], filter_step(spectra, real, imag), ((0,), (0,)))
+        for r in range(2):
+            goes_ref[pl.ds(256 * u + r, LANES, stride=2), :] = values[:, r * CH : (r + 1) * CH]
+    groups = [goes_ref[256 * u : 256 * u + 256, :].reshape(PEERS, 8, CH) for u in range(3)]
+    out_ref[:, 32:, :] = jnp.concatenate(groups, axis=1).astype(BF16)
 
 
 def spectral_back_kernel(
@@ -205,16 +238,35 @@
     return jnp.where(cycle_ref[j] < NLAT, 1.0, 0.0).astype(F32)
 
 
-def mlp_kernel(x_ref, values_ref, inverse_ref, expand_ref, reduce_ref, cycle_ref, out_ref):
-    for half in range(2):
-        values = from_blocks(values_ref, 2 + half)
-        for h in range(2):
-            j = 2 * half + h
-            mixed = x_ref[j].astype(F32) + matmul(inverse_ref[...], values[h])
-            pre = matmul(mixed.astype(BF16), expand_ref[...])
-            hidden = (0.5 * pre * (1.0 + lax.erf(pre * ROOT_HALF))).astype(BF16)
-            result = mixed + matmul(hidden, reduce_ref[...])
-            out_ref[j] = (result * live(cycle_ref, j)).astype(BF16)
+def mlp_kernel(
+    x_ref,
+    values_ref,
+    lent_a_ref,
+    lent_b_ref,
+    lent_c_ref,
+    inverse_ref,
+    expand_ref,
+    reduce_ref,
+    cycle_ref,
+    out_ref,
+    work_ref,
+):
+    own = values_ref[:, 32:, :].astype(F32)
+    lent = [ref[...].astype(F32) for ref in (lent_a_ref, lent_b_ref, lent_c_ref)]
+    for u in range(3):
+        work_ref[256 * u : 256 * u + 256, :] = own[:, 8 * u : 8 * u + 8].reshape(256, CH)
+    work_ref[768:, :] = (lent[0] + lent[1] + lent[2]).reshape(256, CH)
+    for j in range(ROWS):
+        parts = [
+            work_ref[pl.ds(place // 2 * 256 + j * 2 + place % 2, PEERS, stride=8), :]
+            for place in range(8)
+        ]
+        values = jnp.concatenate(parts, axis=0).astype(BF16)
+        mixed = x_ref[j].astype(F32) + matmul(inverse_ref[...], values)
+        pre = matmul(mixed.astype(BF16), expand_ref[...])
+        hidden = (0.5 * pre * (1.0 + lax.erf(pre * ROOT_HALF))).astype(BF16)
+        result = mixed + matmul(hidden, reduce_ref[...])
+        out_ref[j] = (result * live(cycle_ref, j)).astype(BF16)
 
 
 def mlp_back_kernel(
@@ -333,7 +385,9 @@
     )(*args)
 
 
-PAIRED = jax.ShapeDtypeStruct((PEERS, 64, CH), BF16)
+PAIRED = jax.ShapeDtypeStruct((PEERS, 56, CH), BF16)
+OWN = jax.ShapeDtypeStruct((PEERS, 24, CH), BF16)
+LENT = jax.ShapeDtypeStruct((PEERS, 8, CH), BF16)
 SUMMED = jax.ShapeDtypeStruct((PEERS, 48, CH), BF16)
 BLOCKS = jax.ShapeDtypeStruct((PEERS, 32, CH), BF16)
 TOKENS = jax.ShapeDtypeStruct((ROWS, NLON, CH), BF16)
@@ -351,6 +405,10 @@
     devices = range(lax.axis_size(axis))
     route = [(i - distance, i) for i in devices if i - distance in devices]
     return lax.ppermute(block, axis, route)
+
+
+def to_last(block):
+    return [lax.ppermute(block, "pipe", [(p, 3)]) for p in range(3)]
 
 
 def halved(blocks, axis, route, kept):
@@ -383,8 +441,7 @@
 
 
 def on_device(
-    forward_np,
-    inverse_np,
+    tables_np,
     orders_np,
     fresh_input,
     saved_input,
@@ -397,7 +454,11 @@
     position = lax.axis_index(SP)
     fresh, saved, cotangent = fresh_input[0, 0], saved_input[0, 0], output_grad[0, 0]
     expand, contract, filt = expand_weight[0], reduce_weight[0], filter_weight[0]
+    forward_np, inverse_np, fresh_forward_np, fresh_inverse_np = tables_np
     forward = jnp.asarray(forward_np)
+    fresh_forward_t = jnp.asarray(np.ascontiguousarray(fresh_forward_np.T))
+    fresh_inverse = jnp.asarray(fresh_inverse_np)
+    last = lax.axis_index("pipe") == 3
     forward_t = jnp.asarray(np.ascontiguousarray(forward_np.T))
     inverse = jnp.asarray(inverse_np)
     inverse_t = jnp.asarray(np.ascontiguousarray(inverse_np.T))
@@ -421,12 +482,14 @@
     )[0]
     saved_at_orders = exchange(saved_blocks, SP)
     kept = [inverse, inverse_t, expand, contract]
-    fresh_blocks, inverse, inverse_t, expand, contract = call(
+    fresh_own, fresh_lent, inverse, inverse_t, expand, contract = call(
         fresh_coeffs_kernel,
-        [BLOCKS] + [jax.ShapeDtypeStruct(k.shape, BF16) for k in kept],
-        [fresh, forward_t, *kept],
+        [OWN, LENT] + [jax.ShapeDtypeStruct(k.shape, BF16) for k in kept],
+        [fresh, fresh_forward_t, *kept],
+        [pltpu.VMEM((LANES * 8, CH), F32)],
         flops=dft,
     )
+    fresh_blocks = jnp.where(last, jnp.concatenate(to_last(fresh_lent), axis=1), fresh_own)
 
     lat_live = (cycle_table < NLAT).astype(F32)
     colatitude = math.pi * (jnp.minimum(cycle_table, NLAT - 1).astype(F32) + 0.5) / NLAT
@@ -452,6 +515,8 @@
         SPECTRAL_SCRATCH,
         flops=leg,
     )
+    lent_filt, values_fresh = lax.optimization_barrier((filt, values_fresh))
+    lent_filters = to_last(lent_filt)
     values_fresh = exchange(values_fresh, SP)
 
     narrow = pltpu.VMEM((ROWS * NLON, CH), BF16)
@@ -472,20 +537,33 @@
     grads_fresh = call(
         fresh_spectral_kernel,
         [PAIRED],
-        [values_fresh, ana, syn, filt, grad_values],
+        [
+            values_fresh,
+            ana,
+            syn,
+            filt,
+            *lent_filters,
+            last.astype(jnp.int32)[None],
+            grad_values,
+        ],
         SPECTRAL_SCRATCH,
         flops=leg,
+        smem=(7,),
     )[0]
     grads_fresh = exchange(grads_fresh, SP)
     share_blocks = share_blocks_of(shares)
 
+    lent_values = [
+        lax.ppermute(grads_fresh[:, 32 + 8 * p : 40 + 8 * p], "pipe", [(3, p)]) for p in range(3)
+    ]
     block = call(
         mlp_kernel,
         [TOKENS],
-        [fresh, grads_fresh, inverse, expand, contract, own_cycles],
+        [fresh, grads_fresh, *lent_values, fresh_inverse, expand, contract, own_cycles],
+        [pltpu.VMEM((LANES * 8, CH), F32)],
         flops=2 * mlp + dft,
         transcendentals=ROWS * NLON * HID,
-        smem=(5,),
+        smem=(8,),
     )[0]
     next_input = from_behind(block, "pipe", 1)
     coeffs_summed = call(
@@ -552,8 +630,7 @@
         P("pipe", "dp", None),
         P("pipe", None, None, None),
     )
-    forward, inverse = fourier_constants()
-    program = functools.partial(on_device, forward, inverse, order_constants())
+    program = functools.partial(on_device, fourier_constants(), order_constants())
     return jax.shard_map(
         program, mesh=finer, in_specs=in_specs, out_specs=out_specs, check_vma=False
     )

time: 192 us -> 188 us (0.979)
  waiting for transfers between devices: 110 us -> 90 us
  starting transfers between devices: 60.5 us -> 75.3 us
    all_to_all x6, waiting for transfers between devices: 101 us -> 78 us  [exchange(): return lax.all_to_all(blocks, axes, split_axis=0, concat_axis=0, tiled=True)]
    ppermute x0 -> x9, starting transfers between devices: none -> 14.1 us  [the longest x6 11.4 us: to_last(): return [lax.ppermute(block, 'pipe', [(p, 3)]) for p in range(3)]]
    ppermute x0 -> x9, waiting for transfers between devices: none -> 3.89 us  [the longest x3 3.88 us: on_device(): lax.ppermute(grads_fresh[:, 32 + 8 * p:40 + 8 * p], 'pipe', [(3, p)])]
  transfers between devices with their start and end apart: 13 -> 22, of which waited for: 10 -> 11; matrix products, arithmetic and copies ran while one was open for 1% -> 1% of each run, Pallas kernels for 2% -> 5%
where the time goes in v9:
time: 188 us; the launch traced here: 187 us
  waiting for transfers between devices  90 us (48%)
  starting transfers between devices  75.3 us (40%)
  Pallas kernels  16.5 us (9%)
  local copies, waits for them, and re-layouts  3.74 us (2%)
    all_to_all x6, waiting for transfers between devices, exchange(): return lax.all_to_all(blocks, axes, split_axis=0, concat_axis=0, tiled=True)  78 us
    all_to_all x6, starting transfers between devices, exchange(): return lax.all_to_all(blocks, axes, split_axis=0, concat_axis=0, tiled=True)  41 us
    pallas_call x12, Pallas kernels, call(): pl.pallas_call(kernel, out_shape=outs, in_specs=specs, out_specs=[pl.Bloc...  16.5 us
    ppermute x6, starting transfers between devices, to_last(): return [lax.ppermute(block, 'pipe', [(p, 3)]) for p in range(3)]  11.4 us
    ppermute x3, starting transfers between devices, around(): lax.ppermute(block, axis, [(i, (i + distance) % count) for i in range(cou...  10.7 us
    ppermute x2, starting transfers between devices, from_behind(): return lax.ppermute(block, axis, route)  5.38 us
    ppermute x3, waiting for transfers between devices, on_device(): lax.ppermute(grads_fresh[:, 32 + 8 * p:40 + 8 * p], 'pipe', [(3, p)])  3.88 us
  transfers between devices with their start and end apart: 22, of which 11 were waited for; matrix products, arithmetic and copies ran while one was open for 1% of the time, Pallas kernels for 5%

profile of v9, /device:TPU:1, one launch (start us, length us, event | category | flops | bytes accessed | tf_op | source)
XLA Modules:
  0.0 187.0 jit_solution(738614826034176147)
XLA Ops:
  0.7 2.2 %shard_map.173 = bf16[32,32,128]{2,1,0:T(8,128)(2,1)} custom-call(bf16[4,240,128]{2,1,0:T(8,128)(2,1)} %bitcast.47, bf16[256,240]{1,0:T(8,128)(2,1)} %constant.107.clone.forward_hbm), custom_call_target="tpu_custom_call" | custom-call | flops 62914560 | bytes 630784 | tf_op jit(solution)/shard_map/pallas_call | solution.py:375
  2.9 16.9 %all-to-all-start = ((bf16[32,32,128]{2,1,0:T(8,128)(2,1)}), bf16[32,32,128]{2,1,0:T(8,128)(2,1)S(1)}, u32[]{:S(2)}, u32[]{:S(2)}) async-start(bf16[32,32,128]{2,1,0:T(8,128)(2,1)} %shard_map.173), calls=%async_computation | async-start | bytes 524288 | tf_op jit(solution)/shard_map/all_to_all | solution.py:401
  20.2 4.4 %collective-permute-start = (bf16[32,8,128]{2,1,0:T(8,128)(2,1)S(1)}, bf16[32,8,128]{2,1,0:T(8,128)(2,1)S(1)}, u32[]{:S(2)}, u32[]{:S(2)}) collective-permute-start(bf16[32,8,128]{2,1,0:T(8,128)(2,1)S(1)} %get-tuple-element.29), channel_id=1, source_target_pairs={{0,384},{1,385},{2,386},{3,387},{4,388},{5,389},{6,390},{7,391},{8... | collective-permute-start | bytes 196616 | tf_op jit(solution)/shard_map/ppermute | solution.py:411
  27.5 14.3 %all-to-all-done.arrived_ref = bf16[32,32,128]{2,1,0:T(8,128)(2,1)S(1)} async-done(((bf16[32,32,128]{2,1,0:T(8,128)(2,1)}), bf16[32,32,128]{2,1,0:T(8,128)(2,1)S(1)}, u32[]{:S(2)}, u32[]{:S(2)}) %all-to-all-start) | async-done | bytes 262176 | tf_op jit(solution)/shard_map/all_to_all | solution.py:401
  41.8 1.3 shard_map.176
  43.1 4.7 %all-to-all-start.1 = ((bf16[32,56,128]{2,1,0:T(8,128)(2,1)}), bf16[32,56,128]{2,1,0:T(8,128)(2,1)S(1)}, u32[]{:S(2)}, u32[]{:S(2)}) async-start(bf16[32,56,128]{2,1,0:T(8,128)(2,1)} %get-tuple-element.32), calls=%async_computation.1 | async-start | bytes 917504 | tf_op jit(solution)/shard_map/all_to_all | solution.py:401
  47.7 4.4 %collective-permute-start.3 = (f32[2,120,128]{2,1,0:T(8,128)S(1)}, f32[2,120,128]{2,1,0:T(8,128)S(1)}, u32[]{:S(2)}, u32[]{:S(2)}) collective-permute-start(f32[2,120,128]{2,1,0:T(8,128)S(1)} %bitcast.40), channel_id=1, source_target_pairs={{0,384},{1,385},{2,386},{3,387},{4,388},{5,389},{6,390},{7,391},{8... | collective-permute-start | bytes 368648 | tf_op jit(solution)/shard_map/ppermute | solution.py:411
  53.6 25.0 %all-to-all-done.1.values_ref.arrived_ref = bf16[32,56,128]{2,1,0:T(8,128)(2,1)S(1)} async-done(((bf16[32,56,128]{2,1,0:T(8,128)(2,1)}), bf16[32,56,128]{2,1,0:T(8,128)(2,1)S(1)}, u32[]{:S(2)}, u32[]{:S(2)}) %all-to-all-start.1) | async-done | bytes 458784 | tf_op jit(solution)/shard_map/all_to_all | solution.py:401
  81.3 4.3 %shard_map.177 = (bf16[32,32,128]{2,1,0:T(8,128)(2,1)S(1)}, f32[4,240,128]{2,1,0:T(8,128)S(1)}, bf16[2,4,192,128]{3,2,1,0:T(8,128)(2,1)S(1)}) custom-call(bf16[4,240,128]{2,1,0:T(8,128)(2,1)S(1)} %bitcast.48, bf16[32,56,128]{2,1,0:T(8,128)(2,1)S(1)} %all-to-all-done.1.values_ref.arrived_ref, bf16[4,240,128]{2,1,0:T(8,128)(2,1)S(1)} %bitcast.51, ...), custom_call_target="tpu_custom_call" | custom-call | flops 1069547520 | bytes 2736144 | tf_op jit(solution)/shard_map/pallas_call | solution.py:375
  85.6 1.2 shard_map.178
  86.8 4.3 %all-to-all-start.2 = ((bf16[32,56,128]{2,1,0:T(8,128)(2,1)}), bf16[32,56,128]{2,1,0:T(8,128)(2,1)S(1)}, u32[]{:S(2)}, u32[]{:S(2)}) async-start(bf16[32,56,128]{2,1,0:T(8,128)(2,1)} %shard_map.178), calls=%async_computation.2 | async-start | bytes 917504 | tf_op jit(solution)/shard_map/all_to_all | solution.py:401
  91.1 2.3 %collective-permute-start.6 = (bf16[4,192,128]{2,1,0:T(8,128)(2,1)S(1)}, bf16[4,192,128]{2,1,0:T(8,128)(2,1)S(1)}, u32[]{:S(2)}, u32[]{:S(2)}) collective-permute-start(bf16[4,192,128]{2,1,0:T(8,128)(2,1)S(1)} %dynamic-slice_bitcast_fusion), channel_id=1, source_target_pairs={{0,4},{4,0},{1,5},{5,1},{2,6},{6,2},{3,7},{7,3},{8,12},{12,8},{9,1... | collective-permute-start | bytes 589832 | tf_op jit(solution)/shard_map/ppermute | solution.py:417
  94.6 3.2 %collective-permute-start.7 = (bf16[192,128]{1,0:T(8,128)(2,1)S(1)}, bf16[192,128]{1,0:T(8,128)(2,1)S(1)}, u32[]{:S(2)}, u32[]{:S(2)}) collective-permute-start(bf16[192,128]{1,0:T(8,128)(2,1)S(1)} %get-tuple-element.52), channel_id=1, source_target_pairs={{0,1},{1,2},{2,3},{3,0},{4,5},{5,6},{6,7},{7,4},{8,9},{9,10},{10,1... | collective-permute-start | bytes 147464 | tf_op jit(solution)/shard_map/ppermute | solution.py:423
  97.8 4.5 %collective-permute-start.8 = (bf16[192,128]{1,0:T(8,128)(2,1)S(1)}, bf16[192,128]{1,0:T(8,128)(2,1)S(1)}, u32[]{:S(2)}, u32[]{:S(2)}) collective-permute-start(bf16[192,128]{1,0:T(8,128)(2,1)S(1)} %get-tuple-element.54), channel_id=1, source_target_pairs={{0,2},{1,3},{2,0},{3,1},{4,6},{5,7},{6,4},{7,5},{8,10},{9,11},{10,... | collective-permute-start | bytes 147464 | tf_op jit(solution)/shard_map/ppermute | solution.py:423
  102.3 3.0 %collective-permute-start.9 = (bf16[192,128]{1,0:T(8,128)(2,1)S(1)}, bf16[192,128]{1,0:T(8,128)(2,1)S(1)}, u32[]{:S(2)}, u32[]{:S(2)}) collective-permute-start(bf16[192,128]{1,0:T(8,128)(2,1)S(1)} %get-tuple-element.53), channel_id=1, source_target_pairs={{0,3},{1,0},{2,1},{3,2},{4,7},{5,4},{6,5},{7,6},{8,11},{9,8},{10,9... | collective-permute-start | bytes 147464 | tf_op jit(solution)/shard_map/ppermute | solution.py:423
  105.3 2.1 %collective-permute-done.9 = bf16[192,128]{1,0:T(8,128)(2,1)S(1)} collective-permute-done((bf16[192,128]{1,0:T(8,128)(2,1)S(1)}, bf16[192,128]{1,0:T(8,128)(2,1)S(1)}, u32[]{:S(2)}, u32[]{:S(2)}) %collective-permute-start.9) | collective-permute-done | bytes 49184 | tf_op jit(solution)/shard_map/ppermute | solution.py:423
  107.5 14.4 %all-to-all-done.2.arrived_ref.values_ref = bf16[32,56,128]{2,1,0:T(8,128)(2,1)S(1)} async-done(((bf16[32,56,128]{2,1,0:T(8,128)(2,1)}), bf16[32,56,128]{2,1,0:T(8,128)(2,1)S(1)}, u32[]{:S(2)}, u32[]{:S(2)}) %all-to-all-start.2) | async-done | bytes 458784 | tf_op jit(solution)/shard_map/all_to_all | solution.py:401
  121.9 1.2 shard_map.179
  123.1 4.3 %all-to-all-start.3 = ((bf16[32,48,128]{2,1,0:T(8,128)(2,1)}), bf16[32,48,128]{2,1,0:T(8,128)(2,1)S(1)}, u32[]{:S(2)}, u32[]{:S(2)}) async-start(bf16[32,48,128]{2,1,0:T(8,128)(2,1)} %shard_map.179), calls=%async_computation.3 | async-start | bytes 786432 | tf_op jit(solution)/shard_map/all_to_all | solution.py:401
  127.5 1.3 collective-permute-start.10
  130.1 3.9 %collective-permute-done.10.lent_a_ref = bf16[32,8,128]{2,1,0:T(8,128)(2,1)S(1)} collective-permute-done((bf16[32,8,128]{2,1,0:T(8,128)(2,1)S(1)}, bf16[32,8,128]{2,1,0:T(8,128)(2,1)S(1)}, u32[]{:S(2)}, u32[]{:S(2)}) %collective-permute-start.10) | collective-permute-done | bytes 65568 | tf_op jit(solution)/shard_map/ppermute | solution.py:557
  134.0 2.2 %shard_map.180 = bf16[4,240,128]{2,1,0:T(8,128)(2,1)S(1)} custom-call(bf16[4,240,128]{2,1,0:T(8,128)(2,1)S(1)} %bitcast.46, bf16[32,56,128]{2,1,0:T(8,128)(2,1)S(1)} %all-to-all-done.2.arrived_ref.values_ref, bf16[32,8,128]{2,1,0:T(8,128)(2,1)S(1)} %collective-permute-done.10.lent_a_ref, bf16[32,8,128]{2,1,0:T(8,128)(2,1)S(1)} %collective-permute-done.11.lent_b_ref, ...), custom_call_target="tpu_custom_call" | custom-call | flops 440401920 | bytes 1662992 | tf_op jit(solution)/shard_map/pallas_call | solution.py:375
  136.3 4.1 %collective-permute-start.13 = (bf16[4,240,128]{2,1,0:T(8,128)(2,1)S(1)}, bf16[4,240,128]{2,1,0:T(8,128)(2,1)S(1)}, u32[]{:S(2)}, u32[]{:S(2)}) collective-permute-start(bf16[4,240,128]{2,1,0:T(8,128)(2,1)S(1)} %shard_map.180), channel_id=1, source_target_pairs={{0,128},{128,256},{256,384},{1,129},{129,257},{257,385},{2,130},{1... | collective-permute-start | bytes 737288 | tf_op jit(solution)/shard_map/ppermute | solution.py:407
  140.4 3.7 %collective-permute-done.13.next_ref = bf16[4,240,128]{2,1,0:T(8,128)(2,1)S(1)} collective-permute-done((bf16[4,240,128]{2,1,0:T(8,128)(2,1)S(1)}, bf16[4,240,128]{2,1,0:T(8,128)(2,1)S(1)}, u32[]{:S(2)}, u32[]{:S(2)}) %collective-permute-start.13) | collective-permute-done | bytes 245792 | tf_op jit(solution)/shard_map/ppermute | solution.py:407
  144.1 11.4 %all-to-all-done.3.arrived_ref.coeffs_ref = bf16[32,48,128]{2,1,0:T(8,128)(2,1)S(1)} async-done(((bf16[32,48,128]{2,1,0:T(8,128)(2,1)}), bf16[32,48,128]{2,1,0:T(8,128)(2,1)S(1)}, u32[]{:S(2)}, u32[]{:S(2)}) %all-to-all-start.3) | async-done | bytes 393248 | tf_op jit(solution)/shard_map/all_to_all | solution.py:401
  156.1 3.6 %all-to-all-start.4 = ((bf16[16,24,128]{2,1,0:T(8,128)(2,1)}), bf16[16,24,128]{2,1,0:T(8,128)(2,1)S(1)}, u32[]{:S(2)}, u32[]{:S(2)}) async-start(bf16[16,24,128]{2,1,0:T(8,128)(2,1)} %shard_map.181), calls=%async_computation.4 | async-start | bytes 196608 | tf_op jit(solution)/shard_map/all_to_all | solution.py:401
  160.6 1.3 collective-permute-start.15
  161.9 9.6 %all-to-all-done.4.pieces_ref = bf16[16,24,128]{2,1,0:T(8,128)(2,1)S(1)} async-done(((bf16[16,24,128]{2,1,0:T(8,128)(2,1)}), bf16[16,24,128]{2,1,0:T(8,128)(2,1)S(1)}, u32[]{:S(2)}, u32[]{:S(2)}) %all-to-all-start.4) | async-done | bytes 98336 | tf_op jit(solution)/shard_map/all_to_all | solution.py:401
  172.3 7.2 %all-to-all-start.5 = ((bf16[8,128,128]{2,1,0:T(8,128)(2,1)}), bf16[8,128,128]{2,1,0:T(8,128)(2,1)S(1)}, u32[]{:S(2)}, u32[]{:S(2)}) async-start(bf16[8,128,128]{2,1,0:T(8,128)(2,1)} %shard_map.182), calls=%async_computation.5 | async-start | bytes 524288 | tf_op jit(solution)/shard_map/all_to_all | solution.py:401
  179.5 1.9 %collective-permute-start.14 = (bf16[16,24,128]{2,1,0:T(8,128)(2,1)S(1)}, bf16[16,24,128]{2,1,0:T(8,128)(2,1)S(1)}, u32[]{:S(2)}, u32[]{:S(2)}) collective-permute-start(bf16[16,24,128]{2,1,0:T(8,128)(2,1)S(1)} %all-to-all-done.4.pieces_ref), channel_id=1, source_target_pairs={{0,4},{4,0},{1,5},{5,1},{2,6},{6,2},{3,7},{7,3},{8,12},{12,8},{9,1... | collective-permute-start | bytes 294920 | tf_op jit(solution)/shard_map/ppermute | solution.py:586
  181.4 1.3 collective-permute-done.14.other_ref
  182.7 3.4 %all-to-all-done.5.filter_rows_ref = bf16[8,128,128]{2,1,0:T(8,128)(2,1)S(1)} async-done(((bf16[8,128,128]{2,1,0:T(8,128)(2,1)}), bf16[8,128,128]{2,1,0:T(8,128)(2,1)S(1)}, u32[]{:S(2)}, u32[]{:S(2)}) %all-to-all-start.5) | async-done | bytes 262176 | tf_op jit(solution)/shard_map/all_to_all | solution.py:401
  (69 shorter events, 13.1 us)
Async XLA Ops:
  0.6 19.2 %copy-start.4 = (bf16[1,768,128]{2,1,0:T(8,128)(2,1)S(1)}, bf16[1,768,128]{2,1,0:T(8,128)(2,1)}, u32[]{:S(2)}) copy-start(bf16[1,768,128]{2,1,0:T(8,128)(2,1)} %param.18) | copy-start | bytes 589828
  0.6 19.2 %copy-start.5 = (bf16[256,240]{1,0:T(8,128)(2,1)S(1)}, bf16[256,240]{1,0:T(8,128)(2,1)}, u32[]{:S(2)}) copy-start(bf16[256,240]{1,0:T(8,128)(2,1)} %constant.105.clone.forward_ref) | copy-start | bytes 368644
  0.7 19.2 %copy-start.6 = (bf16[256,240]{1,0:T(8,128)(2,1)S(1)}, bf16[256,240]{1,0:T(8,128)(2,1)}, u32[]{:S(2)}) copy-start(bf16[256,240]{1,0:T(8,128)(2,1)} %constant.109.clone.rest_1_) | copy-start | bytes 368644
  0.7 19.2 %copy-start.9 = (bf16[240,256]{1,0:T(8,128)(2,1)S(1)}, bf16[240,256]{1,0:T(8,128)(2,1)}, u32[]{:S(2)}) copy-start(bf16[240,256]{1,0:T(8,128)(2,1)} %constant.108.clone.rest_0_) | copy-start | bytes 368644
  2.9 17.0 %copy-start.1 = (bf16[1,1,4,240,128]{4,3,2,1,0:T(8,128)(2,1)S(1)}, bf16[1,1,4,240,128]{4,3,2,1,0:T(8,128)(2,1)}, u32[]{:S(2)}) copy-start(bf16[1,1,4,240,128]{4,3,2,1,0:T(8,128)(2,1)} %param.14) | copy-start | bytes 737284
  2.9 17.0 %copy-start.3 = (bf16[1,128,768]{2,1,0:T(8,128)(2,1)S(1)}, bf16[1,128,768]{2,1,0:T(8,128)(2,1)}, u32[]{:S(2)}) copy-start(bf16[1,128,768]{2,1,0:T(8,128)(2,1)} %param.17) | copy-start | bytes 589828
  2.9 38.9 %all-to-all-start = ((bf16[32,32,128]{2,1,0:T(8,128)(2,1)}), bf16[32,32,128]{2,1,0:T(8,128)(2,1)S(1)}, u32[]{:S(2)}, u32[]{:S(2)}) async-start(bf16[32,32,128]{2,1,0:T(8,128)(2,1)} %shard_map.173), calls=%async_computation | async-start | bytes 524288 | tf_op jit(solution)/shard_map/all_to_all | solution.py:401
  20.2 7.2 %copy-start.11 = (bf16[256,240]{1,0:T(8,128)(2,1)}, bf16[256,240]{1,0:T(8,128)(2,1)S(1)}, u32[]{:S(2)}) copy-start(bf16[256,240]{1,0:T(8,128)(2,1)S(1)} %get-tuple-element.35.inverse_t_ref) | copy-start | bytes 368644
  20.2 7.2 %copy-start.13 = (bf16[240,256]{1,0:T(8,128)(2,1)}, bf16[240,256]{1,0:T(8,128)(2,1)S(1)}, u32[]{:S(2)}) copy-start(bf16[240,256]{1,0:T(8,128)(2,1)S(1)} %get-tuple-element.34.inverse_ref) | copy-start | bytes 368644
  20.2 7.1 %collective-permute-start = (bf16[32,8,128]{2,1,0:T(8,128)(2,1)S(1)}, bf16[32,8,128]{2,1,0:T(8,128)(2,1)S(1)}, u32[]{:S(2)}, u32[]{:S(2)}) collective-permute-start(bf16[32,8,128]{2,1,0:T(8,128)(2,1)S(1)} %get-tuple-element.29), channel_id=1, source_target_pairs={{0,384},{1,385},{2,386},{3,387},{4,388},{5,389},{6,390},{7,391},{8... | collective-permute-start | bytes 196616 | tf_op jit(solution)/shard_map/ppermute | solution.py:411
  24.6 2.7 %collective-permute-start.1 = (bf16[32,8,128]{2,1,0:T(8,128)(2,1)S(1)}, bf16[32,8,128]{2,1,0:T(8,128)(2,1)S(1)}, u32[]{:S(2)}, u32[]{:S(2)}) collective-permute-start(bf16[32,8,128]{2,1,0:T(8,128)(2,1)S(1)} %get-tuple-element.29), channel_id=1, source_target_pairs={{128,384},{129,385},{130,386},{131,387},{132,388},{133,389},{134,3... | collective-permute-start | bytes 196616 | tf_op jit(solution)/shard_map/ppermute | solution.py:411
  25.3 2.1 %collective-permute-start.2 = (bf16[32,8,128]{2,1,0:T(8,128)(2,1)S(1)}, bf16[32,8,128]{2,1,0:T(8,128)(2,1)S(1)}, u32[]{:S(2)}, u32[]{:S(2)}) collective-permute-start(bf16[32,8,128]{2,1,0:T(8,128)(2,1)S(1)} %get-tuple-element.29), channel_id=1, source_target_pairs={{256,384},{257,385},{258,386},{259,387},{260,388},{261,389},{262,3... | collective-permute-start | bytes 196616 | tf_op jit(solution)/shard_map/ppermute | solution.py:411
  27.4 14.4 %copy-start = (f32[1,2,120,128]{3,2,1,0:T(8,128)S(1)}, f32[1,2,120,128]{3,2,1,0:T(8,128)}, u32[]{:S(2)}) copy-start(f32[1,2,120,128]{3,2,1,0:T(8,128)} %param.19) | copy-start | bytes 368644
  43.1 35.5 %copy-start.2 = (bf16[1,1,4,240,128]{4,3,2,1,0:T(8,128)(2,1)S(1)}, bf16[1,1,4,240,128]{4,3,2,1,0:T(8,128)(2,1)}, u32[]{:S(2)}) copy-start(bf16[1,1,4,240,128]{4,3,2,1,0:T(8,128)(2,1)} %param.15) | copy-start | bytes 737284
  43.1 35.5 %all-to-all-start.1 = ((bf16[32,56,128]{2,1,0:T(8,128)(2,1)}), bf16[32,56,128]{2,1,0:T(8,128)(2,1)S(1)}, u32[]{:S(2)}, u32[]{:S(2)}) async-start(bf16[32,56,128]{2,1,0:T(8,128)(2,1)} %get-tuple-element.32), calls=%async_computation.1 | async-start | bytes 917504 | tf_op jit(solution)/shard_map/all_to_all | solution.py:401
  47.7 37.8 %collective-permute-start.3 = (f32[2,120,128]{2,1,0:T(8,128)S(1)}, f32[2,120,128]{2,1,0:T(8,128)S(1)}, u32[]{:S(2)}, u32[]{:S(2)}) collective-permute-start(f32[2,120,128]{2,1,0:T(8,128)S(1)} %bitcast.40), channel_id=1, source_target_pairs={{0,384},{1,385},{2,386},{3,387},{4,388},{5,389},{6,390},{7,391},{8... | collective-permute-start | bytes 368648 | tf_op jit(solution)/shard_map/ppermute | solution.py:411
  52.1 33.4 %collective-permute-start.4 = (f32[2,120,128]{2,1,0:T(8,128)S(1)}, f32[2,120,128]{2,1,0:T(8,128)S(1)}, u32[]{:S(2)}, u32[]{:S(2)}) collective-permute-start(f32[2,120,128]{2,1,0:T(8,128)S(1)} %bitcast.41), channel_id=1, source_target_pairs={{128,384},{129,385},{130,386},{131,387},{132,388},{133,389},{134,3... | collective-permute-start | bytes 368648 | tf_op jit(solution)/shard_map/ppermute | solution.py:411
  52.8 32.8 %collective-permute-start.5 = (f32[2,120,128]{2,1,0:T(8,128)S(1)}, f32[2,120,128]{2,1,0:T(8,128)S(1)}, u32[]{:S(2)}, u32[]{:S(2)}) collective-permute-start(f32[2,120,128]{2,1,0:T(8,128)S(1)} %bitcast.42), channel_id=1, source_target_pairs={{256,384},{257,385},{258,386},{259,387},{260,388},{261,389},{262,3... | collective-permute-start | bytes 368648 | tf_op jit(solution)/shard_map/ppermute | solution.py:411
  86.8 35.1 %all-to-all-start.2 = ((bf16[32,56,128]{2,1,0:T(8,128)(2,1)}), bf16[32,56,128]{2,1,0:T(8,128)(2,1)S(1)}, u32[]{:S(2)}, u32[]{:S(2)}) async-start(bf16[32,56,128]{2,1,0:T(8,128)(2,1)} %shard_map.178), calls=%async_computation.2 | async-start | bytes 917504 | tf_op jit(solution)/shard_map/all_to_all | solution.py:401
  91.1 3.3 %collective-permute-start.6 = (bf16[4,192,128]{2,1,0:T(8,128)(2,1)S(1)}, bf16[4,192,128]{2,1,0:T(8,128)(2,1)S(1)}, u32[]{:S(2)}, u32[]{:S(2)}) collective-permute-start(bf16[4,192,128]{2,1,0:T(8,128)(2,1)S(1)} %dynamic-slice_bitcast_fusion), channel_id=1, source_target_pairs={{0,4},{4,0},{1,5},{5,1},{2,6},{6,2},{3,7},{7,3},{8,12},{12,8},{9,1... | collective-permute-start | bytes 589832 | tf_op jit(solution)/shard_map/ppermute | solution.py:417
  94.6 10.7 %collective-permute-start.7 = (bf16[192,128]{1,0:T(8,128)(2,1)S(1)}, bf16[192,128]{1,0:T(8,128)(2,1)S(1)}, u32[]{:S(2)}, u32[]{:S(2)}) collective-permute-start(bf16[192,128]{1,0:T(8,128)(2,1)S(1)} %get-tuple-element.52), channel_id=1, source_target_pairs={{0,1},{1,2},{2,3},{3,0},{4,5},{5,6},{6,7},{7,4},{8,9},{9,10},{10,1... | collective-permute-start | bytes 147464 | tf_op jit(solution)/shard_map/ppermute | solution.py:423
  97.8 7.6 %collective-permute-start.8 = (bf16[192,128]{1,0:T(8,128)(2,1)S(1)}, bf16[192,128]{1,0:T(8,128)(2,1)S(1)}, u32[]{:S(2)}, u32[]{:S(2)}) collective-permute-start(bf16[192,128]{1,0:T(8,128)(2,1)S(1)} %get-tuple-element.54), channel_id=1, source_target_pairs={{0,2},{1,3},{2,0},{3,1},{4,6},{5,7},{6,4},{7,5},{8,10},{9,11},{10,... | collective-permute-start | bytes 147464 | tf_op jit(solution)/shard_map/ppermute | solution.py:423
  102.3 5.1 %collective-permute-start.9 = (bf16[192,128]{1,0:T(8,128)(2,1)S(1)}, bf16[192,128]{1,0:T(8,128)(2,1)S(1)}, u32[]{:S(2)}, u32[]{:S(2)}) collective-permute-start(bf16[192,128]{1,0:T(8,128)(2,1)S(1)} %get-tuple-element.53), channel_id=1, source_target_pairs={{0,3},{1,0},{2,1},{3,2},{4,7},{5,4},{6,5},{7,6},{8,11},{9,8},{10,9... | collective-permute-start | bytes 147464 | tf_op jit(solution)/shard_map/ppermute | solution.py:423
  123.1 32.3 %all-to-all-start.3 = ((bf16[32,48,128]{2,1,0:T(8,128)(2,1)}), bf16[32,48,128]{2,1,0:T(8,128)(2,1)S(1)}, u32[]{:S(2)}, u32[]{:S(2)}) async-start(bf16[32,48,128]{2,1,0:T(8,128)(2,1)} %shard_map.179), calls=%async_computation.3 | async-start | bytes 786432 | tf_op jit(solution)/shard_map/all_to_all | solution.py:401
  127.5 6.5 %collective-permute-start.10 = (bf16[32,8,128]{2,1,0:T(8,128)(2,1)S(1)}, bf16[32,8,128]{2,1,0:T(8,128)(2,1)S(1)}, u32[]{:S(2)}, u32[]{:S(2)}) collective-permute-start(bf16[32,8,128]{2,1,0:T(8,128)(2,1)S(1)} %get-tuple-element.51), channel_id=1, source_target_pairs={{384,0},{385,1},{386,2},{387,3},{388,4},{389,5},{390,6},{391,7},{3... | collective-permute-start | bytes 196616 | tf_op jit(solution)/shard_map/ppermute | solution.py:557
  128.8 5.2 %collective-permute-start.11 = (bf16[32,8,128]{2,1,0:T(8,128)(2,1)S(1)}, bf16[32,8,128]{2,1,0:T(8,128)(2,1)S(1)}, u32[]{:S(2)}, u32[]{:S(2)}) collective-permute-start(bf16[32,8,128]{2,1,0:T(8,128)(2,1)S(1)} %get-tuple-element.50), channel_id=1, source_target_pairs={{384,128},{385,129},{386,130},{387,131},{388,132},{389,133},{390,1... | collective-permute-start | bytes 196616 | tf_op jit(solution)/shard_map/ppermute | solution.py:557
  129.5 4.5 %collective-permute-start.12 = (bf16[32,8,128]{2,1,0:T(8,128)(2,1)S(1)}, bf16[32,8,128]{2,1,0:T(8,128)(2,1)S(1)}, u32[]{:S(2)}, u32[]{:S(2)}) collective-permute-start(bf16[32,8,128]{2,1,0:T(8,128)(2,1)S(1)} %get-tuple-element.49), channel_id=1, source_target_pairs={{384,256},{385,257},{386,258},{387,259},{388,260},{389,261},{390,2... | collective-permute-start | bytes 196616 | tf_op jit(solution)/shard_map/ppermute | solution.py:557
  136.3 7.8 %collective-permute-start.13 = (bf16[4,240,128]{2,1,0:T(8,128)(2,1)S(1)}, bf16[4,240,128]{2,1,0:T(8,128)(2,1)S(1)}, u32[]{:S(2)}, u32[]{:S(2)}) collective-permute-start(bf16[4,240,128]{2,1,0:T(8,128)(2,1)S(1)} %shard_map.180), channel_id=1, source_target_pairs={{0,128},{128,256},{256,384},{1,129},{129,257},{257,385},{2,130},{1... | collective-permute-start | bytes 737288 | tf_op jit(solution)/shard_map/ppermute | solution.py:407
  156.1 15.4 %all-to-all-start.4 = ((bf16[16,24,128]{2,1,0:T(8,128)(2,1)}), bf16[16,24,128]{2,1,0:T(8,128)(2,1)S(1)}, u32[]{:S(2)}, u32[]{:S(2)}) async-start(bf16[16,24,128]{2,1,0:T(8,128)(2,1)} %shard_map.181), calls=%async_computation.4 | async-start | bytes 196608 | tf_op jit(solution)/shard_map/all_to_all | solution.py:401
  160.6 20.8 %collective-permute-start.15 = (bf16[4,240,128]{2,1,0:T(8,128)(2,1)S(1)}, bf16[4,240,128]{2,1,0:T(8,128)(2,1)S(1)}, u32[]{:S(2)}, u32[]{:S(2)}) collective-permute-start(bf16[4,240,128]{2,1,0:T(8,128)(2,1)S(1)} %shard_map.183), channel_id=1, source_target_pairs={{128,0},{256,128},{384,256},{129,1},{257,129},{385,257},{130,2},{2... | collective-permute-start | bytes 737288 | tf_op jit(solution)/shard_map/ppermute | solution.py:407
  172.3 13.8 %all-to-all-start.5 = ((bf16[8,128,128]{2,1,0:T(8,128)(2,1)}), bf16[8,128,128]{2,1,0:T(8,128)(2,1)S(1)}, u32[]{:S(2)}, u32[]{:S(2)}) async-start(bf16[8,128,128]{2,1,0:T(8,128)(2,1)} %shard_map.182), calls=%async_computation.5 | async-start | bytes 524288 | tf_op jit(solution)/shard_map/all_to_all | solution.py:401
  179.5 3.2 %collective-permute-start.14 = (bf16[16,24,128]{2,1,0:T(8,128)(2,1)S(1)}, bf16[16,24,128]{2,1,0:T(8,128)(2,1)S(1)}, u32[]{:S(2)}, u32[]{:S(2)}) collective-permute-start(bf16[16,24,128]{2,1,0:T(8,128)(2,1)S(1)} %all-to-all-done.4.pieces_ref), channel_id=1, source_target_pairs={{0,4},{4,0},{1,5},{5,1},{2,6},{6,2},{3,7},{7,3},{8,12},{12,8},{9,1... | collective-permute-start | bytes 294920 | tf_op jit(solution)/shard_map/ppermute | solution.py:586
  (6 other events, 13.7 us)

commit v10 on v9

--- a/solution.py
+++ b/solution.py
@@ -120,11 +120,14 @@
 
 
 def fresh_coeffs_kernel(x_ref, forward_ref, *rest):
-    *rest, work_ref = rest
-    count = len(rest) // 2 - 1
-    own_ref, lent_ref = rest[count : count + 2]
-    for source, target in zip(rest[:count], rest[count + 2 :]):
-        target[...] = source[...]
+    *sources, own_ref, lent_ref, packed_ref, work_ref = rest
+    row = 0
+    for source in sources:
+        rows, columns = source.shape
+        for start in range(0, columns, CH):
+            width = min(CH, columns - start)
+            packed_ref[row : row + rows, :width] = source[:, start : start + width]
+            row += rows
     for j in range(ROWS):
         coeffs = matmul(forward_ref[...], x_ref[j])
         for place in range(8):
@@ -234,6 +237,26 @@
     out_ref[:, 32:, :] = sums.astype(BF16)
 
 
+PLACES = {}
+for _name, _rows, _columns in (
+    ("contract", HID, CH),
+    ("expand", CH, HID),
+    ("inverse", NLON, 256),
+    ("fresh_inverse", NLON, 256),
+    ("inverse_t", 256, NLON),
+):
+    PLACES[_name] = (sum(r * -(-c // CH) for _, r, c in PLACES.values()), _rows, _columns)
+PACKED_ROWS = sum(r * -(-c // CH) for _, r, c in PLACES.values())
+
+
+def unpacked(packed_ref, name):
+    row, rows, columns = PLACES[name]
+    blocks = [
+        packed_ref[row + n * rows : row + (n + 1) * rows, :] for n in range(-(-columns // CH))
+    ]
+    return jnp.concatenate(blocks, axis=1)[:, :columns] if len(blocks) > 1 else blocks[0]
+
+
 def live(cycle_ref, j):
     return jnp.where(cycle_ref[j] < NLAT, 1.0, 0.0).astype(F32)
 
@@ -244,13 +267,13 @@
     lent_a_ref,
     lent_b_ref,
     lent_c_ref,
-    inverse_ref,
-    expand_ref,
-    reduce_ref,
+    packed_ref,
     cycle_ref,
     out_ref,
     work_ref,
 ):
+    names = ("fresh_inverse", "expand", "contract")
+    inverse, expand, contract = [unpacked(packed_ref, name) for name in names]
     own = values_ref[:, 32:, :].astype(F32)
     lent = [ref[...].astype(F32) for ref in (lent_a_ref, lent_b_ref, lent_c_ref)]
     for u in range(3):
@@ -262,10 +285,10 @@
             for place in range(8)
         ]
         values = jnp.concatenate(parts, axis=0).astype(BF16)
-        mixed = x_ref[j].astype(F32) + matmul(inverse_ref[...], values)
-        pre = matmul(mixed.astype(BF16), expand_ref[...])
+        mixed = x_ref[j].astype(F32) + matmul(inverse, values)
+        pre = matmul(mixed.astype(BF16), expand)
         hidden = (0.5 * pre * (1.0 + lax.erf(pre * ROOT_HALF))).astype(BF16)
-        result = mixed + matmul(hidden, reduce_ref[...])
+        result = mixed + matmul(hidden, contract)
         out_ref[j] = (result * live(cycle_ref, j)).astype(BF16)
 
 
@@ -273,10 +296,7 @@
     x_ref,
     values_ref,
     cotangent_ref,
-    inverse_ref,
-    inverse_t_ref,
-    expand_ref,
-    reduce_ref,
+    packed_ref,
     cycle_ref,
     out_ref,
     grad_mixed_ref,
@@ -286,28 +306,30 @@
     hidden_ref,
     grad_pre_ref,
 ):
+    names = ("inverse", "inverse_t", "expand", "contract")
+    inverse, inverse_t, expand, contract = [unpacked(packed_ref, name) for name in names]
     for half in range(2):
         values = from_blocks(values_ref, half)
         grad_values = []
         for h in range(2):
             j = 2 * half + h
             rows = slice(j * NLON, (j + 1) * NLON)
-            mixed = x_ref[j].astype(F32) + matmul(inverse_ref[...], values[h])
+            mixed = x_ref[j].astype(F32) + matmul(inverse, values[h])
             mixed_b = mixed.astype(BF16)
             masked_f = cotangent_ref[j].astype(F32) * live(cycle_ref, j)
             masked = masked_f.astype(BF16)
             mixed_ref[rows, :] = mixed_b
             masked_ref[rows, :] = masked
-            pre = matmul(mixed_b, expand_ref[...])
+            pre = matmul(mixed_b, expand)
             normal = 0.5 * (1.0 + lax.erf(pre * ROOT_HALF))
             hidden_ref[rows, :] = (pre * normal).astype(BF16)
             slope = normal + pre * jnp.exp(-0.5 * pre * pre) * INV_ROOT_TAU
-            grad_hidden = matmul(masked, reduce_ref[...], ((1,), (1,)))
+            grad_hidden = matmul(masked, contract, ((1,), (1,)))
             grad_pre = (grad_hidden * slope).astype(BF16)
             grad_pre_ref[rows, :] = grad_pre
-            grad_mixed = masked_f + matmul(grad_pre, expand_ref[...], ((1,), (1,)))
+            grad_mixed = masked_f + matmul(grad_pre, expand, ((1,), (1,)))
             grad_mixed_ref[j] = grad_mixed
-            grad_values.append(matmul(inverse_t_ref[...], grad_mixed.astype(BF16)))
+            grad_values.append(matmul(inverse_t, grad_mixed.astype(BF16)))
         to_blocks(out_ref, half, grad_values)
     quarter = HID // 4
     pairs = ((grad_pre_ref, mixed_ref), (hidden_ref, masked_ref))
@@ -481,10 +503,10 @@
         limit=60 * 1024 * 1024,
     )[0]
     saved_at_orders = exchange(saved_blocks, SP)
-    kept = [inverse, inverse_t, expand, contract]
-    fresh_own, fresh_lent, inverse, inverse_t, expand, contract = call(
+    kept = [contract, expand, inverse, fresh_inverse, inverse_t]
+    fresh_own, fresh_lent, packed = call(
         fresh_coeffs_kernel,
-        [OWN, LENT] + [jax.ShapeDtypeStruct(k.shape, BF16) for k in kept],
+        [OWN, LENT, jax.ShapeDtypeStruct((PACKED_ROWS, CH), BF16)],
         [fresh, fresh_forward_t, *kept],
         [pltpu.VMEM((LANES * 8, CH), F32)],
         flops=dft,
@@ -528,11 +550,11 @@
             jax.ShapeDtypeStruct((ROWS, NLON, CH), F32),
             jax.ShapeDtypeStruct((2, 4, HID // 4, CH), BF16),
         ],
-        [saved, values_fresh, cotangent, inverse, inverse_t, expand, contract, own_cycles],
+        [saved, values_fresh, cotangent, packed, own_cycles],
         [narrow, narrow, wide, wide],
         flops=5 * mlp + 2 * dft,
         transcendentals=2 * ROWS * NLON * HID,
-        smem=(7,),
+        smem=(4,),
     )
     grads_fresh = call(
         fresh_spectral_kernel,
@@ -559,11 +581,11 @@
     block = call(
         mlp_kernel,
         [TOKENS],
-        [fresh, grads_fresh, *lent_values, fresh_inverse, expand, contract, own_cycles],
+        [fresh, grads_fresh, *lent_values, packed, own_cycles],
         [pltpu.VMEM((LANES * 8, CH), F32)],
         flops=2 * mlp + dft,
         transcendentals=ROWS * NLON * HID,
-        smem=(8,),
+        smem=(6,),
     )[0]
     next_input = from_behind(block, "pipe", 1)
     coeffs_summed = call(
@@ -574,7 +596,7 @@
         flops=leg,
     )[0]
     coeffs_summed = exchange(coeffs_summed, SP)
-    coeffs_summed, next_input = lax.optimization_barrier((coeffs_summed, next_input))
+    coeffs_summed, _ = lax.optimization_barrier((coeffs_summed, block))
     pieces = call(
         piece_kernel, [jax.ShapeDtypeStruct((PEERS // 2, 24, CH), BF16)], [coeffs_summed]
     )[0]

time: 188 us -> 187 us (level)
    ppermute x2, waiting for transfers between devices: 3.73 us -> 0.01 us  [from_behind(): return lax.ppermute(block, axis, route)]
    ppermute x6, starting transfers between devices: 11.4 us -> 13.3 us  [to_last(): return [lax.ppermute(block, 'pipe', [(p, 3)]) for p in range(3)]]
  transfers between devices with their start and end apart: 22 -> 22, of which waited for: 11 -> 10; matrix products, arithmetic and copies ran while one was open for 1% -> 1% of each run, Pallas kernels for 5% -> 5%
where the time goes in v10:
time: 187 us; the launch traced here: 186 us
  waiting for transfers between devices  88.2 us (47%)
  starting transfers between devices  76.2 us (41%)
  Pallas kernels  17.5 us (9%)
  local copies, waits for them, and re-layouts  1.92 us (1%)
    all_to_all x6, waiting for transfers between devices, exchange(): return lax.all_to_all(blocks, axes, split_axis=0, concat_axis=0, tiled=True)  79.8 us
    all_to_all x6, starting transfers between devices, exchange(): return lax.all_to_all(blocks, axes, split_axis=0, concat_axis=0, tiled=True)  41 us
    pallas_call x12, Pallas kernels, call(): pl.pallas_call(kernel, out_shape=outs, in_specs=specs, out_specs=[pl.Bloc...  17.5 us
    ppermute x6, starting transfers between devices, to_last(): return [lax.ppermute(block, 'pipe', [(p, 3)]) for p in range(3)]  13.3 us
    ppermute x3, starting transfers between devices, around(): lax.ppermute(block, axis, [(i, (i + distance) % count) for i in range(cou...  10.7 us
    ppermute x2, starting transfers between devices, from_behind(): return lax.ppermute(block, axis, route)  4.41 us
    ppermute x3, waiting for transfers between devices, on_device(): lax.ppermute(grads_fresh[:, 32 + 8 * p:40 + 8 * p], 'pipe', [(3, p)])  3.88 us
  transfers between devices with their start and end apart: 22, of which 10 were waited for; matrix products, arithmetic and copies ran while one was open for 1% of the time, Pallas kernels for 5%

profile of v10, /device:TPU:1, one launch (start us, length us, event | category | flops | bytes accessed | tf_op | source)
XLA Modules:
  0.0 186.2 jit_solution(12146480848837307806)
XLA Ops:
  0.7 2.2 %shard_map.173 = bf16[32,32,128]{2,1,0:T(8,128)(2,1)} custom-call(bf16[4,240,128]{2,1,0:T(8,128)(2,1)} %bitcast.47, bf16[256,240]{1,0:T(8,128)(2,1)} %constant.107.clone.forward_hbm), custom_call_target="tpu_custom_call" | custom-call | flops 62914560 | bytes 630784 | tf_op jit(solution)/shard_map/pallas_call | solution.py:397
  2.9 16.9 %all-to-all-start = ((bf16[32,32,128]{2,1,0:T(8,128)(2,1)}), bf16[32,32,128]{2,1,0:T(8,128)(2,1)S(1)}, u32[]{:S(2)}, u32[]{:S(2)}) async-start(bf16[32,32,128]{2,1,0:T(8,128)(2,1)} %shard_map.173), calls=%async_computation | async-start | bytes 524288 | tf_op jit(solution)/shard_map/all_to_all | solution.py:423
  20.3 4.4 %collective-permute-start = (bf16[32,8,128]{2,1,0:T(8,128)(2,1)S(1)}, bf16[32,8,128]{2,1,0:T(8,128)(2,1)S(1)}, u32[]{:S(2)}, u32[]{:S(2)}) collective-permute-start(bf16[32,8,128]{2,1,0:T(8,128)(2,1)S(1)} %get-tuple-element.25), channel_id=1, source_target_pairs={{0,384},{1,385},{2,386},{3,387},{4,388},{5,389},{6,390},{7,391},{8... | collective-permute-start | bytes 196616 | tf_op jit(solution)/shard_map/ppermute | solution.py:433
  27.6 14.3 %all-to-all-done.arrived_ref = bf16[32,32,128]{2,1,0:T(8,128)(2,1)S(1)} async-done(((bf16[32,32,128]{2,1,0:T(8,128)(2,1)}), bf16[32,32,128]{2,1,0:T(8,128)(2,1)S(1)}, u32[]{:S(2)}, u32[]{:S(2)}) %all-to-all-start) | async-done | bytes 262176 | tf_op jit(solution)/shard_map/all_to_all | solution.py:423
  41.8 1.2 shard_map.176
  43.1 4.7 %all-to-all-start.1 = ((bf16[32,56,128]{2,1,0:T(8,128)(2,1)}), bf16[32,56,128]{2,1,0:T(8,128)(2,1)S(1)}, u32[]{:S(2)}, u32[]{:S(2)}) async-start(bf16[32,56,128]{2,1,0:T(8,128)(2,1)} %get-tuple-element.28), calls=%async_computation.1 | async-start | bytes 917504 | tf_op jit(solution)/shard_map/all_to_all | solution.py:423
  47.8 5.0 %collective-permute-start.3 = (f32[2,120,128]{2,1,0:T(8,128)S(1)}, f32[2,120,128]{2,1,0:T(8,128)}, u32[]{:S(2)}, u32[]{:S(2)}) collective-permute-start(f32[2,120,128]{2,1,0:T(8,128)S(1)} %bitcast.40), channel_id=1, source_target_pairs={{0,384},{1,385},{2,386},{3,387},{4,388},{5,389},{6,390},{7,391},{8... | collective-permute-start | bytes 368648 | tf_op jit(solution)/shard_map/ppermute | solution.py:433
  52.8 1.3 collective-permute-start.4
  54.1 1.3 collective-permute-start.5
  55.5 23.1 %all-to-all-done.1.values_ref.arrived_ref = bf16[32,56,128]{2,1,0:T(8,128)(2,1)S(1)} async-done(((bf16[32,56,128]{2,1,0:T(8,128)(2,1)}), bf16[32,56,128]{2,1,0:T(8,128)(2,1)S(1)}, u32[]{:S(2)}, u32[]{:S(2)}) %all-to-all-start.1) | async-done | bytes 458784 | tf_op jit(solution)/shard_map/all_to_all | solution.py:423
  79.5 4.2 %shard_map.177 = (bf16[32,32,128]{2,1,0:T(8,128)(2,1)S(1)}, f32[4,240,128]{2,1,0:T(8,128)S(1)}, bf16[2,4,192,128]{3,2,1,0:T(8,128)(2,1)S(1)}) custom-call(bf16[4,240,128]{2,1,0:T(8,128)(2,1)S(1)} %bitcast.48, bf16[32,56,128]{2,1,0:T(8,128)(2,1)S(1)} %all-to-all-done.1.values_ref.arrived_ref, bf16[4,240,128]{2,1,0:T(8,128)(2,1)S(1)} %bitcast.51, ...), custom_call_target="tpu_custom_call" | custom-call | flops 1069547520 | bytes 2867216 | tf_op jit(solution)/shard_map/pallas_call | solution.py:397
  83.8 2.2 %shard_map.178 = bf16[32,56,128]{2,1,0:T(8,128)(2,1)} custom-call(bf16[32,56,128]{2,1,0:T(8,128)(2,1)S(1)} %all-to-all-done.1.values_ref.arrived_ref, bf16[4,128,128]{2,1,0:T(8,128)(2,1)S(1)} %get-tuple-element.23.ana_ref, bf16[4,128,128]{2,1,0:T(8,128)(2,1)S(1)} %get-tuple-element.24.syn_ref, f32[2,120,128]{2,1,0:T(8,128)S(1)} %bitcast.43, ...), custom_call_target="tpu_custom_call" | custom-call | flops 67108864 | bytes 1933316 | tf_op jit(solution)/shard_map/pallas_call | solution.py:397
  86.0 4.3 %all-to-all-start.2 = ((bf16[32,56,128]{2,1,0:T(8,128)(2,1)}), bf16[32,56,128]{2,1,0:T(8,128)(2,1)S(1)}, u32[]{:S(2)}, u32[]{:S(2)}) async-start(bf16[32,56,128]{2,1,0:T(8,128)(2,1)} %shard_map.178), calls=%async_computation.2 | async-start | bytes 917504 | tf_op jit(solution)/shard_map/all_to_all | solution.py:423
  90.3 2.3 %collective-permute-start.6 = (bf16[4,192,128]{2,1,0:T(8,128)(2,1)S(1)}, bf16[4,192,128]{2,1,0:T(8,128)(2,1)}, u32[]{:S(2)}, u32[]{:S(2)}) collective-permute-start(bf16[4,192,128]{2,1,0:T(8,128)(2,1)S(1)} %dynamic-slice_bitcast_fusion), channel_id=1, source_target_pairs={{0,4},{4,0},{1,5},{5,1},{2,6},{6,2},{3,7},{7,3},{8,12},{12,8},{9,1... | collective-permute-start | bytes 589832 | tf_op jit(solution)/shard_map/ppermute | solution.py:439
  94.8 3.2 %collective-permute-start.7 = (bf16[192,128]{1,0:T(8,128)(2,1)S(1)}, bf16[192,128]{1,0:T(8,128)(2,1)S(1)}, u32[]{:S(2)}, u32[]{:S(2)}) collective-permute-start(bf16[192,128]{1,0:T(8,128)(2,1)S(1)} %get-tuple-element.44), channel_id=1, source_target_pairs={{0,1},{1,2},{2,3},{3,0},{4,5},{5,6},{6,7},{7,4},{8,9},{9,10},{10,1... | collective-permute-start | bytes 147464 | tf_op jit(solution)/shard_map/ppermute | solution.py:445
  98.0 4.5 %collective-permute-start.8 = (bf16[192,128]{1,0:T(8,128)(2,1)S(1)}, bf16[192,128]{1,0:T(8,128)(2,1)S(1)}, u32[]{:S(2)}, u32[]{:S(2)}) collective-permute-start(bf16[192,128]{1,0:T(8,128)(2,1)S(1)} %get-tuple-element.46), channel_id=1, source_target_pairs={{0,2},{1,3},{2,0},{3,1},{4,6},{5,7},{6,4},{7,5},{8,10},{9,11},{10,... | collective-permute-start | bytes 147464 | tf_op jit(solution)/shard_map/ppermute | solution.py:445
  102.6 3.0 %collective-permute-start.9 = (bf16[192,128]{1,0:T(8,128)(2,1)S(1)}, bf16[192,128]{1,0:T(8,128)(2,1)S(1)}, u32[]{:S(2)}, u32[]{:S(2)}) collective-permute-start(bf16[192,128]{1,0:T(8,128)(2,1)S(1)} %get-tuple-element.45), channel_id=1, source_target_pairs={{0,3},{1,0},{2,1},{3,2},{4,7},{5,4},{6,5},{7,6},{8,11},{9,8},{10,9... | collective-permute-start | bytes 147464 | tf_op jit(solution)/shard_map/ppermute | solution.py:445
  105.6 2.1 %collective-permute-done.9 = bf16[192,128]{1,0:T(8,128)(2,1)S(1)} collective-permute-done((bf16[192,128]{1,0:T(8,128)(2,1)S(1)}, bf16[192,128]{1,0:T(8,128)(2,1)S(1)}, u32[]{:S(2)}, u32[]{:S(2)}) %collective-permute-start.9) | collective-permute-done | bytes 49184 | tf_op jit(solution)/shard_map/ppermute | solution.py:445
  107.8 13.3 %all-to-all-done.2.arrived_ref.values_ref = bf16[32,56,128]{2,1,0:T(8,128)(2,1)S(1)} async-done(((bf16[32,56,128]{2,1,0:T(8,128)(2,1)}), bf16[32,56,128]{2,1,0:T(8,128)(2,1)S(1)}, u32[]{:S(2)}, u32[]{:S(2)}) %all-to-all-start.2) | async-done | bytes 458784 | tf_op jit(solution)/shard_map/all_to_all | solution.py:423
  121.1 1.2 shard_map.179
  122.3 4.3 %all-to-all-start.3 = ((bf16[32,48,128]{2,1,0:T(8,128)(2,1)}), bf16[32,48,128]{2,1,0:T(8,128)(2,1)S(1)}, u32[]{:S(2)}, u32[]{:S(2)}) async-start(bf16[32,48,128]{2,1,0:T(8,128)(2,1)} %shard_map.179), calls=%async_computation.3 | async-start | bytes 786432 | tf_op jit(solution)/shard_map/all_to_all | solution.py:423
  126.7 1.3 collective-permute-start.10
  129.3 3.9 %collective-permute-done.10.lent_a_ref = bf16[32,8,128]{2,1,0:T(8,128)(2,1)S(1)} collective-permute-done((bf16[32,8,128]{2,1,0:T(8,128)(2,1)S(1)}, bf16[32,8,128]{2,1,0:T(8,128)(2,1)S(1)}, u32[]{:S(2)}, u32[]{:S(2)}) %collective-permute-start.10) | collective-permute-done | bytes 65568 | tf_op jit(solution)/shard_map/ppermute | solution.py:579
  133.2 2.2 %shard_map.180 = bf16[4,240,128]{2,1,0:T(8,128)(2,1)S(1)} custom-call(bf16[4,240,128]{2,1,0:T(8,128)(2,1)S(1)} %bitcast.46, bf16[32,56,128]{2,1,0:T(8,128)(2,1)S(1)} %all-to-all-done.2.arrived_ref.values_ref, bf16[32,8,128]{2,1,0:T(8,128)(2,1)S(1)} %collective-permute-done.10.lent_a_ref, bf16[32,8,128]{2,1,0:T(8,128)(2,1)S(1)} %collective-permute-done.11.lent_b_ref, ...), custom_call_target="tpu_custom_call" | custom-call | flops 440401920 | bytes 1916944 | tf_op jit(solution)/shard_map/pallas_call | solution.py:397
  135.4 19.2 %all-to-all-done.3.arrived_ref.coeffs_ref = bf16[32,48,128]{2,1,0:T(8,128)(2,1)S(1)} async-done(((bf16[32,48,128]{2,1,0:T(8,128)(2,1)}), bf16[32,48,128]{2,1,0:T(8,128)(2,1)S(1)}, u32[]{:S(2)}, u32[]{:S(2)}) %all-to-all-start.3) | async-done | bytes 393248 | tf_op jit(solution)/shard_map/all_to_all | solution.py:423
  155.3 3.6 %all-to-all-start.4 = ((bf16[16,24,128]{2,1,0:T(8,128)(2,1)}), bf16[16,24,128]{2,1,0:T(8,128)(2,1)S(1)}, u32[]{:S(2)}, u32[]{:S(2)}) async-start(bf16[16,24,128]{2,1,0:T(8,128)(2,1)} %shard_map.181), calls=%async_computation.4 | async-start | bytes 196608 | tf_op jit(solution)/shard_map/all_to_all | solution.py:423
  159.0 3.1 %collective-permute-start.14 = (bf16[4,240,128]{2,1,0:T(8,128)(2,1)S(1)}, bf16[4,240,128]{2,1,0:T(8,128)(2,1)S(1)}, u32[]{:S(2)}, u32[]{:S(2)}) collective-permute-start(bf16[4,240,128]{2,1,0:T(8,128)(2,1)S(1)} %shard_map.180), channel_id=1, source_target_pairs={{0,128},{128,256},{256,384},{1,129},{129,257},{257,385},{2,130},{1... | collective-permute-start | bytes 737288 | tf_op jit(solution)/shard_map/ppermute | solution.py:429
  162.9 1.3 collective-permute-start.15
  164.2 6.5 %all-to-all-done.4.pieces_ref = bf16[16,24,128]{2,1,0:T(8,128)(2,1)S(1)} async-done(((bf16[16,24,128]{2,1,0:T(8,128)(2,1)}), bf16[16,24,128]{2,1,0:T(8,128)(2,1)S(1)}, u32[]{:S(2)}, u32[]{:S(2)}) %all-to-all-start.4) | async-done | bytes 98336 | tf_op jit(solution)/shard_map/all_to_all | solution.py:423
  171.5 7.2 %all-to-all-start.5 = ((bf16[8,128,128]{2,1,0:T(8,128)(2,1)}), bf16[8,128,128]{2,1,0:T(8,128)(2,1)S(1)}, u32[]{:S(2)}, u32[]{:S(2)}) async-start(bf16[8,128,128]{2,1,0:T(8,128)(2,1)} %shard_map.182), calls=%async_computation.5 | async-start | bytes 524288 | tf_op jit(solution)/shard_map/all_to_all | solution.py:423
  178.7 1.9 %collective-permute-start.13 = (bf16[16,24,128]{2,1,0:T(8,128)(2,1)S(1)}, bf16[16,24,128]{2,1,0:T(8,128)(2,1)S(1)}, u32[]{:S(2)}, u32[]{:S(2)}) collective-permute-start(bf16[16,24,128]{2,1,0:T(8,128)(2,1)S(1)} %all-to-all-done.4.pieces_ref), channel_id=1, source_target_pairs={{0,4},{4,0},{1,5},{5,1},{2,6},{6,2},{3,7},{7,3},{8,12},{12,8},{9,1... | collective-permute-start | bytes 294920 | tf_op jit(solution)/shard_map/ppermute | solution.py:608
  181.9 3.4 %all-to-all-done.5.filter_rows_ref = bf16[8,128,128]{2,1,0:T(8,128)(2,1)S(1)} async-done(((bf16[8,128,128]{2,1,0:T(8,128)(2,1)}), bf16[8,128,128]{2,1,0:T(8,128)(2,1)S(1)}, u32[]{:S(2)}, u32[]{:S(2)}) %all-to-all-start.5) | async-done | bytes 262176 | tf_op jit(solution)/shard_map/all_to_all | solution.py:423
  (61 shorter events, 12.3 us)
Async XLA Ops:
  0.6 19.2 %copy-start.4 = (bf16[1,128,768]{2,1,0:T(8,128)(2,1)S(1)}, bf16[1,128,768]{2,1,0:T(8,128)(2,1)}, u32[]{:S(2)}) copy-start(bf16[1,128,768]{2,1,0:T(8,128)(2,1)} %param.17) | copy-start | bytes 589828
  0.6 19.2 %copy-start.5 = (bf16[256,240]{1,0:T(8,128)(2,1)S(1)}, bf16[256,240]{1,0:T(8,128)(2,1)}, u32[]{:S(2)}) copy-start(bf16[256,240]{1,0:T(8,128)(2,1)} %constant.105.clone.forward_ref) | copy-start | bytes 368644
  0.7 19.2 %copy-start.6 = (bf16[256,240]{1,0:T(8,128)(2,1)S(1)}, bf16[256,240]{1,0:T(8,128)(2,1)}, u32[]{:S(2)}) copy-start(bf16[256,240]{1,0:T(8,128)(2,1)} %constant.109.clone.rest_4_) | copy-start | bytes 368644
  0.7 19.2 %copy-start.8 = (bf16[240,256]{1,0:T(8,128)(2,1)S(1)}, bf16[240,256]{1,0:T(8,128)(2,1)}, u32[]{:S(2)}) copy-start(bf16[240,256]{1,0:T(8,128)(2,1)} %constant.106.clone.rest_3_) | copy-start | bytes 368644
  0.7 19.2 %copy-start.9 = (bf16[240,256]{1,0:T(8,128)(2,1)S(1)}, bf16[240,256]{1,0:T(8,128)(2,1)}, u32[]{:S(2)}) copy-start(bf16[240,256]{1,0:T(8,128)(2,1)} %constant.108.clone.rest_2_) | copy-start | bytes 368644
  2.9 17.0 %copy-start.1 = (bf16[1,1,4,240,128]{4,3,2,1,0:T(8,128)(2,1)S(1)}, bf16[1,1,4,240,128]{4,3,2,1,0:T(8,128)(2,1)}, u32[]{:S(2)}) copy-start(bf16[1,1,4,240,128]{4,3,2,1,0:T(8,128)(2,1)} %param.14) | copy-start | bytes 737284
  2.9 17.0 %copy-start.3 = (bf16[1,768,128]{2,1,0:T(8,128)(2,1)S(1)}, bf16[1,768,128]{2,1,0:T(8,128)(2,1)}, u32[]{:S(2)}) copy-start(bf16[1,768,128]{2,1,0:T(8,128)(2,1)} %param.18) | copy-start | bytes 589828
  2.9 38.9 %all-to-all-start = ((bf16[32,32,128]{2,1,0:T(8,128)(2,1)}), bf16[32,32,128]{2,1,0:T(8,128)(2,1)S(1)}, u32[]{:S(2)}, u32[]{:S(2)}) async-start(bf16[32,32,128]{2,1,0:T(8,128)(2,1)} %shard_map.173), calls=%async_computation | async-start | bytes 524288 | tf_op jit(solution)/shard_map/all_to_all | solution.py:423
  20.3 7.1 %collective-permute-start = (bf16[32,8,128]{2,1,0:T(8,128)(2,1)S(1)}, bf16[32,8,128]{2,1,0:T(8,128)(2,1)S(1)}, u32[]{:S(2)}, u32[]{:S(2)}) collective-permute-start(bf16[32,8,128]{2,1,0:T(8,128)(2,1)S(1)} %get-tuple-element.25), channel_id=1, source_target_pairs={{0,384},{1,385},{2,386},{3,387},{4,388},{5,389},{6,390},{7,391},{8... | collective-permute-start | bytes 196616 | tf_op jit(solution)/shard_map/ppermute | solution.py:433
  24.7 2.7 %collective-permute-start.1 = (bf16[32,8,128]{2,1,0:T(8,128)(2,1)S(1)}, bf16[32,8,128]{2,1,0:T(8,128)(2,1)S(1)}, u32[]{:S(2)}, u32[]{:S(2)}) collective-permute-start(bf16[32,8,128]{2,1,0:T(8,128)(2,1)S(1)} %get-tuple-element.25), channel_id=1, source_target_pairs={{128,384},{129,385},{130,386},{131,387},{132,388},{133,389},{134,3... | collective-permute-start | bytes 196616 | tf_op jit(solution)/shard_map/ppermute | solution.py:433
  25.4 2.1 %collective-permute-start.2 = (bf16[32,8,128]{2,1,0:T(8,128)(2,1)S(1)}, bf16[32,8,128]{2,1,0:T(8,128)(2,1)S(1)}, u32[]{:S(2)}, u32[]{:S(2)}) collective-permute-start(bf16[32,8,128]{2,1,0:T(8,128)(2,1)S(1)} %get-tuple-element.25), channel_id=1, source_target_pairs={{256,384},{257,385},{258,386},{259,387},{260,388},{261,389},{262,3... | collective-permute-start | bytes 196616 | tf_op jit(solution)/shard_map/ppermute | solution.py:433
  27.5 14.4 %copy-start = (f32[1,2,120,128]{3,2,1,0:T(8,128)S(1)}, f32[1,2,120,128]{3,2,1,0:T(8,128)}, u32[]{:S(2)}) copy-start(f32[1,2,120,128]{3,2,1,0:T(8,128)} %param.19) | copy-start | bytes 368644
  43.1 35.5 %copy-start.2 = (bf16[1,1,4,240,128]{4,3,2,1,0:T(8,128)(2,1)S(1)}, bf16[1,1,4,240,128]{4,3,2,1,0:T(8,128)(2,1)}, u32[]{:S(2)}) copy-start(bf16[1,1,4,240,128]{4,3,2,1,0:T(8,128)(2,1)} %param.15) | copy-start | bytes 737284
  43.1 35.5 %all-to-all-start.1 = ((bf16[32,56,128]{2,1,0:T(8,128)(2,1)}), bf16[32,56,128]{2,1,0:T(8,128)(2,1)S(1)}, u32[]{:S(2)}, u32[]{:S(2)}) async-start(bf16[32,56,128]{2,1,0:T(8,128)(2,1)} %get-tuple-element.28), calls=%async_computation.1 | async-start | bytes 917504 | tf_op jit(solution)/shard_map/all_to_all | solution.py:423
  47.8 36.0 %collective-permute-start.3 = (f32[2,120,128]{2,1,0:T(8,128)S(1)}, f32[2,120,128]{2,1,0:T(8,128)}, u32[]{:S(2)}, u32[]{:S(2)}) collective-permute-start(f32[2,120,128]{2,1,0:T(8,128)S(1)} %bitcast.40), channel_id=1, source_target_pairs={{0,384},{1,385},{2,386},{3,387},{4,388},{5,389},{6,390},{7,391},{8... | collective-permute-start | bytes 368648 | tf_op jit(solution)/shard_map/ppermute | solution.py:433
  52.8 30.9 %collective-permute-start.4 = (f32[2,120,128]{2,1,0:T(8,128)S(1)}, f32[2,120,128]{2,1,0:T(8,128)}, u32[]{:S(2)}, u32[]{:S(2)}) collective-permute-start(f32[2,120,128]{2,1,0:T(8,128)S(1)} %bitcast.41), channel_id=1, source_target_pairs={{128,384},{129,385},{130,386},{131,387},{132,388},{133,389},{134,3... | collective-permute-start | bytes 368648 | tf_op jit(solution)/shard_map/ppermute | solution.py:433
  54.1 29.7 %collective-permute-start.5 = (f32[2,120,128]{2,1,0:T(8,128)S(1)}, f32[2,120,128]{2,1,0:T(8,128)}, u32[]{:S(2)}, u32[]{:S(2)}) collective-permute-start(f32[2,120,128]{2,1,0:T(8,128)S(1)} %bitcast.42), channel_id=1, source_target_pairs={{256,384},{257,385},{258,386},{259,387},{260,388},{261,389},{262,3... | collective-permute-start | bytes 368648 | tf_op jit(solution)/shard_map/ppermute | solution.py:433
  86.0 35.1 %all-to-all-start.2 = ((bf16[32,56,128]{2,1,0:T(8,128)(2,1)}), bf16[32,56,128]{2,1,0:T(8,128)(2,1)S(1)}, u32[]{:S(2)}, u32[]{:S(2)}) async-start(bf16[32,56,128]{2,1,0:T(8,128)(2,1)} %shard_map.178), calls=%async_computation.2 | async-start | bytes 917504 | tf_op jit(solution)/shard_map/all_to_all | solution.py:423
  90.3 3.5 %collective-permute-start.6 = (bf16[4,192,128]{2,1,0:T(8,128)(2,1)S(1)}, bf16[4,192,128]{2,1,0:T(8,128)(2,1)}, u32[]{:S(2)}, u32[]{:S(2)}) collective-permute-start(bf16[4,192,128]{2,1,0:T(8,128)(2,1)S(1)} %dynamic-slice_bitcast_fusion), channel_id=1, source_target_pairs={{0,4},{4,0},{1,5},{5,1},{2,6},{6,2},{3,7},{7,3},{8,12},{12,8},{9,1... | collective-permute-start | bytes 589832 | tf_op jit(solution)/shard_map/ppermute | solution.py:439
  94.8 10.7 %collective-permute-start.7 = (bf16[192,128]{1,0:T(8,128)(2,1)S(1)}, bf16[192,128]{1,0:T(8,128)(2,1)S(1)}, u32[]{:S(2)}, u32[]{:S(2)}) collective-permute-start(bf16[192,128]{1,0:T(8,128)(2,1)S(1)} %get-tuple-element.44), channel_id=1, source_target_pairs={{0,1},{1,2},{2,3},{3,0},{4,5},{5,6},{6,7},{7,4},{8,9},{9,10},{10,1... | collective-permute-start | bytes 147464 | tf_op jit(solution)/shard_map/ppermute | solution.py:445
  98.0 7.6 %collective-permute-start.8 = (bf16[192,128]{1,0:T(8,128)(2,1)S(1)}, bf16[192,128]{1,0:T(8,128)(2,1)S(1)}, u32[]{:S(2)}, u32[]{:S(2)}) collective-permute-start(bf16[192,128]{1,0:T(8,128)(2,1)S(1)} %get-tuple-element.46), channel_id=1, source_target_pairs={{0,2},{1,3},{2,0},{3,1},{4,6},{5,7},{6,4},{7,5},{8,10},{9,11},{10,... | collective-permute-start | bytes 147464 | tf_op jit(solution)/shard_map/ppermute | solution.py:445
  102.6 5.1 %collective-permute-start.9 = (bf16[192,128]{1,0:T(8,128)(2,1)S(1)}, bf16[192,128]{1,0:T(8,128)(2,1)S(1)}, u32[]{:S(2)}, u32[]{:S(2)}) collective-permute-start(bf16[192,128]{1,0:T(8,128)(2,1)S(1)} %get-tuple-element.45), channel_id=1, source_target_pairs={{0,3},{1,0},{2,1},{3,2},{4,7},{5,4},{6,5},{7,6},{8,11},{9,8},{10,9... | collective-permute-start | bytes 147464 | tf_op jit(solution)/shard_map/ppermute | solution.py:445
  122.3 32.3 %all-to-all-start.3 = ((bf16[32,48,128]{2,1,0:T(8,128)(2,1)}), bf16[32,48,128]{2,1,0:T(8,128)(2,1)S(1)}, u32[]{:S(2)}, u32[]{:S(2)}) async-start(bf16[32,48,128]{2,1,0:T(8,128)(2,1)} %shard_map.179), calls=%async_computation.3 | async-start | bytes 786432 | tf_op jit(solution)/shard_map/all_to_all | solution.py:423
  126.7 6.5 %collective-permute-start.10 = (bf16[32,8,128]{2,1,0:T(8,128)(2,1)S(1)}, bf16[32,8,128]{2,1,0:T(8,128)(2,1)S(1)}, u32[]{:S(2)}, u32[]{:S(2)}) collective-permute-start(bf16[32,8,128]{2,1,0:T(8,128)(2,1)S(1)} %get-tuple-element.43), channel_id=1, source_target_pairs={{384,0},{385,1},{386,2},{387,3},{388,4},{389,5},{390,6},{391,7},{3... | collective-permute-start | bytes 196616 | tf_op jit(solution)/shard_map/ppermute | solution.py:579
  128.0 5.2 %collective-permute-start.11 = (bf16[32,8,128]{2,1,0:T(8,128)(2,1)S(1)}, bf16[32,8,128]{2,1,0:T(8,128)(2,1)S(1)}, u32[]{:S(2)}, u32[]{:S(2)}) collective-permute-start(bf16[32,8,128]{2,1,0:T(8,128)(2,1)S(1)} %get-tuple-element.42), channel_id=1, source_target_pairs={{384,128},{385,129},{386,130},{387,131},{388,132},{389,133},{390,1... | collective-permute-start | bytes 196616 | tf_op jit(solution)/shard_map/ppermute | solution.py:579
  128.6 4.5 %collective-permute-start.12 = (bf16[32,8,128]{2,1,0:T(8,128)(2,1)S(1)}, bf16[32,8,128]{2,1,0:T(8,128)(2,1)S(1)}, u32[]{:S(2)}, u32[]{:S(2)}) collective-permute-start(bf16[32,8,128]{2,1,0:T(8,128)(2,1)S(1)} %get-tuple-element.41), channel_id=1, source_target_pairs={{384,256},{385,257},{386,258},{387,259},{388,260},{389,261},{390,2... | collective-permute-start | bytes 196616 | tf_op jit(solution)/shard_map/ppermute | solution.py:579
  155.3 6.8 %copy-start.7 = (bf16[240,256]{1,0:T(8,128)(2,1)S(1)}, bf16[240,256]{1,0:T(8,128)(2,1)}, u32[]{:S(2)}) copy-start(bf16[240,256]{1,0:T(8,128)(2,1)} %constant.104.clone.forward_ref) | copy-start | bytes 368644
  155.3 15.4 %all-to-all-start.4 = ((bf16[16,24,128]{2,1,0:T(8,128)(2,1)}), bf16[16,24,128]{2,1,0:T(8,128)(2,1)S(1)}, u32[]{:S(2)}, u32[]{:S(2)}) async-start(bf16[16,24,128]{2,1,0:T(8,128)(2,1)} %shard_map.181), calls=%async_computation.4 | async-start | bytes 196608 | tf_op jit(solution)/shard_map/all_to_all | solution.py:423
  159.0 21.7 %collective-permute-start.14 = (bf16[4,240,128]{2,1,0:T(8,128)(2,1)S(1)}, bf16[4,240,128]{2,1,0:T(8,128)(2,1)S(1)}, u32[]{:S(2)}, u32[]{:S(2)}) collective-permute-start(bf16[4,240,128]{2,1,0:T(8,128)(2,1)S(1)} %shard_map.180), channel_id=1, source_target_pairs={{0,128},{128,256},{256,384},{1,129},{129,257},{257,385},{2,130},{1... | collective-permute-start | bytes 737288 | tf_op jit(solution)/shard_map/ppermute | solution.py:429
  162.9 17.7 %collective-permute-start.15 = (bf16[4,240,128]{2,1,0:T(8,128)(2,1)S(1)}, bf16[4,240,128]{2,1,0:T(8,128)(2,1)S(1)}, u32[]{:S(2)}, u32[]{:S(2)}) collective-permute-start(bf16[4,240,128]{2,1,0:T(8,128)(2,1)S(1)} %shard_map.183), channel_id=1, source_target_pairs={{128,0},{256,128},{384,256},{129,1},{257,129},{385,257},{130,2},{2... | collective-permute-start | bytes 737288 | tf_op jit(solution)/shard_map/ppermute | solution.py:429
  171.5 13.8 %all-to-all-start.5 = ((bf16[8,128,128]{2,1,0:T(8,128)(2,1)}), bf16[8,128,128]{2,1,0:T(8,128)(2,1)S(1)}, u32[]{:S(2)}, u32[]{:S(2)}) async-start(bf16[8,128,128]{2,1,0:T(8,128)(2,1)} %shard_map.182), calls=%async_computation.5 | async-start | bytes 524288 | tf_op jit(solution)/shard_map/all_to_all | solution.py:423
  178.7 3.2 %collective-permute-start.13 = (bf16[16,24,128]{2,1,0:T(8,128)(2,1)S(1)}, bf16[16,24,128]{2,1,0:T(8,128)(2,1)S(1)}, u32[]{:S(2)}, u32[]{:S(2)}) collective-permute-start(bf16[16,24,128]{2,1,0:T(8,128)(2,1)S(1)} %all-to-all-done.4.pieces_ref), channel_id=1, source_target_pairs={{0,4},{4,0},{1,5},{5,1},{2,6},{6,2},{3,7},{7,3},{8,12},{12,8},{9,1... | collective-permute-start | bytes 294920 | tf_op jit(solution)/shard_map/ppermute | solution.py:608
  (2 other events, 1.7 us)

commit v11 on v10

--- a/solution.py
+++ b/solution.py
@@ -170,28 +170,12 @@
     out_ref[:, :32, :] = goes_ref[...].reshape(PEERS, 32, CH).astype(BF16)
 
 
-def fresh_spectral_kernel(
-    arrived_ref,
-    ana_ref,
-    syn_ref,
-    filt_ref,
-    lent_a_ref,
-    lent_b_ref,
-    lent_c_ref,
-    last_ref,
-    beside_ref,
-    out_ref,
-    came_ref,
-    goes_ref,
-):
-    out_ref[:, :32, :] = beside_ref[...]
+def fresh_spectral(arrived_ref, ana_ref, syn_ref, filters_ref, last_ref, came_ref, goes_ref):
     came = arrived_ref[:, 32:, :].astype(F32)
     last = last_ref[0]
-    own = padded_filter(filt_ref)
-    for u, lent_ref in enumerate((lent_a_ref, lent_b_ref, lent_c_ref)):
+    for u in range(3):
         came_ref[256 * u : 256 * u + 256, :] = came[:, 8 * u : 8 * u + 8].reshape(256, CH)
-        lent = padded_filter(lent_ref)
-        real, imag = [jnp.where(last == 1, lent[part], own[part]) for part in range(2)]
+        real, imag = padded_filter(filters_ref.at[u])
         t = jnp.where(last == 1, 3, u)
         parts = [came_ref[pl.ds(256 * u + r, LANES, stride=2), :] for r in range(2)]
         spectra = matmul(ana_ref[t], jnp.concatenate(parts, axis=1).astype(BF16))
@@ -199,7 +183,7 @@
         for r in range(2):
             goes_ref[pl.ds(256 * u + r, LANES, stride=2), :] = values[:, r * CH : (r + 1) * CH]
     groups = [goes_ref[256 * u : 256 * u + 256, :].reshape(PEERS, 8, CH) for u in range(3)]
-    out_ref[:, 32:, :] = jnp.concatenate(groups, axis=1).astype(BF16)
+    return jnp.concatenate(groups, axis=1).astype(BF16)
 
 
 def spectral_back_kernel(
@@ -298,6 +282,10 @@
     cotangent_ref,
     packed_ref,
     cycle_ref,
+    ana_ref,
+    syn_ref,
+    filters_ref,
+    last_ref,
     out_ref,
     grad_mixed_ref,
     shares_ref,
@@ -305,6 +293,8 @@
     masked_ref,
     hidden_ref,
     grad_pre_ref,
+    came_ref,
+    goes_ref,
 ):
     names = ("inverse", "inverse_t", "expand", "contract")
     inverse, inverse_t, expand, contract = [unpacked(packed_ref, name) for name in names]
@@ -331,6 +321,15 @@
             grad_mixed_ref[j] = grad_mixed
             grad_values.append(matmul(inverse_t, grad_mixed.astype(BF16)))
         to_blocks(out_ref, half, grad_values)
+    out_ref[:, 32:, :] = fresh_spectral(
+        values_ref,
+        ana_ref,
+        syn_ref,
+        filters_ref,
+        last_ref,
+        came_ref,
+        goes_ref,
+    )
     quarter = HID // 4
     pairs = ((grad_pre_ref, mixed_ref), (hidden_ref, masked_ref))
     for side, (wide_ref, narrow_ref) in enumerate(pairs):
@@ -538,40 +537,34 @@
         flops=leg,
     )
     lent_filt, values_fresh = lax.optimization_barrier((filt, values_fresh))
-    lent_filters = to_last(lent_filt)
+    fresh_filters = jnp.where(last, jnp.stack(to_last(lent_filt)), filt[None])
     values_fresh = exchange(values_fresh, SP)
 
     narrow = pltpu.VMEM((ROWS * NLON, CH), BF16)
     wide = pltpu.VMEM((ROWS * NLON, HID), BF16)
-    grad_values, grad_mixed, shares = call(
+    grads_fresh, grad_mixed, shares = call(
         mlp_back_kernel,
         [
-            BLOCKS,
+            PAIRED,
             jax.ShapeDtypeStruct((ROWS, NLON, CH), F32),
             jax.ShapeDtypeStruct((2, 4, HID // 4, CH), BF16),
         ],
-        [saved, values_fresh, cotangent, packed, own_cycles],
-        [narrow, narrow, wide, wide],
-        flops=5 * mlp + 2 * dft,
-        transcendentals=2 * ROWS * NLON * HID,
-        smem=(4,),
-    )
-    grads_fresh = call(
-        fresh_spectral_kernel,
-        [PAIRED],
         [
+            saved,
             values_fresh,
+            cotangent,
+            packed,
+            own_cycles,
             ana,
             syn,
-            filt,
-            *lent_filters,
+            fresh_filters,
             last.astype(jnp.int32)[None],
-            grad_values,
         ],
-        SPECTRAL_SCRATCH,
-        flops=leg,
-        smem=(7,),
-    )[0]
+        [narrow, narrow, wide, wide, *SPECTRAL_SCRATCH],
+        flops=5 * mlp + 2 * dft + leg,
+        transcendentals=2 * ROWS * NLON * HID,
+        smem=(4, 8),
+    )
     grads_fresh = exchange(grads_fresh, SP)
     share_blocks = share_blocks_of(shares)
 

time: 187 us -> 186 us (level)
  Pallas kernels: 17.5 us -> 15.5 us
  starting transfers between devices: 76.2 us -> 74.2 us
    pallas_call x12 -> x11, Pallas kernels: 17.5 us -> 15.5 us  [call(): pl.pallas_call(kernel, out_shape=outs, in_specs=specs, out_specs=[pl.Bloc...]
    ppermute x6, starting transfers between devices: 13.3 us -> 11.4 us  [to_last(): return [lax.ppermute(block, 'pipe', [(p, 3)]) for p in range(3)]]
  transfers between devices with their start and end apart: 22 -> 22, of which waited for: 10 -> 11; matrix products, arithmetic and copies ran while one was open for 1% -> 2% of each run, Pallas kernels for 5% -> 3%
where the time goes in v11:
time: 186 us; the launch traced here: 185 us
  waiting for transfers between devices  89.2 us (48%)
  starting transfers between devices  74.2 us (40%)
  Pallas kernels  15.5 us (8%)
  local copies, waits for them, and re-layouts  2.91 us (2%)
  other arithmetic  1.93 us (1%)
    all_to_all x6, waiting for transfers between devices, exchange(): return lax.all_to_all(blocks, axes, split_axis=0, concat_axis=0, tiled=True)  80 us
    all_to_all x6, starting transfers between devices, exchange(): return lax.all_to_all(blocks, axes, split_axis=0, concat_axis=0, tiled=True)  40.9 us
    pallas_call x11, Pallas kernels, call(): pl.pallas_call(kernel, out_shape=outs, in_specs=specs, out_specs=[pl.Bloc...  15.5 us
    ppermute x6, starting transfers between devices, to_last(): return [lax.ppermute(block, 'pipe', [(p, 3)]) for p in range(3)]  11.4 us
    ppermute x3, starting transfers between devices, around(): lax.ppermute(block, axis, [(i, (i + distance) % count) for i in range(cou...  10.7 us
    ppermute x2, starting transfers between devices, from_behind(): return lax.ppermute(block, axis, route)  4.42 us
    ppermute x3, waiting for transfers between devices, on_device(): lax.ppermute(grads_fresh[:, 32 + 8 * p:40 + 8 * p], 'pipe', [(3, p)])  3.88 us
  transfers between devices with their start and end apart: 22, of which 11 were waited for; matrix products, arithmetic and copies ran while one was open for 2% of the time, Pallas kernels for 3%

profile of v11, /device:TPU:1, one launch (start us, length us, event | category | flops | bytes accessed | tf_op | source)
XLA Modules:
  0.0 185.0 jit_solution(8707718983413623789)
XLA Ops:
  0.7 2.2 %shard_map.173 = bf16[32,32,128]{2,1,0:T(8,128)(2,1)} custom-call(bf16[4,240,128]{2,1,0:T(8,128)(2,1)} %bitcast.50, bf16[256,240]{1,0:T(8,128)(2,1)} %constant.107.clone.forward_hbm), custom_call_target="tpu_custom_call" | custom-call | flops 62914560 | bytes 630784 | tf_op jit(solution)/shard_map/pallas_call | solution.py:396
  2.9 16.9 %all-to-all-start = ((bf16[32,32,128]{2,1,0:T(8,128)(2,1)}), bf16[32,32,128]{2,1,0:T(8,128)(2,1)S(1)}, u32[]{:S(2)}, u32[]{:S(2)}) async-start(bf16[32,32,128]{2,1,0:T(8,128)(2,1)} %shard_map.173), calls=%async_computation | async-start | bytes 524288 | tf_op jit(solution)/shard_map/all_to_all | solution.py:422
  20.3 4.4 %collective-permute-start = (bf16[32,8,128]{2,1,0:T(8,128)(2,1)S(1)}, bf16[32,8,128]{2,1,0:T(8,128)(2,1)S(1)}, u32[]{:S(2)}, u32[]{:S(2)}) collective-permute-start(bf16[32,8,128]{2,1,0:T(8,128)(2,1)S(1)} %get-tuple-element.25), channel_id=1, source_target_pairs={{0,384},{1,385},{2,386},{3,387},{4,388},{5,389},{6,390},{7,391},{8... | collective-permute-start | bytes 196616 | tf_op jit(solution)/shard_map/ppermute | solution.py:432
  27.6 14.3 %all-to-all-done.arrived_ref = bf16[32,32,128]{2,1,0:T(8,128)(2,1)S(1)} async-done(((bf16[32,32,128]{2,1,0:T(8,128)(2,1)}), bf16[32,32,128]{2,1,0:T(8,128)(2,1)S(1)}, u32[]{:S(2)}, u32[]{:S(2)}) %all-to-all-start) | async-done | bytes 262176 | tf_op jit(solution)/shard_map/all_to_all | solution.py:422
  41.8 1.3 shard_map.176
  43.1 4.5 %all-to-all-start.1 = ((bf16[32,56,128]{2,1,0:T(8,128)(2,1)}), bf16[32,56,128]{2,1,0:T(8,128)(2,1)S(1)}, u32[]{:S(2)}, u32[]{:S(2)}) async-start(bf16[32,56,128]{2,1,0:T(8,128)(2,1)} %get-tuple-element.28), calls=%async_computation.1 | async-start | bytes 917504 | tf_op jit(solution)/shard_map/all_to_all | solution.py:422
  47.6 4.4 %collective-permute-start.3 = (f32[2,120,128]{2,1,0:T(8,128)S(1)}, f32[2,120,128]{2,1,0:T(8,128)S(1)}, u32[]{:S(2)}, u32[]{:S(2)}) collective-permute-start(f32[2,120,128]{2,1,0:T(8,128)S(1)} %bitcast.43), channel_id=1, source_target_pairs={{0,384},{1,385},{2,386},{3,387},{4,388},{5,389},{6,390},{7,391},{8... | collective-permute-start | bytes 368648 | tf_op jit(solution)/shard_map/ppermute | solution.py:432
  55.1 23.3 %all-to-all-done.1.values_ref = bf16[32,56,128]{2,1,0:T(8,128)(2,1)S(1)} async-done(((bf16[32,56,128]{2,1,0:T(8,128)(2,1)}), bf16[32,56,128]{2,1,0:T(8,128)(2,1)S(1)}, u32[]{:S(2)}, u32[]{:S(2)}) %all-to-all-start.1) | async-done | bytes 458784 | tf_op jit(solution)/shard_map/all_to_all | solution.py:422
  80.4 4.4 %shard_map.177 = (bf16[32,56,128]{2,1,0:T(8,128)(2,1)}, f32[4,240,128]{2,1,0:T(8,128)S(1)}, bf16[2,4,192,128]{3,2,1,0:T(8,128)(2,1)S(1)}) custom-call(bf16[4,240,128]{2,1,0:T(8,128)(2,1)S(1)} %bitcast.51, bf16[32,56,128]{2,1,0:T(8,128)(2,1)S(1)} %all-to-all-done.1.values_ref, bf16[4,240,128]{2,1,0:T(8,128)(2,1)S(1)} %bitcast.54, ...), custom_call_target="tpu_custom_call" | custom-call | flops 1136656384 | bytes 3694612 | tf_op jit(solution)/shard_map/pallas_call | solution.py:396
  84.8 4.3 %all-to-all-start.2 = ((bf16[32,56,128]{2,1,0:T(8,128)(2,1)}), bf16[32,56,128]{2,1,0:T(8,128)(2,1)S(1)}, u32[]{:S(2)}, u32[]{:S(2)}) async-start(bf16[32,56,128]{2,1,0:T(8,128)(2,1)} %get-tuple-element.31), calls=%async_computation.2 | async-start | bytes 917504 | tf_op jit(solution)/shard_map/all_to_all | solution.py:422
  89.1 2.3 %collective-permute-start.6 = (bf16[4,192,128]{2,1,0:T(8,128)(2,1)S(1)}, bf16[4,192,128]{2,1,0:T(8,128)(2,1)}, u32[]{:S(2)}, u32[]{:S(2)}) collective-permute-start(bf16[4,192,128]{2,1,0:T(8,128)(2,1)S(1)} %dynamic-slice_bitcast_fusion), channel_id=1, source_target_pairs={{0,4},{4,0},{1,5},{5,1},{2,6},{6,2},{3,7},{7,3},{8,12},{12,8},{9,1... | collective-permute-start | bytes 589832 | tf_op jit(solution)/shard_map/ppermute | solution.py:438
  91.4 1.2 collective-permute-done.6
  92.6 1.0 fusion
  93.6 3.2 %collective-permute-start.7 = (bf16[192,128]{1,0:T(8,128)(2,1)S(1)}, bf16[192,128]{1,0:T(8,128)(2,1)S(1)}, u32[]{:S(2)}, u32[]{:S(2)}) collective-permute-start(bf16[192,128]{1,0:T(8,128)(2,1)S(1)} %get-tuple-element.44), channel_id=1, source_target_pairs={{0,1},{1,2},{2,3},{3,0},{4,5},{5,6},{6,7},{7,4},{8,9},{9,10},{10,1... | collective-permute-start | bytes 147464 | tf_op jit(solution)/shard_map/ppermute | solution.py:444
  96.8 4.5 %collective-permute-start.8 = (bf16[192,128]{1,0:T(8,128)(2,1)S(1)}, bf16[192,128]{1,0:T(8,128)(2,1)S(1)}, u32[]{:S(2)}, u32[]{:S(2)}) collective-permute-start(bf16[192,128]{1,0:T(8,128)(2,1)S(1)} %get-tuple-element.46), channel_id=1, source_target_pairs={{0,2},{1,3},{2,0},{3,1},{4,6},{5,7},{6,4},{7,5},{8,10},{9,11},{10,... | collective-permute-start | bytes 147464 | tf_op jit(solution)/shard_map/ppermute | solution.py:444
  101.4 3.0 %collective-permute-start.9 = (bf16[192,128]{1,0:T(8,128)(2,1)S(1)}, bf16[192,128]{1,0:T(8,128)(2,1)S(1)}, u32[]{:S(2)}, u32[]{:S(2)}) collective-permute-start(bf16[192,128]{1,0:T(8,128)(2,1)S(1)} %get-tuple-element.45), channel_id=1, source_target_pairs={{0,3},{1,0},{2,1},{3,2},{4,7},{5,4},{6,5},{7,6},{8,11},{9,8},{10,9... | collective-permute-start | bytes 147464 | tf_op jit(solution)/shard_map/ppermute | solution.py:444
  104.4 2.1 %collective-permute-done.9 = bf16[192,128]{1,0:T(8,128)(2,1)S(1)} collective-permute-done((bf16[192,128]{1,0:T(8,128)(2,1)S(1)}, bf16[192,128]{1,0:T(8,128)(2,1)S(1)}, u32[]{:S(2)}, u32[]{:S(2)}) %collective-permute-start.9) | collective-permute-done | bytes 49184 | tf_op jit(solution)/shard_map/ppermute | solution.py:444
  106.6 13.3 %all-to-all-done.2.arrived_ref.values_ref = bf16[32,56,128]{2,1,0:T(8,128)(2,1)S(1)} async-done(((bf16[32,56,128]{2,1,0:T(8,128)(2,1)}), bf16[32,56,128]{2,1,0:T(8,128)(2,1)S(1)}, u32[]{:S(2)}, u32[]{:S(2)}) %all-to-all-start.2) | async-done | bytes 458784 | tf_op jit(solution)/shard_map/all_to_all | solution.py:422
  119.9 1.2 shard_map.178
  121.1 4.3 %all-to-all-start.3 = ((bf16[32,48,128]{2,1,0:T(8,128)(2,1)}), bf16[32,48,128]{2,1,0:T(8,128)(2,1)S(1)}, u32[]{:S(2)}, u32[]{:S(2)}) async-start(bf16[32,48,128]{2,1,0:T(8,128)(2,1)} %shard_map.178), calls=%async_computation.3 | async-start | bytes 786432 | tf_op jit(solution)/shard_map/all_to_all | solution.py:422
  125.5 1.3 collective-permute-start.10
  128.1 3.9 %collective-permute-done.10.lent_a_ref = bf16[32,8,128]{2,1,0:T(8,128)(2,1)S(1)} collective-permute-done((bf16[32,8,128]{2,1,0:T(8,128)(2,1)S(1)}, bf16[32,8,128]{2,1,0:T(8,128)(2,1)S(1)}, u32[]{:S(2)}, u32[]{:S(2)}) %collective-permute-start.10) | collective-permute-done | bytes 65568 | tf_op jit(solution)/shard_map/ppermute | solution.py:572
  132.0 2.2 %shard_map.179 = bf16[4,240,128]{2,1,0:T(8,128)(2,1)S(1)} custom-call(bf16[4,240,128]{2,1,0:T(8,128)(2,1)S(1)} %bitcast.49, bf16[32,56,128]{2,1,0:T(8,128)(2,1)S(1)} %all-to-all-done.2.arrived_ref.values_ref, bf16[32,8,128]{2,1,0:T(8,128)(2,1)S(1)} %collective-permute-done.10.lent_a_ref, bf16[32,8,128]{2,1,0:T(8,128)(2,1)S(1)} %collective-permute-done.11.lent_b_ref, ...), custom_call_target="tpu_custom_call" | custom-call | flops 440401920 | bytes 1916944 | tf_op jit(solution)/shard_map/pallas_call | solution.py:396
  134.2 19.2 %all-to-all-done.3.arrived_ref.coeffs_ref = bf16[32,48,128]{2,1,0:T(8,128)(2,1)S(1)} async-done(((bf16[32,48,128]{2,1,0:T(8,128)(2,1)}), bf16[32,48,128]{2,1,0:T(8,128)(2,1)S(1)}, u32[]{:S(2)}, u32[]{:S(2)}) %all-to-all-start.3) | async-done | bytes 393248 | tf_op jit(solution)/shard_map/all_to_all | solution.py:422
  154.1 3.6 %all-to-all-start.4 = ((bf16[16,24,128]{2,1,0:T(8,128)(2,1)}), bf16[16,24,128]{2,1,0:T(8,128)(2,1)S(1)}, u32[]{:S(2)}, u32[]{:S(2)}) async-start(bf16[16,24,128]{2,1,0:T(8,128)(2,1)} %shard_map.180), calls=%async_computation.4 | async-start | bytes 196608 | tf_op jit(solution)/shard_map/all_to_all | solution.py:422
  157.8 3.1 %collective-permute-start.14 = (bf16[4,240,128]{2,1,0:T(8,128)(2,1)S(1)}, bf16[4,240,128]{2,1,0:T(8,128)(2,1)S(1)}, u32[]{:S(2)}, u32[]{:S(2)}) collective-permute-start(bf16[4,240,128]{2,1,0:T(8,128)(2,1)S(1)} %shard_map.179), channel_id=1, source_target_pairs={{0,128},{128,256},{256,384},{1,129},{129,257},{257,385},{2,130},{1... | collective-permute-start | bytes 737288 | tf_op jit(solution)/shard_map/ppermute | solution.py:428
  161.7 1.3 collective-permute-start.15
  163.0 6.5 %all-to-all-done.4.pieces_ref = bf16[16,24,128]{2,1,0:T(8,128)(2,1)S(1)} async-done(((bf16[16,24,128]{2,1,0:T(8,128)(2,1)}), bf16[16,24,128]{2,1,0:T(8,128)(2,1)S(1)}, u32[]{:S(2)}, u32[]{:S(2)}) %all-to-all-start.4) | async-done | bytes 98336 | tf_op jit(solution)/shard_map/all_to_all | solution.py:422
  170.3 7.2 %all-to-all-start.5 = ((bf16[8,128,128]{2,1,0:T(8,128)(2,1)}), bf16[8,128,128]{2,1,0:T(8,128)(2,1)S(1)}, u32[]{:S(2)}, u32[]{:S(2)}) async-start(bf16[8,128,128]{2,1,0:T(8,128)(2,1)} %shard_map.181), calls=%async_computation.5 | async-start | bytes 524288 | tf_op jit(solution)/shard_map/all_to_all | solution.py:422
  177.5 1.9 %collective-permute-start.13 = (bf16[16,24,128]{2,1,0:T(8,128)(2,1)S(1)}, bf16[16,24,128]{2,1,0:T(8,128)(2,1)S(1)}, u32[]{:S(2)}, u32[]{:S(2)}) collective-permute-start(bf16[16,24,128]{2,1,0:T(8,128)(2,1)S(1)} %all-to-all-done.4.pieces_ref), channel_id=1, source_target_pairs={{0,4},{4,0},{1,5},{5,1},{2,6},{6,2},{3,7},{7,3},{8,12},{12,8},{9,1... | collective-permute-start | bytes 294920 | tf_op jit(solution)/shard_map/ppermute | solution.py:601
  179.4 1.2 collective-permute-done.13.other_ref
  180.7 3.4 %all-to-all-done.5.filter_rows_ref = bf16[8,128,128]{2,1,0:T(8,128)(2,1)S(1)} async-done(((bf16[8,128,128]{2,1,0:T(8,128)(2,1)}), bf16[8,128,128]{2,1,0:T(8,128)(2,1)S(1)}, u32[]{:S(2)}, u32[]{:S(2)}) %all-to-all-start.5) | async-done | bytes 262176 | tf_op jit(solution)/shard_map/all_to_all | solution.py:422
  (63 shorter events, 12.9 us)
Async XLA Ops:
  0.6 19.2 %copy-start.5 = (bf16[1,128,768]{2,1,0:T(8,128)(2,1)S(1)}, bf16[1,128,768]{2,1,0:T(8,128)(2,1)}, u32[]{:S(2)}) copy-start(bf16[1,128,768]{2,1,0:T(8,128)(2,1)} %param.17) | copy-start | bytes 589828
  0.6 19.2 %copy-start.6 = (bf16[256,240]{1,0:T(8,128)(2,1)S(1)}, bf16[256,240]{1,0:T(8,128)(2,1)}, u32[]{:S(2)}) copy-start(bf16[256,240]{1,0:T(8,128)(2,1)} %constant.105.clone.forward_ref) | copy-start | bytes 368644
  0.7 19.2 %copy-start.7 = (bf16[256,240]{1,0:T(8,128)(2,1)S(1)}, bf16[256,240]{1,0:T(8,128)(2,1)}, u32[]{:S(2)}) copy-start(bf16[256,240]{1,0:T(8,128)(2,1)} %constant.109.clone.rest_4_) | copy-start | bytes 368644
  0.7 19.2 %copy-start.9 = (bf16[240,256]{1,0:T(8,128)(2,1)S(1)}, bf16[240,256]{1,0:T(8,128)(2,1)}, u32[]{:S(2)}) copy-start(bf16[240,256]{1,0:T(8,128)(2,1)} %constant.106.clone.rest_3_) | copy-start | bytes 368644
  0.7 19.2 %copy-start.10 = (bf16[240,256]{1,0:T(8,128)(2,1)S(1)}, bf16[240,256]{1,0:T(8,128)(2,1)}, u32[]{:S(2)}) copy-start(bf16[240,256]{1,0:T(8,128)(2,1)} %constant.108.clone.rest_2_) | copy-start | bytes 368644
  2.9 17.0 %copy-start.1 = (bf16[1,1,4,240,128]{4,3,2,1,0:T(8,128)(2,1)S(1)}, bf16[1,1,4,240,128]{4,3,2,1,0:T(8,128)(2,1)}, u32[]{:S(2)}) copy-start(bf16[1,1,4,240,128]{4,3,2,1,0:T(8,128)(2,1)} %param.14) | copy-start | bytes 737284
  2.9 17.0 %copy-start.4 = (bf16[1,768,128]{2,1,0:T(8,128)(2,1)S(1)}, bf16[1,768,128]{2,1,0:T(8,128)(2,1)}, u32[]{:S(2)}) copy-start(bf16[1,768,128]{2,1,0:T(8,128)(2,1)} %param.18) | copy-start | bytes 589828
  2.9 38.9 %all-to-all-start = ((bf16[32,32,128]{2,1,0:T(8,128)(2,1)}), bf16[32,32,128]{2,1,0:T(8,128)(2,1)S(1)}, u32[]{:S(2)}, u32[]{:S(2)}) async-start(bf16[32,32,128]{2,1,0:T(8,128)(2,1)} %shard_map.173), calls=%async_computation | async-start | bytes 524288 | tf_op jit(solution)/shard_map/all_to_all | solution.py:422
  20.3 7.1 %collective-permute-start = (bf16[32,8,128]{2,1,0:T(8,128)(2,1)S(1)}, bf16[32,8,128]{2,1,0:T(8,128)(2,1)S(1)}, u32[]{:S(2)}, u32[]{:S(2)}) collective-permute-start(bf16[32,8,128]{2,1,0:T(8,128)(2,1)S(1)} %get-tuple-element.25), channel_id=1, source_target_pairs={{0,384},{1,385},{2,386},{3,387},{4,388},{5,389},{6,390},{7,391},{8... | collective-permute-start | bytes 196616 | tf_op jit(solution)/shard_map/ppermute | solution.py:432
  24.7 2.7 %collective-permute-start.1 = (bf16[32,8,128]{2,1,0:T(8,128)(2,1)S(1)}, bf16[32,8,128]{2,1,0:T(8,128)(2,1)S(1)}, u32[]{:S(2)}, u32[]{:S(2)}) collective-permute-start(bf16[32,8,128]{2,1,0:T(8,128)(2,1)S(1)} %get-tuple-element.25), channel_id=1, source_target_pairs={{128,384},{129,385},{130,386},{131,387},{132,388},{133,389},{134,3... | collective-permute-start | bytes 196616 | tf_op jit(solution)/shard_map/ppermute | solution.py:432
  25.4 2.1 %collective-permute-start.2 = (bf16[32,8,128]{2,1,0:T(8,128)(2,1)S(1)}, bf16[32,8,128]{2,1,0:T(8,128)(2,1)S(1)}, u32[]{:S(2)}, u32[]{:S(2)}) collective-permute-start(bf16[32,8,128]{2,1,0:T(8,128)(2,1)S(1)} %get-tuple-element.25), channel_id=1, source_target_pairs={{256,384},{257,385},{258,386},{259,387},{260,388},{261,389},{262,3... | collective-permute-start | bytes 196616 | tf_op jit(solution)/shard_map/ppermute | solution.py:432
  27.5 14.4 %copy-start = (f32[1,2,120,128]{3,2,1,0:T(8,128)S(1)}, f32[1,2,120,128]{3,2,1,0:T(8,128)}, u32[]{:S(2)}) copy-start(f32[1,2,120,128]{3,2,1,0:T(8,128)} %param.19) | copy-start | bytes 368644
  43.1 35.3 %all-to-all-start.1 = ((bf16[32,56,128]{2,1,0:T(8,128)(2,1)}), bf16[32,56,128]{2,1,0:T(8,128)(2,1)S(1)}, u32[]{:S(2)}, u32[]{:S(2)}) async-start(bf16[32,56,128]{2,1,0:T(8,128)(2,1)} %get-tuple-element.28), calls=%async_computation.1 | async-start | bytes 917504 | tf_op jit(solution)/shard_map/all_to_all | solution.py:422
  47.6 6.7 %collective-permute-start.3 = (f32[2,120,128]{2,1,0:T(8,128)S(1)}, f32[2,120,128]{2,1,0:T(8,128)S(1)}, u32[]{:S(2)}, u32[]{:S(2)}) collective-permute-start(f32[2,120,128]{2,1,0:T(8,128)S(1)} %bitcast.43), channel_id=1, source_target_pairs={{0,384},{1,385},{2,386},{3,387},{4,388},{5,389},{6,390},{7,391},{8... | collective-permute-start | bytes 368648 | tf_op jit(solution)/shard_map/ppermute | solution.py:432
  52.0 2.3 %collective-permute-start.4 = (f32[2,120,128]{2,1,0:T(8,128)S(1)}, f32[2,120,128]{2,1,0:T(8,128)S(1)}, u32[]{:S(2)}, u32[]{:S(2)}) collective-permute-start(f32[2,120,128]{2,1,0:T(8,128)S(1)} %bitcast.44), channel_id=1, source_target_pairs={{128,384},{129,385},{130,386},{131,387},{132,388},{133,389},{134,3... | collective-permute-start | bytes 368648 | tf_op jit(solution)/shard_map/ppermute | solution.py:432
  52.7 1.6 collective-permute-start.5
  54.3 24.1 %copy-start.3 = (bf16[1,1,4,240,128]{4,3,2,1,0:T(8,128)(2,1)S(1)}, bf16[1,1,4,240,128]{4,3,2,1,0:T(8,128)(2,1)}, u32[]{:S(2)}) copy-start(bf16[1,1,4,240,128]{4,3,2,1,0:T(8,128)(2,1)} %param.15) | copy-start | bytes 737284
  84.8 35.1 %all-to-all-start.2 = ((bf16[32,56,128]{2,1,0:T(8,128)(2,1)}), bf16[32,56,128]{2,1,0:T(8,128)(2,1)S(1)}, u32[]{:S(2)}, u32[]{:S(2)}) async-start(bf16[32,56,128]{2,1,0:T(8,128)(2,1)} %get-tuple-element.31), calls=%async_computation.2 | async-start | bytes 917504 | tf_op jit(solution)/shard_map/all_to_all | solution.py:422
  89.1 3.5 %collective-permute-start.6 = (bf16[4,192,128]{2,1,0:T(8,128)(2,1)S(1)}, bf16[4,192,128]{2,1,0:T(8,128)(2,1)}, u32[]{:S(2)}, u32[]{:S(2)}) collective-permute-start(bf16[4,192,128]{2,1,0:T(8,128)(2,1)S(1)} %dynamic-slice_bitcast_fusion), channel_id=1, source_target_pairs={{0,4},{4,0},{1,5},{5,1},{2,6},{6,2},{3,7},{7,3},{8,12},{12,8},{9,1... | collective-permute-start | bytes 589832 | tf_op jit(solution)/shard_map/ppermute | solution.py:438
  93.6 10.7 %collective-permute-start.7 = (bf16[192,128]{1,0:T(8,128)(2,1)S(1)}, bf16[192,128]{1,0:T(8,128)(2,1)S(1)}, u32[]{:S(2)}, u32[]{:S(2)}) collective-permute-start(bf16[192,128]{1,0:T(8,128)(2,1)S(1)} %get-tuple-element.44), channel_id=1, source_target_pairs={{0,1},{1,2},{2,3},{3,0},{4,5},{5,6},{6,7},{7,4},{8,9},{9,10},{10,1... | collective-permute-start | bytes 147464 | tf_op jit(solution)/shard_map/ppermute | solution.py:444
  96.8 7.5 %collective-permute-start.8 = (bf16[192,128]{1,0:T(8,128)(2,1)S(1)}, bf16[192,128]{1,0:T(8,128)(2,1)S(1)}, u32[]{:S(2)}, u32[]{:S(2)}) collective-permute-start(bf16[192,128]{1,0:T(8,128)(2,1)S(1)} %get-tuple-element.46), channel_id=1, source_target_pairs={{0,2},{1,3},{2,0},{3,1},{4,6},{5,7},{6,4},{7,5},{8,10},{9,11},{10,... | collective-permute-start | bytes 147464 | tf_op jit(solution)/shard_map/ppermute | solution.py:444
  101.4 5.1 %collective-permute-start.9 = (bf16[192,128]{1,0:T(8,128)(2,1)S(1)}, bf16[192,128]{1,0:T(8,128)(2,1)S(1)}, u32[]{:S(2)}, u32[]{:S(2)}) collective-permute-start(bf16[192,128]{1,0:T(8,128)(2,1)S(1)} %get-tuple-element.45), channel_id=1, source_target_pairs={{0,3},{1,0},{2,1},{3,2},{4,7},{5,4},{6,5},{7,6},{8,11},{9,8},{10,9... | collective-permute-start | bytes 147464 | tf_op jit(solution)/shard_map/ppermute | solution.py:444
  121.1 32.3 %all-to-all-start.3 = ((bf16[32,48,128]{2,1,0:T(8,128)(2,1)}), bf16[32,48,128]{2,1,0:T(8,128)(2,1)S(1)}, u32[]{:S(2)}, u32[]{:S(2)}) async-start(bf16[32,48,128]{2,1,0:T(8,128)(2,1)} %shard_map.178), calls=%async_computation.3 | async-start | bytes 786432 | tf_op jit(solution)/shard_map/all_to_all | solution.py:422
  125.5 6.5 %collective-permute-start.10 = (bf16[32,8,128]{2,1,0:T(8,128)(2,1)S(1)}, bf16[32,8,128]{2,1,0:T(8,128)(2,1)S(1)}, u32[]{:S(2)}, u32[]{:S(2)}) collective-permute-start(bf16[32,8,128]{2,1,0:T(8,128)(2,1)S(1)} %get-tuple-element.43), channel_id=1, source_target_pairs={{384,0},{385,1},{386,2},{387,3},{388,4},{389,5},{390,6},{391,7},{3... | collective-permute-start | bytes 196616 | tf_op jit(solution)/shard_map/ppermute | solution.py:572
  126.8 5.2 %collective-permute-start.11 = (bf16[32,8,128]{2,1,0:T(8,128)(2,1)S(1)}, bf16[32,8,128]{2,1,0:T(8,128)(2,1)S(1)}, u32[]{:S(2)}, u32[]{:S(2)}) collective-permute-start(bf16[32,8,128]{2,1,0:T(8,128)(2,1)S(1)} %get-tuple-element.42), channel_id=1, source_target_pairs={{384,128},{385,129},{386,130},{387,131},{388,132},{389,133},{390,1... | collective-permute-start | bytes 196616 | tf_op jit(solution)/shard_map/ppermute | solution.py:572
  127.4 4.5 %collective-permute-start.12 = (bf16[32,8,128]{2,1,0:T(8,128)(2,1)S(1)}, bf16[32,8,128]{2,1,0:T(8,128)(2,1)S(1)}, u32[]{:S(2)}, u32[]{:S(2)}) collective-permute-start(bf16[32,8,128]{2,1,0:T(8,128)(2,1)S(1)} %get-tuple-element.41), channel_id=1, source_target_pairs={{384,256},{385,257},{386,258},{387,259},{388,260},{389,261},{390,2... | collective-permute-start | bytes 196616 | tf_op jit(solution)/shard_map/ppermute | solution.py:572
  154.1 6.8 %copy-start.8 = (bf16[240,256]{1,0:T(8,128)(2,1)S(1)}, bf16[240,256]{1,0:T(8,128)(2,1)}, u32[]{:S(2)}) copy-start(bf16[240,256]{1,0:T(8,128)(2,1)} %constant.104.clone.forward_ref) | copy-start | bytes 368644
  154.1 15.4 %all-to-all-start.4 = ((bf16[16,24,128]{2,1,0:T(8,128)(2,1)}), bf16[16,24,128]{2,1,0:T(8,128)(2,1)S(1)}, u32[]{:S(2)}, u32[]{:S(2)}) async-start(bf16[16,24,128]{2,1,0:T(8,128)(2,1)} %shard_map.180), calls=%async_computation.4 | async-start | bytes 196608 | tf_op jit(solution)/shard_map/all_to_all | solution.py:422
  157.8 21.7 %collective-permute-start.14 = (bf16[4,240,128]{2,1,0:T(8,128)(2,1)S(1)}, bf16[4,240,128]{2,1,0:T(8,128)(2,1)S(1)}, u32[]{:S(2)}, u32[]{:S(2)}) collective-permute-start(bf16[4,240,128]{2,1,0:T(8,128)(2,1)S(1)} %shard_map.179), channel_id=1, source_target_pairs={{0,128},{128,256},{256,384},{1,129},{129,257},{257,385},{2,130},{1... | collective-permute-start | bytes 737288 | tf_op jit(solution)/shard_map/ppermute | solution.py:428
  161.7 17.7 %collective-permute-start.15 = (bf16[4,240,128]{2,1,0:T(8,128)(2,1)S(1)}, bf16[4,240,128]{2,1,0:T(8,128)(2,1)S(1)}, u32[]{:S(2)}, u32[]{:S(2)}) collective-permute-start(bf16[4,240,128]{2,1,0:T(8,128)(2,1)S(1)} %shard_map.182), channel_id=1, source_target_pairs={{128,0},{256,128},{384,256},{129,1},{257,129},{385,257},{130,2},{2... | collective-permute-start | bytes 737288 | tf_op jit(solution)/shard_map/ppermute | solution.py:428
  170.3 13.8 %all-to-all-start.5 = ((bf16[8,128,128]{2,1,0:T(8,128)(2,1)}), bf16[8,128,128]{2,1,0:T(8,128)(2,1)S(1)}, u32[]{:S(2)}, u32[]{:S(2)}) async-start(bf16[8,128,128]{2,1,0:T(8,128)(2,1)} %shard_map.181), calls=%async_computation.5 | async-start | bytes 524288 | tf_op jit(solution)/shard_map/all_to_all | solution.py:422
  177.5 3.2 %collective-permute-start.13 = (bf16[16,24,128]{2,1,0:T(8,128)(2,1)S(1)}, bf16[16,24,128]{2,1,0:T(8,128)(2,1)S(1)}, u32[]{:S(2)}, u32[]{:S(2)}) collective-permute-start(bf16[16,24,128]{2,1,0:T(8,128)(2,1)S(1)} %all-to-all-done.4.pieces_ref), channel_id=1, source_target_pairs={{0,4},{4,0},{1,5},{5,1},{2,6},{6,2},{3,7},{7,3},{8,12},{12,8},{9,1... | collective-permute-start | bytes 294920 | tf_op jit(solution)/shard_map/ppermute | solution.py:601
  (3 other events, 2.7 us)

commit v12 on v11

--- a/solution.py
+++ b/solution.py
@@ -155,7 +155,7 @@
     for t in range(ROWS):
         parts = [came_ref[pl.ds(r * ROWS + t, LANES, stride=8), :] for r in range(2)]
         spectra = matmul(ana_ref[t], jnp.concatenate(parts, axis=1).astype(BF16))
-        spectra_ref[t] = spectra
+        spectra_ref[t] = spectra.astype(BF16)
         values = matmul(syn_ref[t], filter_step(spectra, real, imag), ((0,), (0,)))
         for r in range(2):
             goes_ref[pl.ds(r * ROWS + t, LANES, stride=8), :] = values[:, r * CH : (r + 1) * CH]
@@ -205,7 +205,7 @@
         parts = [came_ref[pl.ds(r * ROWS + t, LANES, stride=8), :] for r in range(2)]
         grads = matmul(syn_ref[t], jnp.concatenate(parts, axis=1).astype(BF16))
         first, second = grads[:, :CH], grads[:, CH:]
-        spectra = spectra_ref[t]
+        spectra = spectra_ref[t].astype(F32)
         s_first, s_second = spectra[:, :CH], spectra[:, CH:]
         total_real = total_real + (first * s_first + second * s_second)
         total_imag = total_imag + (second * s_first - first * s_second)
@@ -228,6 +228,7 @@
     ("inverse", NLON, 256),
     ("fresh_inverse", NLON, 256),
     ("inverse_t", 256, NLON),
+    ("cotangent", ROWS * NLON, CH),
 ):
     PLACES[_name] = (sum(r * -(-c // CH) for _, r, c in PLACES.values()), _rows, _columns)
 PACKED_ROWS = sum(r * -(-c // CH) for _, r, c in PLACES.values())
@@ -279,7 +280,6 @@
 def mlp_back_kernel(
     x_ref,
     values_ref,
-    cotangent_ref,
     packed_ref,
     cycle_ref,
     ana_ref,
@@ -298,6 +298,7 @@
 ):
     names = ("inverse", "inverse_t", "expand", "contract")
     inverse, inverse_t, expand, contract = [unpacked(packed_ref, name) for name in names]
+    cotangent = unpacked(packed_ref, "cotangent")
     for half in range(2):
         values = from_blocks(values_ref, half)
         grad_values = []
@@ -306,7 +307,7 @@
             rows = slice(j * NLON, (j + 1) * NLON)
             mixed = x_ref[j].astype(F32) + matmul(inverse, values[h])
             mixed_b = mixed.astype(BF16)
-            masked_f = cotangent_ref[j].astype(F32) * live(cycle_ref, j)
+            masked_f = cotangent[rows].astype(F32) * live(cycle_ref, j)
             masked = masked_f.astype(BF16)
             mixed_ref[rows, :] = mixed_b
             masked_ref[rows, :] = masked
@@ -318,7 +319,7 @@
             grad_pre = (grad_hidden * slope).astype(BF16)
             grad_pre_ref[rows, :] = grad_pre
             grad_mixed = masked_f + matmul(grad_pre, expand, ((1,), (1,)))
-            grad_mixed_ref[j] = grad_mixed
+            grad_mixed_ref[j] = grad_mixed.astype(BF16)
             grad_values.append(matmul(inverse_t, grad_mixed.astype(BF16)))
         to_blocks(out_ref, half, grad_values)
     out_ref[:, 32:, :] = fresh_spectral(
@@ -343,7 +344,7 @@
         values = from_blocks(coeffs_ref, half)
         for h in range(2):
             j = 2 * half + h
-            total = grad_mixed_ref[j] + matmul(forward_ref[...], values[h])
+            total = grad_mixed_ref[j].astype(F32) + matmul(forward_ref[...], values[h])
             out_ref[j] = (total * live(cycle_ref, j)).astype(BF16)
 
 
@@ -503,6 +504,7 @@
     )[0]
     saved_at_orders = exchange(saved_blocks, SP)
     kept = [contract, expand, inverse, fresh_inverse, inverse_t]
+    kept += [tokens.reshape(ROWS * NLON, CH) for tokens in (cotangent,)]
     fresh_own, fresh_lent, packed = call(
         fresh_coeffs_kernel,
         [OWN, LENT, jax.ShapeDtypeStruct((PACKED_ROWS, CH), BF16)],
@@ -528,7 +530,7 @@
         flops=4_000_000,
     )
 
-    spectra_shape = jax.ShapeDtypeStruct((ROWS, LANES, 2 * CH), F32)
+    spectra_shape = jax.ShapeDtypeStruct((ROWS, LANES, 2 * CH), BF16)
     values_fresh, spectra = call(
         saved_spectral_kernel,
         [PAIRED, spectra_shape],
@@ -546,13 +548,12 @@
         mlp_back_kernel,
         [
             PAIRED,
-            jax.ShapeDtypeStruct((ROWS, NLON, CH), F32),
+            TOKENS,
             jax.ShapeDtypeStruct((2, 4, HID // 4, CH), BF16),
         ],
         [
             saved,
             values_fresh,
-            cotangent,
             packed,
             own_cycles,
             ana,
@@ -563,7 +564,7 @@
         [narrow, narrow, wide, wide, *SPECTRAL_SCRATCH],
         flops=5 * mlp + 2 * dft + leg,
         transcendentals=2 * ROWS * NLON * HID,
-        smem=(4, 8),
+        smem=(3, 7),
     )
     grads_fresh = exchange(grads_fresh, SP)
     share_blocks = share_blocks_of(shares)

time: 186 us -> 185 us (level)
  transfers between devices with their start and end apart: 22 -> 22, of which waited for: 11 -> 11; matrix products, arithmetic and copies ran while one was open for 2% -> 1% of each run, Pallas kernels for 3% -> 3%
where the time goes in v12:
time: 185 us; the launch traced here: 184 us
  waiting for transfers between devices  89.1 us (48%)
  starting transfers between devices  74.3 us (40%)
  Pallas kernels  15.5 us (8%)
  local copies, waits for them, and re-layouts  3.7 us (2%)
    all_to_all x6, waiting for transfers between devices, exchange(): return lax.all_to_all(blocks, axes, split_axis=0, concat_axis=0, tiled=True)  80 us
    all_to_all x6, starting transfers between devices, exchange(): return lax.all_to_all(blocks, axes, split_axis=0, concat_axis=0, tiled=True)  40.9 us
    pallas_call x11, Pallas kernels, call(): pl.pallas_call(kernel, out_shape=outs, in_specs=specs, out_specs=[pl.Bloc...  15.5 us
    ppermute x6, starting transfers between devices, to_last(): return [lax.ppermute(block, 'pipe', [(p, 3)]) for p in range(3)]  11.4 us
    ppermute x3, starting transfers between devices, around(): lax.ppermute(block, axis, [(i, (i + distance) % count) for i in range(cou...  10.7 us
    ppermute x2, starting transfers between devices, from_behind(): return lax.ppermute(block, axis, route)  4.43 us
    ppermute x3, waiting for transfers between devices, on_device(): lax.ppermute(grads_fresh[:, 32 + 8 * p:40 + 8 * p], 'pipe', [(3, p)])  3.88 us
  transfers between devices with their start and end apart: 22, of which 11 were waited for; matrix products, arithmetic and copies ran while one was open for 1% of the time, Pallas kernels for 3%

profile of v12, /device:TPU:1, one launch (start us, length us, event | category | flops | bytes accessed | tf_op | source)
XLA Modules:
  0.0 184.0 jit_solution(8251844716759794575)
XLA Ops:
  0.7 2.2 %shard_map.173 = bf16[32,32,128]{2,1,0:T(8,128)(2,1)} custom-call(bf16[4,240,128]{2,1,0:T(8,128)(2,1)} %bitcast.51, bf16[256,240]{1,0:T(8,128)(2,1)} %constant.107.clone.forward_hbm), custom_call_target="tpu_custom_call" | custom-call | flops 62914560 | bytes 630784 | tf_op jit(solution)/shard_map/pallas_call | solution.py:397
  2.9 16.9 %all-to-all-start = ((bf16[32,32,128]{2,1,0:T(8,128)(2,1)}), bf16[32,32,128]{2,1,0:T(8,128)(2,1)S(1)}, u32[]{:S(2)}, u32[]{:S(2)}) async-start(bf16[32,32,128]{2,1,0:T(8,128)(2,1)} %shard_map.173), calls=%async_computation | async-start | bytes 524288 | tf_op jit(solution)/shard_map/all_to_all | solution.py:423
  22.1 4.4 %collective-permute-start = (bf16[32,8,128]{2,1,0:T(8,128)(2,1)S(1)}, bf16[32,8,128]{2,1,0:T(8,128)(2,1)S(1)}, u32[]{:S(2)}, u32[]{:S(2)}) collective-permute-start(bf16[32,8,128]{2,1,0:T(8,128)(2,1)S(1)} %get-tuple-element.25), channel_id=1, source_target_pairs={{0,384},{1,385},{2,386},{3,387},{4,388},{5,389},{6,390},{7,391},{8... | collective-permute-start | bytes 196616 | tf_op jit(solution)/shard_map/ppermute | solution.py:433
  29.3 12.5 %all-to-all-done.arrived_ref = bf16[32,32,128]{2,1,0:T(8,128)(2,1)S(1)} async-done(((bf16[32,32,128]{2,1,0:T(8,128)(2,1)}), bf16[32,32,128]{2,1,0:T(8,128)(2,1)S(1)}, u32[]{:S(2)}, u32[]{:S(2)}) %all-to-all-start) | async-done | bytes 262176 | tf_op jit(solution)/shard_map/all_to_all | solution.py:423
  41.8 1.2 shard_map.176
  43.1 4.5 %all-to-all-start.1 = ((bf16[32,56,128]{2,1,0:T(8,128)(2,1)}), bf16[32,56,128]{2,1,0:T(8,128)(2,1)S(1)}, u32[]{:S(2)}, u32[]{:S(2)}) async-start(bf16[32,56,128]{2,1,0:T(8,128)(2,1)} %get-tuple-element.28), calls=%async_computation.1 | async-start | bytes 917504 | tf_op jit(solution)/shard_map/all_to_all | solution.py:423
  47.6 4.4 %collective-permute-start.3 = (f32[2,120,128]{2,1,0:T(8,128)S(1)}, f32[2,120,128]{2,1,0:T(8,128)S(1)}, u32[]{:S(2)}, u32[]{:S(2)}) collective-permute-start(f32[2,120,128]{2,1,0:T(8,128)S(1)} %bitcast.43), channel_id=1, source_target_pairs={{0,384},{1,385},{2,386},{3,387},{4,388},{5,389},{6,390},{7,391},{8... | collective-permute-start | bytes 368648 | tf_op jit(solution)/shard_map/ppermute | solution.py:433
  54.3 24.1 %all-to-all-done.1.values_ref = bf16[32,56,128]{2,1,0:T(8,128)(2,1)S(1)} async-done(((bf16[32,56,128]{2,1,0:T(8,128)(2,1)}), bf16[32,56,128]{2,1,0:T(8,128)(2,1)S(1)}, u32[]{:S(2)}, u32[]{:S(2)}) %all-to-all-start.1) | async-done | bytes 458784 | tf_op jit(solution)/shard_map/all_to_all | solution.py:423
  78.4 0.9 copy-done.3
  79.3 4.4 %shard_map.177 = (bf16[32,56,128]{2,1,0:T(8,128)(2,1)}, bf16[4,240,128]{2,1,0:T(8,128)(2,1)S(1)}, bf16[2,4,192,128]{3,2,1,0:T(8,128)(2,1)S(1)}) custom-call(bf16[4,240,128]{2,1,0:T(8,128)(2,1)S(1)} %bitcast.52, bf16[32,56,128]{2,1,0:T(8,128)(2,1)S(1)} %all-to-all-done.1.values_ref, bf16[3968,128]{1,0:T(8,128)(2,1)S(1)} %get-tuple-element.29.packed_ref, ...), custom_call_target="tpu_custom_call" | custom-call | flops 1136656384 | bytes 3448852 | tf_op jit(solution)/shard_map/pallas_call | solution.py:397
  83.8 4.3 %all-to-all-start.2 = ((bf16[32,56,128]{2,1,0:T(8,128)(2,1)}), bf16[32,56,128]{2,1,0:T(8,128)(2,1)S(1)}, u32[]{:S(2)}, u32[]{:S(2)}) async-start(bf16[32,56,128]{2,1,0:T(8,128)(2,1)} %get-tuple-element.31), calls=%async_computation.2 | async-start | bytes 917504 | tf_op jit(solution)/shard_map/all_to_all | solution.py:423
  88.1 2.3 %collective-permute-start.6 = (bf16[4,192,128]{2,1,0:T(8,128)(2,1)S(1)}, bf16[4,192,128]{2,1,0:T(8,128)(2,1)S(1)}, u32[]{:S(2)}, u32[]{:S(2)}) collective-permute-start(bf16[4,192,128]{2,1,0:T(8,128)(2,1)S(1)} %dynamic-slice_bitcast_fusion), channel_id=1, source_target_pairs={{0,4},{4,0},{1,5},{5,1},{2,6},{6,2},{3,7},{7,3},{8,12},{12,8},{9,1... | collective-permute-start | bytes 589832 | tf_op jit(solution)/shard_map/ppermute | solution.py:439
  90.4 1.0 collective-permute-done.6
  91.5 3.2 %collective-permute-start.7 = (bf16[192,128]{1,0:T(8,128)(2,1)S(1)}, bf16[192,128]{1,0:T(8,128)(2,1)S(1)}, u32[]{:S(2)}, u32[]{:S(2)}) collective-permute-start(bf16[192,128]{1,0:T(8,128)(2,1)S(1)} %get-tuple-element.44), channel_id=1, source_target_pairs={{0,1},{1,2},{2,3},{3,0},{4,5},{5,6},{6,7},{7,4},{8,9},{9,10},{10,1... | collective-permute-start | bytes 147464 | tf_op jit(solution)/shard_map/ppermute | solution.py:445
  94.7 4.5 %collective-permute-start.8 = (bf16[192,128]{1,0:T(8,128)(2,1)S(1)}, bf16[192,128]{1,0:T(8,128)(2,1)S(1)}, u32[]{:S(2)}, u32[]{:S(2)}) collective-permute-start(bf16[192,128]{1,0:T(8,128)(2,1)S(1)} %get-tuple-element.46), channel_id=1, source_target_pairs={{0,2},{1,3},{2,0},{3,1},{4,6},{5,7},{6,4},{7,5},{8,10},{9,11},{10,... | collective-permute-start | bytes 147464 | tf_op jit(solution)/shard_map/ppermute | solution.py:445
  99.3 3.0 %collective-permute-start.9 = (bf16[192,128]{1,0:T(8,128)(2,1)S(1)}, bf16[192,128]{1,0:T(8,128)(2,1)S(1)}, u32[]{:S(2)}, u32[]{:S(2)}) collective-permute-start(bf16[192,128]{1,0:T(8,128)(2,1)S(1)} %get-tuple-element.45), channel_id=1, source_target_pairs={{0,3},{1,0},{2,1},{3,2},{4,7},{5,4},{6,5},{7,6},{8,11},{9,8},{10,9... | collective-permute-start | bytes 147464 | tf_op jit(solution)/shard_map/ppermute | solution.py:445
  102.3 2.1 %collective-permute-done.9 = bf16[192,128]{1,0:T(8,128)(2,1)S(1)} collective-permute-done((bf16[192,128]{1,0:T(8,128)(2,1)S(1)}, bf16[192,128]{1,0:T(8,128)(2,1)S(1)}, u32[]{:S(2)}, u32[]{:S(2)}) %collective-permute-start.9) | collective-permute-done | bytes 49184 | tf_op jit(solution)/shard_map/ppermute | solution.py:445
  104.5 14.4 %all-to-all-done.2.arrived_ref.values_ref = bf16[32,56,128]{2,1,0:T(8,128)(2,1)S(1)} async-done(((bf16[32,56,128]{2,1,0:T(8,128)(2,1)}), bf16[32,56,128]{2,1,0:T(8,128)(2,1)S(1)}, u32[]{:S(2)}, u32[]{:S(2)}) %all-to-all-start.2) | async-done | bytes 458784 | tf_op jit(solution)/shard_map/all_to_all | solution.py:423
  118.9 1.3 shard_map.178
  120.1 4.3 %all-to-all-start.3 = ((bf16[32,48,128]{2,1,0:T(8,128)(2,1)}), bf16[32,48,128]{2,1,0:T(8,128)(2,1)S(1)}, u32[]{:S(2)}, u32[]{:S(2)}) async-start(bf16[32,48,128]{2,1,0:T(8,128)(2,1)} %shard_map.178), calls=%async_computation.3 | async-start | bytes 786432 | tf_op jit(solution)/shard_map/all_to_all | solution.py:423
  124.5 1.3 collective-permute-start.10
  127.1 3.9 %collective-permute-done.10.lent_a_ref = bf16[32,8,128]{2,1,0:T(8,128)(2,1)S(1)} collective-permute-done((bf16[32,8,128]{2,1,0:T(8,128)(2,1)S(1)}, bf16[32,8,128]{2,1,0:T(8,128)(2,1)S(1)}, u32[]{:S(2)}, u32[]{:S(2)}) %collective-permute-start.10) | collective-permute-done | bytes 65568 | tf_op jit(solution)/shard_map/ppermute | solution.py:573
  131.0 2.2 %shard_map.179 = bf16[4,240,128]{2,1,0:T(8,128)(2,1)S(1)} custom-call(bf16[4,240,128]{2,1,0:T(8,128)(2,1)S(1)} %bitcast.49, bf16[32,56,128]{2,1,0:T(8,128)(2,1)S(1)} %all-to-all-done.2.arrived_ref.values_ref, bf16[32,8,128]{2,1,0:T(8,128)(2,1)S(1)} %collective-permute-done.10.lent_a_ref, bf16[32,8,128]{2,1,0:T(8,128)(2,1)S(1)} %collective-permute-done.11.lent_b_ref, ...), custom_call_target="tpu_custom_call" | custom-call | flops 440401920 | bytes 2162704 | tf_op jit(solution)/shard_map/pallas_call | solution.py:397
  133.2 19.2 %all-to-all-done.3.arrived_ref.coeffs_ref = bf16[32,48,128]{2,1,0:T(8,128)(2,1)S(1)} async-done(((bf16[32,48,128]{2,1,0:T(8,128)(2,1)}), bf16[32,48,128]{2,1,0:T(8,128)(2,1)S(1)}, u32[]{:S(2)}, u32[]{:S(2)}) %all-to-all-start.3) | async-done | bytes 393248 | tf_op jit(solution)/shard_map/all_to_all | solution.py:423
  153.1 3.6 %all-to-all-start.4 = ((bf16[16,24,128]{2,1,0:T(8,128)(2,1)}), bf16[16,24,128]{2,1,0:T(8,128)(2,1)S(1)}, u32[]{:S(2)}, u32[]{:S(2)}) async-start(bf16[16,24,128]{2,1,0:T(8,128)(2,1)} %shard_map.180), calls=%async_computation.4 | async-start | bytes 196608 | tf_op jit(solution)/shard_map/all_to_all | solution.py:423
  156.8 3.1 %collective-permute-start.14 = (bf16[4,240,128]{2,1,0:T(8,128)(2,1)S(1)}, bf16[4,240,128]{2,1,0:T(8,128)(2,1)S(1)}, u32[]{:S(2)}, u32[]{:S(2)}) collective-permute-start(bf16[4,240,128]{2,1,0:T(8,128)(2,1)S(1)} %shard_map.179), channel_id=1, source_target_pairs={{0,128},{128,256},{256,384},{1,129},{129,257},{257,385},{2,130},{1... | collective-permute-start | bytes 737288 | tf_op jit(solution)/shard_map/ppermute | solution.py:429
  160.7 1.3 collective-permute-start.15
  162.0 6.5 %all-to-all-done.4.pieces_ref = bf16[16,24,128]{2,1,0:T(8,128)(2,1)S(1)} async-done(((bf16[16,24,128]{2,1,0:T(8,128)(2,1)}), bf16[16,24,128]{2,1,0:T(8,128)(2,1)S(1)}, u32[]{:S(2)}, u32[]{:S(2)}) %all-to-all-start.4) | async-done | bytes 98336 | tf_op jit(solution)/shard_map/all_to_all | solution.py:423
  169.3 7.2 %all-to-all-start.5 = ((bf16[8,128,128]{2,1,0:T(8,128)(2,1)}), bf16[8,128,128]{2,1,0:T(8,128)(2,1)S(1)}, u32[]{:S(2)}, u32[]{:S(2)}) async-start(bf16[8,128,128]{2,1,0:T(8,128)(2,1)} %shard_map.181), calls=%async_computation.5 | async-start | bytes 524288 | tf_op jit(solution)/shard_map/all_to_all | solution.py:423
  176.5 1.9 %collective-permute-start.13 = (bf16[16,24,128]{2,1,0:T(8,128)(2,1)S(1)}, bf16[16,24,128]{2,1,0:T(8,128)(2,1)S(1)}, u32[]{:S(2)}, u32[]{:S(2)}) collective-permute-start(bf16[16,24,128]{2,1,0:T(8,128)(2,1)S(1)} %all-to-all-done.4.pieces_ref), channel_id=1, source_target_pairs={{0,4},{4,0},{1,5},{5,1},{2,6},{6,2},{3,7},{7,3},{8,12},{12,8},{9,1... | collective-permute-start | bytes 294920 | tf_op jit(solution)/shard_map/ppermute | solution.py:602
  178.5 1.2 collective-permute-done.13.other_ref
  179.7 3.4 %all-to-all-done.5.filter_rows_ref = bf16[8,128,128]{2,1,0:T(8,128)(2,1)S(1)} async-done(((bf16[8,128,128]{2,1,0:T(8,128)(2,1)}), bf16[8,128,128]{2,1,0:T(8,128)(2,1)S(1)}, u32[]{:S(2)}, u32[]{:S(2)}) %all-to-all-start.5) | async-done | bytes 262176 | tf_op jit(solution)/shard_map/all_to_all | solution.py:423
  (61 shorter events, 12.0 us)
Async XLA Ops:
  0.6 19.2 %copy-start.4 = (bf16[1,768,128]{2,1,0:T(8,128)(2,1)S(1)}, bf16[1,768,128]{2,1,0:T(8,128)(2,1)}, u32[]{:S(2)}) copy-start(bf16[1,768,128]{2,1,0:T(8,128)(2,1)} %param.18) | copy-start | bytes 589828
  0.6 19.2 %copy-start.5 = (bf16[1,128,768]{2,1,0:T(8,128)(2,1)S(1)}, bf16[1,128,768]{2,1,0:T(8,128)(2,1)}, u32[]{:S(2)}) copy-start(bf16[1,128,768]{2,1,0:T(8,128)(2,1)} %param.17) | copy-start | bytes 589828
  0.7 19.2 %copy-start.6 = (bf16[256,240]{1,0:T(8,128)(2,1)S(1)}, bf16[256,240]{1,0:T(8,128)(2,1)}, u32[]{:S(2)}) copy-start(bf16[256,240]{1,0:T(8,128)(2,1)} %constant.105.clone.forward_ref) | copy-start | bytes 368644
  0.7 19.2 %copy-start.7 = (bf16[256,240]{1,0:T(8,128)(2,1)S(1)}, bf16[256,240]{1,0:T(8,128)(2,1)}, u32[]{:S(2)}) copy-start(bf16[256,240]{1,0:T(8,128)(2,1)} %constant.109.clone.rest_4_) | copy-start | bytes 368644
  2.9 17.0 %copy-start.1 = (bf16[1,1,4,240,128]{4,3,2,1,0:T(8,128)(2,1)S(1)}, bf16[1,1,4,240,128]{4,3,2,1,0:T(8,128)(2,1)}, u32[]{:S(2)}) copy-start(bf16[1,1,4,240,128]{4,3,2,1,0:T(8,128)(2,1)} %param.14) | copy-start | bytes 737284
  2.9 17.0 %copy-start.2 = (bf16[1,1,4,240,128]{4,3,2,1,0:T(8,128)(2,1)S(1)}, bf16[1,1,4,240,128]{4,3,2,1,0:T(8,128)(2,1)}, u32[]{:S(2)}) copy-start(bf16[1,1,4,240,128]{4,3,2,1,0:T(8,128)(2,1)} %param.16) | copy-start | bytes 737284
  2.9 38.9 %all-to-all-start = ((bf16[32,32,128]{2,1,0:T(8,128)(2,1)}), bf16[32,32,128]{2,1,0:T(8,128)(2,1)S(1)}, u32[]{:S(2)}, u32[]{:S(2)}) async-start(bf16[32,32,128]{2,1,0:T(8,128)(2,1)} %shard_map.173), calls=%async_computation | async-start | bytes 524288 | tf_op jit(solution)/shard_map/all_to_all | solution.py:423
  19.9 0.9 copy-start.9
  22.1 7.1 %collective-permute-start = (bf16[32,8,128]{2,1,0:T(8,128)(2,1)S(1)}, bf16[32,8,128]{2,1,0:T(8,128)(2,1)S(1)}, u32[]{:S(2)}, u32[]{:S(2)}) collective-permute-start(bf16[32,8,128]{2,1,0:T(8,128)(2,1)S(1)} %get-tuple-element.25), channel_id=1, source_target_pairs={{0,384},{1,385},{2,386},{3,387},{4,388},{5,389},{6,390},{7,391},{8... | collective-permute-start | bytes 196616 | tf_op jit(solution)/shard_map/ppermute | solution.py:433
  26.5 2.7 %collective-permute-start.1 = (bf16[32,8,128]{2,1,0:T(8,128)(2,1)S(1)}, bf16[32,8,128]{2,1,0:T(8,128)(2,1)S(1)}, u32[]{:S(2)}, u32[]{:S(2)}) collective-permute-start(bf16[32,8,128]{2,1,0:T(8,128)(2,1)S(1)} %get-tuple-element.25), channel_id=1, source_target_pairs={{128,384},{129,385},{130,386},{131,387},{132,388},{133,389},{134,3... | collective-permute-start | bytes 196616 | tf_op jit(solution)/shard_map/ppermute | solution.py:433
  27.2 2.1 %collective-permute-start.2 = (bf16[32,8,128]{2,1,0:T(8,128)(2,1)S(1)}, bf16[32,8,128]{2,1,0:T(8,128)(2,1)S(1)}, u32[]{:S(2)}, u32[]{:S(2)}) collective-permute-start(bf16[32,8,128]{2,1,0:T(8,128)(2,1)S(1)} %get-tuple-element.25), channel_id=1, source_target_pairs={{256,384},{257,385},{258,386},{259,387},{260,388},{261,389},{262,3... | collective-permute-start | bytes 196616 | tf_op jit(solution)/shard_map/ppermute | solution.py:433
  29.3 12.5 %copy-start = (f32[1,2,120,128]{3,2,1,0:T(8,128)S(1)}, f32[1,2,120,128]{3,2,1,0:T(8,128)}, u32[]{:S(2)}) copy-start(f32[1,2,120,128]{3,2,1,0:T(8,128)} %param.19) | copy-start | bytes 368644
  43.1 35.3 %all-to-all-start.1 = ((bf16[32,56,128]{2,1,0:T(8,128)(2,1)}), bf16[32,56,128]{2,1,0:T(8,128)(2,1)S(1)}, u32[]{:S(2)}, u32[]{:S(2)}) async-start(bf16[32,56,128]{2,1,0:T(8,128)(2,1)} %get-tuple-element.28), calls=%async_computation.1 | async-start | bytes 917504 | tf_op jit(solution)/shard_map/all_to_all | solution.py:423
  47.6 6.7 %collective-permute-start.3 = (f32[2,120,128]{2,1,0:T(8,128)S(1)}, f32[2,120,128]{2,1,0:T(8,128)S(1)}, u32[]{:S(2)}, u32[]{:S(2)}) collective-permute-start(f32[2,120,128]{2,1,0:T(8,128)S(1)} %bitcast.43), channel_id=1, source_target_pairs={{0,384},{1,385},{2,386},{3,387},{4,388},{5,389},{6,390},{7,391},{8... | collective-permute-start | bytes 368648 | tf_op jit(solution)/shard_map/ppermute | solution.py:433
  52.0 2.3 %collective-permute-start.4 = (f32[2,120,128]{2,1,0:T(8,128)S(1)}, f32[2,120,128]{2,1,0:T(8,128)S(1)}, u32[]{:S(2)}, u32[]{:S(2)}) collective-permute-start(f32[2,120,128]{2,1,0:T(8,128)S(1)} %bitcast.44), channel_id=1, source_target_pairs={{128,384},{129,385},{130,386},{131,387},{132,388},{133,389},{134,3... | collective-permute-start | bytes 368648 | tf_op jit(solution)/shard_map/ppermute | solution.py:433
  52.7 1.6 collective-permute-start.5
  78.4 0.9 copy-start.3
  83.8 35.1 %all-to-all-start.2 = ((bf16[32,56,128]{2,1,0:T(8,128)(2,1)}), bf16[32,56,128]{2,1,0:T(8,128)(2,1)S(1)}, u32[]{:S(2)}, u32[]{:S(2)}) async-start(bf16[32,56,128]{2,1,0:T(8,128)(2,1)} %get-tuple-element.31), calls=%async_computation.2 | async-start | bytes 917504 | tf_op jit(solution)/shard_map/all_to_all | solution.py:423
  88.1 3.3 %collective-permute-start.6 = (bf16[4,192,128]{2,1,0:T(8,128)(2,1)S(1)}, bf16[4,192,128]{2,1,0:T(8,128)(2,1)S(1)}, u32[]{:S(2)}, u32[]{:S(2)}) collective-permute-start(bf16[4,192,128]{2,1,0:T(8,128)(2,1)S(1)} %dynamic-slice_bitcast_fusion), channel_id=1, source_target_pairs={{0,4},{4,0},{1,5},{5,1},{2,6},{6,2},{3,7},{7,3},{8,12},{12,8},{9,1... | collective-permute-start | bytes 589832 | tf_op jit(solution)/shard_map/ppermute | solution.py:439
  91.5 10.8 %collective-permute-start.7 = (bf16[192,128]{1,0:T(8,128)(2,1)S(1)}, bf16[192,128]{1,0:T(8,128)(2,1)S(1)}, u32[]{:S(2)}, u32[]{:S(2)}) collective-permute-start(bf16[192,128]{1,0:T(8,128)(2,1)S(1)} %get-tuple-element.44), channel_id=1, source_target_pairs={{0,1},{1,2},{2,3},{3,0},{4,5},{5,6},{6,7},{7,4},{8,9},{9,10},{10,1... | collective-permute-start | bytes 147464 | tf_op jit(solution)/shard_map/ppermute | solution.py:445
  94.7 7.6 %collective-permute-start.8 = (bf16[192,128]{1,0:T(8,128)(2,1)S(1)}, bf16[192,128]{1,0:T(8,128)(2,1)S(1)}, u32[]{:S(2)}, u32[]{:S(2)}) collective-permute-start(bf16[192,128]{1,0:T(8,128)(2,1)S(1)} %get-tuple-element.46), channel_id=1, source_target_pairs={{0,2},{1,3},{2,0},{3,1},{4,6},{5,7},{6,4},{7,5},{8,10},{9,11},{10,... | collective-permute-start | bytes 147464 | tf_op jit(solution)/shard_map/ppermute | solution.py:445
  99.3 5.1 %collective-permute-start.9 = (bf16[192,128]{1,0:T(8,128)(2,1)S(1)}, bf16[192,128]{1,0:T(8,128)(2,1)S(1)}, u32[]{:S(2)}, u32[]{:S(2)}) collective-permute-start(bf16[192,128]{1,0:T(8,128)(2,1)S(1)} %get-tuple-element.45), channel_id=1, source_target_pairs={{0,3},{1,0},{2,1},{3,2},{4,7},{5,4},{6,5},{7,6},{8,11},{9,8},{10,9... | collective-permute-start | bytes 147464 | tf_op jit(solution)/shard_map/ppermute | solution.py:445
  120.1 32.3 %all-to-all-start.3 = ((bf16[32,48,128]{2,1,0:T(8,128)(2,1)}), bf16[32,48,128]{2,1,0:T(8,128)(2,1)S(1)}, u32[]{:S(2)}, u32[]{:S(2)}) async-start(bf16[32,48,128]{2,1,0:T(8,128)(2,1)} %shard_map.178), calls=%async_computation.3 | async-start | bytes 786432 | tf_op jit(solution)/shard_map/all_to_all | solution.py:423
  124.5 6.5 %collective-permute-start.10 = (bf16[32,8,128]{2,1,0:T(8,128)(2,1)S(1)}, bf16[32,8,128]{2,1,0:T(8,128)(2,1)S(1)}, u32[]{:S(2)}, u32[]{:S(2)}) collective-permute-start(bf16[32,8,128]{2,1,0:T(8,128)(2,1)S(1)} %get-tuple-element.43), channel_id=1, source_target_pairs={{384,0},{385,1},{386,2},{387,3},{388,4},{389,5},{390,6},{391,7},{3... | collective-permute-start | bytes 196616 | tf_op jit(solution)/shard_map/ppermute | solution.py:573
  125.8 5.2 %collective-permute-start.11 = (bf16[32,8,128]{2,1,0:T(8,128)(2,1)S(1)}, bf16[32,8,128]{2,1,0:T(8,128)(2,1)S(1)}, u32[]{:S(2)}, u32[]{:S(2)}) collective-permute-start(bf16[32,8,128]{2,1,0:T(8,128)(2,1)S(1)} %get-tuple-element.42), channel_id=1, source_target_pairs={{384,128},{385,129},{386,130},{387,131},{388,132},{389,133},{390,1... | collective-permute-start | bytes 196616 | tf_op jit(solution)/shard_map/ppermute | solution.py:573
  126.4 4.5 %collective-permute-start.12 = (bf16[32,8,128]{2,1,0:T(8,128)(2,1)S(1)}, bf16[32,8,128]{2,1,0:T(8,128)(2,1)S(1)}, u32[]{:S(2)}, u32[]{:S(2)}) collective-permute-start(bf16[32,8,128]{2,1,0:T(8,128)(2,1)S(1)} %get-tuple-element.41), channel_id=1, source_target_pairs={{384,256},{385,257},{386,258},{387,259},{388,260},{389,261},{390,2... | collective-permute-start | bytes 196616 | tf_op jit(solution)/shard_map/ppermute | solution.py:573
  153.1 6.8 %copy-start.8 = (bf16[240,256]{1,0:T(8,128)(2,1)S(1)}, bf16[240,256]{1,0:T(8,128)(2,1)}, u32[]{:S(2)}) copy-start(bf16[240,256]{1,0:T(8,128)(2,1)} %constant.104.clone.forward_ref) | copy-start | bytes 368644
  153.1 15.4 %all-to-all-start.4 = ((bf16[16,24,128]{2,1,0:T(8,128)(2,1)}), bf16[16,24,128]{2,1,0:T(8,128)(2,1)S(1)}, u32[]{:S(2)}, u32[]{:S(2)}) async-start(bf16[16,24,128]{2,1,0:T(8,128)(2,1)} %shard_map.180), calls=%async_computation.4 | async-start | bytes 196608 | tf_op jit(solution)/shard_map/all_to_all | solution.py:423
  156.8 21.7 %collective-permute-start.14 = (bf16[4,240,128]{2,1,0:T(8,128)(2,1)S(1)}, bf16[4,240,128]{2,1,0:T(8,128)(2,1)S(1)}, u32[]{:S(2)}, u32[]{:S(2)}) collective-permute-start(bf16[4,240,128]{2,1,0:T(8,128)(2,1)S(1)} %shard_map.179), channel_id=1, source_target_pairs={{0,128},{128,256},{256,384},{1,129},{129,257},{257,385},{2,130},{1... | collective-permute-start | bytes 737288 | tf_op jit(solution)/shard_map/ppermute | solution.py:429
  160.7 17.7 %collective-permute-start.15 = (bf16[4,240,128]{2,1,0:T(8,128)(2,1)S(1)}, bf16[4,240,128]{2,1,0:T(8,128)(2,1)S(1)}, u32[]{:S(2)}, u32[]{:S(2)}) collective-permute-start(bf16[4,240,128]{2,1,0:T(8,128)(2,1)S(1)} %shard_map.182), channel_id=1, source_target_pairs={{128,0},{256,128},{384,256},{129,1},{257,129},{385,257},{130,2},{2... | collective-permute-start | bytes 737288 | tf_op jit(solution)/shard_map/ppermute | solution.py:429
  169.3 13.8 %all-to-all-start.5 = ((bf16[8,128,128]{2,1,0:T(8,128)(2,1)}), bf16[8,128,128]{2,1,0:T(8,128)(2,1)S(1)}, u32[]{:S(2)}, u32[]{:S(2)}) async-start(bf16[8,128,128]{2,1,0:T(8,128)(2,1)} %shard_map.181), calls=%async_computation.5 | async-start | bytes 524288 | tf_op jit(solution)/shard_map/all_to_all | solution.py:423
  176.5 3.2 %collective-permute-start.13 = (bf16[16,24,128]{2,1,0:T(8,128)(2,1)S(1)}, bf16[16,24,128]{2,1,0:T(8,128)(2,1)S(1)}, u32[]{:S(2)}, u32[]{:S(2)}) collective-permute-start(bf16[16,24,128]{2,1,0:T(8,128)(2,1)S(1)} %all-to-all-done.4.pieces_ref), channel_id=1, source_target_pairs={{0,4},{4,0},{1,5},{5,1},{2,6},{6,2},{3,7},{7,3},{8,12},{12,8},{9,1... | collective-permute-start | bytes 294920 | tf_op jit(solution)/shard_map/ppermute | solution.py:602
  (2 other events, 1.6 us)

commit v13 on v12

--- a/solution.py
+++ b/solution.py
@@ -128,6 +128,11 @@
             width = min(CH, columns - start)
             packed_ref[row : row + rows, :width] = source[:, start : start + width]
             row += rows
+    contract_ref, expand_ref = sources[:2]
+    for n in range(HID // CH):
+        columns = slice(n * CH, (n + 1) * CH)
+        packed_ref[row + n * CH : row + (n + 1) * CH, :] = contract_ref[columns, :].T
+        packed_ref[row + HID + n * CH : row + HID + (n + 1) * CH, :] = expand_ref[:, columns].T
     for j in range(ROWS):
         coeffs = matmul(forward_ref[...], x_ref[j])
         for place in range(8):
@@ -228,7 +233,8 @@
     ("inverse", NLON, 256),
     ("fresh_inverse", NLON, 256),
     ("inverse_t", 256, NLON),
-    ("cotangent", ROWS * NLON, CH),
+    ("contract_t", CH, HID),
+    ("expand_t", HID, CH),
 ):
     PLACES[_name] = (sum(r * -(-c // CH) for _, r, c in PLACES.values()), _rows, _columns)
 PACKED_ROWS = sum(r * -(-c // CH) for _, r, c in PLACES.values())
@@ -280,6 +286,7 @@
 def mlp_back_kernel(
     x_ref,
     values_ref,
+    cotangent_ref,
     packed_ref,
     cycle_ref,
     ana_ref,
@@ -296,9 +303,8 @@
     came_ref,
     goes_ref,
 ):
-    names = ("inverse", "inverse_t", "expand", "contract")
-    inverse, inverse_t, expand, contract = [unpacked(packed_ref, name) for name in names]
-    cotangent = unpacked(packed_ref, "cotangent")
+    names = ("inverse", "inverse_t", "expand", "contract_t", "expand_t")
+    inverse, inverse_t, expand, contract_t, expand_t = [unpacked(packed_ref, n) for n in names]
     for half in range(2):
         values = from_blocks(values_ref, half)
         grad_values = []
@@ -307,7 +313,7 @@
             rows = slice(j * NLON, (j + 1) * NLON)
             mixed = x_ref[j].astype(F32) + matmul(inverse, values[h])
             mixed_b = mixed.astype(BF16)
-            masked_f = cotangent[rows].astype(F32) * live(cycle_ref, j)
+            masked_f = cotangent_ref[j].astype(F32) * live(cycle_ref, j)
             masked = masked_f.astype(BF16)
             mixed_ref[rows, :] = mixed_b
             masked_ref[rows, :] = masked
@@ -315,10 +321,10 @@
             normal = 0.5 * (1.0 + lax.erf(pre * ROOT_HALF))
             hidden_ref[rows, :] = (pre * normal).astype(BF16)
             slope = normal + pre * jnp.exp(-0.5 * pre * pre) * INV_ROOT_TAU
-            grad_hidden = matmul(masked, contract, ((1,), (1,)))
+            grad_hidden = matmul(masked, contract_t)
             grad_pre = (grad_hidden * slope).astype(BF16)
             grad_pre_ref[rows, :] = grad_pre
-            grad_mixed = masked_f + matmul(grad_pre, expand, ((1,), (1,)))
+            grad_mixed = masked_f + matmul(grad_pre, expand_t)
             grad_mixed_ref[j] = grad_mixed.astype(BF16)
             grad_values.append(matmul(inverse_t, grad_mixed.astype(BF16)))
         to_blocks(out_ref, half, grad_values)
@@ -504,7 +510,6 @@
     )[0]
     saved_at_orders = exchange(saved_blocks, SP)
     kept = [contract, expand, inverse, fresh_inverse, inverse_t]
-    kept += [tokens.reshape(ROWS * NLON, CH) for tokens in (cotangent,)]
     fresh_own, fresh_lent, packed = call(
         fresh_coeffs_kernel,
         [OWN, LENT, jax.ShapeDtypeStruct((PACKED_ROWS, CH), BF16)],
@@ -554,6 +559,7 @@
         [
             saved,
             values_fresh,
+            cotangent,
             packed,
             own_cycles,
             ana,
@@ -564,7 +570,7 @@
         [narrow, narrow, wide, wide, *SPECTRAL_SCRATCH],
         flops=5 * mlp + 2 * dft + leg,
         transcendentals=2 * ROWS * NLON * HID,
-        smem=(3, 7),
+        smem=(4, 8),
     )
     grads_fresh = exchange(grads_fresh, SP)
     share_blocks = share_blocks_of(shares)

time: 185 us -> 186 us (level)
  no operation moved by 1% of the time
where the time goes in v13:
time: 186 us; the launch traced here: 185 us
  waiting for transfers between devices  90.7 us (49%)
  starting transfers between devices  74.3 us (40%)
  Pallas kernels  15.7 us (8%)
  local copies, waits for them, and re-layouts  2.87 us (2%)
    all_to_all x6, waiting for transfers between devices, exchange(): return lax.all_to_all(blocks, axes, split_axis=0, concat_axis=0, tiled=True)  81.7 us
    all_to_all x6, starting transfers between devices, exchange(): return lax.all_to_all(blocks, axes, split_axis=0, concat_axis=0, tiled=True)  40.8 us
    pallas_call x11, Pallas kernels, call(): pl.pallas_call(kernel, out_shape=outs, in_specs=specs, out_specs=[pl.Bloc...  15.7 us
    ppermute x6, starting transfers between devices, to_last(): return [lax.ppermute(block, 'pipe', [(p, 3)]) for p in range(3)]  11.4 us
    ppermute x3, starting transfers between devices, around(): lax.ppermute(block, axis, [(i, (i + distance) % count) for i in range(cou...  10.7 us
    ppermute x2, starting transfers between devices, from_behind(): return lax.ppermute(block, axis, route)  4.41 us
  transfers between devices with their start and end apart: 22, of which 11 were waited for; matrix products, arithmetic and copies ran while one was open for 1% of the time, Pallas kernels for 3%

profile of v13, /device:TPU:1, one launch (start us, length us, event | category | flops | bytes accessed | tf_op | source)
XLA Modules:
  0.0 185.0 jit_solution(4400860413269330122)
XLA Ops:
  0.7 2.2 %shard_map.173 = bf16[32,32,128]{2,1,0:T(8,128)(2,1)} custom-call(bf16[4,240,128]{2,1,0:T(8,128)(2,1)} %bitcast.50, bf16[256,240]{1,0:T(8,128)(2,1)} %constant.107.clone.forward_hbm), custom_call_target="tpu_custom_call" | custom-call | flops 62914560 | bytes 630784 | tf_op jit(solution)/shard_map/pallas_call | solution.py:403
  3.0 16.9 %all-to-all-start = ((bf16[32,32,128]{2,1,0:T(8,128)(2,1)}), bf16[32,32,128]{2,1,0:T(8,128)(2,1)S(1)}, u32[]{:S(2)}, u32[]{:S(2)}) async-start(bf16[32,32,128]{2,1,0:T(8,128)(2,1)} %shard_map.173), calls=%async_computation | async-start | bytes 524288 | tf_op jit(solution)/shard_map/all_to_all | solution.py:429
  20.4 4.4 %collective-permute-start = (bf16[32,8,128]{2,1,0:T(8,128)(2,1)S(1)}, bf16[32,8,128]{2,1,0:T(8,128)(2,1)S(1)}, u32[]{:S(2)}, u32[]{:S(2)}) collective-permute-start(bf16[32,8,128]{2,1,0:T(8,128)(2,1)S(1)} %get-tuple-element.25), channel_id=1, source_target_pairs={{0,384},{1,385},{2,386},{3,387},{4,388},{5,389},{6,390},{7,391},{8... | collective-permute-start | bytes 196616 | tf_op jit(solution)/shard_map/ppermute | solution.py:439
  27.6 14.3 %all-to-all-done.arrived_ref = bf16[32,32,128]{2,1,0:T(8,128)(2,1)S(1)} async-done(((bf16[32,32,128]{2,1,0:T(8,128)(2,1)}), bf16[32,32,128]{2,1,0:T(8,128)(2,1)S(1)}, u32[]{:S(2)}, u32[]{:S(2)}) %all-to-all-start) | async-done | bytes 262176 | tf_op jit(solution)/shard_map/all_to_all | solution.py:429
  41.9 1.3 shard_map.176
  43.2 4.5 %all-to-all-start.1 = ((bf16[32,56,128]{2,1,0:T(8,128)(2,1)}), bf16[32,56,128]{2,1,0:T(8,128)(2,1)S(1)}, u32[]{:S(2)}, u32[]{:S(2)}) async-start(bf16[32,56,128]{2,1,0:T(8,128)(2,1)} %get-tuple-element.28), calls=%async_computation.1 | async-start | bytes 917504 | tf_op jit(solution)/shard_map/all_to_all | solution.py:429
  47.7 4.4 %collective-permute-start.3 = (f32[2,120,128]{2,1,0:T(8,128)S(1)}, f32[2,120,128]{2,1,0:T(8,128)S(1)}, u32[]{:S(2)}, u32[]{:S(2)}) collective-permute-start(f32[2,120,128]{2,1,0:T(8,128)S(1)} %bitcast.43), channel_id=1, source_target_pairs={{0,384},{1,385},{2,386},{3,387},{4,388},{5,389},{6,390},{7,391},{8... | collective-permute-start | bytes 368648 | tf_op jit(solution)/shard_map/ppermute | solution.py:439
  54.4 24.1 %all-to-all-done.1.values_ref = bf16[32,56,128]{2,1,0:T(8,128)(2,1)S(1)} async-done(((bf16[32,56,128]{2,1,0:T(8,128)(2,1)}), bf16[32,56,128]{2,1,0:T(8,128)(2,1)S(1)}, u32[]{:S(2)}, u32[]{:S(2)}) %all-to-all-start.1) | async-done | bytes 458784 | tf_op jit(solution)/shard_map/all_to_all | solution.py:429
  78.5 0.9 copy-done.4
  80.4 4.5 %shard_map.177 = (bf16[32,56,128]{2,1,0:T(8,128)(2,1)}, bf16[4,240,128]{2,1,0:T(8,128)(2,1)S(1)}, bf16[2,4,192,128]{3,2,1,0:T(8,128)(2,1)S(1)}) custom-call(bf16[4,240,128]{2,1,0:T(8,128)(2,1)S(1)} %bitcast.51, bf16[32,56,128]{2,1,0:T(8,128)(2,1)S(1)} %all-to-all-done.1.values_ref, bf16[4,240,128]{2,1,0:T(8,128)(2,1)S(1)} %bitcast.54, ...), custom_call_target="tpu_custom_call" | custom-call | flops 1136656384 | bytes 3842068 | tf_op jit(solution)/shard_map/pallas_call | solution.py:403
  84.9 4.3 %all-to-all-start.2 = ((bf16[32,56,128]{2,1,0:T(8,128)(2,1)}), bf16[32,56,128]{2,1,0:T(8,128)(2,1)S(1)}, u32[]{:S(2)}, u32[]{:S(2)}) async-start(bf16[32,56,128]{2,1,0:T(8,128)(2,1)} %get-tuple-element.31), calls=%async_computation.2 | async-start | bytes 917504 | tf_op jit(solution)/shard_map/all_to_all | solution.py:429
  89.2 2.3 %collective-permute-start.6 = (bf16[4,192,128]{2,1,0:T(8,128)(2,1)S(1)}, bf16[4,192,128]{2,1,0:T(8,128)(2,1)S(1)}, u32[]{:S(2)}, u32[]{:S(2)}) collective-permute-start(bf16[4,192,128]{2,1,0:T(8,128)(2,1)S(1)} %dynamic-slice_bitcast_fusion), channel_id=1, source_target_pairs={{0,4},{4,0},{1,5},{5,1},{2,6},{6,2},{3,7},{7,3},{8,12},{12,8},{9,1... | collective-permute-start | bytes 589832 | tf_op jit(solution)/shard_map/ppermute | solution.py:445
  91.5 1.0 collective-permute-done.6
  92.6 3.2 %collective-permute-start.7 = (bf16[192,128]{1,0:T(8,128)(2,1)S(1)}, bf16[192,128]{1,0:T(8,128)(2,1)S(1)}, u32[]{:S(2)}, u32[]{:S(2)}) collective-permute-start(bf16[192,128]{1,0:T(8,128)(2,1)S(1)} %get-tuple-element.44), channel_id=1, source_target_pairs={{0,1},{1,2},{2,3},{3,0},{4,5},{5,6},{6,7},{7,4},{8,9},{9,10},{10,1... | collective-permute-start | bytes 147464 | tf_op jit(solution)/shard_map/ppermute | solution.py:451
  95.9 4.5 %collective-permute-start.8 = (bf16[192,128]{1,0:T(8,128)(2,1)S(1)}, bf16[192,128]{1,0:T(8,128)(2,1)S(1)}, u32[]{:S(2)}, u32[]{:S(2)}) collective-permute-start(bf16[192,128]{1,0:T(8,128)(2,1)S(1)} %get-tuple-element.46), channel_id=1, source_target_pairs={{0,2},{1,3},{2,0},{3,1},{4,6},{5,7},{6,4},{7,5},{8,10},{9,11},{10,... | collective-permute-start | bytes 147464 | tf_op jit(solution)/shard_map/ppermute | solution.py:451
  100.4 3.0 %collective-permute-start.9 = (bf16[192,128]{1,0:T(8,128)(2,1)S(1)}, bf16[192,128]{1,0:T(8,128)(2,1)S(1)}, u32[]{:S(2)}, u32[]{:S(2)}) collective-permute-start(bf16[192,128]{1,0:T(8,128)(2,1)S(1)} %get-tuple-element.45), channel_id=1, source_target_pairs={{0,3},{1,0},{2,1},{3,2},{4,7},{5,4},{6,5},{7,6},{8,11},{9,8},{10,9... | collective-permute-start | bytes 147464 | tf_op jit(solution)/shard_map/ppermute | solution.py:451
  103.4 2.1 %collective-permute-done.9 = bf16[192,128]{1,0:T(8,128)(2,1)S(1)} collective-permute-done((bf16[192,128]{1,0:T(8,128)(2,1)S(1)}, bf16[192,128]{1,0:T(8,128)(2,1)S(1)}, u32[]{:S(2)}, u32[]{:S(2)}) %collective-permute-start.9) | collective-permute-done | bytes 49184 | tf_op jit(solution)/shard_map/ppermute | solution.py:451
  105.6 14.4 %all-to-all-done.2.arrived_ref.values_ref = bf16[32,56,128]{2,1,0:T(8,128)(2,1)S(1)} async-done(((bf16[32,56,128]{2,1,0:T(8,128)(2,1)}), bf16[32,56,128]{2,1,0:T(8,128)(2,1)S(1)}, u32[]{:S(2)}, u32[]{:S(2)}) %all-to-all-start.2) | async-done | bytes 458784 | tf_op jit(solution)/shard_map/all_to_all | solution.py:429
  120.0 1.3 shard_map.178
  121.2 4.3 %all-to-all-start.3 = ((bf16[32,48,128]{2,1,0:T(8,128)(2,1)}), bf16[32,48,128]{2,1,0:T(8,128)(2,1)S(1)}, u32[]{:S(2)}, u32[]{:S(2)}) async-start(bf16[32,48,128]{2,1,0:T(8,128)(2,1)} %shard_map.178), calls=%async_computation.3 | async-start | bytes 786432 | tf_op jit(solution)/shard_map/all_to_all | solution.py:429
  125.6 1.3 collective-permute-start.10
  128.4 3.7 %collective-permute-done.10.lent_a_ref = bf16[32,8,128]{2,1,0:T(8,128)(2,1)S(1)} collective-permute-done((bf16[32,8,128]{2,1,0:T(8,128)(2,1)S(1)}, bf16[32,8,128]{2,1,0:T(8,128)(2,1)S(1)}, u32[]{:S(2)}, u32[]{:S(2)}) %collective-permute-start.10) | collective-permute-done | bytes 65568 | tf_op jit(solution)/shard_map/ppermute | solution.py:579
  132.1 2.2 %shard_map.179 = bf16[4,240,128]{2,1,0:T(8,128)(2,1)S(1)} custom-call(bf16[4,240,128]{2,1,0:T(8,128)(2,1)S(1)} %bitcast.49, bf16[32,56,128]{2,1,0:T(8,128)(2,1)S(1)} %all-to-all-done.2.arrived_ref.values_ref, bf16[32,8,128]{2,1,0:T(8,128)(2,1)S(1)} %collective-permute-done.10.lent_a_ref, bf16[32,8,128]{2,1,0:T(8,128)(2,1)S(1)} %collective-permute-done.11.lent_b_ref, ...), custom_call_target="tpu_custom_call" | custom-call | flops 440401920 | bytes 2310160 | tf_op jit(solution)/shard_map/pallas_call | solution.py:403
  134.3 19.2 %all-to-all-done.3.arrived_ref.coeffs_ref = bf16[32,48,128]{2,1,0:T(8,128)(2,1)S(1)} async-done(((bf16[32,48,128]{2,1,0:T(8,128)(2,1)}), bf16[32,48,128]{2,1,0:T(8,128)(2,1)S(1)}, u32[]{:S(2)}, u32[]{:S(2)}) %all-to-all-start.3) | async-done | bytes 393248 | tf_op jit(solution)/shard_map/all_to_all | solution.py:429
  154.2 3.5 %all-to-all-start.4 = ((bf16[16,24,128]{2,1,0:T(8,128)(2,1)}), bf16[16,24,128]{2,1,0:T(8,128)(2,1)S(1)}, u32[]{:S(2)}, u32[]{:S(2)}) async-start(bf16[16,24,128]{2,1,0:T(8,128)(2,1)} %shard_map.180), calls=%async_computation.4 | async-start | bytes 196608 | tf_op jit(solution)/shard_map/all_to_all | solution.py:429
  157.7 3.1 %collective-permute-start.14 = (bf16[4,240,128]{2,1,0:T(8,128)(2,1)S(1)}, bf16[4,240,128]{2,1,0:T(8,128)(2,1)S(1)}, u32[]{:S(2)}, u32[]{:S(2)}) collective-permute-start(bf16[4,240,128]{2,1,0:T(8,128)(2,1)S(1)} %shard_map.179), channel_id=1, source_target_pairs={{0,128},{128,256},{256,384},{1,129},{129,257},{257,385},{2,130},{1... | collective-permute-start | bytes 737288 | tf_op jit(solution)/shard_map/ppermute | solution.py:435
  161.7 1.3 collective-permute-start.15
  163.0 6.5 %all-to-all-done.4.pieces_ref = bf16[16,24,128]{2,1,0:T(8,128)(2,1)S(1)} async-done(((bf16[16,24,128]{2,1,0:T(8,128)(2,1)}), bf16[16,24,128]{2,1,0:T(8,128)(2,1)S(1)}, u32[]{:S(2)}, u32[]{:S(2)}) %all-to-all-start.4) | async-done | bytes 98336 | tf_op jit(solution)/shard_map/all_to_all | solution.py:429
  170.2 7.3 %all-to-all-start.5 = ((bf16[8,128,128]{2,1,0:T(8,128)(2,1)}), bf16[8,128,128]{2,1,0:T(8,128)(2,1)S(1)}, u32[]{:S(2)}, u32[]{:S(2)}) async-start(bf16[8,128,128]{2,1,0:T(8,128)(2,1)} %shard_map.181), calls=%async_computation.5 | async-start | bytes 524288 | tf_op jit(solution)/shard_map/all_to_all | solution.py:429
  177.5 1.9 %collective-permute-start.13 = (bf16[16,24,128]{2,1,0:T(8,128)(2,1)S(1)}, bf16[16,24,128]{2,1,0:T(8,128)(2,1)S(1)}, u32[]{:S(2)}, u32[]{:S(2)}) collective-permute-start(bf16[16,24,128]{2,1,0:T(8,128)(2,1)S(1)} %all-to-all-done.4.pieces_ref), channel_id=1, source_target_pairs={{0,4},{4,0},{1,5},{5,1},{2,6},{6,2},{3,7},{7,3},{8,12},{12,8},{9,1... | collective-permute-start | bytes 294920 | tf_op jit(solution)/shard_map/ppermute | solution.py:608
  179.4 1.2 collective-permute-done.13.other_ref
  180.7 3.4 %all-to-all-done.5.filter_rows_ref = bf16[8,128,128]{2,1,0:T(8,128)(2,1)S(1)} async-done(((bf16[8,128,128]{2,1,0:T(8,128)(2,1)}), bf16[8,128,128]{2,1,0:T(8,128)(2,1)S(1)}, u32[]{:S(2)}, u32[]{:S(2)}) %all-to-all-start.5) | async-done | bytes 262176 | tf_op jit(solution)/shard_map/all_to_all | solution.py:429
  (65 shorter events, 11.4 us)
Async XLA Ops:
  0.6 19.3 %copy-start.7 = (bf16[256,240]{1,0:T(8,128)(2,1)S(1)}, bf16[256,240]{1,0:T(8,128)(2,1)}, u32[]{:S(2)}) copy-start(bf16[256,240]{1,0:T(8,128)(2,1)} %constant.105.clone.forward_ref) | copy-start | bytes 368644
  0.6 19.3 %copy-start.10 = (bf16[240,256]{1,0:T(8,128)(2,1)S(1)}, bf16[240,256]{1,0:T(8,128)(2,1)}, u32[]{:S(2)}) copy-start(bf16[240,256]{1,0:T(8,128)(2,1)} %constant.106.clone.rest_3_) | copy-start | bytes 368644
  0.7 19.3 %copy-start.11 = (bf16[240,256]{1,0:T(8,128)(2,1)S(1)}, bf16[240,256]{1,0:T(8,128)(2,1)}, u32[]{:S(2)}) copy-start(bf16[240,256]{1,0:T(8,128)(2,1)} %constant.108.clone.rest_2_) | copy-start | bytes 368644
  0.7 19.3 %copy-start.8 = (bf16[256,240]{1,0:T(8,128)(2,1)S(1)}, bf16[256,240]{1,0:T(8,128)(2,1)}, u32[]{:S(2)}) copy-start(bf16[256,240]{1,0:T(8,128)(2,1)} %constant.109.clone.rest_4_) | copy-start | bytes 368644
  0.7 19.3 %copy-start.1 = (bf16[1,1,4,240,128]{4,3,2,1,0:T(8,128)(2,1)S(1)}, bf16[1,1,4,240,128]{4,3,2,1,0:T(8,128)(2,1)}, u32[]{:S(2)}) copy-start(bf16[1,1,4,240,128]{4,3,2,1,0:T(8,128)(2,1)} %param.14) | copy-start | bytes 737284
  0.7 19.3 %copy-start.5 = (bf16[1,768,128]{2,1,0:T(8,128)(2,1)S(1)}, bf16[1,768,128]{2,1,0:T(8,128)(2,1)}, u32[]{:S(2)}) copy-start(bf16[1,768,128]{2,1,0:T(8,128)(2,1)} %param.18) | copy-start | bytes 589828
  0.7 26.2 %copy-start.13 = (s32[128]{0:T(128)S(1)}, s32[128]{0:T(128)}, u32[]{:S(2)}) copy-start(s32[128]{0:T(128)} %param.20) | copy-start | bytes 1540
  3.0 38.9 %copy-start = (f32[1,2,120,128]{3,2,1,0:T(8,128)S(1)}, f32[1,2,120,128]{3,2,1,0:T(8,128)}, u32[]{:S(2)}) copy-start(f32[1,2,120,128]{3,2,1,0:T(8,128)} %param.19) | copy-start | bytes 368644
  3.0 38.9 %all-to-all-start = ((bf16[32,32,128]{2,1,0:T(8,128)(2,1)}), bf16[32,32,128]{2,1,0:T(8,128)(2,1)S(1)}, u32[]{:S(2)}, u32[]{:S(2)}) async-start(bf16[32,32,128]{2,1,0:T(8,128)(2,1)} %shard_map.173), calls=%async_computation | async-start | bytes 524288 | tf_op jit(solution)/shard_map/all_to_all | solution.py:429
  20.4 7.1 %collective-permute-start = (bf16[32,8,128]{2,1,0:T(8,128)(2,1)S(1)}, bf16[32,8,128]{2,1,0:T(8,128)(2,1)S(1)}, u32[]{:S(2)}, u32[]{:S(2)}) collective-permute-start(bf16[32,8,128]{2,1,0:T(8,128)(2,1)S(1)} %get-tuple-element.25), channel_id=1, source_target_pairs={{0,384},{1,385},{2,386},{3,387},{4,388},{5,389},{6,390},{7,391},{8... | collective-permute-start | bytes 196616 | tf_op jit(solution)/shard_map/ppermute | solution.py:439
  24.8 2.7 %collective-permute-start.1 = (bf16[32,8,128]{2,1,0:T(8,128)(2,1)S(1)}, bf16[32,8,128]{2,1,0:T(8,128)(2,1)S(1)}, u32[]{:S(2)}, u32[]{:S(2)}) collective-permute-start(bf16[32,8,128]{2,1,0:T(8,128)(2,1)S(1)} %get-tuple-element.25), channel_id=1, source_target_pairs={{128,384},{129,385},{130,386},{131,387},{132,388},{133,389},{134,3... | collective-permute-start | bytes 196616 | tf_op jit(solution)/shard_map/ppermute | solution.py:439
  25.5 2.1 %collective-permute-start.2 = (bf16[32,8,128]{2,1,0:T(8,128)(2,1)S(1)}, bf16[32,8,128]{2,1,0:T(8,128)(2,1)S(1)}, u32[]{:S(2)}, u32[]{:S(2)}) collective-permute-start(bf16[32,8,128]{2,1,0:T(8,128)(2,1)S(1)} %get-tuple-element.25), channel_id=1, source_target_pairs={{256,384},{257,385},{258,386},{259,387},{260,388},{261,389},{262,3... | collective-permute-start | bytes 196616 | tf_op jit(solution)/shard_map/ppermute | solution.py:439
  43.2 35.3 %all-to-all-start.1 = ((bf16[32,56,128]{2,1,0:T(8,128)(2,1)}), bf16[32,56,128]{2,1,0:T(8,128)(2,1)S(1)}, u32[]{:S(2)}, u32[]{:S(2)}) async-start(bf16[32,56,128]{2,1,0:T(8,128)(2,1)} %get-tuple-element.28), calls=%async_computation.1 | async-start | bytes 917504 | tf_op jit(solution)/shard_map/all_to_all | solution.py:429
  47.7 6.7 %collective-permute-start.3 = (f32[2,120,128]{2,1,0:T(8,128)S(1)}, f32[2,120,128]{2,1,0:T(8,128)S(1)}, u32[]{:S(2)}, u32[]{:S(2)}) collective-permute-start(f32[2,120,128]{2,1,0:T(8,128)S(1)} %bitcast.43), channel_id=1, source_target_pairs={{0,384},{1,385},{2,386},{3,387},{4,388},{5,389},{6,390},{7,391},{8... | collective-permute-start | bytes 368648 | tf_op jit(solution)/shard_map/ppermute | solution.py:439
  52.1 2.3 %collective-permute-start.4 = (f32[2,120,128]{2,1,0:T(8,128)S(1)}, f32[2,120,128]{2,1,0:T(8,128)S(1)}, u32[]{:S(2)}, u32[]{:S(2)}) collective-permute-start(f32[2,120,128]{2,1,0:T(8,128)S(1)} %bitcast.44), channel_id=1, source_target_pairs={{128,384},{129,385},{130,386},{131,387},{132,388},{133,389},{134,3... | collective-permute-start | bytes 368648 | tf_op jit(solution)/shard_map/ppermute | solution.py:439
  52.8 1.6 collective-permute-start.5
  84.9 35.1 %all-to-all-start.2 = ((bf16[32,56,128]{2,1,0:T(8,128)(2,1)}), bf16[32,56,128]{2,1,0:T(8,128)(2,1)S(1)}, u32[]{:S(2)}, u32[]{:S(2)}) async-start(bf16[32,56,128]{2,1,0:T(8,128)(2,1)} %get-tuple-element.31), calls=%async_computation.2 | async-start | bytes 917504 | tf_op jit(solution)/shard_map/all_to_all | solution.py:429
  89.2 3.3 %collective-permute-start.6 = (bf16[4,192,128]{2,1,0:T(8,128)(2,1)S(1)}, bf16[4,192,128]{2,1,0:T(8,128)(2,1)S(1)}, u32[]{:S(2)}, u32[]{:S(2)}) collective-permute-start(bf16[4,192,128]{2,1,0:T(8,128)(2,1)S(1)} %dynamic-slice_bitcast_fusion), channel_id=1, source_target_pairs={{0,4},{4,0},{1,5},{5,1},{2,6},{6,2},{3,7},{7,3},{8,12},{12,8},{9,1... | collective-permute-start | bytes 589832 | tf_op jit(solution)/shard_map/ppermute | solution.py:445
  92.6 10.8 %collective-permute-start.7 = (bf16[192,128]{1,0:T(8,128)(2,1)S(1)}, bf16[192,128]{1,0:T(8,128)(2,1)S(1)}, u32[]{:S(2)}, u32[]{:S(2)}) collective-permute-start(bf16[192,128]{1,0:T(8,128)(2,1)S(1)} %get-tuple-element.44), channel_id=1, source_target_pairs={{0,1},{1,2},{2,3},{3,0},{4,5},{5,6},{6,7},{7,4},{8,9},{9,10},{10,1... | collective-permute-start | bytes 147464 | tf_op jit(solution)/shard_map/ppermute | solution.py:451
  95.9 7.6 %collective-permute-start.8 = (bf16[192,128]{1,0:T(8,128)(2,1)S(1)}, bf16[192,128]{1,0:T(8,128)(2,1)S(1)}, u32[]{:S(2)}, u32[]{:S(2)}) collective-permute-start(bf16[192,128]{1,0:T(8,128)(2,1)S(1)} %get-tuple-element.46), channel_id=1, source_target_pairs={{0,2},{1,3},{2,0},{3,1},{4,6},{5,7},{6,4},{7,5},{8,10},{9,11},{10,... | collective-permute-start | bytes 147464 | tf_op jit(solution)/shard_map/ppermute | solution.py:451
  100.4 5.1 %collective-permute-start.9 = (bf16[192,128]{1,0:T(8,128)(2,1)S(1)}, bf16[192,128]{1,0:T(8,128)(2,1)S(1)}, u32[]{:S(2)}, u32[]{:S(2)}) collective-permute-start(bf16[192,128]{1,0:T(8,128)(2,1)S(1)} %get-tuple-element.45), channel_id=1, source_target_pairs={{0,3},{1,0},{2,1},{3,2},{4,7},{5,4},{6,5},{7,6},{8,11},{9,8},{10,9... | collective-permute-start | bytes 147464 | tf_op jit(solution)/shard_map/ppermute | solution.py:451
  121.2 32.3 %all-to-all-start.3 = ((bf16[32,48,128]{2,1,0:T(8,128)(2,1)}), bf16[32,48,128]{2,1,0:T(8,128)(2,1)S(1)}, u32[]{:S(2)}, u32[]{:S(2)}) async-start(bf16[32,48,128]{2,1,0:T(8,128)(2,1)} %shard_map.178), calls=%async_computation.3 | async-start | bytes 786432 | tf_op jit(solution)/shard_map/all_to_all | solution.py:429
  125.6 6.5 %collective-permute-start.10 = (bf16[32,8,128]{2,1,0:T(8,128)(2,1)S(1)}, bf16[32,8,128]{2,1,0:T(8,128)(2,1)S(1)}, u32[]{:S(2)}, u32[]{:S(2)}) collective-permute-start(bf16[32,8,128]{2,1,0:T(8,128)(2,1)S(1)} %get-tuple-element.43), channel_id=1, source_target_pairs={{384,0},{385,1},{386,2},{387,3},{388,4},{389,5},{390,6},{391,7},{3... | collective-permute-start | bytes 196616 | tf_op jit(solution)/shard_map/ppermute | solution.py:579
  126.9 5.2 %collective-permute-start.11 = (bf16[32,8,128]{2,1,0:T(8,128)(2,1)S(1)}, bf16[32,8,128]{2,1,0:T(8,128)(2,1)S(1)}, u32[]{:S(2)}, u32[]{:S(2)}) collective-permute-start(bf16[32,8,128]{2,1,0:T(8,128)(2,1)S(1)} %get-tuple-element.42), channel_id=1, source_target_pairs={{384,128},{385,129},{386,130},{387,131},{388,132},{389,133},{390,1... | collective-permute-start | bytes 196616 | tf_op jit(solution)/shard_map/ppermute | solution.py:579
  127.5 33.3 %copy-start.3 = (bf16[4,240,128]{2,1,0:T(8,128)(2,1)S(1)}, bf16[4,240,128]{2,1,0:T(8,128)(2,1)}, u32[]{:S(2)}) copy-start(bf16[4,240,128]{2,1,0:T(8,128)(2,1)} %copy-done.2) | copy-start | bytes 737284
  127.5 33.3 %copy-start.9 = (bf16[240,256]{1,0:T(8,128)(2,1)S(1)}, bf16[240,256]{1,0:T(8,128)(2,1)}, u32[]{:S(2)}) copy-start(bf16[240,256]{1,0:T(8,128)(2,1)} %constant.104.clone.forward_ref) | copy-start | bytes 368644
  127.6 4.5 %collective-permute-start.12 = (bf16[32,8,128]{2,1,0:T(8,128)(2,1)S(1)}, bf16[32,8,128]{2,1,0:T(8,128)(2,1)S(1)}, u32[]{:S(2)}, u32[]{:S(2)}) collective-permute-start(bf16[32,8,128]{2,1,0:T(8,128)(2,1)S(1)} %get-tuple-element.41), channel_id=1, source_target_pairs={{384,256},{385,257},{386,258},{387,259},{388,260},{389,261},{390,2... | collective-permute-start | bytes 196616 | tf_op jit(solution)/shard_map/ppermute | solution.py:579
  154.2 15.3 %all-to-all-start.4 = ((bf16[16,24,128]{2,1,0:T(8,128)(2,1)}), bf16[16,24,128]{2,1,0:T(8,128)(2,1)S(1)}, u32[]{:S(2)}, u32[]{:S(2)}) async-start(bf16[16,24,128]{2,1,0:T(8,128)(2,1)} %shard_map.180), calls=%async_computation.4 | async-start | bytes 196608 | tf_op jit(solution)/shard_map/all_to_all | solution.py:429
  157.7 21.7 %collective-permute-start.14 = (bf16[4,240,128]{2,1,0:T(8,128)(2,1)S(1)}, bf16[4,240,128]{2,1,0:T(8,128)(2,1)S(1)}, u32[]{:S(2)}, u32[]{:S(2)}) collective-permute-start(bf16[4,240,128]{2,1,0:T(8,128)(2,1)S(1)} %shard_map.179), channel_id=1, source_target_pairs={{0,128},{128,256},{256,384},{1,129},{129,257},{257,385},{2,130},{1... | collective-permute-start | bytes 737288 | tf_op jit(solution)/shard_map/ppermute | solution.py:435
  161.7 17.7 %collective-permute-start.15 = (bf16[4,240,128]{2,1,0:T(8,128)(2,1)S(1)}, bf16[4,240,128]{2,1,0:T(8,128)(2,1)S(1)}, u32[]{:S(2)}, u32[]{:S(2)}) collective-permute-start(bf16[4,240,128]{2,1,0:T(8,128)(2,1)S(1)} %shard_map.182), channel_id=1, source_target_pairs={{128,0},{256,128},{384,256},{129,1},{257,129},{385,257},{130,2},{2... | collective-permute-start | bytes 737288 | tf_op jit(solution)/shard_map/ppermute | solution.py:435
  170.2 13.8 %all-to-all-start.5 = ((bf16[8,128,128]{2,1,0:T(8,128)(2,1)}), bf16[8,128,128]{2,1,0:T(8,128)(2,1)S(1)}, u32[]{:S(2)}, u32[]{:S(2)}) async-start(bf16[8,128,128]{2,1,0:T(8,128)(2,1)} %shard_map.181), calls=%async_computation.5 | async-start | bytes 524288 | tf_op jit(solution)/shard_map/all_to_all | solution.py:429
  177.5 3.2 %collective-permute-start.13 = (bf16[16,24,128]{2,1,0:T(8,128)(2,1)S(1)}, bf16[16,24,128]{2,1,0:T(8,128)(2,1)S(1)}, u32[]{:S(2)}, u32[]{:S(2)}) collective-permute-start(bf16[16,24,128]{2,1,0:T(8,128)(2,1)S(1)} %all-to-all-done.4.pieces_ref), channel_id=1, source_target_pairs={{0,4},{4,0},{1,5},{5,1},{2,6},{6,2},{3,7},{7,3},{8,12},{12,8},{9,1... | collective-permute-start | bytes 294920 | tf_op jit(solution)/shard_map/ppermute | solution.py:608
  (4 other events, 39.7 us)

commit v14 on v12

--- a/solution.py
+++ b/solution.py
@@ -229,6 +229,7 @@
     ("fresh_inverse", NLON, 256),
     ("inverse_t", 256, NLON),
     ("cotangent", ROWS * NLON, CH),
+    ("saved", ROWS * NLON, CH),
 ):
     PLACES[_name] = (sum(r * -(-c // CH) for _, r, c in PLACES.values()), _rows, _columns)
 PACKED_ROWS = sum(r * -(-c // CH) for _, r, c in PLACES.values())
@@ -278,7 +279,6 @@
 
 
 def mlp_back_kernel(
-    x_ref,
     values_ref,
     packed_ref,
     cycle_ref,
@@ -299,13 +299,14 @@
     names = ("inverse", "inverse_t", "expand", "contract")
     inverse, inverse_t, expand, contract = [unpacked(packed_ref, name) for name in names]
     cotangent = unpacked(packed_ref, "cotangent")
+    saved = unpacked(packed_ref, "saved")
     for half in range(2):
         values = from_blocks(values_ref, half)
         grad_values = []
         for h in range(2):
             j = 2 * half + h
             rows = slice(j * NLON, (j + 1) * NLON)
-            mixed = x_ref[j].astype(F32) + matmul(inverse, values[h])
+            mixed = saved[rows].astype(F32) + matmul(inverse, values[h])
             mixed_b = mixed.astype(BF16)
             masked_f = cotangent[rows].astype(F32) * live(cycle_ref, j)
             masked = masked_f.astype(BF16)
@@ -504,7 +505,7 @@
     )[0]
     saved_at_orders = exchange(saved_blocks, SP)
     kept = [contract, expand, inverse, fresh_inverse, inverse_t]
-    kept += [tokens.reshape(ROWS * NLON, CH) for tokens in (cotangent,)]
+    kept += [tokens.reshape(ROWS * NLON, CH) for tokens in (cotangent, saved,)]
     fresh_own, fresh_lent, packed = call(
         fresh_coeffs_kernel,
         [OWN, LENT, jax.ShapeDtypeStruct((PACKED_ROWS, CH), BF16)],
@@ -552,7 +553,6 @@
             jax.ShapeDtypeStruct((2, 4, HID // 4, CH), BF16),
         ],
         [
-            saved,
             values_fresh,
             packed,
             own_cycles,
@@ -564,7 +564,7 @@
         [narrow, narrow, wide, wide, *SPECTRAL_SCRATCH],
         flops=5 * mlp + 2 * dft + leg,
         transcendentals=2 * ROWS * NLON * HID,
-        smem=(3, 7),
+        smem=(2, 6),
     )
     grads_fresh = exchange(grads_fresh, SP)
     share_blocks = share_blocks_of(shares)

time: 185 us -> 185 us (level)
  waiting for transfers between devices: 89.1 us -> 83.3 us
  local copies, waits for them, and re-layouts: 3.7 us -> 6.8 us
  other arithmetic: 0.25 us -> 2.65 us
    all_to_all x6, waiting for transfers between devices: 80 us -> 73.9 us  [exchange(): return lax.all_to_all(blocks, axes, split_axis=0, concat_axis=0, tiled=True)]
    unnamed x24 -> x32, local copies, waits for them, and re-layouts: 2.79 us -> 4.38 us
  transfers between devices with their start and end apart: 22 -> 22, of which waited for: 11 -> 11; matrix products, arithmetic and copies ran while one was open for 1% -> 3% of each run, Pallas kernels for 3% -> 3%
where the time goes in v14:
time: 185 us; the launch traced here: 184 us
  waiting for transfers between devices  83.3 us (45%)
  starting transfers between devices  74.2 us (40%)
  Pallas kernels  15.5 us (8%)
  local copies, waits for them, and re-layouts  6.8 us (4%)
  other arithmetic  2.65 us (1%)
    all_to_all x6, waiting for transfers between devices, exchange(): return lax.all_to_all(blocks, axes, split_axis=0, concat_axis=0, tiled=True)  73.9 us
    all_to_all x6, starting transfers between devices, exchange(): return lax.all_to_all(blocks, axes, split_axis=0, concat_axis=0, tiled=True)  40.8 us
    pallas_call x11, Pallas kernels, call(): pl.pallas_call(kernel, out_shape=outs, in_specs=specs, out_specs=[pl.Bloc...  15.5 us
    ppermute x6, starting transfers between devices, to_last(): return [lax.ppermute(block, 'pipe', [(p, 3)]) for p in range(3)]  11.4 us
    ppermute x3, starting transfers between devices, around(): lax.ppermute(block, axis, [(i, (i + distance) % count) for i in range(cou...  10.7 us
    ppermute x2, starting transfers between devices, from_behind(): return lax.ppermute(block, axis, route)  4.41 us
    unnamed x32, local copies, waits for them, and re-layouts  4.38 us
    ppermute x3, waiting for transfers between devices, on_device(): lax.ppermute(grads_fresh[:, 32 + 8 * p:40 + 8 * p], 'pipe', [(3, p)])  3.72 us
  transfers between devices with their start and end apart: 22, of which 11 were waited for; matrix products, arithmetic and copies ran while one was open for 3% of the time, Pallas kernels for 3%

profile of v14, /device:TPU:1, one launch (start us, length us, event | category | flops | bytes accessed | tf_op | source)
XLA Modules:
  0.0 183.7 jit_solution(223283113408087919)
XLA Ops:
  0.7 2.2 %shard_map.173 = bf16[32,32,128]{2,1,0:T(8,128)(2,1)} custom-call(bf16[4,240,128]{2,1,0:T(8,128)(2,1)} %bitcast.49, bf16[256,240]{1,0:T(8,128)(2,1)} %constant.107.clone.forward_hbm), custom_call_target="tpu_custom_call" | custom-call | flops 62914560 | bytes 630784 | tf_op jit(solution)/shard_map/pallas_call | solution.py:398
  2.9 16.8 %all-to-all-start = ((bf16[32,32,128]{2,1,0:T(8,128)(2,1)}), bf16[32,32,128]{2,1,0:T(8,128)(2,1)S(1)}, u32[]{:S(2)}, u32[]{:S(2)}) async-start(bf16[32,32,128]{2,1,0:T(8,128)(2,1)} %shard_map.173), calls=%async_computation | async-start | bytes 524288 | tf_op jit(solution)/shard_map/all_to_all | solution.py:424
  23.8 4.4 %collective-permute-start = (bf16[32,8,128]{2,1,0:T(8,128)(2,1)S(1)}, bf16[32,8,128]{2,1,0:T(8,128)(2,1)S(1)}, u32[]{:S(2)}, u32[]{:S(2)}) collective-permute-start(bf16[32,8,128]{2,1,0:T(8,128)(2,1)S(1)} %get-tuple-element.25), channel_id=1, source_target_pairs={{0,384},{1,385},{2,386},{3,387},{4,388},{5,389},{6,390},{7,391},{8... | collective-permute-start | bytes 196616 | tf_op jit(solution)/shard_map/ppermute | solution.py:434
  31.0 10.7 %all-to-all-done.arrived_ref = bf16[32,32,128]{2,1,0:T(8,128)(2,1)S(1)} async-done(((bf16[32,32,128]{2,1,0:T(8,128)(2,1)}), bf16[32,32,128]{2,1,0:T(8,128)(2,1)S(1)}, u32[]{:S(2)}, u32[]{:S(2)}) %all-to-all-start) | async-done | bytes 262176 | tf_op jit(solution)/shard_map/all_to_all | solution.py:424
  41.7 1.3 shard_map.176
  43.7 4.5 %all-to-all-start.1 = ((bf16[32,56,128]{2,1,0:T(8,128)(2,1)}), bf16[32,56,128]{2,1,0:T(8,128)(2,1)S(1)}, u32[]{:S(2)}, u32[]{:S(2)}) async-start(bf16[32,56,128]{2,1,0:T(8,128)(2,1)} %get-tuple-element.28), calls=%async_computation.1 | async-start | bytes 917504 | tf_op jit(solution)/shard_map/all_to_all | solution.py:424
  48.2 4.4 %collective-permute-start.3 = (f32[2,120,128]{2,1,0:T(8,128)S(1)}, f32[2,120,128]{2,1,0:T(8,128)S(1)}, u32[]{:S(2)}, u32[]{:S(2)}) collective-permute-start(f32[2,120,128]{2,1,0:T(8,128)S(1)} %bitcast.44), channel_id=1, source_target_pairs={{0,384},{1,385},{2,386},{3,387},{4,388},{5,389},{6,390},{7,391},{8... | collective-permute-start | bytes 368648 | tf_op jit(solution)/shard_map/ppermute | solution.py:434
  54.9 24.1 %all-to-all-done.1.values_ref = bf16[32,56,128]{2,1,0:T(8,128)(2,1)S(1)} async-done(((bf16[32,56,128]{2,1,0:T(8,128)(2,1)}), bf16[32,56,128]{2,1,0:T(8,128)(2,1)S(1)}, u32[]{:S(2)}, u32[]{:S(2)}) %all-to-all-start.1) | async-done | bytes 458784 | tf_op jit(solution)/shard_map/all_to_all | solution.py:424
  79.0 4.4 %shard_map.177 = (bf16[32,56,128]{2,1,0:T(8,128)(2,1)}, bf16[4,240,128]{2,1,0:T(8,128)(2,1)S(1)}, bf16[2,4,192,128]{3,2,1,0:T(8,128)(2,1)S(1)}) custom-call(bf16[32,56,128]{2,1,0:T(8,128)(2,1)S(1)} %all-to-all-done.1.values_ref, bf16[4928,128]{1,0:T(8,128)(2,1)S(1)} %get-tuple-element.29.packed_ref, s32[4]{0:T(128)S(1)} %dynamic_slice.28.cycle_ref, ...), custom_call_target="tpu_custom_call" | custom-call | flops 1136656384 | bytes 3448852 | tf_op jit(solution)/shard_map/pallas_call | solution.py:398
  83.5 4.4 %all-to-all-start.2 = ((bf16[32,56,128]{2,1,0:T(8,128)(2,1)}), bf16[32,56,128]{2,1,0:T(8,128)(2,1)S(1)}, u32[]{:S(2)}, u32[]{:S(2)}) async-start(bf16[32,56,128]{2,1,0:T(8,128)(2,1)} %get-tuple-element.31), calls=%async_computation.2 | async-start | bytes 917504 | tf_op jit(solution)/shard_map/all_to_all | solution.py:424
  88.6 2.2 %collective-permute-start.6 = (bf16[4,192,128]{2,1,0:T(8,128)(2,1)}, bf16[4,192,128]{2,1,0:T(8,128)(2,1)}, u32[]{:S(2)}, u32[]{:S(2)}) collective-permute-start(bf16[4,192,128]{2,1,0:T(8,128)(2,1)} %dynamic-slice_bitcast_fusion), channel_id=1, source_target_pairs={{0,4},{4,0},{1,5},{5,1},{2,6},{6,2},{3,7},{7,3},{8,12},{12,8},{9,1... | collective-permute-start | bytes 589832 | tf_op jit(solution)/shard_map/ppermute | solution.py:440
  90.9 1.4 collective-permute-done.6
  92.3 1.7 fusion
  94.8 3.2 %collective-permute-start.7 = (bf16[192,128]{1,0:T(8,128)(2,1)S(1)}, bf16[192,128]{1,0:T(8,128)(2,1)S(1)}, u32[]{:S(2)}, u32[]{:S(2)}) collective-permute-start(bf16[192,128]{1,0:T(8,128)(2,1)S(1)} %get-tuple-element.44), channel_id=1, source_target_pairs={{0,1},{1,2},{2,3},{3,0},{4,5},{5,6},{6,7},{7,4},{8,9},{9,10},{10,1... | collective-permute-start | bytes 147464 | tf_op jit(solution)/shard_map/ppermute | solution.py:446
  98.0 4.5 %collective-permute-start.8 = (bf16[192,128]{1,0:T(8,128)(2,1)S(1)}, bf16[192,128]{1,0:T(8,128)(2,1)S(1)}, u32[]{:S(2)}, u32[]{:S(2)}) collective-permute-start(bf16[192,128]{1,0:T(8,128)(2,1)S(1)} %get-tuple-element.46), channel_id=1, source_target_pairs={{0,2},{1,3},{2,0},{3,1},{4,6},{5,7},{6,4},{7,5},{8,10},{9,11},{10,... | collective-permute-start | bytes 147464 | tf_op jit(solution)/shard_map/ppermute | solution.py:446
  102.5 3.0 %collective-permute-start.9 = (bf16[192,128]{1,0:T(8,128)(2,1)S(1)}, bf16[192,128]{1,0:T(8,128)(2,1)S(1)}, u32[]{:S(2)}, u32[]{:S(2)}) collective-permute-start(bf16[192,128]{1,0:T(8,128)(2,1)S(1)} %get-tuple-element.45), channel_id=1, source_target_pairs={{0,3},{1,0},{2,1},{3,2},{4,7},{5,4},{6,5},{7,6},{8,11},{9,8},{10,9... | collective-permute-start | bytes 147464 | tf_op jit(solution)/shard_map/ppermute | solution.py:446
  105.5 2.1 %collective-permute-done.9 = bf16[192,128]{1,0:T(8,128)(2,1)S(1)} collective-permute-done((bf16[192,128]{1,0:T(8,128)(2,1)S(1)}, bf16[192,128]{1,0:T(8,128)(2,1)S(1)}, u32[]{:S(2)}, u32[]{:S(2)}) %collective-permute-start.9) | collective-permute-done | bytes 49184 | tf_op jit(solution)/shard_map/ppermute | solution.py:446
  108.5 10.1 %all-to-all-done.2.arrived_ref.values_ref = bf16[32,56,128]{2,1,0:T(8,128)(2,1)S(1)} async-done(((bf16[32,56,128]{2,1,0:T(8,128)(2,1)}), bf16[32,56,128]{2,1,0:T(8,128)(2,1)S(1)}, u32[]{:S(2)}, u32[]{:S(2)}) %all-to-all-start.2) | async-done | bytes 458784 | tf_op jit(solution)/shard_map/all_to_all | solution.py:424
  118.7 1.3 shard_map.178
  119.9 4.3 %all-to-all-start.3 = ((bf16[32,48,128]{2,1,0:T(8,128)(2,1)}), bf16[32,48,128]{2,1,0:T(8,128)(2,1)S(1)}, u32[]{:S(2)}, u32[]{:S(2)}) async-start(bf16[32,48,128]{2,1,0:T(8,128)(2,1)} %shard_map.178), calls=%async_computation.3 | async-start | bytes 786432 | tf_op jit(solution)/shard_map/all_to_all | solution.py:424
  124.3 1.3 collective-permute-start.10
  127.1 3.7 %collective-permute-done.10.lent_a_ref = bf16[32,8,128]{2,1,0:T(8,128)(2,1)S(1)} collective-permute-done((bf16[32,8,128]{2,1,0:T(8,128)(2,1)S(1)}, bf16[32,8,128]{2,1,0:T(8,128)(2,1)S(1)}, u32[]{:S(2)}, u32[]{:S(2)}) %collective-permute-start.10) | collective-permute-done | bytes 65568 | tf_op jit(solution)/shard_map/ppermute | solution.py:573
  130.8 2.2 %shard_map.179 = bf16[4,240,128]{2,1,0:T(8,128)(2,1)S(1)} custom-call(bf16[4,240,128]{2,1,0:T(8,128)(2,1)S(1)} %bitcast.52, bf16[32,56,128]{2,1,0:T(8,128)(2,1)S(1)} %all-to-all-done.2.arrived_ref.values_ref, bf16[32,8,128]{2,1,0:T(8,128)(2,1)S(1)} %collective-permute-done.10.lent_a_ref, bf16[32,8,128]{2,1,0:T(8,128)(2,1)S(1)} %collective-permute-done.11.lent_b_ref, ...), custom_call_target="tpu_custom_call" | custom-call | flops 440401920 | bytes 2408464 | tf_op jit(solution)/shard_map/pallas_call | solution.py:398
  133.0 19.2 %all-to-all-done.3.arrived_ref.coeffs_ref = bf16[32,48,128]{2,1,0:T(8,128)(2,1)S(1)} async-done(((bf16[32,48,128]{2,1,0:T(8,128)(2,1)}), bf16[32,48,128]{2,1,0:T(8,128)(2,1)S(1)}, u32[]{:S(2)}, u32[]{:S(2)}) %all-to-all-start.3) | async-done | bytes 393248 | tf_op jit(solution)/shard_map/all_to_all | solution.py:424
  152.9 3.5 %all-to-all-start.4 = ((bf16[16,24,128]{2,1,0:T(8,128)(2,1)}), bf16[16,24,128]{2,1,0:T(8,128)(2,1)S(1)}, u32[]{:S(2)}, u32[]{:S(2)}) async-start(bf16[16,24,128]{2,1,0:T(8,128)(2,1)} %shard_map.180), calls=%async_computation.4 | async-start | bytes 196608 | tf_op jit(solution)/shard_map/all_to_all | solution.py:424
  156.4 3.1 %collective-permute-start.14 = (bf16[4,240,128]{2,1,0:T(8,128)(2,1)S(1)}, bf16[4,240,128]{2,1,0:T(8,128)(2,1)S(1)}, u32[]{:S(2)}, u32[]{:S(2)}) collective-permute-start(bf16[4,240,128]{2,1,0:T(8,128)(2,1)S(1)} %shard_map.179), channel_id=1, source_target_pairs={{0,128},{128,256},{256,384},{1,129},{129,257},{257,385},{2,130},{1... | collective-permute-start | bytes 737288 | tf_op jit(solution)/shard_map/ppermute | solution.py:430
  160.4 1.3 collective-permute-start.15
  161.7 6.5 %all-to-all-done.4.pieces_ref = bf16[16,24,128]{2,1,0:T(8,128)(2,1)S(1)} async-done(((bf16[16,24,128]{2,1,0:T(8,128)(2,1)}), bf16[16,24,128]{2,1,0:T(8,128)(2,1)S(1)}, u32[]{:S(2)}, u32[]{:S(2)}) %all-to-all-start.4) | async-done | bytes 98336 | tf_op jit(solution)/shard_map/all_to_all | solution.py:424
  168.9 7.2 %all-to-all-start.5 = ((bf16[8,128,128]{2,1,0:T(8,128)(2,1)}), bf16[8,128,128]{2,1,0:T(8,128)(2,1)S(1)}, u32[]{:S(2)}, u32[]{:S(2)}) async-start(bf16[8,128,128]{2,1,0:T(8,128)(2,1)} %shard_map.181), calls=%async_computation.5 | async-start | bytes 524288 | tf_op jit(solution)/shard_map/all_to_all | solution.py:424
  176.2 1.9 %collective-permute-start.13 = (bf16[16,24,128]{2,1,0:T(8,128)(2,1)S(1)}, bf16[16,24,128]{2,1,0:T(8,128)(2,1)S(1)}, u32[]{:S(2)}, u32[]{:S(2)}) collective-permute-start(bf16[16,24,128]{2,1,0:T(8,128)(2,1)S(1)} %all-to-all-done.4.pieces_ref), channel_id=1, source_target_pairs={{0,4},{4,0},{1,5},{5,1},{2,6},{6,2},{3,7},{7,3},{8,12},{12,8},{9,1... | collective-permute-start | bytes 294920 | tf_op jit(solution)/shard_map/ppermute | solution.py:602
  178.1 1.2 collective-permute-done.13.other_ref
  179.4 3.4 %all-to-all-done.5.filter_rows_ref = bf16[8,128,128]{2,1,0:T(8,128)(2,1)S(1)} async-done(((bf16[8,128,128]{2,1,0:T(8,128)(2,1)}), bf16[8,128,128]{2,1,0:T(8,128)(2,1)S(1)}, u32[]{:S(2)}, u32[]{:S(2)}) %all-to-all-start.5) | async-done | bytes 262176 | tf_op jit(solution)/shard_map/all_to_all | solution.py:424
  (69 shorter events, 17.0 us)
Async XLA Ops:
  0.6 19.1 %copy-start.1 = (bf16[1,1,4,240,128]{4,3,2,1,0:T(8,128)(2,1)S(1)}, bf16[1,1,4,240,128]{4,3,2,1,0:T(8,128)(2,1)}, u32[]{:S(2)}) copy-start(bf16[1,1,4,240,128]{4,3,2,1,0:T(8,128)(2,1)} %param.15) | copy-start | bytes 737284
  0.6 19.1 %copy-start.2 = (bf16[1,1,4,240,128]{4,3,2,1,0:T(8,128)(2,1)S(1)}, bf16[1,1,4,240,128]{4,3,2,1,0:T(8,128)(2,1)}, u32[]{:S(2)}) copy-start(bf16[1,1,4,240,128]{4,3,2,1,0:T(8,128)(2,1)} %param.14) | copy-start | bytes 737284
  0.7 19.1 %copy-start.5 = (bf16[1,1,4,240,128]{4,3,2,1,0:T(8,128)(2,1)S(1)}, bf16[1,1,4,240,128]{4,3,2,1,0:T(8,128)(2,1)}, u32[]{:S(2)}) copy-start(bf16[1,1,4,240,128]{4,3,2,1,0:T(8,128)(2,1)} %param.16) | copy-start | bytes 737284
  0.7 19.1 %copy-start.8 = (bf16[1,768,128]{2,1,0:T(8,128)(2,1)S(1)}, bf16[1,768,128]{2,1,0:T(8,128)(2,1)}, u32[]{:S(2)}) copy-start(bf16[1,768,128]{2,1,0:T(8,128)(2,1)} %param.18) | copy-start | bytes 589828
  2.9 27.4 %copy-start.15 = (s32[128]{0:T(128)S(1)}, s32[128]{0:T(128)}, u32[]{:S(2)}) copy-start(s32[128]{0:T(128)} %param.20) | copy-start | bytes 1540
  2.9 38.8 %all-to-all-start = ((bf16[32,32,128]{2,1,0:T(8,128)(2,1)}), bf16[32,32,128]{2,1,0:T(8,128)(2,1)S(1)}, u32[]{:S(2)}, u32[]{:S(2)}) async-start(bf16[32,32,128]{2,1,0:T(8,128)(2,1)} %shard_map.173), calls=%async_computation | async-start | bytes 524288 | tf_op jit(solution)/shard_map/all_to_all | solution.py:424
  19.7 22.0 %copy-start = (f32[1,2,120,128]{3,2,1,0:T(8,128)S(1)}, f32[1,2,120,128]{3,2,1,0:T(8,128)}, u32[]{:S(2)}) copy-start(f32[1,2,120,128]{3,2,1,0:T(8,128)} %param.19) | copy-start | bytes 368644
  23.8 7.1 %collective-permute-start = (bf16[32,8,128]{2,1,0:T(8,128)(2,1)S(1)}, bf16[32,8,128]{2,1,0:T(8,128)(2,1)S(1)}, u32[]{:S(2)}, u32[]{:S(2)}) collective-permute-start(bf16[32,8,128]{2,1,0:T(8,128)(2,1)S(1)} %get-tuple-element.25), channel_id=1, source_target_pairs={{0,384},{1,385},{2,386},{3,387},{4,388},{5,389},{6,390},{7,391},{8... | collective-permute-start | bytes 196616 | tf_op jit(solution)/shard_map/ppermute | solution.py:434
  28.2 2.7 %collective-permute-start.1 = (bf16[32,8,128]{2,1,0:T(8,128)(2,1)S(1)}, bf16[32,8,128]{2,1,0:T(8,128)(2,1)S(1)}, u32[]{:S(2)}, u32[]{:S(2)}) collective-permute-start(bf16[32,8,128]{2,1,0:T(8,128)(2,1)S(1)} %get-tuple-element.25), channel_id=1, source_target_pairs={{128,384},{129,385},{130,386},{131,387},{132,388},{133,389},{134,3... | collective-permute-start | bytes 196616 | tf_op jit(solution)/shard_map/ppermute | solution.py:434
  28.9 2.1 %collective-permute-start.2 = (bf16[32,8,128]{2,1,0:T(8,128)(2,1)S(1)}, bf16[32,8,128]{2,1,0:T(8,128)(2,1)S(1)}, u32[]{:S(2)}, u32[]{:S(2)}) collective-permute-start(bf16[32,8,128]{2,1,0:T(8,128)(2,1)S(1)} %get-tuple-element.25), channel_id=1, source_target_pairs={{256,384},{257,385},{258,386},{259,387},{260,388},{261,389},{262,3... | collective-permute-start | bytes 196616 | tf_op jit(solution)/shard_map/ppermute | solution.py:434
  43.7 35.3 %all-to-all-start.1 = ((bf16[32,56,128]{2,1,0:T(8,128)(2,1)}), bf16[32,56,128]{2,1,0:T(8,128)(2,1)S(1)}, u32[]{:S(2)}, u32[]{:S(2)}) async-start(bf16[32,56,128]{2,1,0:T(8,128)(2,1)} %get-tuple-element.28), calls=%async_computation.1 | async-start | bytes 917504 | tf_op jit(solution)/shard_map/all_to_all | solution.py:424
  48.2 6.7 %collective-permute-start.3 = (f32[2,120,128]{2,1,0:T(8,128)S(1)}, f32[2,120,128]{2,1,0:T(8,128)S(1)}, u32[]{:S(2)}, u32[]{:S(2)}) collective-permute-start(f32[2,120,128]{2,1,0:T(8,128)S(1)} %bitcast.44), channel_id=1, source_target_pairs={{0,384},{1,385},{2,386},{3,387},{4,388},{5,389},{6,390},{7,391},{8... | collective-permute-start | bytes 368648 | tf_op jit(solution)/shard_map/ppermute | solution.py:434
  52.6 2.3 %collective-permute-start.4 = (f32[2,120,128]{2,1,0:T(8,128)S(1)}, f32[2,120,128]{2,1,0:T(8,128)S(1)}, u32[]{:S(2)}, u32[]{:S(2)}) collective-permute-start(f32[2,120,128]{2,1,0:T(8,128)S(1)} %bitcast.45), channel_id=1, source_target_pairs={{128,384},{129,385},{130,386},{131,387},{132,388},{133,389},{134,3... | collective-permute-start | bytes 368648 | tf_op jit(solution)/shard_map/ppermute | solution.py:434
  53.3 1.6 collective-permute-start.5
  83.4 25.0 %copy-start.6 = (bf16[4,240,128]{2,1,0:T(8,128)(2,1)}, bf16[4,240,128]{2,1,0:T(8,128)(2,1)S(1)}, u32[]{:S(2)}) copy-start(bf16[4,240,128]{2,1,0:T(8,128)(2,1)S(1)} %get-tuple-element.35.grad_mixed_ref) | copy-start | bytes 737284
  83.4 35.2 %copy-start.4 = (bf16[4,128,256]{2,1,0:T(8,128)(2,1)S(1)}, bf16[4,128,256]{2,1,0:T(8,128)(2,1)}, u32[]{:S(2)}) copy-start(bf16[4,128,256]{2,1,0:T(8,128)(2,1)} %copy-done.3) | copy-start | bytes 786436
  83.5 35.2 %all-to-all-start.2 = ((bf16[32,56,128]{2,1,0:T(8,128)(2,1)}), bf16[32,56,128]{2,1,0:T(8,128)(2,1)S(1)}, u32[]{:S(2)}, u32[]{:S(2)}) async-start(bf16[32,56,128]{2,1,0:T(8,128)(2,1)} %get-tuple-element.31), calls=%async_computation.2 | async-start | bytes 917504 | tf_op jit(solution)/shard_map/all_to_all | solution.py:424
  88.6 3.7 %collective-permute-start.6 = (bf16[4,192,128]{2,1,0:T(8,128)(2,1)}, bf16[4,192,128]{2,1,0:T(8,128)(2,1)}, u32[]{:S(2)}, u32[]{:S(2)}) collective-permute-start(bf16[4,192,128]{2,1,0:T(8,128)(2,1)} %dynamic-slice_bitcast_fusion), channel_id=1, source_target_pairs={{0,4},{4,0},{1,5},{5,1},{2,6},{6,2},{3,7},{7,3},{8,12},{12,8},{9,1... | collective-permute-start | bytes 589832 | tf_op jit(solution)/shard_map/ppermute | solution.py:440
  94.8 10.7 %collective-permute-start.7 = (bf16[192,128]{1,0:T(8,128)(2,1)S(1)}, bf16[192,128]{1,0:T(8,128)(2,1)S(1)}, u32[]{:S(2)}, u32[]{:S(2)}) collective-permute-start(bf16[192,128]{1,0:T(8,128)(2,1)S(1)} %get-tuple-element.44), channel_id=1, source_target_pairs={{0,1},{1,2},{2,3},{3,0},{4,5},{5,6},{6,7},{7,4},{8,9},{9,10},{10,1... | collective-permute-start | bytes 147464 | tf_op jit(solution)/shard_map/ppermute | solution.py:446
  98.0 7.5 %collective-permute-start.8 = (bf16[192,128]{1,0:T(8,128)(2,1)S(1)}, bf16[192,128]{1,0:T(8,128)(2,1)S(1)}, u32[]{:S(2)}, u32[]{:S(2)}) collective-permute-start(bf16[192,128]{1,0:T(8,128)(2,1)S(1)} %get-tuple-element.46), channel_id=1, source_target_pairs={{0,2},{1,3},{2,0},{3,1},{4,6},{5,7},{6,4},{7,5},{8,10},{9,11},{10,... | collective-permute-start | bytes 147464 | tf_op jit(solution)/shard_map/ppermute | solution.py:446
  102.5 5.1 %collective-permute-start.9 = (bf16[192,128]{1,0:T(8,128)(2,1)S(1)}, bf16[192,128]{1,0:T(8,128)(2,1)S(1)}, u32[]{:S(2)}, u32[]{:S(2)}) collective-permute-start(bf16[192,128]{1,0:T(8,128)(2,1)S(1)} %get-tuple-element.45), channel_id=1, source_target_pairs={{0,3},{1,0},{2,1},{3,2},{4,7},{5,4},{6,5},{7,6},{8,11},{9,8},{10,9... | collective-permute-start | bytes 147464 | tf_op jit(solution)/shard_map/ppermute | solution.py:446
  119.9 32.3 %all-to-all-start.3 = ((bf16[32,48,128]{2,1,0:T(8,128)(2,1)}), bf16[32,48,128]{2,1,0:T(8,128)(2,1)S(1)}, u32[]{:S(2)}, u32[]{:S(2)}) async-start(bf16[32,48,128]{2,1,0:T(8,128)(2,1)} %shard_map.178), calls=%async_computation.3 | async-start | bytes 786432 | tf_op jit(solution)/shard_map/all_to_all | solution.py:424
  124.3 6.5 %collective-permute-start.10 = (bf16[32,8,128]{2,1,0:T(8,128)(2,1)S(1)}, bf16[32,8,128]{2,1,0:T(8,128)(2,1)S(1)}, u32[]{:S(2)}, u32[]{:S(2)}) collective-permute-start(bf16[32,8,128]{2,1,0:T(8,128)(2,1)S(1)} %get-tuple-element.43), channel_id=1, source_target_pairs={{384,0},{385,1},{386,2},{387,3},{388,4},{389,5},{390,6},{391,7},{3... | collective-permute-start | bytes 196616 | tf_op jit(solution)/shard_map/ppermute | solution.py:573
  125.6 5.2 %collective-permute-start.11 = (bf16[32,8,128]{2,1,0:T(8,128)(2,1)S(1)}, bf16[32,8,128]{2,1,0:T(8,128)(2,1)S(1)}, u32[]{:S(2)}, u32[]{:S(2)}) collective-permute-start(bf16[32,8,128]{2,1,0:T(8,128)(2,1)S(1)} %get-tuple-element.42), channel_id=1, source_target_pairs={{384,128},{385,129},{386,130},{387,131},{388,132},{389,133},{390,1... | collective-permute-start | bytes 196616 | tf_op jit(solution)/shard_map/ppermute | solution.py:573
  126.2 33.3 %copy-start.7 = (bf16[4,240,128]{2,1,0:T(8,128)(2,1)S(1)}, bf16[4,240,128]{2,1,0:T(8,128)(2,1)}, u32[]{:S(2)}) copy-start(bf16[4,240,128]{2,1,0:T(8,128)(2,1)} %copy-done.6) | copy-start | bytes 737284
  126.3 33.3 %copy-start.12 = (bf16[240,256]{1,0:T(8,128)(2,1)S(1)}, bf16[240,256]{1,0:T(8,128)(2,1)}, u32[]{:S(2)}) copy-start(bf16[240,256]{1,0:T(8,128)(2,1)} %constant.104.clone.forward_ref) | copy-start | bytes 368644
  126.3 4.5 %collective-permute-start.12 = (bf16[32,8,128]{2,1,0:T(8,128)(2,1)S(1)}, bf16[32,8,128]{2,1,0:T(8,128)(2,1)S(1)}, u32[]{:S(2)}, u32[]{:S(2)}) collective-permute-start(bf16[32,8,128]{2,1,0:T(8,128)(2,1)S(1)} %get-tuple-element.41), channel_id=1, source_target_pairs={{384,256},{385,257},{386,258},{387,259},{388,260},{389,261},{390,2... | collective-permute-start | bytes 196616 | tf_op jit(solution)/shard_map/ppermute | solution.py:573
  152.9 15.3 %all-to-all-start.4 = ((bf16[16,24,128]{2,1,0:T(8,128)(2,1)}), bf16[16,24,128]{2,1,0:T(8,128)(2,1)S(1)}, u32[]{:S(2)}, u32[]{:S(2)}) async-start(bf16[16,24,128]{2,1,0:T(8,128)(2,1)} %shard_map.180), calls=%async_computation.4 | async-start | bytes 196608 | tf_op jit(solution)/shard_map/all_to_all | solution.py:424
  156.4 21.6 %collective-permute-start.14 = (bf16[4,240,128]{2,1,0:T(8,128)(2,1)S(1)}, bf16[4,240,128]{2,1,0:T(8,128)(2,1)S(1)}, u32[]{:S(2)}, u32[]{:S(2)}) collective-permute-start(bf16[4,240,128]{2,1,0:T(8,128)(2,1)S(1)} %shard_map.179), channel_id=1, source_target_pairs={{0,128},{128,256},{256,384},{1,129},{129,257},{257,385},{2,130},{1... | collective-permute-start | bytes 737288 | tf_op jit(solution)/shard_map/ppermute | solution.py:430
  160.4 17.7 %collective-permute-start.15 = (bf16[4,240,128]{2,1,0:T(8,128)(2,1)S(1)}, bf16[4,240,128]{2,1,0:T(8,128)(2,1)S(1)}, u32[]{:S(2)}, u32[]{:S(2)}) collective-permute-start(bf16[4,240,128]{2,1,0:T(8,128)(2,1)S(1)} %shard_map.182), channel_id=1, source_target_pairs={{128,0},{256,128},{384,256},{129,1},{257,129},{385,257},{130,2},{2... | collective-permute-start | bytes 737288 | tf_op jit(solution)/shard_map/ppermute | solution.py:430
  168.9 13.8 %all-to-all-start.5 = ((bf16[8,128,128]{2,1,0:T(8,128)(2,1)}), bf16[8,128,128]{2,1,0:T(8,128)(2,1)S(1)}, u32[]{:S(2)}, u32[]{:S(2)}) async-start(bf16[8,128,128]{2,1,0:T(8,128)(2,1)} %shard_map.181), calls=%async_computation.5 | async-start | bytes 524288 | tf_op jit(solution)/shard_map/all_to_all | solution.py:424
  176.2 3.2 %collective-permute-start.13 = (bf16[16,24,128]{2,1,0:T(8,128)(2,1)S(1)}, bf16[16,24,128]{2,1,0:T(8,128)(2,1)S(1)}, u32[]{:S(2)}, u32[]{:S(2)}) collective-permute-start(bf16[16,24,128]{2,1,0:T(8,128)(2,1)S(1)} %all-to-all-done.4.pieces_ref), channel_id=1, source_target_pairs={{0,4},{4,0},{1,5},{5,1},{2,6},{6,2},{3,7},{7,3},{8,12},{12,8},{9,1... | collective-permute-start | bytes 294920 | tf_op jit(solution)/shard_map/ppermute | solution.py:602
  (6 other events, 23.4 us)
